TPU v7x, 32 devices: a whole 2x2x4 slice. The times are simulated.
32 devices in a mesh: dp: 8 (over z, y), mp: 4 (over x, core).
Axes of the slice: x: 2, y: 2, z: 4, core: 2. Of those that a mesh axis runs over, the one named last changes fastest.
Arguments:
- queries: bfloat16 [3072, 4096], P('dp', 'mp'), may hold values from -16 to 16
- states: bfloat16 [64, 128, 896], P('dp', 'mp'), may hold values from -6 to 6
- key_weight: bfloat16 [896, 4096], P(None, 'mp'), may hold values from -0.1875 to 0.1875
- value_weight: bfloat16 [896, 4096], P(None, 'mp'), may hold values from -0.1875 to 0.1875
- nbr_shard: int32 [48, 2], P('dp'), may hold values from 0 to 7, all different within a row; in each aligned block of 6 rows (0 to 5, 6 to 11, ...) at most 2 rows name the same one
- nbr_row: int32 [48, 2], P('dp'), may hold values from 0 to 7
- out_grad: bfloat16 [3072, 4096], P('dp', 'mp'), may hold values from -6 to 6
Outputs:
- attended: bfloat16 [3072, 4096], P('dp', 'mp')
- query_grad: bfloat16 [3072, 4096], P('dp', 'mp')
- state_grad: float32 [64, 128, 896], P('dp', 'mp')
- key_weight_grad: float32 [896, 4096], P(None, 'mp')
- value_weight_grad: float32 [896, 4096], P(None, 'mp')
Inputs may be any that keep to these rules, and one draw needn't show every extreme that they name: `nbr_shard`: the 2 neighbours of a span lie on different shards; among the 6 spans of one device at most 2 neighbours lie on one shard, and some shard takes exactly 2 of them.
All inputs are finite; a program needn't handle non-finite values.
Results may differ from a plain program's by a relative error of at most 0.02.
Values may be sent and summed in bfloat16 or wider, within the bound.
No kernel may reach another device: no remote copies, remote signals or barrier semaphores. Data moves between devices by JAX's collectives and lax.ppermute only.
A program may use at most 128 MiB of HBM per device.

v0:
```python
import jax
import jax.numpy as jnp
from jax import lax
from jax.sharding import PartitionSpec as P

D = 4096
H = 32


def body(queries, states, key_weight, value_weight, nbr_shard, nbr_row, out_grad):
    shards = lax.axis_size("dp")
    groups = lax.axis_size("mp")
    spans, neighbours = nbr_shard.shape
    pair_count = spans * neighbours
    tokens, local_width = queries.shape
    span_len = tokens // spans
    slab_len = states.shape[1]
    enc_width = states.shape[2]
    full_len = slab_len * groups
    head_dim = D // H
    local_heads = local_width // head_dim
    capacity = max(2, (pair_count + shards - 1) // shards)
    slot_count = shards * capacity
    owners = nbr_shard.reshape(pair_count)
    row_index = nbr_row.reshape(pair_count)
    owner_hot = (owners[:, None] == jnp.arange(shards, dtype=jnp.int32)[None, :]).astype(jnp.int32)
    earlier = (jnp.arange(pair_count)[:, None] > jnp.arange(pair_count)[None, :]).astype(jnp.int32)
    before_count = jnp.dot(earlier, owner_hot)
    ranking = jnp.sum(before_count * owner_hot, axis=1)
    slot_index = owners * capacity + ranking
    matched = slot_index[:, None] == jnp.arange(slot_count, dtype=jnp.int32)[None, :]
    asked_rows = jnp.sum(jnp.where(matched, row_index[:, None], 0), axis=0).reshape(
        shards, capacity
    )
    incoming = lax.all_to_all(asked_rows, "dp", split_axis=0, concat_axis=0, tiled=True)
    slab_rows = jnp.take(states, incoming, axis=0)
    sent_back = lax.all_to_all(slab_rows, "dp", split_axis=0, concat_axis=0, tiled=True)
    flat_recv = sent_back.reshape(slot_count, slab_len, enc_width)
    picked = jnp.take(flat_recv, slot_index, axis=0)
    gathered = lax.all_gather(picked, "mp", axis=1, tiled=True)
    rows_all = gathered.reshape(pair_count * full_len, enc_width)
    key_rows = jnp.dot(rows_all, key_weight, preferred_element_type=jnp.float32).astype(
        jnp.bfloat16
    )
    value_rows = jnp.dot(rows_all, value_weight, preferred_element_type=jnp.float32).astype(
        jnp.bfloat16
    )
    key_heads = key_rows.reshape(spans, neighbours * full_len, local_heads, head_dim)
    value_heads = value_rows.reshape(spans, neighbours * full_len, local_heads, head_dim)
    query_heads = queries.reshape(spans, span_len, local_heads, head_dim)
    grad_heads = out_grad.reshape(spans, span_len, local_heads, head_dim)
    score_scale = 1.0 / head_dim**0.5
    scores = (
        jnp.einsum("cqhd,ckhd->chqk", query_heads, key_heads, preferred_element_type=jnp.float32)
        * score_scale
    )
    probs = jax.nn.softmax(scores, axis=-1)
    probs_low = probs.astype(jnp.bfloat16)
    attended = jnp.einsum(
        "chqk,ckhd->cqhd", probs_low, value_heads, preferred_element_type=jnp.float32
    )
    attended = attended.astype(jnp.bfloat16).reshape(tokens, local_width)
    prob_grad = jnp.einsum(
        "cqhd,ckhd->chqk", grad_heads, value_heads, preferred_element_type=jnp.float32
    )
    row_dot = jnp.sum(probs * prob_grad, axis=-1, keepdims=True)
    score_grad = (score_scale * probs * (prob_grad - row_dot)).astype(jnp.bfloat16)
    query_grad = jnp.einsum(
        "chqk,ckhd->cqhd", score_grad, key_heads, preferred_element_type=jnp.float32
    )
    query_grad = query_grad.astype(jnp.bfloat16).reshape(tokens, local_width)
    key_grad = jnp.einsum(
        "chqk,cqhd->ckhd", score_grad, query_heads, preferred_element_type=jnp.float32
    )
    key_grad = key_grad.astype(jnp.bfloat16).reshape(pair_count * full_len, local_width)
    value_grad = jnp.einsum(
        "chqk,cqhd->ckhd", probs_low, grad_heads, preferred_element_type=jnp.float32
    )
    value_grad = value_grad.astype(jnp.bfloat16).reshape(pair_count * full_len, local_width)
    state_term = lax.dot_general(
        key_grad, key_weight, (((1,), (1,)), ((), ())), preferred_element_type=jnp.float32
    )
    state_term = state_term + lax.dot_general(
        value_grad, value_weight, (((1,), (1,)), ((), ())), preferred_element_type=jnp.float32
    )
    state_term = state_term.reshape(pair_count, full_len, enc_width)
    pair_grad = lax.psum_scatter(
        state_term.astype(jnp.bfloat16), "mp", scatter_dimension=1, tiled=True
    )
    outgoing = jnp.einsum(
        "ps,pte->ste", matched.astype(jnp.bfloat16), pair_grad, preferred_element_type=jnp.float32
    )
    outgoing = outgoing.astype(jnp.bfloat16).reshape(shards, capacity, slab_len, enc_width)
    returned = lax.all_to_all(outgoing, "dp", split_axis=0, concat_axis=0, tiled=True).reshape(
        slot_count, slab_len, enc_width
    )
    owned_hot = (
        incoming.reshape(slot_count)[None, :]
        == jnp.arange(states.shape[0], dtype=jnp.int32)[:, None]
    ).astype(jnp.bfloat16)
    state_total = jnp.einsum("rs,ste->rte", owned_hot, returned, preferred_element_type=jnp.float32)
    key_wgrad = lax.dot_general(
        rows_all, key_grad, (((0,), (0,)), ((), ())), preferred_element_type=jnp.float32
    )
    value_wgrad = lax.dot_general(
        rows_all, value_grad, (((0,), (0,)), ((), ())), preferred_element_type=jnp.float32
    )
    key_total, value_total = lax.psum((key_wgrad, value_wgrad), "dp")
    return (attended, query_grad, state_total, key_total, value_total)


def solution(mesh):
    placed = (
        P("dp", "mp"),
        P("dp", "mp", None),
        P(None, "mp"),
        P(None, "mp"),
        P("dp", None),
        P("dp", None),
        P("dp", "mp"),
    )
    return jax.shard_map(
        body,
        mesh=mesh,
        in_specs=placed,
        out_specs=(P("dp", "mp"), P("dp", "mp"), P("dp", "mp", None), P(None, "mp"), P(None, "mp")),
        check_vma=False,
    )
```

profile of v0, /device:TPU:0, one launch (start us, length us, event | category | flops | bytes accessed | tf_op | source)
XLA Modules:
  0.0 452.6 jit_solution(6387571205383351647)
XLA Ops:
  9.4 13.5 %all_to_all.25 = s32[8,1,2]{2,1,0:T(1,128)S(1)} all-to-all(s32[8,1,2]{2,1,0:T(1,128)S(1)} %bitcast.138), channel_id=1, replica_groups=mesh['dp'=8,'mp'=4] {'dp'}, dimensions={0} | all-to-all | bytes 128 | tf_op jit(solution)/shard_map/all_to_all | solution.py:35
  26.1 3.6 all-to-all-start.1
  29.9 21.7 %all-to-all-done.1 = bf16[8,2,32,896]{3,2,1,0:T(8,128)(2,1)S(1)} async-done(((bf16[8,2,32,896]{3,2,1,0:T(8,128)(2,1)}), bf16[8,2,32,896]{3,2,1,0:T(8,128)(2,1)S(1)}, u32[]{:S(2)}, u32[]{:S(2)}) %all-to-all-start.1) | async-done | bytes 917536 | tf_op jit(solution)/shard_map/all_to_all | solution.py:37
  55.9 22.6 %all-gather.2.cloned.1.call-done = bf16[12,128,896]{2,1,0:T(8,128)(2,1)} async-done(((bf16[12,32,896]{2,1,0:T(8,128)(2,1)}), bf16[12,128,896]{2,1,0:T(8,128)(2,1)}) %all-gather.2.cloned.1.call-update) | async-done | bytes 2752528 | tf_op jit(solution)/shard_map/all_gather | solution.py:40
  78.6 5.4 %fusion.29 = bf16[192,8,8,128]{3,1,2,0:T(8,128)(2,1)S(1)} fusion(bf16[1536,896]{1,0:T(8,128)(2,1)} %bitcast.139, bf16[896,1024]{1,0:T(8,128)(2,1)S(1)} %copy-done), kind=kOutput, calls=%fused_computation.38 | convolution fusion | flops 2820145152 | bytes 7733248 | tf_op jit(solution)/shard_map/dot_general | solution.py:42
  91.0 3.6 fusion.28
  94.7 2.6 copy.76
  97.3 10.5 %convert_bitcast_fusion = bf16[6,256,8,128]{3,1,2,0:T(8,128)(2,1)} fusion(bf16[6,64,8,128]{3,2,1,0:T(8,128)(2,1)S(1)} %bitcast.136, f32[6,8,64]{2,1,0:T(8,128)S(1)} %get-tuple-element.24, f32[6,8,256,64]{2,3,1,0:T(8,128)} %copy-done.4), kind=kOutput, calls=%fused_computation.22 | convolution fusion | flops 206834944 | bytes 7090176 | tf_op jit(solution)/shard_map/chqk,cqhd->ckhd/dot_general | solution.py:76
  107.8 4.4 fusion.8
  114.3 2.4 convert_bitcast_fusion.1
  118.8 3.5 fusion.6
  124.3 3.8 add_convert_fusion
  128.1 3.5 copy.70
  133.5 7.1 %fusion.4 = f32[896,1024]{1,0:T(8,128)} fusion(bf16[1536,896]{1,0:T(8,128)(2,1)} %bitcast.140, bf16[192,8,8,128]{3,2,1,0:T(8,128)(2,1)S(1)} %bitcast.127), kind=kOutput, calls=%fused_computation.9 | convolution fusion | flops 2818572288 | bytes 9568256 | tf_op jit(solution)/shard_map/dot_general | solution.py:102
  140.6 5.0 %fusion.1 = f32[896,1024]{1,0:T(8,128)} fusion(bf16[1536,896]{1,0:T(8,128)(2,1)S(1)} %bitcast.142, bf16[192,8,8,128]{3,2,1,0:T(8,128)(2,1)S(1)} %bitcast.129), kind=kOutput, calls=%fused_computation.6 | convolution fusion | flops 2818572288 | bytes 9568256 | tf_op jit(solution)/shard_map/dot_general | solution.py:105
  145.6 27.4 %reduce-scatter.2.cloned.1.call-done = bf16[12,32,896]{2,0,1:T(8,128)(2,1)} async-done(((bf16[12,128,896]{2,0,1:T(8,128)(2,1)}), bf16[12,32,896]{2,0,1:T(8,128)(2,1)}) %reduce-scatter.2.cloned.1.call-update) | async-done | bytes 688144 | tf_op jit(solution)/shard_map/reduce_scatter | solution.py:87
  173.0 2.5 convolution_convert_fusion.2
  175.5 3.2 reshape.147
  178.7 2.7 copy.71
  181.5 5.8 %all-to-all-start.2 = ((bf16[8,2,32,896]{3,1,2,0:T(2,128)(2,1)}), bf16[8,2,32,896]{3,1,2,0:T(2,128)(2,1)}, u32[]{:S(2)}, u32[]{:S(2)}) async-start(bf16[8,2,32,896]{3,1,2,0:T(2,128)(2,1)} %copy.71), calls=%async_computation.3 | async-start | bytes 1835008 | tf_op jit(solution)/shard_map/all_to_all | solution.py:94
  191.1 9.3 %fusion.37 = bf16[6,64,8,128]{3,1,2,0:T(8,128)(2,1)S(1)} fusion(bf16[6,256,8,128]{3,2,1,0:T(8,128)(2,1)} %bitcast.125, f32[6,8,64]{2,1,0:T(8,128)S(1)} %get-tuple-element.24, f32[6,8,256,64]{2,3,1,0:T(8,128)} %copy-done.4), kind=kOutput, calls=%fused_computation.44 | convolution fusion | flops 205655296 | bytes 7090176 | tf_op jit(solution)/shard_map/chqk,ckhd->cqhd/dot_general | solution.py:59
  202.4 33.0 %all-to-all-done.2 = bf16[8,2,32,896]{3,1,2,0:T(2,128)(2,1)} async-done(((bf16[8,2,32,896]{3,1,2,0:T(2,128)(2,1)}), bf16[8,2,32,896]{3,1,2,0:T(2,128)(2,1)}, u32[]{:S(2)}, u32[]{:S(2)}) %all-to-all-start.2) | async-done | bytes 917536 | tf_op jit(solution)/shard_map/all_to_all | solution.py:94
  238.9 200.4 %all-reduce.3.cloned.1.call-done = (f32[896,1024]{1,0:T(8,128)}, f32[896,1024]{1,0:T(8,128)}) async-done(((f32[896,1024]{1,0:T(8,128)}, f32[896,1024]{1,0:T(8,128)}), (f32[896,1024]{1,0:T(8,128)}, f32[896,1024]{1,0:T(8,128)})) %all-reduce.3.cloned.1.call-update) | async-done | bytes 7340048 | tf_op jit(solution)/shard_map/psum | solution.py:108
  439.3 4.5 copy.130
  (84 shorter events, 36.2 us)
Async XLA Ops:
  7.2 71.4 %copy-start = (bf16[896,1024]{1,0:T(8,128)(2,1)S(1)}, bf16[896,1024]{1,0:T(8,128)(2,1)}, u32[]{:S(2)}) copy-start(bf16[896,1024]{1,0:T(8,128)(2,1)} %param.9) | copy-start | bytes 5505028
  7.2 22.5 %copy-start.12 = (s32[6,2]{0,1:T(2,128)S(1)}, s32[6,2]{0,1:T(2,128)}, u32[]{:S(2)}) copy-start(s32[6,2]{0,1:T(2,128)} %param.11) | copy-start | bytes 148
  26.1 25.5 %all-to-all-start.1 = ((bf16[8,2,32,896]{3,2,1,0:T(8,128)(2,1)}), bf16[8,2,32,896]{3,2,1,0:T(8,128)(2,1)S(1)}, u32[]{:S(2)}, u32[]{:S(2)}) async-start(bf16[8,2,32,896]{3,2,1,0:T(8,128)(2,1)} %broadcast_select_fusion), calls=%async_computation.1 | async-start | bytes 1835008 | tf_op jit(solution)/shard_map/all_to_all | solution.py:37
  29.7 48.9 %all-gather.2.cloned.1.call-start = ((), (), s32[]{:S(2)}) async-start(), calls=%async_computation.4 | async-start | bytes 3440640 | tf_op jit(solution)/shard_map/all_gather | solution.py:40
  53.3 119.8 %reduce-scatter.2.cloned.1.call-start = ((), (), s32[]{:S(2)}) async-start(), calls=%async_computation.5 | async-start | bytes 4587520 | tf_op jit(solution)/shard_map/reduce_scatter | solution.py:87
  84.8 1.6 copy-start.2
  86.4 8.2 %copy-start.4 = (f32[6,8,256,64]{2,3,1,0:T(8,128)}, f32[6,8,256,64]{2,3,1,0:T(8,128)S(1)}, u32[]{:S(2)}) copy-start(f32[6,8,256,64]{2,3,1,0:T(8,128)S(1)} %fusion.23) | copy-start | bytes 9437188
  86.5 3.8 copy-start.13
  86.5 4.6 %copy-start.15 = (bf16[896,1024]{1,0:T(8,128)(2,1)S(1)}, bf16[896,1024]{1,0:T(8,128)(2,1)}, u32[]{:S(2)}) copy-start(bf16[896,1024]{1,0:T(8,128)(2,1)} %param.10) | copy-start | bytes 5505028
  107.8 4.4 copy-start.5
  118.7 3.5 copy-start.7
  118.7 3.5 copy-start.11
  122.3 2.1 copy-start.16
  124.3 3.8 copy-start.9
  131.6 1.9 copy-start.8
  131.6 307.7 %all-reduce.3.cloned.1.call-start = ((), (), s32[]{:S(2)}) async-start(), calls=%async_computation.6 | async-start | bytes 14680064 | tf_op jit(solution)/shard_map/psum | solution.py:108
  133.5 7.1 %copy-start.10 = (bf16[6,256,8,128]{3,2,1,0:T(8,128)(2,1)S(1)}, bf16[6,256,8,128]{3,2,1,0:T(8,128)(2,1)}, u32[]{:S(2)}) copy-start(bf16[6,256,8,128]{3,2,1,0:T(8,128)(2,1)} %copy-done.9) | copy-start | bytes 9437188
  133.5 7.1 %copy-start.14 = (bf16[12,128,896]{2,1,0:T(8,128)(2,1)S(1)}, bf16[12,128,896]{2,1,0:T(8,128)(2,1)}, u32[]{:S(2)}) copy-start(bf16[12,128,896]{2,1,0:T(8,128)(2,1)} %all-gather.2.cloned.1.call-done) | copy-start | bytes 8257540
  175.5 13.0 %copy-start.3 = (bf16[192,8,8,128]{3,2,1,0:T(8,128)(2,1)S(1)}, bf16[192,8,8,128]{3,2,1,0:T(8,128)(2,1)}, u32[]{:S(2)}) copy-start(bf16[192,8,8,128]{3,2,1,0:T(8,128)(2,1)} %copy-done.2) | copy-start | bytes 9437188
  181.5 53.9 %all-to-all-start.2 = ((bf16[8,2,32,896]{3,1,2,0:T(2,128)(2,1)}), bf16[8,2,32,896]{3,1,2,0:T(2,128)(2,1)}, u32[]{:S(2)}, u32[]{:S(2)}) async-start(bf16[8,2,32,896]{3,1,2,0:T(2,128)(2,1)} %copy.71), calls=%async_computation.3 | async-start | bytes 1835008 | tf_op jit(solution)/shard_map/all_to_all | solution.py:94
  439.3 4.5 %copy-start.6 = (f32[896,1024]{1,0:T(8,128)S(1)}, f32[896,1024]{1,0:T(8,128)}, u32[]{:S(2)}) copy-start(f32[896,1024]{1,0:T(8,128)} %get-tuple-element.34) | copy-start | bytes 11010052
  439.3 6.4 %copy-start.1 = (bf16[896,1024]{1,0:T(8,128)(2,1)S(1)}, bf16[896,1024]{1,0:T(8,128)(2,1)}, u32[]{:S(2)}) copy-start(bf16[896,1024]{1,0:T(8,128)(2,1)} %param.9) | copy-start | bytes 5505028
Sparse Core Ops, SparseCore 0:
  53.4 25.1 all-gather.1
  131.7 41.2 reduce-scatter.1
  178.2 261.0 all-reduce.2
where the time goes:
time: 461 us; the launch traced here: 453 us
  waiting for transfers between devices  305 us (66%)
  matrix products  61.1 us (13%)
  local copies, waits for them, and re-layouts  41.4 us (9%)
  between operations  14.5 us (3%)
  blocking collectives  13.5 us (3%)
  starting transfers between devices  9.71 us (2%)
  other arithmetic  7.29 us (2%)
    psum x1, waiting for transfers between devices, body(): key_total, value_total = lax.psum((key_wgrad, value_wgrad), 'dp')  200 us
    all_to_all x1, waiting for transfers between devices, body(): lax.all_to_all(outgoing, 'dp', split_axis=0, concat_axis=0, tiled=True)  33 us
    reduce_scatter x1, waiting for transfers between devices, body(): lax.psum_scatter(state_term.astype(jnp.bfloat16), 'mp', scatter_dimension...  27.4 us
    all_gather x1, waiting for transfers between devices, body(): gathered = lax.all_gather(picked, 'mp', axis=1, tiled=True)  22.6 us
    all_to_all x1, waiting for transfers between devices, body(): lax.all_to_all(slab_rows, 'dp', split_axis=0, concat_axis=0, tiled=True)  21.7 us
    unnamed x43, local copies, waits for them, and re-layouts  19.5 us
    all_to_all x1, blocking collectives, body(): lax.all_to_all(asked_rows, 'dp', split_axis=0, concat_axis=0, tiled=True)  13.5 us
    dot_general x1, matrix products, body(): jnp.einsum('chqk,cqhd->ckhd', probs_low, grad_heads, preferred_element_ty...  10.5 us
  transfers between devices with their start and end apart: 5, of which 5 were waited for; matrix products, arithmetic and copies ran while one was open for 9% of the time, Pallas kernels for 0%

commit v1 on v0

v1 whole, which is shorter than its diff:
```python
import functools

import jax
import jax.numpy as jnp
from jax import lax
from jax.experimental import pallas as pl
from jax.experimental.pallas import tpu as pltpu
from jax.sharding import PartitionSpec as P

D = 4096
H = 32
VMEM_GRANT = 28 * 1024 * 1024
SMALL_GRANT = 12 * 1024 * 1024
CHEAP = pl.CostEstimate(flops=1, bytes_accessed=1, transcendentals=0)


def bits_of(count):
    return count.bit_length() - 1


def swap(value, axis, bit):
    count = lax.axis_size(axis)
    return lax.ppermute(value, axis, [(i, i ^ (1 << bit)) for i in range(count)])


def any_spec():
    return pl.BlockSpec(memory_space=pl.ANY)


def hbm_spec():
    return pl.BlockSpec(memory_space=pltpu.HBM)


def head_kernel(groups, spans, head_dim, start, extra, *refs):
    flag_ref = refs[0]
    slabs = refs[1 : 1 + groups]
    wk_hbm, wv_hbm, q_hbm, g_hbm = refs[1 + groups : 5 + groups]
    att_hbm, dq_hbm, dk_hbm, dv_hbm, keep_ref, send_ref = refs[5 + groups + extra : 11 + groups + extra]
    rows, wk, wv, q_ref, g_ref, keys, values, att_ref, dq_ref, dk_ref, dv_ref, grads, sems = refs[11 + groups + extra :]
    tokens, width = q_ref.shape
    span_len = tokens // spans
    block = rows.shape[0] // groups
    part = block // spans
    scale = 1.0 / head_dim**0.5
    columns = pl.ds(start, width)

    def begin(source, target, sem):
        copy = pltpu.make_async_copy(source, target, sems.at[sem])
        copy.start()
        return copy

    weights_in = [begin(wk_hbm.at[:, columns], wk, groups), begin(wv_hbm.at[:, columns], wv, groups + 1)]
    rows_in = [begin(slabs[r], rows.at[pl.ds(r * block, block)], r) for r in range(groups)]
    tokens_in = [begin(q_hbm.at[:, columns], q_ref, groups + 2), begin(g_hbm.at[:, columns], g_ref, groups + 3)]
    for copy in weights_in:
        copy.wait()
    for r in range(groups):
        rows_in[r].wait()
        at = pl.ds(r * block, block)
        keys[at, :] = jnp.dot(rows[at, :], wk[...], preferred_element_type=jnp.float32).astype(jnp.bfloat16)
        values[at, :] = jnp.dot(rows[at, :], wv[...], preferred_element_type=jnp.float32).astype(jnp.bfloat16)
    for copy in tokens_in:
        copy.wait()

    def spread(x):
        heads = x.shape[1] // head_dim
        lane_head = lax.broadcasted_iota(jnp.int32, x.shape, 1) // head_dim
        zero = jnp.zeros_like(x)
        return jnp.concatenate([jnp.where(lane_head == h, x, zero) for h in range(heads)], axis=0)

    def collect(x):
        out = x[0:span_len]
        lane_head = lax.broadcasted_iota(jnp.int32, out.shape, 1) // head_dim
        for h in range(1, x.shape[1] // head_dim):
            out = jnp.where(lane_head == h, x[h * span_len : (h + 1) * span_len], out)
        return out

    def span_rows(ref, c, cols):
        return jnp.concatenate([ref[pl.ds(r * block + c * part, part), cols] for r in range(groups)], axis=0)

    contract_last = (((1,), (1,)), ((), ()))
    contract_first = (((0,), (0,)), ((), ()))
    at = [pl.ds(c * span_len, span_len) for c in range(spans)]
    swapped = flag_ref[0] == 1
    pair = 2 * head_dim
    for first in range(0, width, pair):
        cols = slice(first, min(first + pair, width))
        send_cols = slice(width + cols.start, width + cols.stop)
        every = range(spans)
        scores = [
            lax.dot_general(
                span_rows(keys, c, cols), spread(q_ref[at[c], cols]), contract_last,
                preferred_element_type=jnp.float32,
            )
            * scale
            for c in every
        ]
        prob_grad = [
            lax.dot_general(
                span_rows(values, c, cols), spread(g_ref[at[c], cols]), contract_last,
                preferred_element_type=jnp.float32,
            )
            for c in every
        ]
        weights = [jnp.exp(x - jnp.max(x, axis=0, keepdims=True)) for x in scores]
        probs = [x * (1.0 / jnp.sum(x, axis=0, keepdims=True)) for x in weights]
        low = [x.astype(jnp.bfloat16) for x in probs]
        row_dot = [jnp.sum(p * d, axis=0, keepdims=True) for p, d in zip(probs, prob_grad)]
        score_grad = [(scale * p * (d - t)).astype(jnp.bfloat16) for p, d, t in zip(probs, prob_grad, row_dot)]
        for c in every:
            dk = jnp.dot(score_grad[c], spread(q_ref[at[c], cols]), preferred_element_type=jnp.float32)
            dv = jnp.dot(low[c], spread(g_ref[at[c], cols]), preferred_element_type=jnp.float32)
            dk, dv = dk.astype(jnp.bfloat16), dv.astype(jnp.bfloat16)
            for r in range(groups):
                to = pl.ds(r * block + c * part, part)
                piece = slice(r * part, (r + 1) * part)
                dk_ref[to, cols] = dk[piece]
                dv_ref[to, cols] = dv[piece]
                grads[to, cols] = jnp.where(swapped, dv[piece], dk[piece])
                grads[to, send_cols] = jnp.where(swapped, dk[piece], dv[piece])
        for c in every:
            att = lax.dot_general(
                low[c], span_rows(values, c, cols), contract_first, preferred_element_type=jnp.float32
            )
            att_ref[at[c], cols] = collect(att).astype(jnp.bfloat16)
            dq = lax.dot_general(
                score_grad[c], span_rows(keys, c, cols), contract_first, preferred_element_type=jnp.float32
            )
            dq_ref[at[c], cols] = collect(dq).astype(jnp.bfloat16)
    results = [
        begin(att_ref, att_hbm.at[:, columns], 0),
        begin(dq_ref, dq_hbm.at[:, columns], 1),
        begin(dk_ref, dk_hbm, 2),
        begin(dv_ref, dv_hbm, 3),
    ]
    both = lax.dot_general(rows[...], grads[...], contract_first, preferred_element_type=jnp.float32)
    keep_ref[...] = both[:, :width]
    send_ref[...] = both[:, width:].astype(jnp.bfloat16)
    for copy in results:
        copy.wait()


def run_heads(start, chunk, flag, slabs, key_weight, value_weight, queries, out_grad, chain, after, spans, head_dim):
    groups = len(slabs)
    tokens, local_width = queries.shape
    block, enc = slabs[0].shape
    total = groups * block
    bf = jnp.bfloat16
    extra = list(chain) + list(after)
    outs = pl.pallas_call(
        functools.partial(head_kernel, groups, spans, head_dim, start, len(extra)),
        out_shape=[
            jax.ShapeDtypeStruct((tokens, local_width), bf),
            jax.ShapeDtypeStruct((tokens, local_width), bf),
            jax.ShapeDtypeStruct((total, chunk), bf),
            jax.ShapeDtypeStruct((total, chunk), bf),
            jax.ShapeDtypeStruct((enc, chunk), jnp.float32),
            jax.ShapeDtypeStruct((enc, chunk), bf),
        ],
        in_specs=[pl.BlockSpec(memory_space=pltpu.SMEM)]
        + [any_spec()] * groups
        + [hbm_spec()] * (4 + len(chain))
        + [any_spec()] * len(after),
        out_specs=[hbm_spec()] * 4 + [pl.BlockSpec(memory_space=pltpu.VMEM)] * 2,
        scratch_shapes=[
            pltpu.VMEM((total, enc), bf),
            pltpu.VMEM((enc, chunk), bf),
            pltpu.VMEM((enc, chunk), bf),
            pltpu.VMEM((tokens, chunk), bf),
            pltpu.VMEM((tokens, chunk), bf),
            pltpu.VMEM((total, chunk), bf),
            pltpu.VMEM((total, chunk), bf),
            pltpu.VMEM((tokens, chunk), bf),
            pltpu.VMEM((tokens, chunk), bf),
            pltpu.VMEM((total, chunk), bf),
            pltpu.VMEM((total, chunk), bf),
            pltpu.VMEM((total, 2 * chunk), bf),
            pltpu.SemaphoreType.DMA((groups + 4,)),
        ],
        input_output_aliases={5 + groups + i: i for i in range(len(chain))},
        compiler_params=pltpu.CompilerParams(vmem_limit_bytes=VMEM_GRANT),
        cost_estimate=pl.CostEstimate(
            flops=2 * total * enc * chunk * 8, bytes_accessed=4 * total * enc, transcendentals=total * tokens
        ),
        name="heads",
    )(flag, *slabs, key_weight, value_weight, queries, out_grad, *extra)
    return outs[:2], outs[2], outs[3], outs[4:]


def state_kernel(groups, widths, extra, *refs):
    count = len(widths)
    dk_hbm, dv_hbm = refs[:count], refs[count : 2 * count]
    wk_hbm, wv_hbm = refs[2 * count : 2 * count + 2]
    keep_ref, send_ref, grads, weights, sems = refs[2 * count + 2 + extra :]
    half = weights.shape[1] // 2
    block = grads.shape[0] // groups

    copies = [
        pltpu.make_async_copy(wk_hbm, weights.at[:, pl.ds(0, half)], sems.at[0, 0]),
        pltpu.make_async_copy(wv_hbm, weights.at[:, pl.ds(half, half)], sems.at[0, 1]),
    ]
    blocks = []
    for r in range(groups):
        rows = pl.ds(r * block, block)
        parts = []
        for j in range(count):
            first = sum(widths[:j])
            for k, source in enumerate((dk_hbm[j], dv_hbm[j])):
                target = grads.at[rows, pl.ds(k * half + first, widths[j])]
                parts.append(pltpu.make_async_copy(source.at[rows, :], target, sems.at[1 + r, 2 * j + k]))
        blocks.append(parts)
    for copy in copies:
        copy.start()
    for parts in blocks:
        for copy in parts:
            copy.start()
    for copy in copies:
        copy.wait()
    for r in range(groups):
        for copy in blocks[r]:
            copy.wait()
        term = lax.dot_general(
            grads[pl.ds(r * block, block), :], weights[...], (((1,), (1,)), ((), ())),
            preferred_element_type=jnp.float32,
        )
        to = pl.ds((r // 2) * block, block)
        if r % 2:
            send_ref[to, :] = term.astype(jnp.bfloat16)
        else:
            keep_ref[to, :] = term


def run_state(groups, dk, dv, key_weight, value_weight, after):
    total = dk[0].shape[0]
    enc, local_width = key_weight.shape
    widths = [x.shape[1] for x in dk]
    vmem = pl.BlockSpec(memory_space=pltpu.VMEM)
    return pl.pallas_call(
        functools.partial(state_kernel, groups, widths, len(after)),
        out_shape=[
            jax.ShapeDtypeStruct((total // 2, enc), jnp.float32),
            jax.ShapeDtypeStruct((total // 2, enc), jnp.bfloat16),
        ],
        in_specs=[hbm_spec()] * (2 * len(dk) + 2) + [any_spec()] * len(after),
        out_specs=[vmem, vmem],
        scratch_shapes=[
            pltpu.VMEM((total, 2 * local_width), jnp.bfloat16),
            pltpu.VMEM((enc, 2 * local_width), jnp.bfloat16),
            pltpu.SemaphoreType.DMA((groups + 1, max(2, 2 * len(dk)))),
        ],
        compiler_params=pltpu.CompilerParams(vmem_limit_bytes=VMEM_GRANT),
        cost_estimate=pl.CostEstimate(
            flops=8 * total * enc * local_width, bytes_accessed=8 * total * enc, transcendentals=0
        ),
        name="state_terms",
    )(*dk, *dv, key_weight, value_weight, *after)


def fold_kernel(rows_ref, returned_ref, *refs):
    out_ref = refs[-1]
    out_ref[...] = jnp.zeros_like(out_ref)
    count = out_ref.shape[0]
    for s in range(returned_ref.shape[0]):
        row = rows_ref[s]

        @pl.when(row < count)
        def _():
            out_ref[row] += returned_ref[s].astype(jnp.float32)


def halve_kernel(choice_ref, keep_ref, recv_ref, *refs):
    stay_ref, send_ref = refs[-2:]
    total = keep_ref[...] + recv_ref[...].astype(jnp.float32)
    half = stay_ref.shape[0]
    upper = choice_ref[0] == 1
    stay_ref[...] = jnp.where(upper, total[half:], total[:half])
    send_ref[...] = jnp.where(upper, total[:half], total[half:]).astype(jnp.bfloat16)


def split_kernel(keep_ref, recv_ref, *refs):
    stay_ref, send_ref = refs[-2:]
    half = stay_ref.shape[0]
    stay_ref[...] = keep_ref[:half] + recv_ref[:half].astype(jnp.float32)
    send_ref[...] = (keep_ref[half:] + recv_ref[half:].astype(jnp.float32)).astype(jnp.bfloat16)


def add_kernel(keep_ref, recv_ref, *refs):
    refs[-1][...] = (keep_ref[...] + recv_ref[...].astype(jnp.float32)).astype(refs[-1].dtype)


def join_kernel(choice_ref, own_ref, recv_ref, *refs):
    out_ref = refs[-1]
    upper = choice_ref[0] == 1
    own, recv = own_ref[...], recv_ref[...]
    rows = own.shape[0]
    if rows % 16:
        own, recv = own.astype(jnp.float32), recv.astype(jnp.float32)
        out = jnp.concatenate([jnp.where(upper, recv, own), jnp.where(upper, own, recv)], axis=0)
        out_ref[...] = out.astype(out_ref.dtype)
    else:
        out_ref[:rows] = jnp.where(upper, recv, own)
        out_ref[rows:] = jnp.where(upper, own, recv)


def place_kernel(start, choice_ref, own_ref, recv_ref, *refs):
    key_hbm, value_hbm, token_ref, key_ref, value_ref, sems = refs[-6:]
    token_ref[...] = jnp.zeros_like(token_ref)
    swapped = choice_ref[0] == 1
    own, recv = own_ref[...].astype(jnp.float32), recv_ref[...].astype(jnp.float32)
    columns = pl.ds(start, own.shape[1])
    key_ref[...] = jnp.where(swapped, recv, own)
    key_out = pltpu.make_async_copy(key_ref, key_hbm.at[:, columns], sems.at[0])
    key_out.start()
    value_ref[...] = jnp.where(swapped, own, recv)
    value_out = pltpu.make_async_copy(value_ref, value_hbm.at[:, columns], sems.at[1])
    value_out.start()
    key_out.wait()
    value_out.wait()


def small(kernel, name, scalars, arrays, outs, after, alias_in=(), out_specs=None, scratch=()):
    vmem = pl.BlockSpec(memory_space=pltpu.VMEM)
    extra = list(alias_in) + list(after)
    first = len(scalars) + len(arrays)
    return pl.pallas_call(
        kernel,
        out_shape=outs,
        in_specs=[pl.BlockSpec(memory_space=pltpu.SMEM)] * len(scalars)
        + [vmem] * len(arrays)
        + [hbm_spec()] * len(alias_in)
        + [any_spec()] * len(after),
        out_specs=out_specs or [vmem] * len(outs),
        scratch_shapes=list(scratch),
        input_output_aliases={first + i: i for i in range(len(alias_in))},
        compiler_params=pltpu.CompilerParams(vmem_limit_bytes=SMALL_GRANT),
        cost_estimate=CHEAP,
        name=name,
    )(*scalars, *arrays, *extra)


class Sum:
    def __init__(self, order, choices, start, enc, width):
        self.choices, self.start, self.enc, self.width = choices, start, enc, width
        self.count = len(order)
        self.steps = list(order) + list(reversed(order))
        self.at = 0

    def begin(self, keep, send):
        self.keep = keep
        self.moving = swap(send, "dp", self.steps[0])

    def load(self, step):
        return self.enc >> (step if step < self.count else 2 * self.count - 1 - step)

    def advance(self, after, outs):
        count, at = self.count, self.at
        self.at += 1
        rows = self.load(at)
        shape = lambda rows, dtype: jax.ShapeDtypeStruct((rows, self.width), dtype)
        if at < count - 1:
            choice = self.choices[self.steps[at + 1]]
            self.keep, send = small(
                halve_kernel, "halve", [choice], [self.keep, self.moving],
                [shape(rows // 2, jnp.float32), shape(rows // 2, jnp.bfloat16)], after,
            )
        elif at == count - 1:
            (send,) = small(add_kernel, "add", [], [self.keep, self.moving], [shape(rows, jnp.bfloat16)], after)
        elif at < 2 * count - 1:
            choice = self.choices[self.steps[at]]
            (send,) = small(
                join_kernel, "join", [choice], [self.own, self.moving], [shape(2 * rows, jnp.bfloat16)], after
            )
        else:
            choice = self.choices[self.steps[at]]
            full = jax.ShapeDtypeStruct(self.full, jnp.float32)
            block = pltpu.VMEM((self.enc, self.width), jnp.float32)
            token = jax.ShapeDtypeStruct((8, 128), jnp.float32)
            *outs, done = small(
                functools.partial(place_kernel, self.start), "place", [choice], [self.own, self.moving],
                [full, full, token], after, alias_in=outs,
                out_specs=[hbm_spec()] * 2 + [pl.BlockSpec(memory_space=pltpu.VMEM)],
                scratch=[block, block, pltpu.SemaphoreType.DMA((2,))],
            )
            return done, outs
        self.own = send
        self.moving = swap(send, "dp", self.steps[at + 1])
        return send, outs


def wavefront(chunks, steps, rest):
    order, period = [], 0
    done = [0] * chunks
    rest_done = 0
    while min(done) < steps or rest_done < rest:
        begun = min(period, chunks)
        if period < chunks:
            order.append(f"heads{period}")
        elif period == chunks:
            order.append("state")
        for j in range(begun):
            if done[j] < steps:
                order.append(f"sum{j}")
                done[j] += 1
        if period > chunks and rest_done < rest and (rest_done < rest - 2 or min(done) >= steps - 1):
            order.append("rest")
            rest_done += 1
        period += 1
    return order


def body(queries, states, key_weight, value_weight, nbr_shard, nbr_row, out_grad):
    shards = lax.axis_size("dp")
    groups = lax.axis_size("mp")
    dp_bits, mp_bits = bits_of(shards), bits_of(groups)
    dp_index = lax.axis_index("dp")
    spans, neighbours = nbr_shard.shape
    pair_count = spans * neighbours
    tokens, local_width = queries.shape
    stored, slab_len, enc_width = states.shape
    head_dim = D // H
    capacity = max(2, (pair_count + shards - 1) // shards)
    slot_count = shards * capacity

    owners = nbr_shard.reshape(pair_count)
    row_index = nbr_row.reshape(pair_count)
    pair_ids = jnp.arange(pair_count, dtype=jnp.int32)
    before = (owners[:, None] == owners[None, :]) & (pair_ids[None, :] < pair_ids[:, None])
    slot_index = owners * capacity + jnp.sum(before.astype(jnp.int32), axis=1)
    matched = slot_index[:, None] == jnp.arange(slot_count, dtype=jnp.int32)[None, :]
    asked = stored + jnp.sum(jnp.where(matched, row_index[:, None] - stored, 0), axis=0)
    slot_pair = jnp.sum(jnp.where(matched, pair_ids[:, None], 0), axis=0)
    incoming = lax.all_to_all(
        asked.reshape(shards, capacity), "dp", split_axis=0, concat_axis=0, tiled=True
    ).reshape(slot_count)
    slab_rows = jnp.take(states, jnp.minimum(incoming, stored - 1), axis=0, mode="clip")
    sent_back = lax.all_to_all(
        slab_rows.reshape(shards, capacity, slab_len, enc_width), "dp", split_axis=0, concat_axis=0, tiled=True
    ).reshape(slot_count, slab_len, enc_width)
    picked = jnp.take(sent_back, slot_index, axis=0, mode="clip").reshape(pair_count * slab_len, enc_width)

    blocks = {0: picked}
    for bit in reversed(range(mp_bits)):
        for r in list(blocks):
            blocks[r | (1 << bit)] = swap(blocks[r], "mp", bit)
    slabs = [blocks[r] for r in range(groups)]

    heads = local_width // head_dim
    counts = [min(2, heads - first) for first in range(0, heads, 2)]
    bits = list(range(dp_bits))
    choices = [((dp_index >> bit) & 1).astype(jnp.int32).reshape(1) for bit in bits]
    sums = []
    for j, count in enumerate(counts):
        sums.append(Sum(bits, choices, sum(counts[:j]) * head_dim, enc_width, count * head_dim))
        sums[j].full = key_weight.shape

    after, chain, outs, dk, dv = [], [], [], [], []
    rest_bit = 0
    for name in wavefront(len(sums), 2 * dp_bits, mp_bits + 1):
        kind = name.rstrip("0123456789")
        number = int(name[len(kind) :] or 0)
        if kind == "heads":
            part = sums[number]
            chain, dk_part, dv_part, (keep, send) = run_heads(
                part.start, part.width, choices[part.steps[0]], slabs, key_weight, value_weight, queries, out_grad,
                chain, after, spans, head_dim,
            )
            dk.append(dk_part)
            dv.append(dv_part)
            part.begin(keep, send)
            after = [send]
        elif kind == "sum":
            done, outs = sums[number].advance(after, outs)
            after = [done]
        elif kind == "state":
            keep, send = run_state(groups, dk, dv, key_weight, value_weight, after)
            moving = swap(send, "mp", 0)
            after = [send]
        elif rest_bit < mp_bits - 1:
            half = keep.shape[0] // 2
            keep, send = small(
                split_kernel, "split", [], [keep, moving],
                [jax.ShapeDtypeStruct((half, enc_width), t) for t in (jnp.float32, jnp.bfloat16)], after,
            )
            moving = swap(send, "mp", mp_bits - 1 - rest_bit)
            after = [send]
            rest_bit += 1
        elif rest_bit == mp_bits - 1:
            (pair_grad,) = small(
                add_kernel, "add", [], [keep, moving], [jax.ShapeDtypeStruct(keep.shape, jnp.bfloat16)], after
            )
            after = [pair_grad]
            outgoing = jnp.take(
                pair_grad.reshape(pair_count, slab_len, enc_width), slot_pair, axis=0, mode="clip"
            ).reshape(shards, capacity, slab_len, enc_width)
            returned = lax.all_to_all(outgoing, "dp", split_axis=0, concat_axis=0, tiled=True)
            rest_bit += 1
        else:
            (state_total,) = small(
                fold_kernel, "fold", [incoming], [returned.reshape(slot_count, slab_len, enc_width)],
                [jax.ShapeDtypeStruct(states.shape, jnp.float32)], after,
            )
    return (chain[0], chain[1], state_total, outs[0], outs[1])


def solution(mesh):
    placed = (
        P("dp", "mp"),
        P("dp", "mp", None),
        P(None, "mp"),
        P(None, "mp"),
        P("dp", None),
        P("dp", None),
        P("dp", "mp"),
    )
    return jax.shard_map(
        body,
        mesh=mesh,
        in_specs=placed,
        out_specs=(P("dp", "mp"), P("dp", "mp"), P("dp", "mp", None), P(None, "mp"), P(None, "mp")),
        check_vma=False,
    )
```

time: 461 us -> 215 us (0.47); the launches traced: 453 us -> 215 us
  waiting for transfers between devices: 305 us -> 95.9 us
  matrix products: 61.1 us -> 0 us
  Pallas kernels: 0 us -> 44.4 us
  starting transfers between devices: 9.71 us -> 46.2 us
  local copies, waits for them, and re-layouts: 41.4 us -> 11.8 us
  between operations: 14.5 us -> 1.06 us
  other arithmetic: 7.29 us -> 1.67 us
    psum x1 -> x0, waiting for transfers between devices: 200 us -> none  [body(): key_total, value_total = lax.psum((key_wgrad, value_wgrad), 'dp')]
    ppermute x0 -> x29, waiting for transfers between devices: none -> 74.2 us  [swap(): return lax.ppermute(value, axis, [(i, i ^ 1 << bit) for i in range(count)])]
    dot_general x15 -> x0, matrix products: 61.1 us -> none  [the longest x1 10.5 us: body(): jnp.einsum('chqk,cqhd->ckhd', probs_low, grad_heads, preferred_element_ty...]
    pallas_call x0 -> x32, Pallas kernels: none -> 44.4 us  [the longest x4 26.4 us: run_heads(): pl.pallas_call(functools.partial(head_kernel, groups, spans, head_dim, st...]
    ppermute x0 -> x29, starting transfers between devices: none -> 38.6 us  [swap(): return lax.ppermute(value, axis, [(i, i ^ 1 << bit) for i in range(count)])]
    all_to_all x1, waiting for transfers between devices: 33 us -> 0.01 us  [body(): lax.all_to_all(outgoing, 'dp', split_axis=0, concat_axis=0, tiled=True)]
    reduce_scatter x1 -> x0, waiting for transfers between devices: 27.4 us -> none  [body(): lax.psum_scatter(state_term.astype(jnp.bfloat16), 'mp', scatter_dimension...]
    all_gather x1 -> x0, waiting for transfers between devices: 22.6 us -> none  [body(): gathered = lax.all_gather(picked, 'mp', axis=1, tiled=True)]
  transfers between devices with their start and end apart: 5 -> 31, of which waited for: 5 -> 15; matrix products, arithmetic and copies ran while one was open for 9% -> 0% of each run, Pallas kernels for 0% -> 12%
where the time goes in v1:
time: 215 us
  waiting for transfers between devices  95.9 us (45%)
  starting transfers between devices  46.2 us (21%)
  Pallas kernels  44.4 us (21%)
  blocking collectives  13.5 us (6%)
  local copies, waits for them, and re-layouts  11.8 us (5%)
    ppermute x29, waiting for transfers between devices, swap(): return lax.ppermute(value, axis, [(i, i ^ 1 << bit) for i in range(count)])  74.2 us
    ppermute x29, starting transfers between devices, swap(): return lax.ppermute(value, axis, [(i, i ^ 1 << bit) for i in range(count)])  38.6 us
    pallas_call x4, Pallas kernels, run_heads(): pl.pallas_call(functools.partial(head_kernel, groups, spans, head_dim, st...  26.4 us
    all_to_all x1, waiting for transfers between devices, body(): lax.all_to_all(slab_rows.reshape(shards, capacity, slab_len, enc_width),...  21.7 us
    all_to_all x1, blocking collectives, body(): lax.all_to_all(asked.reshape(shards, capacity), 'dp', split_axis=0, conca...  13.5 us
    pallas_call x1, Pallas kernels, run_state(): pl.pallas_call(functools.partial(state_kernel, groups, widths, len(after)...  9.26 us
    pallas_call x27, Pallas kernels, small(): pl.pallas_call(kernel, out_shape=outs, in_specs=[pl.BlockSpec(memory_spac...  8.69 us
    unnamed x21, local copies, waits for them, and re-layouts  5.63 us
  transfers between devices with their start and end apart: 31, of which 15 were waited for; matrix products, arithmetic and copies ran while one was open for 0% of the time, Pallas kernels for 12%

profile of v1, /device:TPU:0, one launch (start us, length us, event | category | flops | bytes accessed | tf_op | source)
XLA Modules:
  0.0 214.6 jit_solution(2868886725086640446)
XLA Ops:
  2.9 13.5 %all_to_all.16 = s32[8,1,2]{2,1,0:T(1,128)S(1)} all-to-all(s32[8,1,2]{2,1,0:T(1,128)S(1)} %bitcast.25), channel_id=1, replica_groups=mesh['dp'=8,'mp'=4] {'dp'}, dimensions={0} | all-to-all | bytes 128 | tf_op jit(solution)/shard_map/all_to_all | solution.py:432
  19.3 3.6 %all-to-all-start.1 = ((bf16[8,2,32,896]{3,2,1,0:T(8,128)(2,1)}), bf16[8,2,32,896]{3,2,1,0:T(8,128)(2,1)S(1)}, u32[]{:S(2)}, u32[]{:S(2)}) async-start(bf16[8,2,32,896]{3,2,1,0:T(8,128)(2,1)} %bitcast.2), calls=%async_computation.1 | async-start | bytes 1835008 | tf_op jit(solution)/shard_map/all_to_all | solution.py:436
  23.1 21.7 %all-to-all-done.1 = bf16[8,2,32,896]{3,2,1,0:T(8,128)(2,1)S(1)} async-done(((bf16[8,2,32,896]{3,2,1,0:T(8,128)(2,1)}), bf16[8,2,32,896]{3,2,1,0:T(8,128)(2,1)S(1)}, u32[]{:S(2)}, u32[]{:S(2)}) %all-to-all-start.1) | async-done | bytes 917536 | tf_op jit(solution)/shard_map/all_to_all | solution.py:436
  49.1 13.5 %collective-permute-done.1.refs_3_ = bf16[384,896]{1,0:T(8,128)(2,1)} collective-permute-done((bf16[384,896]{1,0:T(8,128)(2,1)S(1)}, bf16[384,896]{1,0:T(8,128)(2,1)}, u32[]{:S(2)}, u32[]{:S(2)}) %collective-permute-start.1) | collective-permute-done | bytes 688160 | tf_op jit(solution)/shard_map/ppermute | solution.py:23
  62.6 2.5 %collective-permute-done.2.refs_4_ = bf16[384,896]{1,0:T(8,128)(2,1)} collective-permute-done((bf16[384,896]{1,0:T(8,128)(2,1)}, bf16[384,896]{1,0:T(8,128)(2,1)}, u32[]{:S(2)}, u32[]{:S(2)}) %collective-permute-start.2) | collective-permute-done | bytes 688160 | tf_op jit(solution)/shard_map/ppermute | solution.py:23
  68.9 6.6 %heads.4 = (bf16[384,1024]{1,0:T(8,128)(2,1)}, bf16[384,1024]{1,0:T(8,128)(2,1)}, bf16[1536,256]{1,0:T(8,128)(2,1)S(1)}, bf16[1536,256]{1,0:T(8,128)(2,1)S(1)}, ...) custom-call(s32[1]{0:T(128)} %bitcast.refs_0_.choice_ref, bf16[384,896]{1,0:T(8,128)(2,1)S(1)} %bitcast.20, ...), custom_call_target="tpu_custom_call" | custom-call | flops 5637144576 | bytes 5505024 | tf_op jit(solution)/shard_map/heads/pallas_call | solution.py:150
  77.9 6.5 %heads.5 = (bf16[384,1024]{1,0:T(8,128)(2,1)}, bf16[384,1024]{1,0:T(8,128)(2,1)}, bf16[1536,256]{1,0:T(8,128)(2,1)S(1)}, bf16[1536,256]{1,0:T(8,128)(2,1)S(1)}, ...) custom-call(s32[1]{0:T(128)} %bitcast.refs_0_.choice_ref, ...), custom_call_target="tpu_custom_call", output_to_operand_aliasing={{0}: (9, {}), {1}: (10, {})} | custom-call | flops 5637144576 | bytes 5505024 | tf_op jit(solution)/shard_map/heads/pallas_call | solution.py:150
  84.5 4.7 %collective-permute-done.3.recv_ref = bf16[896,256]{1,0:T(8,128)(2,1)S(1)} collective-permute-done((bf16[896,256]{1,0:T(8,128)(2,1)S(1)}, bf16[896,256]{1,0:T(8,128)(2,1)S(1)}, u32[]{:S(2)}, u32[]{:S(2)}) %collective-permute-start.3) | collective-permute-done | bytes 458784 | tf_op jit(solution)/shard_map/ppermute | solution.py:23
  89.5 6.7 %heads.6 = (bf16[384,1024]{1,0:T(8,128)(2,1)}, bf16[384,1024]{1,0:T(8,128)(2,1)}, bf16[1536,256]{1,0:T(8,128)(2,1)S(1)}, bf16[1536,256]{1,0:T(8,128)(2,1)S(1)}, ...) custom-call(s32[1]{0:T(128)} %bitcast.refs_0_.choice_ref, ...), custom_call_target="tpu_custom_call", output_to_operand_aliasing={{0}: (9, {}), {1}: (10, {})} | custom-call | flops 5637144576 | bytes 5505024 | tf_op jit(solution)/shard_map/heads/pallas_call | solution.py:150
  98.4 3.3 %collective-permute-start.8 = (bf16[224,256]{1,0:T(8,128)(2,1)S(1)}, bf16[224,256]{1,0:T(8,128)(2,1)S(1)}, u32[]{:S(2)}, u32[]{:S(2)}) collective-permute-start(bf16[224,256]{1,0:T(8,128)(2,1)S(1)} %get-tuple-element.74.refs_0_), channel_id=1, source_target_pairs={{0,16},{4,20},{8,24},{12,28},{16,0},{20,4},{24,8},{28,12},{1,17},{... | collective-permute-start | bytes 344072 | tf_op jit(solution)/shard_map/ppermute | solution.py:23
  101.9 6.7 %heads.7 = (bf16[384,1024]{1,0:T(8,128)(2,1)}, bf16[384,1024]{1,0:T(8,128)(2,1)}, bf16[1536,256]{1,0:T(8,128)(2,1)S(1)}, bf16[1536,256]{1,0:T(8,128)(2,1)S(1)}, ...) custom-call(s32[1]{0:T(128)} %bitcast.refs_0_.choice_ref, ...), custom_call_target="tpu_custom_call", output_to_operand_aliasing={{0}: (9, {}), {1}: (10, {})} | custom-call | flops 5637144576 | bytes 5505024 | tf_op jit(solution)/shard_map/heads/pallas_call | solution.py:150
  108.9 9.3 %state_terms.1 = (f32[768,896]{1,0:T(8,128)S(1)}, bf16[768,896]{1,0:T(8,128)(2,1)S(1)}) custom-call(bf16[1536,256]{1,0:T(8,128)(2,1)S(1)} %get-tuple-element.78.refs_0_, bf16[1536,256]{1,0:T(8,128)(2,1)S(1)} %get-tuple-element.79.refs_1_, bf16[1536,256]{1,0:T(8,128)(2,1)S(1)} %get-tuple-element.80.refs_2_, bf16[1536,256]{1,0:T(8,128)(2,1)S(1)} %get-tuple-element.81.refs_3_, ...), custom_call_target="tpu_custom_call" | custom-call | flops 11274289152 | bytes 11010048 | tf_op jit(solution)/shard_map/state_terms/pallas_call | solution.py:238
  123.0 5.3 %collective-permute-done.13.recv_ref = bf16[224,256]{1,0:T(8,128)(2,1)S(1)} collective-permute-done((bf16[224,256]{1,0:T(8,128)(2,1)S(1)}, bf16[224,256]{1,0:T(8,128)(2,1)S(1)}, u32[]{:S(2)}, u32[]{:S(2)}) %collective-permute-start.13) | collective-permute-done | bytes 114720 | tf_op jit(solution)/shard_map/ppermute | solution.py:23
  128.5 3.3 %collective-permute-start.12 = (bf16[224,256]{1,0:T(8,128)(2,1)S(1)}, bf16[224,256]{1,0:T(8,128)(2,1)S(1)}, u32[]{:S(2)}, u32[]{:S(2)}) collective-permute-start(bf16[224,256]{1,0:T(8,128)(2,1)S(1)} %get-tuple-element.90.refs_0_), channel_id=1, source_target_pairs={{0,16},{4,20},{8,24},{12,28},{16,0},{20,4},{24,8},{28,12},{1,17},{... | collective-permute-start | bytes 344072 | tf_op jit(solution)/shard_map/ppermute | solution.py:23
  131.8 5.0 %collective-permute-done.12.recv_ref = bf16[224,256]{1,0:T(8,128)(2,1)S(1)} collective-permute-done((bf16[224,256]{1,0:T(8,128)(2,1)S(1)}, bf16[224,256]{1,0:T(8,128)(2,1)S(1)}, u32[]{:S(2)}, u32[]{:S(2)}) %collective-permute-start.12) | collective-permute-done | bytes 114720 | tf_op jit(solution)/shard_map/ppermute | solution.py:23
  142.0 4.1 %collective-permute-done.16.recv_ref = bf16[224,256]{1,0:T(8,128)(2,1)S(1)} collective-permute-done((bf16[224,256]{1,0:T(8,128)(2,1)S(1)}, bf16[224,256]{1,0:T(8,128)(2,1)S(1)}, u32[]{:S(2)}, u32[]{:S(2)}) %collective-permute-start.16) | collective-permute-done | bytes 114720 | tf_op jit(solution)/shard_map/ppermute | solution.py:23
  149.4 5.8 %collective-permute-done.15.recv_ref = bf16[224,256]{1,0:T(8,128)(2,1)S(1)} collective-permute-done((bf16[224,256]{1,0:T(8,128)(2,1)S(1)}, bf16[224,256]{1,0:T(8,128)(2,1)S(1)}, u32[]{:S(2)}, u32[]{:S(2)}) %collective-permute-start.15) | collective-permute-done | bytes 114720 | tf_op jit(solution)/shard_map/ppermute | solution.py:23
  158.4 3.4 %collective-permute-start.20 = (bf16[224,256]{1,0:T(8,128)(2,1)S(1)}, bf16[224,256]{1,0:T(8,128)(2,1)S(1)}, u32[]{:S(2)}, u32[]{:S(2)}) collective-permute-start(bf16[224,256]{1,0:T(8,128)(2,1)S(1)} %add.57.refs_0_.own_ref), channel_id=1, source_target_pairs={{0,16},{4,20},{8,24},{12,28},{16,0},{20,4},{24,8},{28,12},{1,17},{... | collective-permute-start | bytes 344072 | tf_op jit(solution)/shard_map/ppermute | solution.py:23
  161.8 3.1 %collective-permute-done.20.recv_ref = bf16[224,256]{1,0:T(8,128)(2,1)S(1)} collective-permute-done((bf16[224,256]{1,0:T(8,128)(2,1)S(1)}, bf16[224,256]{1,0:T(8,128)(2,1)S(1)}, u32[]{:S(2)}, u32[]{:S(2)}) %collective-permute-start.20) | collective-permute-done | bytes 114720 | tf_op jit(solution)/shard_map/ppermute | solution.py:23
  170.0 5.7 %collective-permute-done.19.recv_ref = bf16[224,256]{1,0:T(8,128)(2,1)S(1)} collective-permute-done((bf16[224,256]{1,0:T(8,128)(2,1)S(1)}, bf16[224,256]{1,0:T(8,128)(2,1)S(1)}, u32[]{:S(2)}, u32[]{:S(2)}) %collective-permute-start.19) | collective-permute-done | bytes 114720 | tf_op jit(solution)/shard_map/ppermute | solution.py:23
  178.8 6.4 %collective-permute-done.23.recv_ref = bf16[224,256]{1,0:T(8,128)(2,1)S(1)} collective-permute-done((bf16[224,256]{1,0:T(8,128)(2,1)S(1)}, bf16[224,256]{1,0:T(8,128)(2,1)S(1)}, u32[]{:S(2)}, u32[]{:S(2)}) %collective-permute-start.23) | collective-permute-done | bytes 114720 | tf_op jit(solution)/shard_map/ppermute | solution.py:23
  187.1 4.2 %collective-permute-done.26.recv_ref = bf16[448,256]{1,0:T(8,128)(2,1)S(1)} collective-permute-done((bf16[448,256]{1,0:T(8,128)(2,1)S(1)}, bf16[448,256]{1,0:T(8,128)(2,1)S(1)}, u32[]{:S(2)}, u32[]{:S(2)}) %collective-permute-start.26) | collective-permute-done | bytes 229408 | tf_op jit(solution)/shard_map/ppermute | solution.py:23
  193.0 4.1 %all-to-all-start.2 = ((bf16[8,2,32,896]{3,2,1,0:T(8,128)(2,1)}), bf16[8,2,32,896]{3,2,1,0:T(8,128)(2,1)S(1)}, u32[]{:S(2)}, u32[]{:S(2)}) async-start(bf16[8,2,32,896]{3,2,1,0:T(8,128)(2,1)} %bitcast.10), calls=%async_computation.2 | async-start | bytes 1835008 | tf_op jit(solution)/shard_map/all_to_all | solution.py:495
  199.2 12.2 %collective-permute-done.28.recv_ref = bf16[896,256]{1,0:T(8,128)(2,1)S(1)} collective-permute-done((bf16[896,256]{1,0:T(8,128)(2,1)S(1)}, bf16[896,256]{1,0:T(8,128)(2,1)S(1)}, u32[]{:S(2)}, u32[]{:S(2)}) %collective-permute-start.28) | collective-permute-done | bytes 458784 | tf_op jit(solution)/shard_map/ppermute | solution.py:23
  (115 shorter events, 52.4 us)
Async XLA Ops:
  19.3 25.5 %all-to-all-start.1 = ((bf16[8,2,32,896]{3,2,1,0:T(8,128)(2,1)}), bf16[8,2,32,896]{3,2,1,0:T(8,128)(2,1)S(1)}, u32[]{:S(2)}, u32[]{:S(2)}) async-start(bf16[8,2,32,896]{3,2,1,0:T(8,128)(2,1)} %bitcast.2), calls=%async_computation.1 | async-start | bytes 1835008 | tf_op jit(solution)/shard_map/all_to_all | solution.py:436
  47.5 15.1 %collective-permute-start.1 = (bf16[384,896]{1,0:T(8,128)(2,1)S(1)}, bf16[384,896]{1,0:T(8,128)(2,1)}, u32[]{:S(2)}, u32[]{:S(2)}) collective-permute-start(bf16[384,896]{1,0:T(8,128)(2,1)S(1)} %bitcast.18), channel_id=1, source_target_pairs={{0,2},{1,3},{2,0},{3,1},{4,6},{5,7},{6,4},{7,5},{8,10},{9,11},{10,... | collective-permute-start | bytes 2064392 | tf_op jit(solution)/shard_map/ppermute | solution.py:23
  49.1 13.5 %collective-permute-start = (bf16[384,896]{1,0:T(8,128)(2,1)S(1)}, bf16[384,896]{1,0:T(8,128)(2,1)}, u32[]{:S(2)}, u32[]{:S(2)}) collective-permute-start(bf16[384,896]{1,0:T(8,128)(2,1)S(1)} %bitcast.19), channel_id=1, source_target_pairs={{0,1},{1,0},{2,3},{3,2},{4,5},{5,4},{6,7},{7,6},{8,9},{9,8},{10,11... | collective-permute-start | bytes 2064392 | tf_op jit(solution)/shard_map/ppermute | solution.py:23
  75.5 13.7 %collective-permute-start.3 = (bf16[896,256]{1,0:T(8,128)(2,1)S(1)}, bf16[896,256]{1,0:T(8,128)(2,1)S(1)}, u32[]{:S(2)}, u32[]{:S(2)}) collective-permute-start(bf16[896,256]{1,0:T(8,128)(2,1)S(1)} %get-tuple-element.63.refs_11_), channel_id=1, source_target_pairs={{0,4},{4,0},{8,12},{12,8},{16,20},{20,16},{24,28},{28,24},{1,5},{5... | collective-permute-start | bytes 1376264 | tf_op jit(solution)/shard_map/ppermute | solution.py:23
  84.4 17.3 %collective-permute-start.4 = (bf16[896,256]{1,0:T(8,128)(2,1)S(1)}, bf16[896,256]{1,0:T(8,128)(2,1)S(1)}, u32[]{:S(2)}, u32[]{:S(2)}) collective-permute-start(bf16[896,256]{1,0:T(8,128)(2,1)S(1)} %get-tuple-element.67.refs_0_), channel_id=1, source_target_pairs={{0,4},{4,0},{8,12},{12,8},{16,20},{20,16},{24,28},{28,24},{1,5},{5... | collective-permute-start | bytes 1376264 | tf_op jit(solution)/shard_map/ppermute | solution.py:23
  89.3 9.0 %collective-permute-start.5 = (bf16[448,256]{1,0:T(8,128)(2,1)S(1)}, bf16[448,256]{1,0:T(8,128)(2,1)S(1)}, u32[]{:S(2)}, u32[]{:S(2)}) collective-permute-start(bf16[448,256]{1,0:T(8,128)(2,1)S(1)} %get-tuple-element.68.refs_11_), channel_id=1, source_target_pairs={{0,8},{4,12},{8,0},{12,4},{16,24},{20,28},{24,16},{28,20},{1,9},{5... | collective-permute-start | bytes 688136 | tf_op jit(solution)/shard_map/ppermute | solution.py:23
  96.2 12.5 %collective-permute-start.6 = (bf16[896,256]{1,0:T(8,128)(2,1)S(1)}, bf16[896,256]{1,0:T(8,128)(2,1)S(1)}, u32[]{:S(2)}, u32[]{:S(2)}) collective-permute-start(bf16[896,256]{1,0:T(8,128)(2,1)S(1)} %get-tuple-element.73.refs_0_), channel_id=1, source_target_pairs={{0,4},{4,0},{8,12},{12,8},{16,20},{20,16},{24,28},{28,24},{1,5},{5... | collective-permute-start | bytes 1376264 | tf_op jit(solution)/shard_map/ppermute | solution.py:23
  98.4 10.2 %collective-permute-start.8 = (bf16[224,256]{1,0:T(8,128)(2,1)S(1)}, bf16[224,256]{1,0:T(8,128)(2,1)S(1)}, u32[]{:S(2)}, u32[]{:S(2)}) collective-permute-start(bf16[224,256]{1,0:T(8,128)(2,1)S(1)} %get-tuple-element.74.refs_0_), channel_id=1, source_target_pairs={{0,16},{4,20},{8,24},{12,28},{16,0},{20,4},{24,8},{28,12},{1,17},{... | collective-permute-start | bytes 344072 | tf_op jit(solution)/shard_map/ppermute | solution.py:23
  118.1 37.1 %collective-permute-start.9 = (bf16[768,896]{1,0:T(8,128)(2,1)S(1)}, bf16[768,896]{1,0:T(8,128)(2,1)S(1)}, u32[]{:S(2)}, u32[]{:S(2)}) collective-permute-start(bf16[768,896]{1,0:T(8,128)(2,1)S(1)} %get-tuple-element.93.refs_0_), channel_id=1, source_target_pairs={{0,1},{1,0},{2,3},{3,2},{4,5},{5,4},{6,7},{7,6},{8,9},{9,8},{10,11... | collective-permute-start | bytes 4128776 | tf_op jit(solution)/shard_map/ppermute | solution.py:23
  118.2 18.7 %collective-permute-start.10 = (bf16[896,256]{1,0:T(8,128)(2,1)S(1)}, bf16[896,256]{1,0:T(8,128)(2,1)S(1)}, u32[]{:S(2)}, u32[]{:S(2)}) collective-permute-start(bf16[896,256]{1,0:T(8,128)(2,1)S(1)} %get-tuple-element.89.refs_0_), channel_id=1, source_target_pairs={{0,4},{4,0},{8,12},{12,8},{16,20},{20,16},{24,28},{28,24},{1,5},{5... | collective-permute-start | bytes 1376264 | tf_op jit(solution)/shard_map/ppermute | solution.py:23
  119.7 8.7 %collective-permute-start.13 = (bf16[224,256]{1,0:T(8,128)(2,1)S(1)}, bf16[224,256]{1,0:T(8,128)(2,1)S(1)}, u32[]{:S(2)}, u32[]{:S(2)}) collective-permute-start(bf16[224,256]{1,0:T(8,128)(2,1)S(1)} %add.55.refs_0_.own_ref), channel_id=1, source_target_pairs={{0,16},{4,20},{8,24},{12,28},{16,0},{20,4},{24,8},{28,12},{1,17},{... | collective-permute-start | bytes 344072 | tf_op jit(solution)/shard_map/ppermute | solution.py:23
  121.7 15.1 %collective-permute-start.11 = (bf16[448,256]{1,0:T(8,128)(2,1)S(1)}, bf16[448,256]{1,0:T(8,128)(2,1)S(1)}, u32[]{:S(2)}, u32[]{:S(2)}) collective-permute-start(bf16[448,256]{1,0:T(8,128)(2,1)S(1)} %get-tuple-element.91.refs_10_), channel_id=1, source_target_pairs={{0,8},{4,12},{8,0},{12,4},{16,24},{20,28},{24,16},{28,20},{1,9},{5... | collective-permute-start | bytes 688136 | tf_op jit(solution)/shard_map/ppermute | solution.py:23
  128.4 10.2 %collective-permute-start.17 = (bf16[448,256]{1,0:T(8,128)(2,1)S(1)}, bf16[448,256]{1,0:T(8,128)(2,1)S(1)}, u32[]{:S(2)}, u32[]{:S(2)}) collective-permute-start(bf16[448,256]{1,0:T(8,128)(2,1)S(1)} %join.8.refs_0_.own_ref), channel_id=1, source_target_pairs={{0,8},{4,12},{8,0},{12,4},{16,24},{20,28},{24,16},{28,20},{1,9},{5... | collective-permute-start | bytes 688136 | tf_op jit(solution)/shard_map/ppermute | solution.py:23
  128.5 8.4 %collective-permute-start.12 = (bf16[224,256]{1,0:T(8,128)(2,1)S(1)}, bf16[224,256]{1,0:T(8,128)(2,1)S(1)}, u32[]{:S(2)}, u32[]{:S(2)}) collective-permute-start(bf16[224,256]{1,0:T(8,128)(2,1)S(1)} %get-tuple-element.90.refs_0_), channel_id=1, source_target_pairs={{0,16},{4,20},{8,24},{12,28},{16,0},{20,4},{24,8},{28,12},{1,17},{... | collective-permute-start | bytes 344072 | tf_op jit(solution)/shard_map/ppermute | solution.py:23
  138.6 16.9 %collective-permute-start.22 = (bf16[896,256]{1,0:T(8,128)(2,1)S(1)}, bf16[896,256]{1,0:T(8,128)(2,1)S(1)}, u32[]{:S(2)}, u32[]{:S(2)}) collective-permute-start(bf16[896,256]{1,0:T(8,128)(2,1)S(1)} %join.9.refs_0_.own_ref), channel_id=1, source_target_pairs={{0,4},{4,0},{8,12},{12,8},{16,20},{20,16},{24,28},{28,24},{1,5},{5... | collective-permute-start | bytes 1376264 | tf_op jit(solution)/shard_map/ppermute | solution.py:23
  138.8 7.2 %collective-permute-start.16 = (bf16[224,256]{1,0:T(8,128)(2,1)S(1)}, bf16[224,256]{1,0:T(8,128)(2,1)S(1)}, u32[]{:S(2)}, u32[]{:S(2)}) collective-permute-start(bf16[224,256]{1,0:T(8,128)(2,1)S(1)} %add.56.refs_0_.own_ref), channel_id=1, source_target_pairs={{0,16},{4,20},{8,24},{12,28},{16,0},{20,4},{24,8},{28,12},{1,17},{... | collective-permute-start | bytes 344072 | tf_op jit(solution)/shard_map/ppermute | solution.py:23
  141.2 14.0 %collective-permute-start.14 = (bf16[448,256]{1,0:T(8,128)(2,1)S(1)}, bf16[448,256]{1,0:T(8,128)(2,1)S(1)}, u32[]{:S(2)}, u32[]{:S(2)}) collective-permute-start(bf16[448,256]{1,0:T(8,128)(2,1)S(1)} %get-tuple-element.99.refs_0_), channel_id=1, source_target_pairs={{0,8},{4,12},{8,0},{12,4},{16,24},{20,28},{24,16},{28,20},{1,9},{5... | collective-permute-start | bytes 688136 | tf_op jit(solution)/shard_map/ppermute | solution.py:23
  146.1 10.8 %collective-permute-start.21 = (bf16[448,256]{1,0:T(8,128)(2,1)S(1)}, bf16[448,256]{1,0:T(8,128)(2,1)S(1)}, u32[]{:S(2)}, u32[]{:S(2)}) collective-permute-start(bf16[448,256]{1,0:T(8,128)(2,1)S(1)} %join.10.refs_0_.own_ref), channel_id=1, source_target_pairs={{0,8},{4,12},{8,0},{12,4},{16,24},{20,28},{24,16},{28,20},{1,9},{5... | collective-permute-start | bytes 688136 | tf_op jit(solution)/shard_map/ppermute | solution.py:23
  156.9 18.8 %collective-permute-start.25 = (bf16[896,256]{1,0:T(8,128)(2,1)S(1)}, bf16[896,256]{1,0:T(8,128)(2,1)S(1)}, u32[]{:S(2)}, u32[]{:S(2)}) collective-permute-start(bf16[896,256]{1,0:T(8,128)(2,1)S(1)} %join.11.refs_0_.own_ref), channel_id=1, source_target_pairs={{0,4},{4,0},{8,12},{12,8},{16,20},{20,16},{24,28},{28,24},{1,5},{5... | collective-permute-start | bytes 1376264 | tf_op jit(solution)/shard_map/ppermute | solution.py:23
  164.9 12.2 %collective-permute-start.24 = (bf16[448,256]{1,0:T(8,128)(2,1)S(1)}, bf16[448,256]{1,0:T(8,128)(2,1)S(1)}, u32[]{:S(2)}, u32[]{:S(2)}) collective-permute-start(bf16[448,256]{1,0:T(8,128)(2,1)S(1)} %join.12.refs_0_.own_ref), channel_id=1, source_target_pairs={{0,8},{4,12},{8,0},{12,4},{16,24},{20,28},{24,16},{28,20},{1,9},{5... | collective-permute-start | bytes 688136 | tf_op jit(solution)/shard_map/ppermute | solution.py:23
  167.3 24.0 %collective-permute-start.18 = (bf16[384,896]{1,0:T(8,128)(2,1)S(1)}, bf16[384,896]{1,0:T(8,128)(2,1)S(1)}, u32[]{:S(2)}, u32[]{:S(2)}) collective-permute-start(bf16[384,896]{1,0:T(8,128)(2,1)S(1)} %get-tuple-element.103.refs_0_), channel_id=1, source_target_pairs={{0,2},{1,3},{2,0},{3,1},{4,6},{5,7},{6,4},{7,5},{8,10},{9,11},{10,... | collective-permute-start | bytes 2064392 | tf_op jit(solution)/shard_map/ppermute | solution.py:23
  177.2 8.5 %collective-permute-start.27 = (bf16[896,256]{1,0:T(8,128)(2,1)S(1)}, bf16[896,256]{1,0:T(8,128)(2,1)S(1)}, u32[]{:S(2)}, u32[]{:S(2)}) collective-permute-start(bf16[896,256]{1,0:T(8,128)(2,1)S(1)} %join.13.refs_0_.own_ref), channel_id=1, source_target_pairs={{0,4},{4,0},{8,12},{12,8},{16,20},{20,16},{24,28},{28,24},{1,5},{5... | collective-permute-start | bytes 1376264 | tf_op jit(solution)/shard_map/ppermute | solution.py:23
  193.0 19.8 %all-to-all-start.2 = ((bf16[8,2,32,896]{3,2,1,0:T(8,128)(2,1)}), bf16[8,2,32,896]{3,2,1,0:T(8,128)(2,1)S(1)}, u32[]{:S(2)}, u32[]{:S(2)}) async-start(bf16[8,2,32,896]{3,2,1,0:T(8,128)(2,1)} %bitcast.10), calls=%async_computation.2 | async-start | bytes 1835008 | tf_op jit(solution)/shard_map/all_to_all | solution.py:495
  197.1 14.3 %collective-permute-start.28 = (bf16[896,256]{1,0:T(8,128)(2,1)S(1)}, bf16[896,256]{1,0:T(8,128)(2,1)S(1)}, u32[]{:S(2)}, u32[]{:S(2)}) collective-permute-start(bf16[896,256]{1,0:T(8,128)(2,1)S(1)} %join.15.refs_0_.own_ref), channel_id=1, source_target_pairs={{0,4},{4,0},{8,12},{12,8},{16,20},{20,16},{24,28},{28,24},{1,5},{5... | collective-permute-start | bytes 1376264 | tf_op jit(solution)/shard_map/ppermute | solution.py:23
  (17 other events, 175.8 us)

commit v2 on v1

--- a/solution.py
+++ b/solution.py
@@ -27,19 +27,89 @@
     return pl.BlockSpec(memory_space=pl.ANY)
 
 
+def in_hbm(arrays):
+    return [pltpu.with_memory_space_constraint(x, pltpu.HBM) for x in arrays]
+
+
 def hbm_spec():
     return pl.BlockSpec(memory_space=pltpu.HBM)
 
 
-def head_kernel(groups, spans, head_dim, start, extra, *refs):
+def turn_kernel(wk, wv, out_ref, held, sem):
+    half = held.shape[0] // 2
+    held[:half] = wk[...].T
+    held[half:] = wv[...].T
+    copy = pltpu.make_async_copy(held, out_ref, sem)
+    copy.start()
+    copy.wait()
+
+
+def run_turn(key_weight, value_weight):
+    enc, width = key_weight.shape
+    vmem = pl.BlockSpec(memory_space=pltpu.VMEM)
+    return pl.pallas_call(
+        turn_kernel,
+        out_shape=pltpu.HBM((2 * width, enc), key_weight.dtype),
+        in_specs=[vmem, vmem],
+        out_specs=hbm_spec(),
+        scratch_shapes=[pltpu.VMEM((2 * width, enc), key_weight.dtype), pltpu.SemaphoreType.DMA],
+        compiler_params=pltpu.CompilerParams(vmem_limit_bytes=VMEM_GRANT),
+        cost_estimate=pl.CostEstimate(flops=enc * width * 2000, bytes_accessed=8 * enc * width, transcendentals=0),
+        name="turn",
+    )(key_weight, value_weight)
+
+
+def project_kernel(count, *refs):
+    slabs = refs[:count]
+    wk, wv = refs[count : count + 2]
+    outs, (keys, values, turned, sems) = refs[-7:-4], refs[-4:]
+
+    def store(i, held, value):
+        held[...] = value.astype(jnp.bfloat16)
+        copy = pltpu.make_async_copy(held, outs[i], sems.at[i])
+        copy.start()
+        return copy
+
+    rows = slabs[0][...] if count == 1 else jnp.concatenate([slab[...] for slab in slabs], axis=0)
+    copies = [
+        store(0, keys, jnp.dot(rows, wk[...], preferred_element_type=jnp.float32)),
+        store(1, values, jnp.dot(rows, wv[...], preferred_element_type=jnp.float32)),
+        store(2, turned, rows.T),
+    ]
+    for copy in copies:
+        copy.wait()
+
+
+def run_project(slabs, key_weight, value_weight, after):
+    enc, width = key_weight.shape
+    rows = sum(slab.shape[0] for slab in slabs)
+    vmem = pl.BlockSpec(memory_space=pltpu.VMEM)
+    shapes = [(rows, width), (rows, width), (enc, rows)]
+    return pl.pallas_call(
+        functools.partial(project_kernel, len(slabs)),
+        out_shape=[pltpu.HBM(shape, jnp.bfloat16) for shape in shapes],
+        in_specs=[vmem] * (len(slabs) + 2) + [hbm_spec()] * len(after),
+        out_specs=[hbm_spec()] * 3,
+        scratch_shapes=[pltpu.VMEM(shape, jnp.bfloat16) for shape in shapes] + [pltpu.SemaphoreType.DMA((3,))],
+        compiler_params=pltpu.CompilerParams(vmem_limit_bytes=VMEM_GRANT),
+        cost_estimate=pl.CostEstimate(
+            flops=4 * rows * enc * width, bytes_accessed=4 * (rows + enc) * width, transcendentals=0
+        ),
+        name="project",
+    )(*slabs, key_weight, value_weight, *in_hbm(after))
+
+
+def head_kernel(groups, spans, head_dim, start, parts, extra, *refs):
     flag_ref = refs[0]
-    slabs = refs[1 : 1 + groups]
-    wk_hbm, wv_hbm, q_hbm, g_hbm = refs[1 + groups : 5 + groups]
-    att_hbm, dq_hbm, dk_hbm, dv_hbm, keep_ref, send_ref = refs[5 + groups + extra : 11 + groups + extra]
-    rows, wk, wv, q_ref, g_ref, keys, values, att_ref, dq_ref, dk_ref, dv_ref, grads, sems = refs[11 + groups + extra :]
+    count = len(parts)
+    keys_hbm, values_hbm, turned_hbm = refs[1 : 1 + count], refs[1 + count : 1 + 2 * count], refs[1 + 2 * count : 1 + 3 * count]
+    q_hbm, g_hbm = refs[1 + 3 * count : 3 + 3 * count]
+    refs = refs[3 + 3 * count + extra :]
+    att_hbm, dq_hbm, dk_hbm, dv_hbm, keep_ref, send_ref = refs[:6]
+    turned, q_ref, g_ref, keys, values, att_ref, dq_ref, dk_ref, dv_ref, grads, sems = refs[6:]
     tokens, width = q_ref.shape
     span_len = tokens // spans
-    block = rows.shape[0] // groups
+    block = keys.shape[0] // groups
     part = block // spans
     scale = 1.0 / head_dim**0.5
     columns = pl.ds(start, width)
@@ -49,17 +119,18 @@
         copy.start()
         return copy
 
-    weights_in = [begin(wk_hbm.at[:, columns], wk, groups), begin(wv_hbm.at[:, columns], wv, groups + 1)]
-    rows_in = [begin(slabs[r], rows.at[pl.ds(r * block, block)], r) for r in range(groups)]
-    tokens_in = [begin(q_hbm.at[:, columns], q_ref, groups + 2), begin(g_hbm.at[:, columns], g_ref, groups + 3)]
-    for copy in weights_in:
-        copy.wait()
-    for r in range(groups):
-        rows_in[r].wait()
-        at = pl.ds(r * block, block)
-        keys[at, :] = jnp.dot(rows[at, :], wk[...], preferred_element_type=jnp.float32).astype(jnp.bfloat16)
-        values[at, :] = jnp.dot(rows[at, :], wv[...], preferred_element_type=jnp.float32).astype(jnp.bfloat16)
-    for copy in tokens_in:
+    copies = [begin(q_hbm.at[:, columns], q_ref, 0), begin(g_hbm.at[:, columns], g_ref, 1)]
+    first = 0
+    for i, size in enumerate(parts):
+        to = pl.ds(first, size)
+        copies.append(begin(keys_hbm[i].at[:, columns], keys.at[to], 2 + 3 * i))
+        copies.append(begin(values_hbm[i].at[:, columns], values.at[to], 3 + 3 * i))
+        first += size
+    later, first = [], 0
+    for i, size in enumerate(parts):
+        later.append(begin(turned_hbm[i], turned.at[:, pl.ds(first, size)], 4 + 3 * i))
+        first += size
+    for copy in copies:
         copy.wait()
 
     def spread(x):
@@ -75,97 +146,87 @@
             out = jnp.where(lane_head == h, x[h * span_len : (h + 1) * span_len], out)
         return out
 
-    def span_rows(ref, c, cols):
-        return jnp.concatenate([ref[pl.ds(r * block + c * part, part), cols] for r in range(groups)], axis=0)
+    def span_rows(ref, c):
+        return jnp.concatenate([ref[pl.ds(r * block + c * part, part), :] for r in range(groups)], axis=0)
 
     contract_last = (((1,), (1,)), ((), ()))
     contract_first = (((0,), (0,)), ((), ()))
     at = [pl.ds(c * span_len, span_len) for c in range(spans)]
     swapped = flag_ref[0] == 1
-    pair = 2 * head_dim
-    for first in range(0, width, pair):
-        cols = slice(first, min(first + pair, width))
-        send_cols = slice(width + cols.start, width + cols.stop)
-        every = range(spans)
-        scores = [
-            lax.dot_general(
-                span_rows(keys, c, cols), spread(q_ref[at[c], cols]), contract_last,
-                preferred_element_type=jnp.float32,
-            )
-            * scale
-            for c in every
-        ]
-        prob_grad = [
-            lax.dot_general(
-                span_rows(values, c, cols), spread(g_ref[at[c], cols]), contract_last,
-                preferred_element_type=jnp.float32,
-            )
-            for c in every
-        ]
-        weights = [jnp.exp(x - jnp.max(x, axis=0, keepdims=True)) for x in scores]
-        probs = [x * (1.0 / jnp.sum(x, axis=0, keepdims=True)) for x in weights]
-        low = [x.astype(jnp.bfloat16) for x in probs]
-        row_dot = [jnp.sum(p * d, axis=0, keepdims=True) for p, d in zip(probs, prob_grad)]
-        score_grad = [(scale * p * (d - t)).astype(jnp.bfloat16) for p, d, t in zip(probs, prob_grad, row_dot)]
-        for c in every:
-            dk = jnp.dot(score_grad[c], spread(q_ref[at[c], cols]), preferred_element_type=jnp.float32)
-            dv = jnp.dot(low[c], spread(g_ref[at[c], cols]), preferred_element_type=jnp.float32)
-            dk, dv = dk.astype(jnp.bfloat16), dv.astype(jnp.bfloat16)
-            for r in range(groups):
-                to = pl.ds(r * block + c * part, part)
-                piece = slice(r * part, (r + 1) * part)
-                dk_ref[to, cols] = dk[piece]
-                dv_ref[to, cols] = dv[piece]
-                grads[to, cols] = jnp.where(swapped, dv[piece], dk[piece])
-                grads[to, send_cols] = jnp.where(swapped, dk[piece], dv[piece])
-        for c in every:
-            att = lax.dot_general(
-                low[c], span_rows(values, c, cols), contract_first, preferred_element_type=jnp.float32
-            )
-            att_ref[at[c], cols] = collect(att).astype(jnp.bfloat16)
-            dq = lax.dot_general(
-                score_grad[c], span_rows(keys, c, cols), contract_first, preferred_element_type=jnp.float32
-            )
-            dq_ref[at[c], cols] = collect(dq).astype(jnp.bfloat16)
+    every = range(spans)
+    scores = [
+        lax.dot_general(
+            span_rows(keys, c), spread(q_ref[at[c], :]), contract_last, preferred_element_type=jnp.float32
+        )
+        * scale
+        for c in every
+    ]
+    prob_grad = [
+        lax.dot_general(
+            span_rows(values, c), spread(g_ref[at[c], :]), contract_last, preferred_element_type=jnp.float32
+        )
+        for c in every
+    ]
+    weights = [jnp.exp(x - jnp.max(x, axis=0, keepdims=True)) for x in scores]
+    probs = [x * (1.0 / jnp.sum(x, axis=0, keepdims=True)) for x in weights]
+    low = [x.astype(jnp.bfloat16) for x in probs]
+    row_dot = [jnp.sum(p * d, axis=0, keepdims=True) for p, d in zip(probs, prob_grad)]
+    score_grad = [(scale * p * (d - t)).astype(jnp.bfloat16) for p, d, t in zip(probs, prob_grad, row_dot)]
+    for c in every:
+        dk = jnp.dot(score_grad[c], spread(q_ref[at[c], :]), preferred_element_type=jnp.float32)
+        dv = jnp.dot(low[c], spread(g_ref[at[c], :]), preferred_element_type=jnp.float32)
+        dk, dv = dk.astype(jnp.bfloat16), dv.astype(jnp.bfloat16)
+        for r in range(groups):
+            to = pl.ds(r * block + c * part, part)
+            piece = slice(r * part, (r + 1) * part)
+            dk_ref[to, :] = dk[piece]
+            dv_ref[to, :] = dv[piece]
+            grads[to, :width] = jnp.where(swapped, dv[piece], dk[piece])
+            grads[to, width:] = jnp.where(swapped, dk[piece], dv[piece])
+    for c in every:
+        att = lax.dot_general(low[c], span_rows(values, c), contract_first, preferred_element_type=jnp.float32)
+        att_ref[at[c], :] = collect(att).astype(jnp.bfloat16)
+        dq = lax.dot_general(score_grad[c], span_rows(keys, c), contract_first, preferred_element_type=jnp.float32)
+        dq_ref[at[c], :] = collect(dq).astype(jnp.bfloat16)
     results = [
         begin(att_ref, att_hbm.at[:, columns], 0),
         begin(dq_ref, dq_hbm.at[:, columns], 1),
         begin(dk_ref, dk_hbm, 2),
         begin(dv_ref, dv_hbm, 3),
     ]
-    both = lax.dot_general(rows[...], grads[...], contract_first, preferred_element_type=jnp.float32)
+    for copy in later:
+        copy.wait()
+    both = jnp.dot(turned[...], grads[...], preferred_element_type=jnp.float32)
     keep_ref[...] = both[:, :width]
     send_ref[...] = both[:, width:].astype(jnp.bfloat16)
     for copy in results:
         copy.wait()
 
 
-def run_heads(start, chunk, flag, slabs, key_weight, value_weight, queries, out_grad, chain, after, spans, head_dim):
-    groups = len(slabs)
+def run_heads(start, chunk, flag, parts, groups, queries, out_grad, chain, after, spans, head_dim):
     tokens, local_width = queries.shape
-    block, enc = slabs[0].shape
-    total = groups * block
+    keys, values, turned = zip(*parts)
+    sizes = [k.shape[0] for k in keys]
+    total, enc = sum(sizes), turned[0].shape[0]
     bf = jnp.bfloat16
     extra = list(chain) + list(after)
+    first = 3 + 3 * len(parts)
     outs = pl.pallas_call(
-        functools.partial(head_kernel, groups, spans, head_dim, start, len(extra)),
+        functools.partial(head_kernel, groups, spans, head_dim, start, sizes, len(extra)),
         out_shape=[
-            jax.ShapeDtypeStruct((tokens, local_width), bf),
-            jax.ShapeDtypeStruct((tokens, local_width), bf),
-            jax.ShapeDtypeStruct((total, chunk), bf),
-            jax.ShapeDtypeStruct((total, chunk), bf),
+            pltpu.HBM((tokens, local_width), bf),
+            pltpu.HBM((tokens, local_width), bf),
+            pltpu.HBM((total, chunk), bf),
+            pltpu.HBM((total, chunk), bf),
             jax.ShapeDtypeStruct((enc, chunk), jnp.float32),
             jax.ShapeDtypeStruct((enc, chunk), bf),
         ],
         in_specs=[pl.BlockSpec(memory_space=pltpu.SMEM)]
-        + [any_spec()] * groups
-        + [hbm_spec()] * (4 + len(chain))
+        + [hbm_spec()] * (3 * len(parts) + 2 + len(chain))
         + [any_spec()] * len(after),
         out_specs=[hbm_spec()] * 4 + [pl.BlockSpec(memory_space=pltpu.VMEM)] * 2,
         scratch_shapes=[
-            pltpu.VMEM((total, enc), bf),
-            pltpu.VMEM((enc, chunk), bf),
-            pltpu.VMEM((enc, chunk), bf),
+            pltpu.VMEM((enc, total), bf),
             pltpu.VMEM((tokens, chunk), bf),
             pltpu.VMEM((tokens, chunk), bf),
             pltpu.VMEM((total, chunk), bf),
@@ -175,30 +236,27 @@
             pltpu.VMEM((total, chunk), bf),
             pltpu.VMEM((total, chunk), bf),
             pltpu.VMEM((total, 2 * chunk), bf),
-            pltpu.SemaphoreType.DMA((groups + 4,)),
+            pltpu.SemaphoreType.DMA((2 + 3 * len(parts),)),
         ],
-        input_output_aliases={5 + groups + i: i for i in range(len(chain))},
+        input_output_aliases={first + i: i for i in range(len(chain))},
         compiler_params=pltpu.CompilerParams(vmem_limit_bytes=VMEM_GRANT),
         cost_estimate=pl.CostEstimate(
-            flops=2 * total * enc * chunk * 8, bytes_accessed=4 * total * enc, transcendentals=total * tokens
+            flops=2 * total * enc * chunk * 6, bytes_accessed=4 * total * enc, transcendentals=total * tokens
         ),
         name="heads",
-    )(flag, *slabs, key_weight, value_weight, queries, out_grad, *extra)
+    )(flag, *in_hbm([*keys, *values, *turned, queries, out_grad, *chain]), *after)
     return outs[:2], outs[2], outs[3], outs[4:]
 
 
 def state_kernel(groups, widths, extra, *refs):
     count = len(widths)
-    dk_hbm, dv_hbm = refs[:count], refs[count : 2 * count]
-    wk_hbm, wv_hbm = refs[2 * count : 2 * count + 2]
-    keep_ref, send_ref, grads, weights, sems = refs[2 * count + 2 + extra :]
-    half = weights.shape[1] // 2
+    dk_hbm, dv_hbm, weights_hbm = refs[:count], refs[count : 2 * count], refs[2 * count]
+    keep_ref, send_ref, grads, weights, sems = refs[2 * count + 1 + extra :]
+    half = weights.shape[0] // 2
     block = grads.shape[0] // groups
 
-    copies = [
-        pltpu.make_async_copy(wk_hbm, weights.at[:, pl.ds(0, half)], sems.at[0, 0]),
-        pltpu.make_async_copy(wv_hbm, weights.at[:, pl.ds(half, half)], sems.at[0, 1]),
-    ]
+    load = pltpu.make_async_copy(weights_hbm, weights, sems.at[0, 0])
+    load.start()
     blocks = []
     for r in range(groups):
         rows = pl.ds(r * block, block)
@@ -209,55 +267,46 @@
                 target = grads.at[rows, pl.ds(k * half + first, widths[j])]
                 parts.append(pltpu.make_async_copy(source.at[rows, :], target, sems.at[1 + r, 2 * j + k]))
         blocks.append(parts)
-    for copy in copies:
-        copy.start()
     for parts in blocks:
         for copy in parts:
             copy.start()
-    for copy in copies:
-        copy.wait()
+    load.wait()
     for r in range(groups):
         for copy in blocks[r]:
             copy.wait()
-        term = lax.dot_general(
-            grads[pl.ds(r * block, block), :], weights[...], (((1,), (1,)), ((), ())),
-            preferred_element_type=jnp.float32,
-        )
+        term = jnp.dot(grads[pl.ds(r * block, block), :], weights[...], preferred_element_type=jnp.float32)
         to = pl.ds((r // 2) * block, block)
-        if r % 2:
-            send_ref[to, :] = term.astype(jnp.bfloat16)
-        else:
-            keep_ref[to, :] = term
-
-
-def run_state(groups, dk, dv, key_weight, value_weight, after):
+        (send_ref if r % 2 else keep_ref)[to, :] = term.astype(jnp.bfloat16)
+
+
+def run_state(groups, dk, dv, weights, after):
     total = dk[0].shape[0]
-    enc, local_width = key_weight.shape
+    enc = weights.shape[1]
     widths = [x.shape[1] for x in dk]
     vmem = pl.BlockSpec(memory_space=pltpu.VMEM)
     return pl.pallas_call(
         functools.partial(state_kernel, groups, widths, len(after)),
         out_shape=[
-            jax.ShapeDtypeStruct((total // 2, enc), jnp.float32),
+            jax.ShapeDtypeStruct((total // 2, enc), jnp.bfloat16),
             jax.ShapeDtypeStruct((total // 2, enc), jnp.bfloat16),
         ],
-        in_specs=[hbm_spec()] * (2 * len(dk) + 2) + [any_spec()] * len(after),
+        in_specs=[hbm_spec()] * (2 * len(dk) + 1) + [any_spec()] * len(after),
         out_specs=[vmem, vmem],
         scratch_shapes=[
-            pltpu.VMEM((total, 2 * local_width), jnp.bfloat16),
-            pltpu.VMEM((enc, 2 * local_width), jnp.bfloat16),
-            pltpu.SemaphoreType.DMA((groups + 1, max(2, 2 * len(dk)))),
+            pltpu.VMEM((total, weights.shape[0]), jnp.bfloat16),
+            pltpu.VMEM(weights.shape, jnp.bfloat16),
+            pltpu.SemaphoreType.DMA((groups + 1, 2 * len(dk))),
         ],
         compiler_params=pltpu.CompilerParams(vmem_limit_bytes=VMEM_GRANT),
         cost_estimate=pl.CostEstimate(
-            flops=8 * total * enc * local_width, bytes_accessed=8 * total * enc, transcendentals=0
+            flops=2 * total * enc * weights.shape[0], bytes_accessed=8 * total * enc, transcendentals=0
         ),
         name="state_terms",
-    )(*dk, *dv, key_weight, value_weight, *after)
+    )(*in_hbm([*dk, *dv, weights]), *after)
 
 
 def fold_kernel(rows_ref, returned_ref, *refs):
-    out_ref = refs[-1]
+    out_hbm, out_ref, sem = refs[-3:]
     out_ref[...] = jnp.zeros_like(out_ref)
     count = out_ref.shape[0]
     for s in range(returned_ref.shape[0]):
@@ -266,6 +315,10 @@
         @pl.when(row < count)
         def _():
             out_ref[row] += returned_ref[s].astype(jnp.float32)
+
+    copy = pltpu.make_async_copy(out_ref, out_hbm, sem)
+    copy.start()
+    copy.wait()
 
 
 def halve_kernel(choice_ref, keep_ref, recv_ref, *refs):
@@ -280,12 +333,14 @@
 def split_kernel(keep_ref, recv_ref, *refs):
     stay_ref, send_ref = refs[-2:]
     half = stay_ref.shape[0]
-    stay_ref[...] = keep_ref[:half] + recv_ref[:half].astype(jnp.float32)
-    send_ref[...] = (keep_ref[half:] + recv_ref[half:].astype(jnp.float32)).astype(jnp.bfloat16)
+    total = keep_ref[...].astype(jnp.float32) + recv_ref[...].astype(jnp.float32)
+    stay_ref[...] = total[:half]
+    send_ref[...] = total[half:].astype(jnp.bfloat16)
 
 
 def add_kernel(keep_ref, recv_ref, *refs):
-    refs[-1][...] = (keep_ref[...] + recv_ref[...].astype(jnp.float32)).astype(refs[-1].dtype)
+    total = keep_ref[...].astype(jnp.float32) + recv_ref[...].astype(jnp.float32)
+    refs[-1][...] = total.astype(refs[-1].dtype)
 
 
 def join_kernel(choice_ref, own_ref, recv_ref, *refs):
@@ -372,7 +427,7 @@
             )
         else:
             choice = self.choices[self.steps[at]]
-            full = jax.ShapeDtypeStruct(self.full, jnp.float32)
+            full = pltpu.HBM(self.full, jnp.float32)
             block = pltpu.VMEM((self.enc, self.width), jnp.float32)
             token = jax.ShapeDtypeStruct((8, 128), jnp.float32)
             *outs, done = small(
@@ -388,20 +443,15 @@
 
 
 def wavefront(chunks, steps, rest):
-    order, period = [], 0
-    done = [0] * chunks
-    rest_done = 0
+    order = [f"heads{j}" for j in range(chunks)] + ["sum0", "state"] + ["sum1"] * (chunks > 1)
+    done = [1, 1][:chunks] + [0] * (chunks - 2)
+    rest_done, period = 0, 1
     while min(done) < steps or rest_done < rest:
-        begun = min(period, chunks)
-        if period < chunks:
-            order.append(f"heads{period}")
-        elif period == chunks:
-            order.append("state")
-        for j in range(begun):
-            if done[j] < steps:
+        for j in range(min(period + 1, chunks)):
+            if done[j] < steps and (period, j) != (1, 1):
                 order.append(f"sum{j}")
                 done[j] += 1
-        if period > chunks and rest_done < rest and (rest_done < rest - 2 or min(done) >= steps - 1):
+        if period > 2 and rest_done < rest and (rest_done < rest - 2 or min(done) >= steps - 1):
             order.append("rest")
             rest_done += 1
         period += 1
@@ -438,11 +488,21 @@
     ).reshape(slot_count, slab_len, enc_width)
     picked = jnp.take(sent_back, slot_index, axis=0, mode="clip").reshape(pair_count * slab_len, enc_width)
 
+    turned_weights = run_turn(key_weight, value_weight)
     blocks = {0: picked}
+    parts = []
     for bit in reversed(range(mp_bits)):
-        for r in list(blocks):
-            blocks[r | (1 << bit)] = swap(blocks[r], "mp", bit)
-    slabs = [blocks[r] for r in range(groups)]
+        across = {r | (1 << bit): swap(blocks[r], "mp", bit) for r in blocks}
+        if bit == mp_bits - 1 and groups > 2:
+            near = [picked, swap(picked, "mp", 0)]
+            parts.append(run_project(near, key_weight, value_weight, [turned_weights]))
+            across, parts[0] = lax.optimization_barrier((across, parts[0]))
+        blocks.update(across)
+    if groups > 2:
+        blocks[1] = near[1]
+    rest = [blocks[r] for r in range(2 * len(parts), groups)]
+    cuts = [rest[: len(rest) // 2], rest[len(rest) // 2 :]] if groups == 4 else [rest]
+    parts += [run_project(cut, key_weight, value_weight, [turned_weights]) for cut in cuts]
 
     heads = local_width // head_dim
     counts = [min(2, heads - first) for first in range(0, heads, 2)]
@@ -454,14 +514,14 @@
         sums[j].full = key_weight.shape
 
     after, chain, outs, dk, dv = [], [], [], [], []
-    rest_bit = 0
+    rest_bit, pending = 0, None
     for name in wavefront(len(sums), 2 * dp_bits, mp_bits + 1):
         kind = name.rstrip("0123456789")
         number = int(name[len(kind) :] or 0)
         if kind == "heads":
             part = sums[number]
             chain, dk_part, dv_part, (keep, send) = run_heads(
-                part.start, part.width, choices[part.steps[0]], slabs, key_weight, value_weight, queries, out_grad,
+                part.start, part.width, choices[part.steps[0]], parts, groups, queries, out_grad,
                 chain, after, spans, head_dim,
             )
             dk.append(dk_part)
@@ -471,10 +531,12 @@
         elif kind == "sum":
             done, outs = sums[number].advance(after, outs)
             after = [done]
+            if pending is not None:
+                pending, _ = lax.optimization_barrier((pending, done))
+                moving, pending = swap(pending, "mp", 0), None
         elif kind == "state":
-            keep, send = run_state(groups, dk, dv, key_weight, value_weight, after)
-            moving = swap(send, "mp", 0)
-            after = [send]
+            keep, send = run_state(groups, dk, dv, turned_weights, after)
+            pending, after = send, [send]
         elif rest_bit < mp_bits - 1:
             half = keep.shape[0] // 2
             keep, send = small(
@@ -497,7 +559,8 @@
         else:
             (state_total,) = small(
                 fold_kernel, "fold", [incoming], [returned.reshape(slot_count, slab_len, enc_width)],
-                [jax.ShapeDtypeStruct(states.shape, jnp.float32)], after,
+                [pltpu.HBM(states.shape, jnp.float32)], after, out_specs=[hbm_spec()],
+                scratch=[pltpu.VMEM(states.shape, jnp.float32), pltpu.SemaphoreType.DMA],
             )
     return (chain[0], chain[1], state_total, outs[0], outs[1])
 

time: 215 us -> 226 us (1.051)
  Pallas kernels: 44.4 us -> 58.6 us
  waiting for transfers between devices: 95.9 us -> 92.3 us
  starting transfers between devices: 46.2 us -> 43.9 us
    pallas_call x0 -> x4, Pallas kernels: none -> 15.3 us  [the longest x3 12.5 us: run_project(): pl.pallas_call(functools.partial(project_kernel, len(slabs)), out_shape=[...]
    pallas_call x4, Pallas kernels: 26.4 us -> 19.4 us  [run_heads(): pl.pallas_call(functools.partial(head_kernel, groups, spans, head_dim, st...]
    pallas_call x27, Pallas kernels: 8.69 us -> 14 us  [small(): pl.pallas_call(kernel, out_shape=outs, in_specs=[pl.BlockSpec(memory_spac...]
    ppermute x29, waiting for transfers between devices: 74.2 us -> 70.5 us  [swap(): return lax.ppermute(value, axis, [(i, i ^ 1 << bit) for i in range(count)])]
    ppermute x29, starting transfers between devices: 38.6 us -> 35.9 us  [swap(): return lax.ppermute(value, axis, [(i, i ^ 1 << bit) for i in range(count)])]
    unnamed x21 -> x27, local copies, waits for them, and re-layouts: 5.63 us -> 7.84 us
  transfers between devices with their start and end apart: 31 -> 31, of which waited for: 15 -> 14; matrix products, arithmetic and copies ran while one was open for 0% -> 0% of each run, Pallas kernels for 12% -> 22%
where the time goes in v2:
time: 226 us; the launch traced here: 225 us
  waiting for transfers between devices  92.3 us (41%)
  Pallas kernels  58.6 us (26%)
  starting transfers between devices  43.9 us (19%)
  local copies, waits for them, and re-layouts  14 us (6%)
  blocking collectives  13.5 us (6%)
    ppermute x29, waiting for transfers between devices, swap(): return lax.ppermute(value, axis, [(i, i ^ 1 << bit) for i in range(count)])  70.5 us
    ppermute x29, starting transfers between devices, swap(): return lax.ppermute(value, axis, [(i, i ^ 1 << bit) for i in range(count)])  35.9 us
    all_to_all x1, waiting for transfers between devices, body(): lax.all_to_all(slab_rows.reshape(shards, capacity, slab_len, enc_width),...  21.8 us
    pallas_call x4, Pallas kernels, run_heads(): pl.pallas_call(functools.partial(head_kernel, groups, spans, head_dim, st...  19.4 us
    pallas_call x27, Pallas kernels, small(): pl.pallas_call(kernel, out_shape=outs, in_specs=[pl.BlockSpec(memory_spac...  14 us
    all_to_all x1, blocking collectives, body(): lax.all_to_all(asked.reshape(shards, capacity), 'dp', split_axis=0, conca...  13.5 us
    pallas_call x3, Pallas kernels, run_project(): pl.pallas_call(functools.partial(project_kernel, len(slabs)), out_shape=[...  12.5 us
    pallas_call x1, Pallas kernels, run_state(): pl.pallas_call(functools.partial(state_kernel, groups, widths, len(after)...  9.98 us
  transfers between devices with their start and end apart: 31, of which 14 were waited for; matrix products, arithmetic and copies ran while one was open for 0% of the time, Pallas kernels for 22%

profile of v2, /device:TPU:0, one launch (start us, length us, event | category | flops | bytes accessed | tf_op | source)
XLA Modules:
  0.0 225.4 jit_solution(15135720140387426722)
XLA Ops:
  2.9 13.5 %all_to_all.16 = s32[8,1,2]{2,1,0:T(1,128)S(1)} all-to-all(s32[8,1,2]{2,1,0:T(1,128)S(1)} %bitcast.21), channel_id=1, replica_groups=mesh['dp'=8,'mp'=4] {'dp'}, dimensions={0} | all-to-all | bytes 128 | tf_op jit(solution)/shard_map/all_to_all | solution.py:482
  19.3 4.2 %all-to-all-start.1 = ((bf16[8,2,32,896]{3,2,1,0:T(8,128)(2,1)}), bf16[8,2,32,896]{3,2,1,0:T(8,128)(2,1)}, u32[]{:S(2)}, u32[]{:S(2)}) async-start(bf16[8,2,32,896]{3,2,1,0:T(8,128)(2,1)} %bitcast.2), calls=%async_computation.1 | async-start | bytes 1835008 | tf_op jit(solution)/shard_map/all_to_all | solution.py:486
  23.7 21.8 %all-to-all-done.1 = bf16[8,2,32,896]{3,2,1,0:T(8,128)(2,1)} async-done(((bf16[8,2,32,896]{3,2,1,0:T(8,128)(2,1)}), bf16[8,2,32,896]{3,2,1,0:T(8,128)(2,1)}, u32[]{:S(2)}, u32[]{:S(2)}) %all-to-all-start.1) | async-done | bytes 917536 | tf_op jit(solution)/shard_map/all_to_all | solution.py:486
  53.4 5.5 %project.3 = (bf16[768,1024]{1,0:T(8,128)(2,1)}, bf16[768,1024]{1,0:T(8,128)(2,1)}, bf16[896,768]{1,0:T(8,128)(2,1)}) custom-call(bf16[384,896]{1,0:T(8,128)(2,1)S(1)} %bitcast.20, bf16[384,896]{1,0:T(8,128)(2,1)S(1)} %collective-permute-done.1.refs_1_, bf16[896,1024]{1,0:T(8,128)(2,1)S(1)} %copy-done.2, bf16[896,1024]{1,0:T(8,128)(2,1)S(1)} %copy-done.3, ...), custom_call_target="tpu_custom_call" | custom-call | flops 2818572288 | bytes 6815744 | tf_op jit(solution)/shard_map/project/pallas_call | solution.py:88
  58.8 6.6 %collective-permute-done.refs_0_ = bf16[384,896]{1,0:T(8,128)(2,1)} collective-permute-done((bf16[384,896]{1,0:T(8,128)(2,1)S(1)}, bf16[384,896]{1,0:T(8,128)(2,1)}, u32[]{:S(2)}, u32[]{:S(2)}) %collective-permute-start) | collective-permute-done | bytes 688160 | tf_op jit(solution)/shard_map/ppermute | solution.py:23
  66.9 4.0 %project.4 = (bf16[384,1024]{1,0:T(8,128)(2,1)}, bf16[384,1024]{1,0:T(8,128)(2,1)}, bf16[896,384]{1,0:T(8,128)(2,1)}) custom-call(bf16[384,896]{1,0:T(8,128)(2,1)} %collective-permute-done.refs_0_, bf16[896,1024]{1,0:T(8,128)(2,1)S(1)} %copy-done.2, bf16[896,1024]{1,0:T(8,128)(2,1)S(1)} %copy-done.4, bf16[2048,896]{1,0:T(8,128)(2,1)} %turn.1.refs_4_.refs_3_.refs_8_), custom_call_target="tpu_custom_call" | custom-call | flops 1409286144 | bytes 5242880 | tf_op jit(solution)/shard_map/project/pallas_call | solution.py:88
  71.0 3.0 %project.5 = (bf16[384,1024]{1,0:T(8,128)(2,1)}, bf16[384,1024]{1,0:T(8,128)(2,1)}, bf16[896,384]{1,0:T(8,128)(2,1)}) custom-call(bf16[384,896]{1,0:T(8,128)(2,1)S(1)} %collective-permute-done.2.refs_0_, bf16[896,1024]{1,0:T(8,128)(2,1)S(1)} %copy-done.2, bf16[896,1024]{1,0:T(8,128)(2,1)S(1)} %copy-done.4, bf16[2048,896]{1,0:T(8,128)(2,1)} %turn.1.refs_4_.refs_3_.refs_8_), custom_call_target="tpu_custom_call" | custom-call | flops 1409286144 | bytes 5242880 | tf_op jit(solution)/shard_map/project/pallas_call | solution.py:88
  74.0 4.6 %heads.4 = (bf16[384,1024]{1,0:T(8,128)(2,1)}, bf16[384,1024]{1,0:T(8,128)(2,1)}, bf16[1536,256]{1,0:T(8,128)(2,1)}, bf16[1536,256]{1,0:T(8,128)(2,1)}, f32[896,...) custom-call(s32[1]{0:T(128)} %bitcast.refs_0_.choice_ref, bf16[768,1024]{1,0:T(8,128)(2,1)} %get-tuple-element.78.refs_1_, ...), custom_call_target="tpu_custom_call" | custom-call | flops 4227858432 | bytes 5505024 | tf_op jit(solution)/shard_map/heads/pallas_call | solution.py:214
  79.9 4.6 %heads.5 = (bf16[384,1024]{1,0:T(8,128)(2,1)}, bf16[384,1024]{1,0:T(8,128)(2,1)}, bf16[1536,256]{1,0:T(8,128)(2,1)}, bf16[1536,256]{1,0:T(8,128)(2,1)}, f32[896,...) custom-call(s32[1]{0:T(128)} %bitcast.refs_0_.choice_ref, ...), custom_call_target="tpu_custom_call", output_to_operand_aliasing={{0}: (12, {}), {1}: (13, {})} | custom-call | flops 4227858432 | bytes 5505024 | tf_op jit(solution)/shard_map/heads/pallas_call | solution.py:214
  85.3 5.5 %heads.6 = (bf16[384,1024]{1,0:T(8,128)(2,1)}, bf16[384,1024]{1,0:T(8,128)(2,1)}, bf16[1536,256]{1,0:T(8,128)(2,1)}, bf16[1536,256]{1,0:T(8,128)(2,1)}, f32[896,...) custom-call(s32[1]{0:T(128)} %bitcast.refs_0_.choice_ref, ...), custom_call_target="tpu_custom_call", output_to_operand_aliasing={{0}: (12, {}), {1}: (13, {})} | custom-call | flops 4227858432 | bytes 5505024 | tf_op jit(solution)/shard_map/heads/pallas_call | solution.py:214
  91.8 4.6 %heads.7 = (bf16[384,1024]{1,0:T(8,128)(2,1)}, bf16[384,1024]{1,0:T(8,128)(2,1)}, bf16[1536,256]{1,0:T(8,128)(2,1)}, bf16[1536,256]{1,0:T(8,128)(2,1)}, f32[896,...) custom-call(s32[1]{0:T(128)} %bitcast.refs_0_.choice_ref, ...), custom_call_target="tpu_custom_call", output_to_operand_aliasing={{0}: (12, {}), {1}: (13, {})} | custom-call | flops 4227858432 | bytes 5505024 | tf_op jit(solution)/shard_map/heads/pallas_call | solution.py:214
  97.4 10.0 %state_terms.1 = (bf16[768,896]{1,0:T(8,128)(2,1)S(1)}, bf16[768,896]{1,0:T(8,128)(2,1)S(1)}) custom-call(bf16[1536,256]{1,0:T(8,128)(2,1)} %get-tuple-element.99.refs_0_, bf16[1536,256]{1,0:T(8,128)(2,1)} %get-tuple-element.100.refs_1_, bf16[1536,256]{1,0:T(8,128)(2,1)} %get-tuple-element.101.refs_2_, bf16[1536,256]{1,0:T(8,128)(2,1)} %get-tuple-element.102.refs_3_, ...), custom_call_target="tpu_custom_call" | custom-call | flops 5637144576 | bytes 11010048 | tf_op jit(solution)/shard_map/state_terms/pallas_call | solution.py:287
  112.4 5.9 %collective-permute-done.9.recv_ref = bf16[448,256]{1,0:T(8,128)(2,1)} collective-permute-done((bf16[448,256]{1,0:T(8,128)(2,1)}, bf16[448,256]{1,0:T(8,128)(2,1)}, u32[]{:S(2)}, u32[]{:S(2)}) %collective-permute-start.9) | collective-permute-done | bytes 229408 | tf_op jit(solution)/shard_map/ppermute | solution.py:23
  119.4 7.1 %collective-permute-done.10.recv_ref = bf16[224,256]{1,0:T(8,128)(2,1)S(1)} collective-permute-done((bf16[224,256]{1,0:T(8,128)(2,1)S(1)}, bf16[224,256]{1,0:T(8,128)(2,1)S(1)}, u32[]{:S(2)}, u32[]{:S(2)}) %collective-permute-start.10) | collective-permute-done | bytes 114720 | tf_op jit(solution)/shard_map/ppermute | solution.py:23
  136.1 7.0 %collective-permute-done.12.recv_ref = bf16[224,256]{1,0:T(8,128)(2,1)S(1)} collective-permute-done((bf16[224,256]{1,0:T(8,128)(2,1)S(1)}, bf16[224,256]{1,0:T(8,128)(2,1)S(1)}, u32[]{:S(2)}, u32[]{:S(2)}) %collective-permute-start.12) | collective-permute-done | bytes 114720 | tf_op jit(solution)/shard_map/ppermute | solution.py:23
  153.6 4.4 %collective-permute-start.21 = (bf16[448,256]{1,0:T(8,128)(2,1)S(1)}, bf16[448,256]{1,0:T(8,128)(2,1)S(1)}, u32[]{:S(2)}, u32[]{:S(2)}) collective-permute-start(bf16[448,256]{1,0:T(8,128)(2,1)S(1)} %join.10.refs_0_.own_ref), channel_id=1, source_target_pairs={{0,8},{4,12},{8,0},{12,4},{16,24},{20,28},{24,16},{28,20},{1,9},{5... | collective-permute-start | bytes 688136 | tf_op jit(solution)/shard_map/ppermute | solution.py:23
  158.4 5.8 %collective-permute-done.16.recv_ref = bf16[224,256]{1,0:T(8,128)(2,1)S(1)} collective-permute-done((bf16[224,256]{1,0:T(8,128)(2,1)S(1)}, bf16[224,256]{1,0:T(8,128)(2,1)S(1)}, u32[]{:S(2)}, u32[]{:S(2)}) %collective-permute-start.16) | collective-permute-done | bytes 114720 | tf_op jit(solution)/shard_map/ppermute | solution.py:23
  168.9 3.5 %collective-permute-done.20.recv_ref = bf16[224,256]{1,0:T(8,128)(2,1)S(1)} collective-permute-done((bf16[224,256]{1,0:T(8,128)(2,1)S(1)}, bf16[224,256]{1,0:T(8,128)(2,1)S(1)}, u32[]{:S(2)}, u32[]{:S(2)}) %collective-permute-start.20) | collective-permute-done | bytes 114720 | tf_op jit(solution)/shard_map/ppermute | solution.py:23
  172.4 4.4 %collective-permute-start.24 = (bf16[448,256]{1,0:T(8,128)(2,1)S(1)}, bf16[448,256]{1,0:T(8,128)(2,1)S(1)}, u32[]{:S(2)}, u32[]{:S(2)}) collective-permute-start(bf16[448,256]{1,0:T(8,128)(2,1)S(1)} %join.12.refs_0_.own_ref), channel_id=1, source_target_pairs={{0,8},{4,12},{8,0},{12,4},{16,24},{20,28},{24,16},{28,20},{1,9},{5... | collective-permute-start | bytes 688136 | tf_op jit(solution)/shard_map/ppermute | solution.py:23
  178.5 8.5 %collective-permute-done.19.recv_ref = bf16[224,256]{1,0:T(8,128)(2,1)S(1)} collective-permute-done((bf16[224,256]{1,0:T(8,128)(2,1)S(1)}, bf16[224,256]{1,0:T(8,128)(2,1)S(1)}, u32[]{:S(2)}, u32[]{:S(2)}) %collective-permute-start.19) | collective-permute-done | bytes 114720 | tf_op jit(solution)/shard_map/ppermute | solution.py:23
  189.9 5.7 %collective-permute-done.23.recv_ref = bf16[224,256]{1,0:T(8,128)(2,1)S(1)} collective-permute-done((bf16[224,256]{1,0:T(8,128)(2,1)S(1)}, bf16[224,256]{1,0:T(8,128)(2,1)S(1)}, u32[]{:S(2)}, u32[]{:S(2)}) %collective-permute-start.23) | collective-permute-done | bytes 114720 | tf_op jit(solution)/shard_map/ppermute | solution.py:23
  198.6 4.3 %collective-permute-done.26.recv_ref = bf16[448,256]{1,0:T(8,128)(2,1)S(1)} collective-permute-done((bf16[448,256]{1,0:T(8,128)(2,1)S(1)}, bf16[448,256]{1,0:T(8,128)(2,1)S(1)}, u32[]{:S(2)}, u32[]{:S(2)}) %collective-permute-start.26) | collective-permute-done | bytes 229408 | tf_op jit(solution)/shard_map/ppermute | solution.py:23
  204.6 3.8 %all-to-all-start.2 = ((bf16[8,2,32,896]{3,2,1,0:T(8,128)(2,1)}), bf16[8,2,32,896]{3,2,1,0:T(8,128)(2,1)S(1)}, u32[]{:S(2)}, u32[]{:S(2)}) async-start(bf16[8,2,32,896]{3,2,1,0:T(8,128)(2,1)} %bitcast.10), calls=%async_computation.2 | async-start | bytes 1835008 | tf_op jit(solution)/shard_map/all_to_all | solution.py:557
  210.5 11.5 %collective-permute-done.28.recv_ref = bf16[896,256]{1,0:T(8,128)(2,1)S(1)} collective-permute-done((bf16[896,256]{1,0:T(8,128)(2,1)S(1)}, bf16[896,256]{1,0:T(8,128)(2,1)S(1)}, u32[]{:S(2)}, u32[]{:S(2)}) %collective-permute-start.28) | collective-permute-done | bytes 458784 | tf_op jit(solution)/shard_map/ppermute | solution.py:23
  (125 shorter events, 64.1 us)
Async XLA Ops:
  19.3 26.2 %all-to-all-start.1 = ((bf16[8,2,32,896]{3,2,1,0:T(8,128)(2,1)}), bf16[8,2,32,896]{3,2,1,0:T(8,128)(2,1)}, u32[]{:S(2)}, u32[]{:S(2)}) async-start(bf16[8,2,32,896]{3,2,1,0:T(8,128)(2,1)} %bitcast.2), calls=%async_computation.1 | async-start | bytes 1835008 | tf_op jit(solution)/shard_map/all_to_all | solution.py:486
  47.4 18.0 %collective-permute-start = (bf16[384,896]{1,0:T(8,128)(2,1)S(1)}, bf16[384,896]{1,0:T(8,128)(2,1)}, u32[]{:S(2)}, u32[]{:S(2)}) collective-permute-start(bf16[384,896]{1,0:T(8,128)(2,1)S(1)} %bitcast.19), channel_id=1, source_target_pairs={{0,2},{1,3},{2,0},{3,1},{4,6},{5,7},{6,4},{7,5},{8,10},{9,11},{10,... | collective-permute-start | bytes 2064392 | tf_op jit(solution)/shard_map/ppermute | solution.py:23
  78.6 17.9 %collective-permute-start.3 = (bf16[896,256]{1,0:T(8,128)(2,1)S(1)}, bf16[896,256]{1,0:T(8,128)(2,1)S(1)}, u32[]{:S(2)}, u32[]{:S(2)}) collective-permute-start(bf16[896,256]{1,0:T(8,128)(2,1)S(1)} %get-tuple-element.90.refs_14_), channel_id=1, source_target_pairs={{0,4},{4,0},{8,12},{12,8},{16,20},{20,16},{24,28},{28,24},{1,5},{5... | collective-permute-start | bytes 1376264 | tf_op jit(solution)/shard_map/ppermute | solution.py:23
  84.5 23.0 %collective-permute-start.4 = (bf16[896,256]{1,0:T(8,128)(2,1)S(1)}, bf16[896,256]{1,0:T(8,128)(2,1)S(1)}, u32[]{:S(2)}, u32[]{:S(2)}) collective-permute-start(bf16[896,256]{1,0:T(8,128)(2,1)S(1)} %get-tuple-element.93.refs_14_), channel_id=1, source_target_pairs={{0,4},{4,0},{8,12},{12,8},{16,20},{20,16},{24,28},{28,24},{1,5},{5... | collective-permute-start | bytes 1376264 | tf_op jit(solution)/shard_map/ppermute | solution.py:23
  108.4 35.0 %collective-permute-start.5 = (bf16[768,896]{1,0:T(8,128)(2,1)S(1)}, bf16[768,896]{1,0:T(8,128)(2,1)}, u32[]{:S(2)}, u32[]{:S(2)}) collective-permute-start(bf16[768,896]{1,0:T(8,128)(2,1)S(1)} %get-tuple-element.114.refs_0_), channel_id=1, source_target_pairs={{0,1},{1,0},{2,3},{3,2},{4,5},{5,4},{6,7},{7,6},{8,9},{9,8},{10,11... | collective-permute-start | bytes 4128776 | tf_op jit(solution)/shard_map/ppermute | solution.py:23
  108.4 20.3 %collective-permute-start.7 = (bf16[896,256]{1,0:T(8,128)(2,1)}, bf16[896,256]{1,0:T(8,128)(2,1)}, u32[]{:S(2)}, u32[]{:S(2)}) collective-permute-start(bf16[896,256]{1,0:T(8,128)(2,1)} %get-tuple-element.96.refs_14_), channel_id=1, source_target_pairs={{0,4},{4,0},{8,12},{12,8},{16,20},{20,16},{24,28},{28,24},{1,5},{5... | collective-permute-start | bytes 1376264 | tf_op jit(solution)/shard_map/ppermute | solution.py:23
  109.6 8.8 %collective-permute-start.9 = (bf16[448,256]{1,0:T(8,128)(2,1)}, bf16[448,256]{1,0:T(8,128)(2,1)}, u32[]{:S(2)}, u32[]{:S(2)}) collective-permute-start(bf16[448,256]{1,0:T(8,128)(2,1)} %get-tuple-element.109.refs_9_), channel_id=1, source_target_pairs={{0,8},{4,12},{8,0},{12,4},{16,24},{20,28},{24,16},{28,20},{1,9},{5... | collective-permute-start | bytes 688136 | tf_op jit(solution)/shard_map/ppermute | solution.py:23
  109.6 17.0 %collective-permute-start.8 = (bf16[448,256]{1,0:T(8,128)(2,1)S(1)}, bf16[448,256]{1,0:T(8,128)(2,1)}, u32[]{:S(2)}, u32[]{:S(2)}) collective-permute-start(bf16[448,256]{1,0:T(8,128)(2,1)S(1)} %get-tuple-element.113.refs_0_), channel_id=1, source_target_pairs={{0,8},{4,12},{8,0},{12,4},{16,24},{20,28},{24,16},{28,20},{1,9},{5... | collective-permute-start | bytes 688136 | tf_op jit(solution)/shard_map/ppermute | solution.py:23
  111.6 31.6 %collective-permute-start.6 = (bf16[896,256]{1,0:T(8,128)(2,1)}, bf16[896,256]{1,0:T(8,128)(2,1)S(1)}, u32[]{:S(2)}, u32[]{:S(2)}) collective-permute-start(bf16[896,256]{1,0:T(8,128)(2,1)} %copy-done.11), channel_id=1, source_target_pairs={{0,4},{4,0},{8,12},{12,8},{16,20},{20,16},{24,28},{28,24},{1,5},{5... | collective-permute-start | bytes 1376264 | tf_op jit(solution)/shard_map/ppermute | solution.py:23
  119.4 7.2 %collective-permute-start.10 = (bf16[224,256]{1,0:T(8,128)(2,1)S(1)}, bf16[224,256]{1,0:T(8,128)(2,1)S(1)}, u32[]{:S(2)}, u32[]{:S(2)}) collective-permute-start(bf16[224,256]{1,0:T(8,128)(2,1)S(1)} %get-tuple-element.120.refs_0_), channel_id=1, source_target_pairs={{0,16},{4,20},{8,24},{12,28},{16,0},{20,4},{24,8},{28,12},{1,17},{... | collective-permute-start | bytes 344072 | tf_op jit(solution)/shard_map/ppermute | solution.py:23
  131.0 12.2 %collective-permute-start.11 = (bf16[448,256]{1,0:T(8,128)(2,1)S(1)}, bf16[448,256]{1,0:T(8,128)(2,1)S(1)}, u32[]{:S(2)}, u32[]{:S(2)}) collective-permute-start(bf16[448,256]{1,0:T(8,128)(2,1)S(1)} %get-tuple-element.123.refs_0_), channel_id=1, source_target_pairs={{0,8},{4,12},{8,0},{12,4},{16,24},{20,28},{24,16},{28,20},{1,9},{5... | collective-permute-start | bytes 688136 | tf_op jit(solution)/shard_map/ppermute | solution.py:23
  133.5 11.9 %collective-permute-start.18 = (bf16[448,256]{1,0:T(8,128)(2,1)S(1)}, bf16[448,256]{1,0:T(8,128)(2,1)S(1)}, u32[]{:S(2)}, u32[]{:S(2)}) collective-permute-start(bf16[448,256]{1,0:T(8,128)(2,1)S(1)} %join.8.refs_0_.own_ref), channel_id=1, source_target_pairs={{0,8},{4,12},{8,0},{12,4},{16,24},{20,28},{24,16},{28,20},{1,9},{5... | collective-permute-start | bytes 688136 | tf_op jit(solution)/shard_map/ppermute | solution.py:23
  133.6 9.5 %collective-permute-start.12 = (bf16[224,256]{1,0:T(8,128)(2,1)S(1)}, bf16[224,256]{1,0:T(8,128)(2,1)S(1)}, u32[]{:S(2)}, u32[]{:S(2)}) collective-permute-start(bf16[224,256]{1,0:T(8,128)(2,1)S(1)} %get-tuple-element.121.refs_0_), channel_id=1, source_target_pairs={{0,16},{4,20},{8,24},{12,28},{16,0},{20,4},{24,8},{28,12},{1,17},{... | collective-permute-start | bytes 344072 | tf_op jit(solution)/shard_map/ppermute | solution.py:23
  145.5 18.8 %collective-permute-start.22 = (bf16[896,256]{1,0:T(8,128)(2,1)S(1)}, bf16[896,256]{1,0:T(8,128)(2,1)S(1)}, u32[]{:S(2)}, u32[]{:S(2)}) collective-permute-start(bf16[896,256]{1,0:T(8,128)(2,1)S(1)} %join.9.refs_0_.own_ref), channel_id=1, source_target_pairs={{0,4},{4,0},{8,12},{12,8},{16,20},{20,16},{24,28},{28,24},{1,5},{5... | collective-permute-start | bytes 1376264 | tf_op jit(solution)/shard_map/ppermute | solution.py:23
  149.6 14.7 %collective-permute-start.15 = (bf16[448,256]{1,0:T(8,128)(2,1)S(1)}, bf16[448,256]{1,0:T(8,128)(2,1)S(1)}, u32[]{:S(2)}, u32[]{:S(2)}) collective-permute-start(bf16[448,256]{1,0:T(8,128)(2,1)S(1)} %get-tuple-element.126.refs_0_), channel_id=1, source_target_pairs={{0,8},{4,12},{8,0},{12,4},{16,24},{20,28},{24,16},{28,20},{1,9},{5... | collective-permute-start | bytes 688136 | tf_op jit(solution)/shard_map/ppermute | solution.py:23
  153.6 12.1 %collective-permute-start.21 = (bf16[448,256]{1,0:T(8,128)(2,1)S(1)}, bf16[448,256]{1,0:T(8,128)(2,1)S(1)}, u32[]{:S(2)}, u32[]{:S(2)}) collective-permute-start(bf16[448,256]{1,0:T(8,128)(2,1)S(1)} %join.10.refs_0_.own_ref), channel_id=1, source_target_pairs={{0,8},{4,12},{8,0},{12,4},{16,24},{20,28},{24,16},{28,20},{1,9},{5... | collective-permute-start | bytes 688136 | tf_op jit(solution)/shard_map/ppermute | solution.py:23
  165.8 21.3 %collective-permute-start.25 = (bf16[896,256]{1,0:T(8,128)(2,1)S(1)}, bf16[896,256]{1,0:T(8,128)(2,1)S(1)}, u32[]{:S(2)}, u32[]{:S(2)}) collective-permute-start(bf16[896,256]{1,0:T(8,128)(2,1)S(1)} %join.11.refs_0_.own_ref), channel_id=1, source_target_pairs={{0,4},{4,0},{8,12},{12,8},{16,20},{20,16},{24,28},{28,24},{1,5},{5... | collective-permute-start | bytes 1376264 | tf_op jit(solution)/shard_map/ppermute | solution.py:23
  172.4 16.1 %collective-permute-start.24 = (bf16[448,256]{1,0:T(8,128)(2,1)S(1)}, bf16[448,256]{1,0:T(8,128)(2,1)S(1)}, u32[]{:S(2)}, u32[]{:S(2)}) collective-permute-start(bf16[448,256]{1,0:T(8,128)(2,1)S(1)} %join.12.refs_0_.own_ref), channel_id=1, source_target_pairs={{0,8},{4,12},{8,0},{12,4},{16,24},{20,28},{24,16},{28,20},{1,9},{5... | collective-permute-start | bytes 688136 | tf_op jit(solution)/shard_map/ppermute | solution.py:23
  176.8 26.1 %collective-permute-start.14 = (bf16[384,896]{1,0:T(8,128)(2,1)S(1)}, bf16[384,896]{1,0:T(8,128)(2,1)S(1)}, u32[]{:S(2)}, u32[]{:S(2)}) collective-permute-start(bf16[384,896]{1,0:T(8,128)(2,1)S(1)} %get-tuple-element.128.refs_0_), channel_id=1, source_target_pairs={{0,2},{1,3},{2,0},{3,1},{4,6},{5,7},{6,4},{7,5},{8,10},{9,11},{10,... | collective-permute-start | bytes 2064392 | tf_op jit(solution)/shard_map/ppermute | solution.py:23
  178.3 8.8 %collective-permute-start.19 = (bf16[224,256]{1,0:T(8,128)(2,1)S(1)}, bf16[224,256]{1,0:T(8,128)(2,1)S(1)}, u32[]{:S(2)}, u32[]{:S(2)}) collective-permute-start(bf16[224,256]{1,0:T(8,128)(2,1)S(1)} %get-tuple-element.132.refs_0_), channel_id=1, source_target_pairs={{0,16},{4,20},{8,24},{12,28},{16,0},{20,4},{24,8},{28,12},{1,17},{... | collective-permute-start | bytes 344072 | tf_op jit(solution)/shard_map/ppermute | solution.py:23
  188.6 8.5 %collective-permute-start.27 = (bf16[896,256]{1,0:T(8,128)(2,1)S(1)}, bf16[896,256]{1,0:T(8,128)(2,1)S(1)}, u32[]{:S(2)}, u32[]{:S(2)}) collective-permute-start(bf16[896,256]{1,0:T(8,128)(2,1)S(1)} %join.13.refs_0_.own_ref), channel_id=1, source_target_pairs={{0,4},{4,0},{8,12},{12,8},{16,20},{20,16},{24,28},{28,24},{1,5},{5... | collective-permute-start | bytes 1376264 | tf_op jit(solution)/shard_map/ppermute | solution.py:23
  195.6 7.3 %collective-permute-start.26 = (bf16[448,256]{1,0:T(8,128)(2,1)S(1)}, bf16[448,256]{1,0:T(8,128)(2,1)S(1)}, u32[]{:S(2)}, u32[]{:S(2)}) collective-permute-start(bf16[448,256]{1,0:T(8,128)(2,1)S(1)} %join.14.refs_2_.own_ref), channel_id=1, source_target_pairs={{0,8},{4,12},{8,0},{12,4},{16,24},{20,28},{24,16},{28,20},{1,9},{5... | collective-permute-start | bytes 688136 | tf_op jit(solution)/shard_map/ppermute | solution.py:23
  204.6 18.8 %all-to-all-start.2 = ((bf16[8,2,32,896]{3,2,1,0:T(8,128)(2,1)}), bf16[8,2,32,896]{3,2,1,0:T(8,128)(2,1)S(1)}, u32[]{:S(2)}, u32[]{:S(2)}) async-start(bf16[8,2,32,896]{3,2,1,0:T(8,128)(2,1)} %bitcast.10), calls=%async_computation.2 | async-start | bytes 1835008 | tf_op jit(solution)/shard_map/all_to_all | solution.py:557
  208.4 13.6 %collective-permute-start.28 = (bf16[896,256]{1,0:T(8,128)(2,1)S(1)}, bf16[896,256]{1,0:T(8,128)(2,1)S(1)}, u32[]{:S(2)}, u32[]{:S(2)}) collective-permute-start(bf16[896,256]{1,0:T(8,128)(2,1)S(1)} %join.15.refs_0_.own_ref), channel_id=1, source_target_pairs={{0,4},{4,0},{8,12},{12,8},{16,20},{20,16},{24,28},{28,24},{1,5},{5... | collective-permute-start | bytes 1376264 | tf_op jit(solution)/shard_map/ppermute | solution.py:23
  (20 other events, 195.1 us)

commit v3 on v1

--- a/solution.py
+++ b/solution.py
@@ -25,6 +25,10 @@
 
 def any_spec():
     return pl.BlockSpec(memory_space=pl.ANY)
+
+
+def in_hbm(arrays):
+    return [pltpu.with_memory_space_constraint(x, pltpu.HBM) for x in arrays]
 
 
 def hbm_spec():
@@ -133,9 +137,12 @@
         begin(dk_ref, dk_hbm, 2),
         begin(dv_ref, dv_hbm, 3),
     ]
-    both = lax.dot_general(rows[...], grads[...], contract_first, preferred_element_type=jnp.float32)
-    keep_ref[...] = both[:, :width]
-    send_ref[...] = both[:, width:].astype(jnp.bfloat16)
+    tile = 128
+    for first in range(0, rows.shape[1], tile):
+        to = slice(first, first + tile)
+        both = lax.dot_general(rows[:, to], grads[...], contract_first, preferred_element_type=jnp.float32)
+        keep_ref[to, :] = both[:, :width]
+        send_ref[to, :] = both[:, width:].astype(jnp.bfloat16)
     for copy in results:
         copy.wait()
 
@@ -150,10 +157,10 @@
     outs = pl.pallas_call(
         functools.partial(head_kernel, groups, spans, head_dim, start, len(extra)),
         out_shape=[
-            jax.ShapeDtypeStruct((tokens, local_width), bf),
-            jax.ShapeDtypeStruct((tokens, local_width), bf),
-            jax.ShapeDtypeStruct((total, chunk), bf),
-            jax.ShapeDtypeStruct((total, chunk), bf),
+            pltpu.HBM((tokens, local_width), bf),
+            pltpu.HBM((tokens, local_width), bf),
+            pltpu.HBM((total, chunk), bf),
+            pltpu.HBM((total, chunk), bf),
             jax.ShapeDtypeStruct((enc, chunk), jnp.float32),
             jax.ShapeDtypeStruct((enc, chunk), bf),
         ],
@@ -183,7 +190,7 @@
             flops=2 * total * enc * chunk * 8, bytes_accessed=4 * total * enc, transcendentals=total * tokens
         ),
         name="heads",
-    )(flag, *slabs, key_weight, value_weight, queries, out_grad, *extra)
+    )(flag, *slabs, *in_hbm([key_weight, value_weight, queries, out_grad, *chain]), *after)
     return outs[:2], outs[2], outs[3], outs[4:]
 
 
@@ -219,15 +226,14 @@
     for r in range(groups):
         for copy in blocks[r]:
             copy.wait()
-        term = lax.dot_general(
-            grads[pl.ds(r * block, block), :], weights[...], (((1,), (1,)), ((), ())),
-            preferred_element_type=jnp.float32,
-        )
         to = pl.ds((r // 2) * block, block)
-        if r % 2:
-            send_ref[to, :] = term.astype(jnp.bfloat16)
-        else:
-            keep_ref[to, :] = term
+        for first in range(0, weights.shape[0], 256):
+            cols = slice(first, min(first + 256, weights.shape[0]))
+            term = lax.dot_general(
+                grads[pl.ds(r * block, block), :], weights[cols, :], (((1,), (1,)), ((), ())),
+                preferred_element_type=jnp.float32,
+            )
+            (send_ref if r % 2 else keep_ref)[to, cols] = term.astype(jnp.bfloat16)
 
 
 def run_state(groups, dk, dv, key_weight, value_weight, after):
@@ -238,7 +244,7 @@
     return pl.pallas_call(
         functools.partial(state_kernel, groups, widths, len(after)),
         out_shape=[
-            jax.ShapeDtypeStruct((total // 2, enc), jnp.float32),
+            jax.ShapeDtypeStruct((total // 2, enc), jnp.bfloat16),
             jax.ShapeDtypeStruct((total // 2, enc), jnp.bfloat16),
         ],
         in_specs=[hbm_spec()] * (2 * len(dk) + 2) + [any_spec()] * len(after),
@@ -253,11 +259,11 @@
             flops=8 * total * enc * local_width, bytes_accessed=8 * total * enc, transcendentals=0
         ),
         name="state_terms",
-    )(*dk, *dv, key_weight, value_weight, *after)
+    )(*in_hbm([*dk, *dv, key_weight, value_weight]), *after)
 
 
 def fold_kernel(rows_ref, returned_ref, *refs):
-    out_ref = refs[-1]
+    out_hbm, out_ref, sem = refs[-3:]
     out_ref[...] = jnp.zeros_like(out_ref)
     count = out_ref.shape[0]
     for s in range(returned_ref.shape[0]):
@@ -266,6 +272,10 @@
         @pl.when(row < count)
         def _():
             out_ref[row] += returned_ref[s].astype(jnp.float32)
+
+    copy = pltpu.make_async_copy(out_ref, out_hbm, sem)
+    copy.start()
+    copy.wait()
 
 
 def halve_kernel(choice_ref, keep_ref, recv_ref, *refs):
@@ -280,12 +290,14 @@
 def split_kernel(keep_ref, recv_ref, *refs):
     stay_ref, send_ref = refs[-2:]
     half = stay_ref.shape[0]
-    stay_ref[...] = keep_ref[:half] + recv_ref[:half].astype(jnp.float32)
-    send_ref[...] = (keep_ref[half:] + recv_ref[half:].astype(jnp.float32)).astype(jnp.bfloat16)
+    total = keep_ref[...].astype(jnp.float32) + recv_ref[...].astype(jnp.float32)
+    stay_ref[...] = total[:half]
+    send_ref[...] = total[half:].astype(jnp.bfloat16)
 
 
 def add_kernel(keep_ref, recv_ref, *refs):
-    refs[-1][...] = (keep_ref[...] + recv_ref[...].astype(jnp.float32)).astype(refs[-1].dtype)
+    total = keep_ref[...].astype(jnp.float32) + recv_ref[...].astype(jnp.float32)
+    refs[-1][...] = total.astype(refs[-1].dtype)
 
 
 def join_kernel(choice_ref, own_ref, recv_ref, *refs):
@@ -372,7 +384,7 @@
             )
         else:
             choice = self.choices[self.steps[at]]
-            full = jax.ShapeDtypeStruct(self.full, jnp.float32)
+            full = pltpu.HBM(self.full, jnp.float32)
             block = pltpu.VMEM((self.enc, self.width), jnp.float32)
             token = jax.ShapeDtypeStruct((8, 128), jnp.float32)
             *outs, done = small(
@@ -387,24 +399,56 @@
         return send, outs
 
 
-def wavefront(chunks, steps, rest):
-    order, period = [], 0
-    done = [0] * chunks
-    rest_done = 0
-    while min(done) < steps or rest_done < rest:
-        begun = min(period, chunks)
-        if period < chunks:
-            order.append(f"heads{period}")
-        elif period == chunks:
-            order.append("state")
-        for j in range(begun):
-            if done[j] < steps:
-                order.append(f"sum{j}")
-                done[j] += 1
-        if period > chunks and rest_done < rest and (rest_done < rest - 2 or min(done) >= steps - 1):
-            order.append("rest")
-            rest_done += 1
-        period += 1
+def plan(sums, rest):
+    rate, event, start, lag = 84e3, 1.0, 1.5, 1.5
+    chains = {}
+    for j, s in enumerate(sums):
+        chains[f"sum{j}"] = []
+        for k, bit in enumerate(s.steps):
+            time = 4 * s.load(k) * s.width / rate
+            chains[f"sum{j}"].append({"y": time} if bit == 0 else {"ends": time, "middle": time * (1 + (bit > 1))})
+    chains["rest"] = [{"core": 3.0}] + [{"x": 17.0}] * (rest - 2) + [{"y": 9.0, "ends": 14.0, "middle": 18.0}]
+    last = f"sum{len(sums) - 1}"
+    heavy = [(f"heads{j}", 1.0 + 2.75 * s.width / 128, f"sum{j}") for j, s in enumerate(sums)]
+    heavy.append(("state", 9.5, "rest"))
+    left = {name: len(steps) for name, steps in chains.items()}
+    free, waiting, order, now = {}, {}, [], 0.0
+
+    def send(name):
+        nonlocal now
+        now += start
+        loads = chains[name][-left[name]]
+        begin = max([now] + [free.get(link, 0.0) for link in loads])
+        for link, time in loads.items():
+            free[link] = max(free.get(link, 0.0), now) + time
+        waiting[name] = max([begin + max(loads.values())] + [free[link] for link in loads]) + lag
+
+    def step(name):
+        nonlocal now
+        now = max(now, waiting.pop(name)) + event
+        order.append(name)
+        left[name] -= 1
+        if left[name]:
+            send(name)
+
+    for period, (name, time, begun) in enumerate(heavy):
+        now += time
+        order.append(name)
+        if begun != "rest":
+            send(begun)
+        for name in [f"sum{j}" for j in range(period)] if begun != "rest" else sorted(waiting, key=waiting.get):
+            step(name)
+    send("rest")
+    while waiting:
+        open_now = [name for name in waiting if not (name == "rest" and left[name] == 2 and left[last] > 1)]
+        ready = [name for name in open_now if waiting[name] <= now]
+        moving = [name for name in ready if left[name] > 1]
+        if moving:
+            step(min(moving, key=lambda name: (-left[name], waiting[name])))
+        elif ready:
+            step(ready[0])
+        else:
+            step(min(open_now, key=lambda name: waiting[name]))
     return order
 
 
@@ -454,14 +498,14 @@
         sums[j].full = key_weight.shape
 
     after, chain, outs, dk, dv = [], [], [], [], []
-    rest_bit = 0
-    for name in wavefront(len(sums), 2 * dp_bits, mp_bits + 1):
+    rest_bit, pending, held_for = 0, None, 0
+    for name in plan(sums, mp_bits + 1):
         kind = name.rstrip("0123456789")
         number = int(name[len(kind) :] or 0)
         if kind == "heads":
             part = sums[number]
             chain, dk_part, dv_part, (keep, send) = run_heads(
-                part.start, part.width, choices[part.steps[0]], slabs, key_weight, value_weight, queries, out_grad,
+                part.start, part.width, choices[0], slabs, key_weight, value_weight, queries, out_grad,
                 chain, after, spans, head_dim,
             )
             dk.append(dk_part)
@@ -471,10 +515,13 @@
         elif kind == "sum":
             done, outs = sums[number].advance(after, outs)
             after = [done]
+            held_for -= 1
+            if pending is not None and not held_for:
+                pending, _ = lax.optimization_barrier((pending, done))
+                moving, pending = swap(pending, "mp", 0), None
         elif kind == "state":
             keep, send = run_state(groups, dk, dv, key_weight, value_weight, after)
-            moving = swap(send, "mp", 0)
-            after = [send]
+            pending, after, held_for = send, [send], len(sums)
         elif rest_bit < mp_bits - 1:
             half = keep.shape[0] // 2
             keep, send = small(
@@ -497,7 +544,8 @@
         else:
             (state_total,) = small(
                 fold_kernel, "fold", [incoming], [returned.reshape(slot_count, slab_len, enc_width)],
-                [jax.ShapeDtypeStruct(states.shape, jnp.float32)], after,
+                [pltpu.HBM(states.shape, jnp.float32)], after, out_specs=[hbm_spec()],
+                scratch=[pltpu.VMEM(states.shape, jnp.float32), pltpu.SemaphoreType.DMA],
             )
     return (chain[0], chain[1], state_total, outs[0], outs[1])
 

time: 215 us -> 212 us (0.986)
  waiting for transfers between devices: 95.9 us -> 107 us
  starting transfers between devices: 46.2 us -> 36.8 us
  local copies, waits for them, and re-layouts: 11.8 us -> 5.82 us
    ppermute x29, waiting for transfers between devices: 74.2 us -> 85.2 us  [swap(): return lax.ppermute(value, axis, [(i, i ^ 1 << bit) for i in range(count)])]
    ppermute x29, starting transfers between devices: 38.6 us -> 29.4 us  [swap(): return lax.ppermute(value, axis, [(i, i ^ 1 << bit) for i in range(count)])]
    unnamed x21 -> x5, local copies, waits for them, and re-layouts: 5.63 us -> 0.84 us
  transfers between devices with their start and end apart: 31 -> 31, of which waited for: 15 -> 14; matrix products, arithmetic and copies ran while one was open for 0% -> 0% of each run, Pallas kernels for 12% -> 18%
where the time goes in v3:
time: 212 us; the launch traced here: 211 us
  waiting for transfers between devices  107 us (50%)
  Pallas kernels  45.6 us (22%)
  starting transfers between devices  36.8 us (17%)
  blocking collectives  13.5 us (6%)
  local copies, waits for them, and re-layouts  5.82 us (3%)
    ppermute x29, waiting for transfers between devices, swap(): return lax.ppermute(value, axis, [(i, i ^ 1 << bit) for i in range(count)])  85.2 us
    ppermute x29, starting transfers between devices, swap(): return lax.ppermute(value, axis, [(i, i ^ 1 << bit) for i in range(count)])  29.4 us
    pallas_call x4, Pallas kernels, run_heads(): pl.pallas_call(functools.partial(head_kernel, groups, spans, head_dim, st...  25.7 us
    all_to_all x1, waiting for transfers between devices, body(): lax.all_to_all(slab_rows.reshape(shards, capacity, slab_len, enc_width),...  21.7 us
    all_to_all x1, blocking collectives, body(): lax.all_to_all(asked.reshape(shards, capacity), 'dp', split_axis=0, conca...  13.5 us
    pallas_call x1, Pallas kernels, run_state(): pl.pallas_call(functools.partial(state_kernel, groups, widths, len(after)...  10.1 us
    pallas_call x27, Pallas kernels, small(): pl.pallas_call(kernel, out_shape=outs, in_specs=[pl.BlockSpec(memory_spac...  9.77 us
  transfers between devices with their start and end apart: 31, of which 14 were waited for; matrix products, arithmetic and copies ran while one was open for 0% of the time, Pallas kernels for 18%

profile of v3, /device:TPU:0, one launch (start us, length us, event | category | flops | bytes accessed | tf_op | source)
XLA Modules:
  0.0 211.5 jit_solution(4759501827656841658)
XLA Ops:
  2.8 13.5 %all_to_all.16 = s32[8,1,2]{2,1,0:T(1,128)S(1)} all-to-all(s32[8,1,2]{2,1,0:T(1,128)S(1)} %bitcast.26), channel_id=1, replica_groups=mesh['dp'=8,'mp'=4] {'dp'}, dimensions={0} | all-to-all | bytes 128 | tf_op jit(solution)/shard_map/all_to_all | solution.py:476
  19.2 3.6 %all-to-all-start.1 = ((bf16[8,2,32,896]{3,2,1,0:T(8,128)(2,1)}), bf16[8,2,32,896]{3,2,1,0:T(8,128)(2,1)S(1)}, u32[]{:S(2)}, u32[]{:S(2)}) async-start(bf16[8,2,32,896]{3,2,1,0:T(8,128)(2,1)} %bitcast.2), calls=%async_computation.1 | async-start | bytes 1835008 | tf_op jit(solution)/shard_map/all_to_all | solution.py:480
  23.0 21.7 %all-to-all-done.1 = bf16[8,2,32,896]{3,2,1,0:T(8,128)(2,1)S(1)} async-done(((bf16[8,2,32,896]{3,2,1,0:T(8,128)(2,1)}), bf16[8,2,32,896]{3,2,1,0:T(8,128)(2,1)S(1)}, u32[]{:S(2)}, u32[]{:S(2)}) %all-to-all-start.1) | async-done | bytes 917536 | tf_op jit(solution)/shard_map/all_to_all | solution.py:480
  46.9 13.4 %collective-permute-done.1.refs_3_ = bf16[384,896]{1,0:T(8,128)(2,1)S(1)} collective-permute-done((bf16[384,896]{1,0:T(8,128)(2,1)S(1)}, bf16[384,896]{1,0:T(8,128)(2,1)S(1)}, u32[]{:S(2)}, u32[]{:S(2)}) %collective-permute-start.1) | collective-permute-done | bytes 688160 | tf_op jit(solution)/shard_map/ppermute | solution.py:23
  62.5 6.4 %heads.4 = (bf16[384,1024]{1,0:T(8,128)(2,1)}, bf16[384,1024]{1,0:T(8,128)(2,1)}, bf16[1536,256]{1,0:T(8,128)(2,1)}, bf16[1536,256]{1,0:T(8,128)(2,1)}, f32[896,...) custom-call(s32[1]{0:T(128)} %bitcast.refs_0_.choice_ref, bf16[384,896]{1,0:T(8,128)(2,1)S(1)} %bitcast.20, ...), custom_call_target="tpu_custom_call" | custom-call | flops 5637144576 | bytes 5505024 | tf_op jit(solution)/shard_map/heads/pallas_call | solution.py:157
  68.9 2.4 %collective-permute-start.3 = (bf16[896,256]{1,0:T(8,128)(2,1)S(1)}, bf16[896,256]{1,0:T(8,128)(2,1)S(1)}, u32[]{:S(2)}, u32[]{:S(2)}) collective-permute-start(bf16[896,256]{1,0:T(8,128)(2,1)S(1)} %get-tuple-element.64.refs_11_), channel_id=1, source_target_pairs={{0,4},{4,0},{8,12},{12,8},{16,20},{20,16},{24,28},{28,24},{1,5},{5... | collective-permute-start | bytes 1376264 | tf_op jit(solution)/shard_map/ppermute | solution.py:23
  71.3 6.4 %heads.5 = (bf16[384,1024]{1,0:T(8,128)(2,1)}, bf16[384,1024]{1,0:T(8,128)(2,1)}, bf16[1536,256]{1,0:T(8,128)(2,1)}, bf16[1536,256]{1,0:T(8,128)(2,1)}, f32[896,...) custom-call(s32[1]{0:T(128)} %bitcast.refs_0_.choice_ref, ...), custom_call_target="tpu_custom_call", output_to_operand_aliasing={{0}: (9, {}), {1}: (10, {})} | custom-call | flops 5637144576 | bytes 5505024 | tf_op jit(solution)/shard_map/heads/pallas_call | solution.py:157
  77.8 4.8 %collective-permute-done.3.recv_ref = bf16[896,256]{1,0:T(8,128)(2,1)S(1)} collective-permute-done((bf16[896,256]{1,0:T(8,128)(2,1)S(1)}, bf16[896,256]{1,0:T(8,128)(2,1)S(1)}, u32[]{:S(2)}, u32[]{:S(2)}) %collective-permute-start.3) | collective-permute-done | bytes 458784 | tf_op jit(solution)/shard_map/ppermute | solution.py:23
  82.9 6.5 %heads.6 = (bf16[384,1024]{1,0:T(8,128)(2,1)}, bf16[384,1024]{1,0:T(8,128)(2,1)}, bf16[1536,256]{1,0:T(8,128)(2,1)}, bf16[1536,256]{1,0:T(8,128)(2,1)}, f32[896,...) custom-call(s32[1]{0:T(128)} %bitcast.refs_0_.choice_ref, ...), custom_call_target="tpu_custom_call", output_to_operand_aliasing={{0}: (9, {}), {1}: (10, {})} | custom-call | flops 5637144576 | bytes 5505024 | tf_op jit(solution)/shard_map/heads/pallas_call | solution.py:157
  91.6 3.3 %collective-permute-start.8 = (bf16[224,256]{1,0:T(8,128)(2,1)S(1)}, bf16[224,256]{1,0:T(8,128)(2,1)S(1)}, u32[]{:S(2)}, u32[]{:S(2)}) collective-permute-start(bf16[224,256]{1,0:T(8,128)(2,1)S(1)} %get-tuple-element.75.refs_0_), channel_id=1, source_target_pairs={{0,16},{4,20},{8,24},{12,28},{16,0},{20,4},{24,8},{28,12},{1,17},{... | collective-permute-start | bytes 344072 | tf_op jit(solution)/shard_map/ppermute | solution.py:23
  95.1 6.4 %heads.7 = (bf16[384,1024]{1,0:T(8,128)(2,1)}, bf16[384,1024]{1,0:T(8,128)(2,1)}, bf16[1536,256]{1,0:T(8,128)(2,1)}, bf16[1536,256]{1,0:T(8,128)(2,1)}, f32[896,...) custom-call(s32[1]{0:T(128)} %bitcast.refs_0_.choice_ref, ...), custom_call_target="tpu_custom_call", output_to_operand_aliasing={{0}: (9, {}), {1}: (10, {})} | custom-call | flops 5637144576 | bytes 5505024 | tf_op jit(solution)/shard_map/heads/pallas_call | solution.py:157
  101.7 3.0 %collective-permute-start.12 = (bf16[224,256]{1,0:T(8,128)(2,1)S(1)}, bf16[224,256]{1,0:T(8,128)(2,1)S(1)}, u32[]{:S(2)}, u32[]{:S(2)}) collective-permute-start(bf16[224,256]{1,0:T(8,128)(2,1)S(1)} %add.55.refs_0_.own_ref), channel_id=1, source_target_pairs={{0,16},{4,20},{8,24},{12,28},{16,0},{20,4},{24,8},{28,12},{1,17},{... | collective-permute-start | bytes 344072 | tf_op jit(solution)/shard_map/ppermute | solution.py:23
  107.0 10.1 %state_terms.1 = (bf16[768,896]{1,0:T(8,128)(2,1)S(1)}, bf16[768,896]{1,0:T(8,128)(2,1)S(1)}) custom-call(bf16[1536,256]{1,0:T(8,128)(2,1)} %get-tuple-element.79.refs_0_, bf16[1536,256]{1,0:T(8,128)(2,1)} %get-tuple-element.80.refs_1_, bf16[1536,256]{1,0:T(8,128)(2,1)} %get-tuple-element.81.refs_2_, bf16[1536,256]{1,0:T(8,128)(2,1)} %get-tuple-element.82.refs_3_, ...), custom_call_target="tpu_custom_call" | custom-call | flops 11274289152 | bytes 11010048 | tf_op jit(solution)/shard_map/state_terms/pallas_call | solution.py:244
  119.6 6.4 %collective-permute-done.15.recv_ref = bf16[448,256]{1,0:T(8,128)(2,1)S(1)} collective-permute-done((bf16[448,256]{1,0:T(8,128)(2,1)S(1)}, bf16[448,256]{1,0:T(8,128)(2,1)S(1)}, u32[]{:S(2)}, u32[]{:S(2)}) %collective-permute-start.15) | collective-permute-done | bytes 229408 | tf_op jit(solution)/shard_map/ppermute | solution.py:23
  130.8 4.6 %collective-permute-done.20.recv_ref = bf16[224,256]{1,0:T(8,128)(2,1)S(1)} collective-permute-done((bf16[224,256]{1,0:T(8,128)(2,1)S(1)}, bf16[224,256]{1,0:T(8,128)(2,1)S(1)}, u32[]{:S(2)}, u32[]{:S(2)}) %collective-permute-start.20) | collective-permute-done | bytes 114720 | tf_op jit(solution)/shard_map/ppermute | solution.py:23
  140.0 8.3 %collective-permute-done.19.recv_ref = bf16[224,256]{1,0:T(8,128)(2,1)S(1)} collective-permute-done((bf16[224,256]{1,0:T(8,128)(2,1)S(1)}, bf16[224,256]{1,0:T(8,128)(2,1)S(1)}, u32[]{:S(2)}, u32[]{:S(2)}) %collective-permute-start.19) | collective-permute-done | bytes 114720 | tf_op jit(solution)/shard_map/ppermute | solution.py:23
  150.0 2.9 %collective-permute-start.21 = (bf16[224,256]{1,0:T(8,128)(2,1)S(1)}, bf16[224,256]{1,0:T(8,128)(2,1)S(1)}, u32[]{:S(2)}, u32[]{:S(2)}) collective-permute-start(bf16[224,256]{1,0:T(8,128)(2,1)S(1)} %add.58.refs_0_.own_ref), channel_id=1, source_target_pairs={{0,16},{4,20},{8,24},{12,28},{16,0},{20,4},{24,8},{28,12},{1,17},{... | collective-permute-start | bytes 344072 | tf_op jit(solution)/shard_map/ppermute | solution.py:23
  152.9 7.0 %collective-permute-done.22.recv_ref = bf16[224,256]{1,0:T(8,128)(2,1)S(1)} collective-permute-done((bf16[224,256]{1,0:T(8,128)(2,1)S(1)}, bf16[224,256]{1,0:T(8,128)(2,1)S(1)}, u32[]{:S(2)}, u32[]{:S(2)}) %collective-permute-start.22) | collective-permute-done | bytes 114720 | tf_op jit(solution)/shard_map/ppermute | solution.py:23
  163.5 5.0 %collective-permute-done.25.recv_ref = bf16[448,256]{1,0:T(8,128)(2,1)S(1)} collective-permute-done((bf16[448,256]{1,0:T(8,128)(2,1)S(1)}, bf16[448,256]{1,0:T(8,128)(2,1)S(1)}, u32[]{:S(2)}, u32[]{:S(2)}) %collective-permute-start.25) | collective-permute-done | bytes 229408 | tf_op jit(solution)/shard_map/ppermute | solution.py:23
  168.6 2.9 %collective-permute-done.24.recv_ref = bf16[448,256]{1,0:T(8,128)(2,1)S(1)} collective-permute-done((bf16[448,256]{1,0:T(8,128)(2,1)S(1)}, bf16[448,256]{1,0:T(8,128)(2,1)S(1)}, u32[]{:S(2)}, u32[]{:S(2)}) %collective-permute-start.24) | collective-permute-done | bytes 229408 | tf_op jit(solution)/shard_map/ppermute | solution.py:23
  173.2 3.8 %all-to-all-start.2 = ((bf16[8,2,32,896]{3,2,1,0:T(8,128)(2,1)}), bf16[8,2,32,896]{3,2,1,0:T(8,128)(2,1)S(1)}, u32[]{:S(2)}, u32[]{:S(2)}) async-start(bf16[8,2,32,896]{3,2,1,0:T(8,128)(2,1)} %bitcast.24), calls=%async_computation.2 | async-start | bytes 1835008 | tf_op jit(solution)/shard_map/all_to_all | solution.py:542
  179.1 20.3 %collective-permute-done.28.recv_ref = bf16[896,256]{1,0:T(8,128)(2,1)S(1)} collective-permute-done((bf16[896,256]{1,0:T(8,128)(2,1)S(1)}, bf16[896,256]{1,0:T(8,128)(2,1)S(1)}, u32[]{:S(2)}, u32[]{:S(2)}) %collective-permute-start.28) | collective-permute-done | bytes 458784 | tf_op jit(solution)/shard_map/ppermute | solution.py:23
  200.8 6.3 %collective-permute-done.27.recv_ref = bf16[896,256]{1,0:T(8,128)(2,1)} collective-permute-done((bf16[896,256]{1,0:T(8,128)(2,1)S(1)}, bf16[896,256]{1,0:T(8,128)(2,1)}, u32[]{:S(2)}, u32[]{:S(2)}) %collective-permute-start.27) | collective-permute-done | bytes 458784 | tf_op jit(solution)/shard_map/ppermute | solution.py:23
  207.1 2.4 %place.7 = (f32[896,1024]{1,0:T(8,128)}, f32[896,1024]{1,0:T(8,128)}, f32[8,128]{1,0:T(8,128)S(1)}) custom-call(s32[1]{0:T(128)} %bitcast.refs_0_.choice_ref, bf16[896,256]{1,0:T(8,128)(2,1)S(1)} %join.15.refs_0_.own_ref, bf16[896,256]{1,0:T(8,128)(2,1)} %collective-permute-done.27.recv_ref, ...), custom_call_target="tpu_custom_call", output_to_operand_aliasing={{0}: (3, {}), {1}: (4, {})} | custom-call | flops 1 | bytes 1 | tf_op jit(solution)/shard_map/place/pallas_call | solution.py:337
  (99 shorter events, 38.8 us)
Async XLA Ops:
  19.2 25.5 %all-to-all-start.1 = ((bf16[8,2,32,896]{3,2,1,0:T(8,128)(2,1)}), bf16[8,2,32,896]{3,2,1,0:T(8,128)(2,1)S(1)}, u32[]{:S(2)}, u32[]{:S(2)}) async-start(bf16[8,2,32,896]{3,2,1,0:T(8,128)(2,1)} %bitcast.2), calls=%async_computation.1 | async-start | bytes 1835008 | tf_op jit(solution)/shard_map/all_to_all | solution.py:480
  45.3 15.0 %collective-permute-start.1 = (bf16[384,896]{1,0:T(8,128)(2,1)S(1)}, bf16[384,896]{1,0:T(8,128)(2,1)S(1)}, u32[]{:S(2)}, u32[]{:S(2)}) collective-permute-start(bf16[384,896]{1,0:T(8,128)(2,1)S(1)} %bitcast.18), channel_id=1, source_target_pairs={{0,2},{1,3},{2,0},{3,1},{4,6},{5,7},{6,4},{7,5},{8,10},{9,11},{10,... | collective-permute-start | bytes 2064392 | tf_op jit(solution)/shard_map/ppermute | solution.py:23
  46.9 13.4 %collective-permute-start = (bf16[384,896]{1,0:T(8,128)(2,1)S(1)}, bf16[384,896]{1,0:T(8,128)(2,1)S(1)}, u32[]{:S(2)}, u32[]{:S(2)}) collective-permute-start(bf16[384,896]{1,0:T(8,128)(2,1)S(1)} %bitcast.19), channel_id=1, source_target_pairs={{0,1},{1,0},{2,3},{3,2},{4,5},{5,4},{6,7},{7,6},{8,9},{9,8},{10,11... | collective-permute-start | bytes 2064392 | tf_op jit(solution)/shard_map/ppermute | solution.py:23
  68.9 13.7 %collective-permute-start.3 = (bf16[896,256]{1,0:T(8,128)(2,1)S(1)}, bf16[896,256]{1,0:T(8,128)(2,1)S(1)}, u32[]{:S(2)}, u32[]{:S(2)}) collective-permute-start(bf16[896,256]{1,0:T(8,128)(2,1)S(1)} %get-tuple-element.64.refs_11_), channel_id=1, source_target_pairs={{0,4},{4,0},{8,12},{12,8},{16,20},{20,16},{24,28},{28,24},{1,5},{5... | collective-permute-start | bytes 1376264 | tf_op jit(solution)/shard_map/ppermute | solution.py:23
  77.8 17.1 %collective-permute-start.4 = (bf16[896,256]{1,0:T(8,128)(2,1)S(1)}, bf16[896,256]{1,0:T(8,128)(2,1)S(1)}, u32[]{:S(2)}, u32[]{:S(2)}) collective-permute-start(bf16[896,256]{1,0:T(8,128)(2,1)S(1)} %get-tuple-element.68.refs_0_), channel_id=1, source_target_pairs={{0,4},{4,0},{8,12},{12,8},{16,20},{20,16},{24,28},{28,24},{1,5},{5... | collective-permute-start | bytes 1376264 | tf_op jit(solution)/shard_map/ppermute | solution.py:23
  89.4 15.4 %collective-permute-start.6 = (bf16[896,256]{1,0:T(8,128)(2,1)S(1)}, bf16[896,256]{1,0:T(8,128)(2,1)S(1)}, u32[]{:S(2)}, u32[]{:S(2)}) collective-permute-start(bf16[896,256]{1,0:T(8,128)(2,1)S(1)} %get-tuple-element.74.refs_0_), channel_id=1, source_target_pairs={{0,4},{4,0},{8,12},{12,8},{16,20},{20,16},{24,28},{28,24},{1,5},{5... | collective-permute-start | bytes 1376264 | tf_op jit(solution)/shard_map/ppermute | solution.py:23
  91.6 10.1 %collective-permute-start.8 = (bf16[224,256]{1,0:T(8,128)(2,1)S(1)}, bf16[224,256]{1,0:T(8,128)(2,1)S(1)}, u32[]{:S(2)}, u32[]{:S(2)}) collective-permute-start(bf16[224,256]{1,0:T(8,128)(2,1)S(1)} %get-tuple-element.75.refs_0_), channel_id=1, source_target_pairs={{0,16},{4,20},{8,24},{12,28},{16,0},{20,4},{24,8},{28,12},{1,17},{... | collective-permute-start | bytes 344072 | tf_op jit(solution)/shard_map/ppermute | solution.py:23
  101.6 15.6 %collective-permute-start.11 = (bf16[896,256]{1,0:T(8,128)(2,1)S(1)}, bf16[896,256]{1,0:T(8,128)(2,1)S(1)}, u32[]{:S(2)}, u32[]{:S(2)}) collective-permute-start(bf16[896,256]{1,0:T(8,128)(2,1)S(1)} %get-tuple-element.90.refs_0_), channel_id=1, source_target_pairs={{0,4},{4,0},{8,12},{12,8},{16,20},{20,16},{24,28},{28,24},{1,5},{5... | collective-permute-start | bytes 1376264 | tf_op jit(solution)/shard_map/ppermute | solution.py:23
  101.7 15.4 %collective-permute-start.12 = (bf16[224,256]{1,0:T(8,128)(2,1)S(1)}, bf16[224,256]{1,0:T(8,128)(2,1)S(1)}, u32[]{:S(2)}, u32[]{:S(2)}) collective-permute-start(bf16[224,256]{1,0:T(8,128)(2,1)S(1)} %add.55.refs_0_.own_ref), channel_id=1, source_target_pairs={{0,16},{4,20},{8,24},{12,28},{16,0},{20,4},{24,8},{28,12},{1,17},{... | collective-permute-start | bytes 344072 | tf_op jit(solution)/shard_map/ppermute | solution.py:23
  104.7 12.6 %collective-permute-start.10 = (bf16[224,256]{1,0:T(8,128)(2,1)S(1)}, bf16[224,256]{1,0:T(8,128)(2,1)S(1)}, u32[]{:S(2)}, u32[]{:S(2)}) collective-permute-start(bf16[224,256]{1,0:T(8,128)(2,1)S(1)} %get-tuple-element.91.refs_0_), channel_id=1, source_target_pairs={{0,16},{4,20},{8,24},{12,28},{16,0},{20,4},{24,8},{28,12},{1,17},{... | collective-permute-start | bytes 344072 | tf_op jit(solution)/shard_map/ppermute | solution.py:23
  104.9 12.4 %collective-permute-start.9 = (bf16[448,256]{1,0:T(8,128)(2,1)S(1)}, bf16[448,256]{1,0:T(8,128)(2,1)S(1)}, u32[]{:S(2)}, u32[]{:S(2)}) collective-permute-start(bf16[448,256]{1,0:T(8,128)(2,1)S(1)} %get-tuple-element.92.refs_10_), channel_id=1, source_target_pairs={{0,8},{4,12},{8,0},{12,4},{16,24},{20,28},{24,16},{28,20},{1,9},{5... | collective-permute-start | bytes 688136 | tf_op jit(solution)/shard_map/ppermute | solution.py:23
  117.4 13.1 %collective-permute-start.13 = (bf16[768,896]{1,0:T(8,128)(2,1)S(1)}, bf16[768,896]{1,0:T(8,128)(2,1)S(1)}, u32[]{:S(2)}, u32[]{:S(2)}) collective-permute-start(bf16[768,896]{1,0:T(8,128)(2,1)S(1)} %get-tuple-element.100.refs_0_), channel_id=1, source_target_pairs={{0,1},{1,0},{2,3},{3,2},{4,5},{5,4},{6,7},{7,6},{8,9},{9,8},{10,11... | collective-permute-start | bytes 4128776 | tf_op jit(solution)/shard_map/ppermute | solution.py:23
  117.6 12.8 %collective-permute-start.14 = (bf16[448,256]{1,0:T(8,128)(2,1)S(1)}, bf16[448,256]{1,0:T(8,128)(2,1)S(1)}, u32[]{:S(2)}, u32[]{:S(2)}) collective-permute-start(bf16[448,256]{1,0:T(8,128)(2,1)S(1)} %get-tuple-element.98.refs_0_), channel_id=1, source_target_pairs={{0,8},{4,12},{8,0},{12,4},{16,24},{20,28},{24,16},{28,20},{1,9},{5... | collective-permute-start | bytes 688136 | tf_op jit(solution)/shard_map/ppermute | solution.py:23
  126.0 22.3 %collective-permute-start.18 = (bf16[896,256]{1,0:T(8,128)(2,1)S(1)}, bf16[896,256]{1,0:T(8,128)(2,1)S(1)}, u32[]{:S(2)}, u32[]{:S(2)}) collective-permute-start(bf16[896,256]{1,0:T(8,128)(2,1)S(1)} %join.9.refs_0_.own_ref), channel_id=1, source_target_pairs={{0,4},{4,0},{8,12},{12,8},{16,20},{20,16},{24,28},{28,24},{1,5},{5... | collective-permute-start | bytes 1376264 | tf_op jit(solution)/shard_map/ppermute | solution.py:23
  135.4 14.4 %collective-permute-start.23 = (bf16[448,256]{1,0:T(8,128)(2,1)S(1)}, bf16[448,256]{1,0:T(8,128)(2,1)S(1)}, u32[]{:S(2)}, u32[]{:S(2)}) collective-permute-start(bf16[448,256]{1,0:T(8,128)(2,1)S(1)} %join.10.refs_0_.own_ref), channel_id=1, source_target_pairs={{0,8},{4,12},{8,0},{12,4},{16,24},{20,28},{24,16},{28,20},{1,9},{5... | collective-permute-start | bytes 688136 | tf_op jit(solution)/shard_map/ppermute | solution.py:23
  135.5 36.0 %collective-permute-start.16 = (bf16[384,896]{1,0:T(8,128)(2,1)S(1)}, bf16[384,896]{1,0:T(8,128)(2,1)S(1)}, u32[]{:S(2)}, u32[]{:S(2)}) collective-permute-start(bf16[384,896]{1,0:T(8,128)(2,1)S(1)} %get-tuple-element.104.refs_0_), channel_id=1, source_target_pairs={{0,2},{1,3},{2,0},{3,1},{4,6},{5,7},{6,4},{7,5},{8,10},{9,11},{10,... | collective-permute-start | bytes 2064392 | tf_op jit(solution)/shard_map/ppermute | solution.py:23
  137.1 11.3 %collective-permute-start.19 = (bf16[224,256]{1,0:T(8,128)(2,1)S(1)}, bf16[224,256]{1,0:T(8,128)(2,1)S(1)}, u32[]{:S(2)}, u32[]{:S(2)}) collective-permute-start(bf16[224,256]{1,0:T(8,128)(2,1)S(1)} %get-tuple-element.99.refs_0_), channel_id=1, source_target_pairs={{0,16},{4,20},{8,24},{12,28},{16,0},{20,4},{24,8},{28,12},{1,17},{... | collective-permute-start | bytes 344072 | tf_op jit(solution)/shard_map/ppermute | solution.py:23
  138.6 11.2 %collective-permute-start.17 = (bf16[224,256]{1,0:T(8,128)(2,1)S(1)}, bf16[224,256]{1,0:T(8,128)(2,1)S(1)}, u32[]{:S(2)}, u32[]{:S(2)}) collective-permute-start(bf16[224,256]{1,0:T(8,128)(2,1)S(1)} %get-tuple-element.102.refs_0_), channel_id=1, source_target_pairs={{0,16},{4,20},{8,24},{12,28},{16,0},{20,4},{24,8},{28,12},{1,17},{... | collective-permute-start | bytes 344072 | tf_op jit(solution)/shard_map/ppermute | solution.py:23
  149.9 12.3 %collective-permute-start.26 = (bf16[896,256]{1,0:T(8,128)(2,1)S(1)}, bf16[896,256]{1,0:T(8,128)(2,1)S(1)}, u32[]{:S(2)}, u32[]{:S(2)}) collective-permute-start(bf16[896,256]{1,0:T(8,128)(2,1)S(1)} %join.11.refs_0_.own_ref), channel_id=1, source_target_pairs={{0,4},{4,0},{8,12},{12,8},{16,20},{20,16},{24,28},{28,24},{1,5},{5... | collective-permute-start | bytes 1376264 | tf_op jit(solution)/shard_map/ppermute | solution.py:23
  149.9 10.0 %collective-permute-start.22 = (bf16[224,256]{1,0:T(8,128)(2,1)S(1)}, bf16[224,256]{1,0:T(8,128)(2,1)S(1)}, u32[]{:S(2)}, u32[]{:S(2)}) collective-permute-start(bf16[224,256]{1,0:T(8,128)(2,1)S(1)} %add.57.refs_0_.own_ref), channel_id=1, source_target_pairs={{0,16},{4,20},{8,24},{12,28},{16,0},{20,4},{24,8},{28,12},{1,17},{... | collective-permute-start | bytes 344072 | tf_op jit(solution)/shard_map/ppermute | solution.py:23
  150.0 11.7 %collective-permute-start.21 = (bf16[224,256]{1,0:T(8,128)(2,1)S(1)}, bf16[224,256]{1,0:T(8,128)(2,1)S(1)}, u32[]{:S(2)}, u32[]{:S(2)}) collective-permute-start(bf16[224,256]{1,0:T(8,128)(2,1)S(1)} %add.58.refs_0_.own_ref), channel_id=1, source_target_pairs={{0,16},{4,20},{8,24},{12,28},{16,0},{20,4},{24,8},{28,12},{1,17},{... | collective-permute-start | bytes 344072 | tf_op jit(solution)/shard_map/ppermute | solution.py:23
  173.2 36.3 %all-to-all-start.2 = ((bf16[8,2,32,896]{3,2,1,0:T(8,128)(2,1)}), bf16[8,2,32,896]{3,2,1,0:T(8,128)(2,1)S(1)}, u32[]{:S(2)}, u32[]{:S(2)}) async-start(bf16[8,2,32,896]{3,2,1,0:T(8,128)(2,1)} %bitcast.24), calls=%async_computation.2 | async-start | bytes 1835008 | tf_op jit(solution)/shard_map/all_to_all | solution.py:542
  177.0 22.4 %collective-permute-start.28 = (bf16[896,256]{1,0:T(8,128)(2,1)S(1)}, bf16[896,256]{1,0:T(8,128)(2,1)S(1)}, u32[]{:S(2)}, u32[]{:S(2)}) collective-permute-start(bf16[896,256]{1,0:T(8,128)(2,1)S(1)} %join.14.refs_0_.own_ref), channel_id=1, source_target_pairs={{0,4},{4,0},{8,12},{12,8},{16,20},{20,16},{24,28},{28,24},{1,5},{5... | collective-permute-start | bytes 1376264 | tf_op jit(solution)/shard_map/ppermute | solution.py:23
  179.0 28.1 %collective-permute-start.27 = (bf16[896,256]{1,0:T(8,128)(2,1)S(1)}, bf16[896,256]{1,0:T(8,128)(2,1)}, u32[]{:S(2)}, u32[]{:S(2)}) collective-permute-start(bf16[896,256]{1,0:T(8,128)(2,1)S(1)} %join.15.refs_0_.own_ref), channel_id=1, source_target_pairs={{0,4},{4,0},{8,12},{12,8},{16,20},{20,16},{24,28},{28,24},{1,5},{5... | collective-permute-start | bytes 1376264 | tf_op jit(solution)/shard_map/ppermute | solution.py:23
  (9 other events, 93.8 us)

commit v4 on v3

--- a/solution.py
+++ b/solution.py
@@ -300,6 +300,13 @@
     refs[-1][...] = total.astype(refs[-1].dtype)
 
 
+def order_kernel(halves, pairs, keep_ref, recv_ref, *refs):
+    total = keep_ref[...].astype(jnp.float32) + recv_ref[...].astype(jnp.float32)
+    piece = total.shape[0] // (halves * pairs)
+    parts = [total[(h * pairs + p) * piece :][:piece] for p in range(pairs) for h in range(halves)]
+    refs[-1][...] = jnp.concatenate(parts, axis=0).astype(refs[-1].dtype)
+
+
 def join_kernel(choice_ref, own_ref, recv_ref, *refs):
     out_ref = refs[-1]
     upper = choice_ref[0] == 1
@@ -399,56 +406,40 @@
         return send, outs
 
 
-def plan(sums, rest):
-    rate, event, start, lag = 84e3, 1.0, 1.5, 1.5
-    chains = {}
-    for j, s in enumerate(sums):
-        chains[f"sum{j}"] = []
-        for k, bit in enumerate(s.steps):
-            time = 4 * s.load(k) * s.width / rate
-            chains[f"sum{j}"].append({"y": time} if bit == 0 else {"ends": time, "middle": time * (1 + (bit > 1))})
-    chains["rest"] = [{"core": 3.0}] + [{"x": 17.0}] * (rest - 2) + [{"y": 9.0, "ends": 14.0, "middle": 18.0}]
-    last = f"sum{len(sums) - 1}"
-    heavy = [(f"heads{j}", 1.0 + 2.75 * s.width / 128, f"sum{j}") for j, s in enumerate(sums)]
-    heavy.append(("state", 9.5, "rest"))
-    left = {name: len(steps) for name, steps in chains.items()}
-    free, waiting, order, now = {}, {}, [], 0.0
-
-    def send(name):
-        nonlocal now
-        now += start
-        loads = chains[name][-left[name]]
-        begin = max([now] + [free.get(link, 0.0) for link in loads])
-        for link, time in loads.items():
-            free[link] = max(free.get(link, 0.0), now) + time
-        waiting[name] = max([begin + max(loads.values())] + [free[link] for link in loads]) + lag
-
-    def step(name):
-        nonlocal now
-        now = max(now, waiting.pop(name)) + event
-        order.append(name)
-        left[name] -= 1
-        if left[name]:
-            send(name)
-
-    for period, (name, time, begun) in enumerate(heavy):
-        now += time
-        order.append(name)
-        if begun != "rest":
-            send(begun)
-        for name in [f"sum{j}" for j in range(period)] if begun != "rest" else sorted(waiting, key=waiting.get):
-            step(name)
-    send("rest")
-    while waiting:
-        open_now = [name for name in waiting if not (name == "rest" and left[name] == 2 and left[last] > 1)]
-        ready = [name for name in open_now if waiting[name] <= now]
-        moving = [name for name in ready if left[name] > 1]
-        if moving:
-            step(min(moving, key=lambda name: (-left[name], waiting[name])))
-        elif ready:
-            step(ready[0])
-        else:
-            step(min(open_now, key=lambda name: waiting[name]))
+def wavefront(chunks, steps, rest):
+    order, done = [], [0] * chunks
+
+    def step(j):
+        order.append(f"sum{j}")
+        done[j] += 1
+
+    for j in range(chunks):
+        order.append(f"heads{j}")
+        for earlier in range(j):
+            if done[earlier] < steps - 1:
+                step(earlier)
+    order.append("state")
+    for j in [0] + list(range(chunks - 1, 0, -1)):
+        step(j)
+    period, left, launched = 0, rest, False
+    while min(done) < steps or left:
+        turn = list(done)
+        for j in range(chunks):
+            if turn[j] < steps - 1:
+                step(j)
+        if left > 1 and period != 1:
+            order.append("rest")
+            left -= 1
+        for j in range(chunks):
+            if turn[j] == steps - 1:
+                step(j)
+        if left == 1 and not launched and min(done) >= steps - 1:
+            order.append("launch")
+            launched = True
+        if left == 1 and launched and min(done) == steps:
+            order.append("rest")
+            left = 0
+        period += 1
     return order
 
 
@@ -477,16 +468,21 @@
         asked.reshape(shards, capacity), "dp", split_axis=0, concat_axis=0, tiled=True
     ).reshape(slot_count)
     slab_rows = jnp.take(states, jnp.minimum(incoming, stored - 1), axis=0, mode="clip")
-    sent_back = lax.all_to_all(
-        slab_rows.reshape(shards, capacity, slab_len, enc_width), "dp", split_axis=0, concat_axis=0, tiled=True
-    ).reshape(slot_count, slab_len, enc_width)
-    picked = jnp.take(sent_back, slot_index, axis=0, mode="clip").reshape(pair_count * slab_len, enc_width)
-
-    blocks = {0: picked}
-    for bit in reversed(range(mp_bits)):
-        for r in list(blocks):
-            blocks[r | (1 << bit)] = swap(blocks[r], "mp", bit)
-    slabs = [blocks[r] for r in range(groups)]
+    halves = 2
+    piece = slab_len // halves
+    came = []
+    for h in range(halves):
+        out = slab_rows[:, h * piece : (h + 1) * piece].reshape(shards, capacity, piece, enc_width)
+        came.append(lax.all_to_all(out, "dp", split_axis=0, concat_axis=0, tiled=True))
+    blocks = {}
+    for h in range(halves):
+        back = came[h].reshape(slot_count, piece, enc_width)
+        picked = jnp.take(back, slot_index, axis=0, mode="clip").reshape(pair_count * piece, enc_width)
+        blocks[0, h] = picked
+        for bit in reversed(range(mp_bits)):
+            for r in [r for r, k in blocks if k == h]:
+                blocks[r | (1 << bit), h] = swap(blocks[r, h], "mp", bit)
+    slabs = [blocks[r, h] for r in range(groups) for h in range(halves)]
 
     heads = local_width // head_dim
     counts = [min(2, heads - first) for first in range(0, heads, 2)]
@@ -499,7 +495,7 @@
 
     after, chain, outs, dk, dv = [], [], [], [], []
     rest_bit, pending, held_for = 0, None, 0
-    for name in plan(sums, mp_bits + 1):
+    for name in wavefront(len(sums), len(sums[0].steps), mp_bits + 1):
         kind = name.rstrip("0123456789")
         number = int(name[len(kind) :] or 0)
         if kind == "heads":
@@ -522,6 +518,9 @@
         elif kind == "state":
             keep, send = run_state(groups, dk, dv, key_weight, value_weight, after)
             pending, after, held_for = send, [send], len(sums)
+        elif kind == "launch":
+            outgoing, _ = lax.optimization_barrier((outgoing, after))
+            returned = lax.all_to_all(outgoing, "dp", split_axis=0, concat_axis=0, tiled=True)
         elif rest_bit < mp_bits - 1:
             half = keep.shape[0] // 2
             keep, send = small(
@@ -533,13 +532,13 @@
             rest_bit += 1
         elif rest_bit == mp_bits - 1:
             (pair_grad,) = small(
-                add_kernel, "add", [], [keep, moving], [jax.ShapeDtypeStruct(keep.shape, jnp.bfloat16)], after
+                functools.partial(order_kernel, halves, pair_count), "add", [], [keep, moving],
+                [jax.ShapeDtypeStruct(keep.shape, jnp.bfloat16)], after,
             )
             after = [pair_grad]
             outgoing = jnp.take(
                 pair_grad.reshape(pair_count, slab_len, enc_width), slot_pair, axis=0, mode="clip"
             ).reshape(shards, capacity, slab_len, enc_width)
-            returned = lax.all_to_all(outgoing, "dp", split_axis=0, concat_axis=0, tiled=True)
             rest_bit += 1
         else:
             (state_total,) = small(

time: 212 us -> 196 us (0.925)
  waiting for transfers between devices: 107 us -> 62.9 us
  blocking collectives: 13.5 us -> 28 us
  starting transfers between devices: 36.8 us -> 47.9 us
  Pallas kernels: 45.6 us -> 47.8 us
    ppermute x29 -> x32, waiting for transfers between devices: 85.2 us -> 52.6 us  [swap(): return lax.ppermute(value, axis, [(i, i ^ 1 << bit) for i in range(count)])]
    all_to_all x0 -> x1, blocking collectives: none -> 14.4 us  [body(): lax.all_to_all(out, 'dp', split_axis=0, concat_axis=0, tiled=True)]
    all_to_all x1, waiting for transfers between devices: 21.7 us -> 10.3 us  [body(): lax.all_to_all(out, 'dp', split_axis=0, concat_axis=0, tiled=True)]
    ppermute x29 -> x32, starting transfers between devices: 29.4 us -> 40.8 us  [swap(): return lax.ppermute(value, axis, [(i, i ^ 1 << bit) for i in range(count)])]
    pallas_call x4, Pallas kernels: 25.7 us -> 28.9 us  [run_heads(): pl.pallas_call(functools.partial(head_kernel, groups, spans, head_dim, st...]
  transfers between devices with their start and end apart: 31 -> 34, of which waited for: 14 -> 12; matrix products, arithmetic and copies ran while one was open for 0% -> 2% of each run, Pallas kernels for 18% -> 19%
where the time goes in v4:
time: 196 us
  waiting for transfers between devices  62.9 us (32%)
  starting transfers between devices  47.9 us (24%)
  Pallas kernels  47.8 us (24%)
  blocking collectives  28 us (14%)
  local copies, waits for them, and re-layouts  6.34 us (3%)
    ppermute x32, waiting for transfers between devices, swap(): return lax.ppermute(value, axis, [(i, i ^ 1 << bit) for i in range(count)])  52.6 us
    ppermute x32, starting transfers between devices, swap(): return lax.ppermute(value, axis, [(i, i ^ 1 << bit) for i in range(count)])  40.8 us
    pallas_call x4, Pallas kernels, run_heads(): pl.pallas_call(functools.partial(head_kernel, groups, spans, head_dim, st...  28.9 us
    all_to_all x1, blocking collectives, body(): lax.all_to_all(out, 'dp', split_axis=0, concat_axis=0, tiled=True)  14.4 us
    all_to_all x1, blocking collectives, body(): lax.all_to_all(asked.reshape(shards, capacity), 'dp', split_axis=0, conca...  13.5 us
    all_to_all x1, waiting for transfers between devices, body(): lax.all_to_all(out, 'dp', split_axis=0, concat_axis=0, tiled=True)  10.3 us
    pallas_call x1, Pallas kernels, run_state(): pl.pallas_call(functools.partial(state_kernel, groups, widths, len(after)...  10.1 us
    pallas_call x27, Pallas kernels, small(): pl.pallas_call(kernel, out_shape=outs, in_specs=[pl.BlockSpec(memory_spac...  8.83 us
  transfers between devices with their start and end apart: 34, of which 12 were waited for; matrix products, arithmetic and copies ran while one was open for 2% of the time, Pallas kernels for 19%

profile of v4, /device:TPU:0, one launch (start us, length us, event | category | flops | bytes accessed | tf_op | source)
XLA Modules:
  0.0 195.7 jit_solution(12829027048426686274)
XLA Ops:
  2.8 13.5 %all_to_all.21 = s32[8,1,2]{2,1,0:T(1,128)S(1)} all-to-all(s32[8,1,2]{2,1,0:T(1,128)S(1)} %bitcast.36), channel_id=1, replica_groups=mesh['dp'=8,'mp'=4] {'dp'}, dimensions={0} | all-to-all | bytes 128 | tf_op jit(solution)/shard_map/all_to_all | solution.py:467
  19.2 14.4 %all_to_all.22 = bf16[8,2,16,896]{3,2,1,0:T(8,128)(2,1)S(1)} all-to-all(bf16[8,2,16,896]{3,2,1,0:T(8,128)(2,1)S(1)} %bitcast.33), channel_id=1, replica_groups=mesh['dp'=8,'mp'=4] {'dp'}, dimensions={0} | all-to-all | bytes 917504 | tf_op jit(solution)/shard_map/all_to_all | solution.py:476
  33.6 3.5 %all-to-all-start.1 = ((bf16[8,2,16,896]{3,2,1,0:T(8,128)(2,1)}), bf16[8,2,16,896]{3,2,1,0:T(8,128)(2,1)S(1)}, u32[]{:S(2)}, u32[]{:S(2)}) async-start(bf16[8,2,16,896]{3,2,1,0:T(8,128)(2,1)} %bitcast.2), calls=%async_computation.1 | async-start | bytes 917504 | tf_op jit(solution)/shard_map/all_to_all | solution.py:476
  39.5 10.3 %all-to-all-done.1 = bf16[8,2,16,896]{3,2,1,0:T(8,128)(2,1)S(1)} async-done(((bf16[8,2,16,896]{3,2,1,0:T(8,128)(2,1)}), bf16[8,2,16,896]{3,2,1,0:T(8,128)(2,1)S(1)}, u32[]{:S(2)}, u32[]{:S(2)}) %all-to-all-start.1) | async-done | bytes 458784 | tf_op jit(solution)/shard_map/all_to_all | solution.py:476
  52.4 5.2 %collective-permute-done.2.refs_5_ = bf16[192,896]{1,0:T(8,128)(2,1)S(1)} collective-permute-done((bf16[192,896]{1,0:T(8,128)(2,1)S(1)}, bf16[192,896]{1,0:T(8,128)(2,1)S(1)}, u32[]{:S(2)}, u32[]{:S(2)}) %collective-permute-start.2) | collective-permute-done | bytes 344096 | tf_op jit(solution)/shard_map/ppermute | solution.py:23
  59.3 7.2 %heads.4 = (bf16[384,1024]{1,0:T(8,128)(2,1)}, bf16[384,1024]{1,0:T(8,128)(2,1)}, bf16[1536,256]{1,0:T(8,128)(2,1)}, bf16[1536,256]{1,0:T(8,128)(2,1)}, f32[896,...) custom-call(s32[1]{0:T(128)} %bitcast.refs_0_.choice_ref, bf16[192,896]{1,0:T(8,128)(2,1)S(1)} %bitcast.29, ...), custom_call_target="tpu_custom_call" | custom-call | flops 5637144576 | bytes 5505024 | tf_op jit(solution)/shard_map/heads/pallas_call | solution.py:157
  66.5 2.7 %collective-permute-start.6 = (bf16[896,256]{1,0:T(8,128)(2,1)S(1)}, bf16[896,256]{1,0:T(8,128)(2,1)S(1)}, u32[]{:S(2)}, u32[]{:S(2)}) collective-permute-start(bf16[896,256]{1,0:T(8,128)(2,1)S(1)} %get-tuple-element.65.refs_15_), channel_id=1, source_target_pairs={{0,4},{4,0},{8,12},{12,8},{16,20},{20,16},{24,28},{28,24},{1,5},{5... | collective-permute-start | bytes 1376264 | tf_op jit(solution)/shard_map/ppermute | solution.py:23
  69.2 7.2 %heads.5 = (bf16[384,1024]{1,0:T(8,128)(2,1)}, bf16[384,1024]{1,0:T(8,128)(2,1)}, bf16[1536,256]{1,0:T(8,128)(2,1)}, bf16[1536,256]{1,0:T(8,128)(2,1)}, f32[896,...) custom-call(s32[1]{0:T(128)} %bitcast.refs_0_.choice_ref, ...), custom_call_target="tpu_custom_call", output_to_operand_aliasing={{0}: (13, {}), {1}: (14, {})} | custom-call | flops 5637144576 | bytes 5505024 | tf_op jit(solution)/shard_map/heads/pallas_call | solution.py:157
  76.5 4.0 %collective-permute-done.6.recv_ref = bf16[896,256]{1,0:T(8,128)(2,1)S(1)} collective-permute-done((bf16[896,256]{1,0:T(8,128)(2,1)S(1)}, bf16[896,256]{1,0:T(8,128)(2,1)S(1)}, u32[]{:S(2)}, u32[]{:S(2)}) %collective-permute-start.6) | collective-permute-done | bytes 458784 | tf_op jit(solution)/shard_map/ppermute | solution.py:23
  81.0 7.3 %heads.6 = (bf16[384,1024]{1,0:T(8,128)(2,1)}, bf16[384,1024]{1,0:T(8,128)(2,1)}, bf16[1536,256]{1,0:T(8,128)(2,1)}, bf16[1536,256]{1,0:T(8,128)(2,1)}, f32[896,...) custom-call(s32[1]{0:T(128)} %bitcast.refs_0_.choice_ref, ...), custom_call_target="tpu_custom_call", output_to_operand_aliasing={{0}: (13, {}), {1}: (14, {})} | custom-call | flops 5637144576 | bytes 5505024 | tf_op jit(solution)/shard_map/heads/pallas_call | solution.py:157
  90.2 2.8 %collective-permute-start.11 = (bf16[224,256]{1,0:T(8,128)(2,1)S(1)}, bf16[224,256]{1,0:T(8,128)(2,1)S(1)}, u32[]{:S(2)}, u32[]{:S(2)}) collective-permute-start(bf16[224,256]{1,0:T(8,128)(2,1)S(1)} %get-tuple-element.76.refs_0_), channel_id=1, source_target_pairs={{0,16},{4,20},{8,24},{12,28},{16,0},{20,4},{24,8},{28,12},{1,17},{... | collective-permute-start | bytes 344072 | tf_op jit(solution)/shard_map/ppermute | solution.py:23
  93.3 7.2 %heads.7 = (bf16[384,1024]{1,0:T(8,128)(2,1)}, bf16[384,1024]{1,0:T(8,128)(2,1)}, bf16[1536,256]{1,0:T(8,128)(2,1)}, bf16[1536,256]{1,0:T(8,128)(2,1)}, f32[896,...) custom-call(s32[1]{0:T(128)} %bitcast.refs_0_.choice_ref, ...), custom_call_target="tpu_custom_call", output_to_operand_aliasing={{0}: (13, {}), {1}: (14, {})} | custom-call | flops 5637144576 | bytes 5505024 | tf_op jit(solution)/shard_map/heads/pallas_call | solution.py:157
  106.0 10.1 %state_terms.1 = (bf16[768,896]{1,0:T(8,128)(2,1)S(1)}, bf16[768,896]{1,0:T(8,128)(2,1)S(1)}) custom-call(bf16[1536,256]{1,0:T(8,128)(2,1)} %get-tuple-element.80.refs_0_, bf16[1536,256]{1,0:T(8,128)(2,1)} %get-tuple-element.81.refs_1_, bf16[1536,256]{1,0:T(8,128)(2,1)} %get-tuple-element.82.refs_2_, bf16[1536,256]{1,0:T(8,128)(2,1)} %get-tuple-element.83.refs_3_, ...), custom_call_target="tpu_custom_call" | custom-call | flops 11274289152 | bytes 11010048 | tf_op jit(solution)/shard_map/state_terms/pallas_call | solution.py:244
  118.8 2.6 %collective-permute-start.18 = (bf16[224,256]{1,0:T(8,128)(2,1)S(1)}, bf16[224,256]{1,0:T(8,128)(2,1)S(1)}, u32[]{:S(2)}, u32[]{:S(2)}) collective-permute-start(bf16[224,256]{1,0:T(8,128)(2,1)S(1)} %get-tuple-element.100.refs_0_), channel_id=1, source_target_pairs={{0,16},{4,20},{8,24},{12,28},{16,0},{20,4},{24,8},{28,12},{1,17},{... | collective-permute-start | bytes 344072 | tf_op jit(solution)/shard_map/ppermute | solution.py:23
  121.5 8.4 %collective-permute-done.20.recv_ref = bf16[448,256]{1,0:T(8,128)(2,1)S(1)} collective-permute-done((bf16[448,256]{1,0:T(8,128)(2,1)S(1)}, bf16[448,256]{1,0:T(8,128)(2,1)S(1)}, u32[]{:S(2)}, u32[]{:S(2)}) %collective-permute-start.20) | collective-permute-done | bytes 229408 | tf_op jit(solution)/shard_map/ppermute | solution.py:23
  133.0 3.4 %collective-permute-start.23 = (bf16[224,256]{1,0:T(8,128)(2,1)S(1)}, bf16[224,256]{1,0:T(8,128)(2,1)S(1)}, u32[]{:S(2)}, u32[]{:S(2)}) collective-permute-start(bf16[224,256]{1,0:T(8,128)(2,1)S(1)} %add.57.refs_0_.own_ref), channel_id=1, source_target_pairs={{0,16},{4,20},{8,24},{12,28},{16,0},{20,4},{24,8},{28,12},{1,17},{... | collective-permute-start | bytes 344072 | tf_op jit(solution)/shard_map/ppermute | solution.py:23
  138.4 3.2 %collective-permute-done.24.recv_ref = bf16[448,256]{1,0:T(8,128)(2,1)S(1)} collective-permute-done((bf16[448,256]{1,0:T(8,128)(2,1)S(1)}, bf16[448,256]{1,0:T(8,128)(2,1)S(1)}, u32[]{:S(2)}, u32[]{:S(2)}) %collective-permute-start.24) | collective-permute-done | bytes 229408 | tf_op jit(solution)/shard_map/ppermute | solution.py:23
  146.2 3.5 %collective-permute-done.22.recv_ref = bf16[224,256]{1,0:T(8,128)(2,1)S(1)} collective-permute-done((bf16[224,256]{1,0:T(8,128)(2,1)S(1)}, bf16[224,256]{1,0:T(8,128)(2,1)S(1)}, u32[]{:S(2)}, u32[]{:S(2)}) %collective-permute-start.22) | collective-permute-done | bytes 114720 | tf_op jit(solution)/shard_map/ppermute | solution.py:23
  151.7 2.1 %collective-permute-start.28 = (bf16[896,256]{1,0:T(8,128)(2,1)S(1)}, bf16[896,256]{1,0:T(8,128)(2,1)S(1)}, u32[]{:S(2)}, u32[]{:S(2)}) collective-permute-start(bf16[896,256]{1,0:T(8,128)(2,1)S(1)} %join.13.refs_0_.own_ref), channel_id=1, source_target_pairs={{0,4},{4,0},{8,12},{12,8},{16,20},{20,16},{24,28},{28,24},{1,5},{5... | collective-permute-start | bytes 1376264 | tf_op jit(solution)/shard_map/ppermute | solution.py:23
  153.7 2.9 %collective-permute-start.25 = (bf16[224,256]{1,0:T(8,128)(2,1)S(1)}, bf16[224,256]{1,0:T(8,128)(2,1)S(1)}, u32[]{:S(2)}, u32[]{:S(2)}) collective-permute-start(bf16[224,256]{1,0:T(8,128)(2,1)S(1)} %add.58.refs_0_.own_ref), channel_id=1, source_target_pairs={{0,16},{4,20},{8,24},{12,28},{16,0},{20,4},{24,8},{28,12},{1,17},{... | collective-permute-start | bytes 344072 | tf_op jit(solution)/shard_map/ppermute | solution.py:23
  156.7 5.3 %collective-permute-done.25.recv_ref = bf16[224,256]{1,0:T(8,128)(2,1)S(1)} collective-permute-done((bf16[224,256]{1,0:T(8,128)(2,1)S(1)}, bf16[224,256]{1,0:T(8,128)(2,1)S(1)}, u32[]{:S(2)}, u32[]{:S(2)}) %collective-permute-start.25) | collective-permute-done | bytes 114720 | tf_op jit(solution)/shard_map/ppermute | solution.py:23
  163.9 4.1 %collective-permute-done.30.recv_ref = bf16[448,256]{1,0:T(8,128)(2,1)S(1)} collective-permute-done((bf16[448,256]{1,0:T(8,128)(2,1)S(1)}, bf16[448,256]{1,0:T(8,128)(2,1)S(1)}, u32[]{:S(2)}, u32[]{:S(2)}) %collective-permute-start.30) | collective-permute-done | bytes 229408 | tf_op jit(solution)/shard_map/ppermute | solution.py:23
  171.0 3.6 %all-to-all-start.3 = ((bf16[8,2,32,896]{3,2,1,0:T(8,128)(2,1)}), bf16[8,2,32,896]{3,2,1,0:T(8,128)(2,1)S(1)}, u32[]{:S(2)}, u32[]{:S(2)}) async-start(bf16[8,2,32,896]{3,2,1,0:T(8,128)(2,1)} %bitcast.13), calls=%async_computation.3 | async-start | bytes 1835008 | tf_op jit(solution)/shard_map/all_to_all | solution.py:523
  176.6 15.7 %collective-permute-done.31.recv_ref = bf16[896,256]{1,0:T(8,128)(2,1)S(1)} collective-permute-done((bf16[896,256]{1,0:T(8,128)(2,1)S(1)}, bf16[896,256]{1,0:T(8,128)(2,1)S(1)}, u32[]{:S(2)}, u32[]{:S(2)}) %collective-permute-start.31) | collective-permute-done | bytes 458784 | tf_op jit(solution)/shard_map/ppermute | solution.py:23
  (108 shorter events, 44.3 us)
Async XLA Ops:
  33.6 16.2 %all-to-all-start.1 = ((bf16[8,2,16,896]{3,2,1,0:T(8,128)(2,1)}), bf16[8,2,16,896]{3,2,1,0:T(8,128)(2,1)S(1)}, u32[]{:S(2)}, u32[]{:S(2)}) async-start(bf16[8,2,16,896]{3,2,1,0:T(8,128)(2,1)} %bitcast.2), calls=%async_computation.1 | async-start | bytes 917504 | tf_op jit(solution)/shard_map/all_to_all | solution.py:476
  37.9 14.5 %collective-permute-start.3 = (bf16[192,896]{1,0:T(8,128)(2,1)S(1)}, bf16[192,896]{1,0:T(8,128)(2,1)S(1)}, u32[]{:S(2)}, u32[]{:S(2)}) collective-permute-start(bf16[192,896]{1,0:T(8,128)(2,1)S(1)} %bitcast.21), channel_id=1, source_target_pairs={{0,2},{1,3},{2,0},{3,1},{4,6},{5,7},{6,4},{7,5},{8,10},{9,11},{10,... | collective-permute-start | bytes 1032200 | tf_op jit(solution)/shard_map/ppermute | solution.py:23
  66.5 14.0 %collective-permute-start.6 = (bf16[896,256]{1,0:T(8,128)(2,1)S(1)}, bf16[896,256]{1,0:T(8,128)(2,1)S(1)}, u32[]{:S(2)}, u32[]{:S(2)}) collective-permute-start(bf16[896,256]{1,0:T(8,128)(2,1)S(1)} %get-tuple-element.65.refs_15_), channel_id=1, source_target_pairs={{0,4},{4,0},{8,12},{12,8},{16,20},{20,16},{24,28},{28,24},{1,5},{5... | collective-permute-start | bytes 1376264 | tf_op jit(solution)/shard_map/ppermute | solution.py:23
  76.4 16.6 %collective-permute-start.7 = (bf16[896,256]{1,0:T(8,128)(2,1)S(1)}, bf16[896,256]{1,0:T(8,128)(2,1)S(1)}, u32[]{:S(2)}, u32[]{:S(2)}) collective-permute-start(bf16[896,256]{1,0:T(8,128)(2,1)S(1)} %get-tuple-element.69.refs_0_), channel_id=1, source_target_pairs={{0,4},{4,0},{8,12},{12,8},{16,20},{20,16},{24,28},{28,24},{1,5},{5... | collective-permute-start | bytes 1376264 | tf_op jit(solution)/shard_map/ppermute | solution.py:23
  88.3 16.1 %collective-permute-start.9 = (bf16[896,256]{1,0:T(8,128)(2,1)S(1)}, bf16[896,256]{1,0:T(8,128)(2,1)S(1)}, u32[]{:S(2)}, u32[]{:S(2)}) collective-permute-start(bf16[896,256]{1,0:T(8,128)(2,1)S(1)} %get-tuple-element.75.refs_0_), channel_id=1, source_target_pairs={{0,4},{4,0},{8,12},{12,8},{16,20},{20,16},{24,28},{28,24},{1,5},{5... | collective-permute-start | bytes 1376264 | tf_op jit(solution)/shard_map/ppermute | solution.py:23
  90.2 11.0 %collective-permute-start.11 = (bf16[224,256]{1,0:T(8,128)(2,1)S(1)}, bf16[224,256]{1,0:T(8,128)(2,1)S(1)}, u32[]{:S(2)}, u32[]{:S(2)}) collective-permute-start(bf16[224,256]{1,0:T(8,128)(2,1)S(1)} %get-tuple-element.76.refs_0_), channel_id=1, source_target_pairs={{0,16},{4,20},{8,24},{12,28},{16,0},{20,4},{24,8},{28,12},{1,17},{... | collective-permute-start | bytes 344072 | tf_op jit(solution)/shard_map/ppermute | solution.py:23
  93.2 9.6 %collective-permute-start.10 = (bf16[448,256]{1,0:T(8,128)(2,1)S(1)}, bf16[448,256]{1,0:T(8,128)(2,1)S(1)}, u32[]{:S(2)}, u32[]{:S(2)}) collective-permute-start(bf16[448,256]{1,0:T(8,128)(2,1)S(1)} %get-tuple-element.77.refs_15_), channel_id=1, source_target_pairs={{0,8},{4,12},{8,0},{12,4},{16,24},{20,28},{24,16},{28,20},{1,9},{5... | collective-permute-start | bytes 688136 | tf_op jit(solution)/shard_map/ppermute | solution.py:23
  100.5 15.7 %collective-permute-start.14 = (bf16[896,256]{1,0:T(8,128)(2,1)S(1)}, bf16[896,256]{1,0:T(8,128)(2,1)S(1)}, u32[]{:S(2)}, u32[]{:S(2)}) collective-permute-start(bf16[896,256]{1,0:T(8,128)(2,1)S(1)} %get-tuple-element.91.refs_0_), channel_id=1, source_target_pairs={{0,4},{4,0},{8,12},{12,8},{16,20},{20,16},{24,28},{28,24},{1,5},{5... | collective-permute-start | bytes 1376264 | tf_op jit(solution)/shard_map/ppermute | solution.py:23
  101.3 14.8 %collective-permute-start.15 = (bf16[224,256]{1,0:T(8,128)(2,1)S(1)}, bf16[224,256]{1,0:T(8,128)(2,1)S(1)}, u32[]{:S(2)}, u32[]{:S(2)}) collective-permute-start(bf16[224,256]{1,0:T(8,128)(2,1)S(1)} %add.55.refs_0_.own_ref), channel_id=1, source_target_pairs={{0,16},{4,20},{8,24},{12,28},{16,0},{20,4},{24,8},{28,12},{1,17},{... | collective-permute-start | bytes 344072 | tf_op jit(solution)/shard_map/ppermute | solution.py:23
  102.9 13.5 %collective-permute-start.12 = (bf16[224,256]{1,0:T(8,128)(2,1)S(1)}, bf16[224,256]{1,0:T(8,128)(2,1)S(1)}, u32[]{:S(2)}, u32[]{:S(2)}) collective-permute-start(bf16[224,256]{1,0:T(8,128)(2,1)S(1)} %get-tuple-element.92.refs_0_), channel_id=1, source_target_pairs={{0,16},{4,20},{8,24},{12,28},{16,0},{20,4},{24,8},{28,12},{1,17},{... | collective-permute-start | bytes 344072 | tf_op jit(solution)/shard_map/ppermute | solution.py:23
  104.5 11.7 %collective-permute-start.13 = (bf16[448,256]{1,0:T(8,128)(2,1)S(1)}, bf16[448,256]{1,0:T(8,128)(2,1)S(1)}, u32[]{:S(2)}, u32[]{:S(2)}) collective-permute-start(bf16[448,256]{1,0:T(8,128)(2,1)S(1)} %get-tuple-element.93.refs_10_), channel_id=1, source_target_pairs={{0,8},{4,12},{8,0},{12,4},{16,24},{20,28},{24,16},{28,20},{1,9},{5... | collective-permute-start | bytes 688136 | tf_op jit(solution)/shard_map/ppermute | solution.py:23
  116.4 20.2 %collective-permute-start.16 = (bf16[768,896]{1,0:T(8,128)(2,1)S(1)}, bf16[768,896]{1,0:T(8,128)(2,1)S(1)}, u32[]{:S(2)}, u32[]{:S(2)}) collective-permute-start(bf16[768,896]{1,0:T(8,128)(2,1)S(1)} %get-tuple-element.101.refs_0_), channel_id=1, source_target_pairs={{0,1},{1,0},{2,3},{3,2},{4,5},{5,4},{6,7},{7,6},{8,9},{9,8},{10,11... | collective-permute-start | bytes 4128776 | tf_op jit(solution)/shard_map/ppermute | solution.py:23
  116.5 13.4 %collective-permute-start.20 = (bf16[448,256]{1,0:T(8,128)(2,1)S(1)}, bf16[448,256]{1,0:T(8,128)(2,1)S(1)}, u32[]{:S(2)}, u32[]{:S(2)}) collective-permute-start(bf16[448,256]{1,0:T(8,128)(2,1)S(1)} %join.8.refs_0_.own_ref), channel_id=1, source_target_pairs={{0,8},{4,12},{8,0},{12,4},{16,24},{20,28},{24,16},{28,20},{1,9},{5... | collective-permute-start | bytes 688136 | tf_op jit(solution)/shard_map/ppermute | solution.py:23
  117.2 12.7 %collective-permute-start.19 = (bf16[224,256]{1,0:T(8,128)(2,1)S(1)}, bf16[224,256]{1,0:T(8,128)(2,1)S(1)}, u32[]{:S(2)}, u32[]{:S(2)}) collective-permute-start(bf16[224,256]{1,0:T(8,128)(2,1)S(1)} %add.56.refs_0_.own_ref), channel_id=1, source_target_pairs={{0,16},{4,20},{8,24},{12,28},{16,0},{20,4},{24,8},{28,12},{1,17},{... | collective-permute-start | bytes 344072 | tf_op jit(solution)/shard_map/ppermute | solution.py:23
  118.6 17.8 %collective-permute-start.17 = (bf16[448,256]{1,0:T(8,128)(2,1)S(1)}, bf16[448,256]{1,0:T(8,128)(2,1)S(1)}, u32[]{:S(2)}, u32[]{:S(2)}) collective-permute-start(bf16[448,256]{1,0:T(8,128)(2,1)S(1)} %get-tuple-element.99.refs_0_), channel_id=1, source_target_pairs={{0,8},{4,12},{8,0},{12,4},{16,24},{20,28},{24,16},{28,20},{1,9},{5... | collective-permute-start | bytes 688136 | tf_op jit(solution)/shard_map/ppermute | solution.py:23
  118.8 14.2 %collective-permute-start.18 = (bf16[224,256]{1,0:T(8,128)(2,1)S(1)}, bf16[224,256]{1,0:T(8,128)(2,1)S(1)}, u32[]{:S(2)}, u32[]{:S(2)}) collective-permute-start(bf16[224,256]{1,0:T(8,128)(2,1)S(1)} %get-tuple-element.100.refs_0_), channel_id=1, source_target_pairs={{0,16},{4,20},{8,24},{12,28},{16,0},{20,4},{24,8},{28,12},{1,17},{... | collective-permute-start | bytes 344072 | tf_op jit(solution)/shard_map/ppermute | solution.py:23
  129.9 11.7 %collective-permute-start.24 = (bf16[448,256]{1,0:T(8,128)(2,1)S(1)}, bf16[448,256]{1,0:T(8,128)(2,1)S(1)}, u32[]{:S(2)}, u32[]{:S(2)}) collective-permute-start(bf16[448,256]{1,0:T(8,128)(2,1)S(1)} %join.10.refs_0_.own_ref), channel_id=1, source_target_pairs={{0,8},{4,12},{8,0},{12,4},{16,24},{20,28},{24,16},{28,20},{1,9},{5... | collective-permute-start | bytes 688136 | tf_op jit(solution)/shard_map/ppermute | solution.py:23
  130.0 19.7 %collective-permute-start.27 = (bf16[896,256]{1,0:T(8,128)(2,1)S(1)}, bf16[896,256]{1,0:T(8,128)(2,1)S(1)}, u32[]{:S(2)}, u32[]{:S(2)}) collective-permute-start(bf16[896,256]{1,0:T(8,128)(2,1)S(1)} %join.9.refs_0_.own_ref), channel_id=1, source_target_pairs={{0,4},{4,0},{8,12},{12,8},{16,20},{20,16},{24,28},{28,24},{1,5},{5... | collective-permute-start | bytes 1376264 | tf_op jit(solution)/shard_map/ppermute | solution.py:23
  136.9 25.5 %collective-permute-start.21 = (bf16[384,896]{1,0:T(8,128)(2,1)S(1)}, bf16[384,896]{1,0:T(8,128)(2,1)S(1)}, u32[]{:S(2)}, u32[]{:S(2)}) collective-permute-start(bf16[384,896]{1,0:T(8,128)(2,1)S(1)} %get-tuple-element.106.refs_0_), channel_id=1, source_target_pairs={{0,2},{1,3},{2,0},{3,1},{4,6},{5,7},{6,4},{7,5},{8,10},{9,11},{10,... | collective-permute-start | bytes 2064392 | tf_op jit(solution)/shard_map/ppermute | solution.py:23
  141.7 9.9 %collective-permute-start.26 = (bf16[448,256]{1,0:T(8,128)(2,1)S(1)}, bf16[448,256]{1,0:T(8,128)(2,1)S(1)}, u32[]{:S(2)}, u32[]{:S(2)}) collective-permute-start(bf16[448,256]{1,0:T(8,128)(2,1)S(1)} %join.12.refs_0_.own_ref), channel_id=1, source_target_pairs={{0,8},{4,12},{8,0},{12,4},{16,24},{20,28},{24,16},{28,20},{1,9},{5... | collective-permute-start | bytes 688136 | tf_op jit(solution)/shard_map/ppermute | solution.py:23
  144.2 18.3 %collective-permute-start.29 = (bf16[896,256]{1,0:T(8,128)(2,1)S(1)}, bf16[896,256]{1,0:T(8,128)(2,1)S(1)}, u32[]{:S(2)}, u32[]{:S(2)}) collective-permute-start(bf16[896,256]{1,0:T(8,128)(2,1)S(1)} %join.11.refs_0_.own_ref), channel_id=1, source_target_pairs={{0,4},{4,0},{8,12},{12,8},{16,20},{20,16},{24,28},{28,24},{1,5},{5... | collective-permute-start | bytes 1376264 | tf_op jit(solution)/shard_map/ppermute | solution.py:23
  151.7 18.0 %collective-permute-start.28 = (bf16[896,256]{1,0:T(8,128)(2,1)S(1)}, bf16[896,256]{1,0:T(8,128)(2,1)S(1)}, u32[]{:S(2)}, u32[]{:S(2)}) collective-permute-start(bf16[896,256]{1,0:T(8,128)(2,1)S(1)} %join.13.refs_0_.own_ref), channel_id=1, source_target_pairs={{0,4},{4,0},{8,12},{12,8},{16,20},{20,16},{24,28},{28,24},{1,5},{5... | collective-permute-start | bytes 1376264 | tf_op jit(solution)/shard_map/ppermute | solution.py:23
  171.0 22.7 %all-to-all-start.3 = ((bf16[8,2,32,896]{3,2,1,0:T(8,128)(2,1)}), bf16[8,2,32,896]{3,2,1,0:T(8,128)(2,1)S(1)}, u32[]{:S(2)}, u32[]{:S(2)}) async-start(bf16[8,2,32,896]{3,2,1,0:T(8,128)(2,1)} %bitcast.13), calls=%async_computation.3 | async-start | bytes 1835008 | tf_op jit(solution)/shard_map/all_to_all | solution.py:523
  174.6 17.7 %collective-permute-start.31 = (bf16[896,256]{1,0:T(8,128)(2,1)S(1)}, bf16[896,256]{1,0:T(8,128)(2,1)S(1)}, u32[]{:S(2)}, u32[]{:S(2)}) collective-permute-start(bf16[896,256]{1,0:T(8,128)(2,1)S(1)} %join.15.refs_2_.own_ref), channel_id=1, source_target_pairs={{0,4},{4,0},{8,12},{12,8},{16,20},{20,16},{24,28},{28,24},{1,5},{5... | collective-permute-start | bytes 1376264 | tf_op jit(solution)/shard_map/ppermute | solution.py:23
  (12 other events, 118.8 us)

commit v5 on v4

--- a/solution.py
+++ b/solution.py
@@ -58,9 +58,10 @@
     tokens_in = [begin(q_hbm.at[:, columns], q_ref, groups + 2), begin(g_hbm.at[:, columns], g_ref, groups + 3)]
     for copy in weights_in:
         copy.wait()
-    for r in range(groups):
+    for r in range(0, groups, 2):
         rows_in[r].wait()
-        at = pl.ds(r * block, block)
+        rows_in[r + 1].wait()
+        at = pl.ds(r * block, 2 * block)
         keys[at, :] = jnp.dot(rows[at, :], wk[...], preferred_element_type=jnp.float32).astype(jnp.bfloat16)
         values[at, :] = jnp.dot(rows[at, :], wv[...], preferred_element_type=jnp.float32).astype(jnp.bfloat16)
     for copy in tokens_in:
@@ -433,7 +434,7 @@
         for j in range(chunks):
             if turn[j] == steps - 1:
                 step(j)
-        if left == 1 and not launched and min(done) >= steps - 1:
+        if left == 1 and not launched and min(done) >= steps - 2:
             order.append("launch")
             launched = True
         if left == 1 and launched and min(done) == steps:
@@ -539,6 +540,7 @@
             outgoing = jnp.take(
                 pair_grad.reshape(pair_count, slab_len, enc_width), slot_pair, axis=0, mode="clip"
             ).reshape(shards, capacity, slab_len, enc_width)
+            after = [outgoing]
             rest_bit += 1
         else:
             (state_total,) = small(

time: 196 us -> 204 us (1.041)
  waiting for transfers between devices: 62.9 us -> 78 us
  starting transfers between devices: 47.9 us -> 43.9 us
  Pallas kernels: 47.8 us -> 44.9 us
    ppermute x32, waiting for transfers between devices: 52.6 us -> 67.7 us  [swap(): return lax.ppermute(value, axis, [(i, i ^ 1 << bit) for i in range(count)])]
    ppermute x32, starting transfers between devices: 40.8 us -> 36.8 us  [swap(): return lax.ppermute(value, axis, [(i, i ^ 1 << bit) for i in range(count)])]
    pallas_call x4, Pallas kernels: 28.9 us -> 26 us  [run_heads(): pl.pallas_call(functools.partial(head_kernel, groups, spans, head_dim, st...]
  transfers between devices with their start and end apart: 34 -> 34, of which waited for: 12 -> 16; matrix products, arithmetic and copies ran while one was open for 2% -> 1% of each run, Pallas kernels for 19% -> 17%
where the time goes in v5:
time: 204 us
  waiting for transfers between devices  78 us (38%)
  Pallas kernels  44.9 us (22%)
  starting transfers between devices  43.9 us (22%)
  blocking collectives  28 us (14%)
  local copies, waits for them, and re-layouts  6.34 us (3%)
    ppermute x32, waiting for transfers between devices, swap(): return lax.ppermute(value, axis, [(i, i ^ 1 << bit) for i in range(count)])  67.7 us
    ppermute x32, starting transfers between devices, swap(): return lax.ppermute(value, axis, [(i, i ^ 1 << bit) for i in range(count)])  36.8 us
    pallas_call x4, Pallas kernels, run_heads(): pl.pallas_call(functools.partial(head_kernel, groups, spans, head_dim, st...  26 us
    all_to_all x1, blocking collectives, body(): lax.all_to_all(out, 'dp', split_axis=0, concat_axis=0, tiled=True)  14.4 us
    all_to_all x1, blocking collectives, body(): lax.all_to_all(asked.reshape(shards, capacity), 'dp', split_axis=0, conca...  13.5 us
    all_to_all x1, waiting for transfers between devices, body(): lax.all_to_all(out, 'dp', split_axis=0, concat_axis=0, tiled=True)  10.3 us
    pallas_call x1, Pallas kernels, run_state(): pl.pallas_call(functools.partial(state_kernel, groups, widths, len(after)...  10.1 us
    pallas_call x27, Pallas kernels, small(): pl.pallas_call(kernel, out_shape=outs, in_specs=[pl.BlockSpec(memory_spac...  8.76 us
  transfers between devices with their start and end apart: 34, of which 16 were waited for; matrix products, arithmetic and copies ran while one was open for 1% of the time, Pallas kernels for 17%

profile of v5, /device:TPU:0, one launch (start us, length us, event | category | flops | bytes accessed | tf_op | source)
XLA Modules:
  0.0 203.9 jit_solution(10949566659818657927)
XLA Ops:
  2.8 13.5 %all_to_all.21 = s32[8,1,2]{2,1,0:T(1,128)S(1)} all-to-all(s32[8,1,2]{2,1,0:T(1,128)S(1)} %bitcast.36), channel_id=1, replica_groups=mesh['dp'=8,'mp'=4] {'dp'}, dimensions={0} | all-to-all | bytes 128 | tf_op jit(solution)/shard_map/all_to_all | solution.py:468
  19.2 14.4 %all_to_all.22 = bf16[8,2,16,896]{3,2,1,0:T(8,128)(2,1)S(1)} all-to-all(bf16[8,2,16,896]{3,2,1,0:T(8,128)(2,1)S(1)} %bitcast.33), channel_id=1, replica_groups=mesh['dp'=8,'mp'=4] {'dp'}, dimensions={0} | all-to-all | bytes 917504 | tf_op jit(solution)/shard_map/all_to_all | solution.py:477
  33.6 3.5 %all-to-all-start.1 = ((bf16[8,2,16,896]{3,2,1,0:T(8,128)(2,1)}), bf16[8,2,16,896]{3,2,1,0:T(8,128)(2,1)S(1)}, u32[]{:S(2)}, u32[]{:S(2)}) async-start(bf16[8,2,16,896]{3,2,1,0:T(8,128)(2,1)} %bitcast.2), calls=%async_computation.1 | async-start | bytes 917504 | tf_op jit(solution)/shard_map/all_to_all | solution.py:477
  39.5 10.3 %all-to-all-done.1 = bf16[8,2,16,896]{3,2,1,0:T(8,128)(2,1)S(1)} async-done(((bf16[8,2,16,896]{3,2,1,0:T(8,128)(2,1)}), bf16[8,2,16,896]{3,2,1,0:T(8,128)(2,1)S(1)}, u32[]{:S(2)}, u32[]{:S(2)}) %all-to-all-start.1) | async-done | bytes 458784 | tf_op jit(solution)/shard_map/all_to_all | solution.py:477
  52.4 5.2 %collective-permute-done.2.refs_5_ = bf16[192,896]{1,0:T(8,128)(2,1)S(1)} collective-permute-done((bf16[192,896]{1,0:T(8,128)(2,1)S(1)}, bf16[192,896]{1,0:T(8,128)(2,1)S(1)}, u32[]{:S(2)}, u32[]{:S(2)}) %collective-permute-start.2) | collective-permute-done | bytes 344096 | tf_op jit(solution)/shard_map/ppermute | solution.py:23
  59.3 6.5 %heads.4 = (bf16[384,1024]{1,0:T(8,128)(2,1)}, bf16[384,1024]{1,0:T(8,128)(2,1)}, bf16[1536,256]{1,0:T(8,128)(2,1)}, bf16[1536,256]{1,0:T(8,128)(2,1)}, f32[896,...) custom-call(s32[1]{0:T(128)} %bitcast.refs_0_.choice_ref, bf16[192,896]{1,0:T(8,128)(2,1)S(1)} %bitcast.29, ...), custom_call_target="tpu_custom_call" | custom-call | flops 5637144576 | bytes 5505024 | tf_op jit(solution)/shard_map/heads/pallas_call | solution.py:158
  65.8 2.7 %collective-permute-start.6 = (bf16[896,256]{1,0:T(8,128)(2,1)S(1)}, bf16[896,256]{1,0:T(8,128)(2,1)S(1)}, u32[]{:S(2)}, u32[]{:S(2)}) collective-permute-start(bf16[896,256]{1,0:T(8,128)(2,1)S(1)} %get-tuple-element.65.refs_15_), channel_id=1, source_target_pairs={{0,4},{4,0},{8,12},{12,8},{16,20},{20,16},{24,28},{28,24},{1,5},{5... | collective-permute-start | bytes 1376264 | tf_op jit(solution)/shard_map/ppermute | solution.py:23
  68.5 6.5 %heads.5 = (bf16[384,1024]{1,0:T(8,128)(2,1)}, bf16[384,1024]{1,0:T(8,128)(2,1)}, bf16[1536,256]{1,0:T(8,128)(2,1)}, bf16[1536,256]{1,0:T(8,128)(2,1)}, f32[896,...) custom-call(s32[1]{0:T(128)} %bitcast.refs_0_.choice_ref, ...), custom_call_target="tpu_custom_call", output_to_operand_aliasing={{0}: (13, {}), {1}: (14, {})} | custom-call | flops 5637144576 | bytes 5505024 | tf_op jit(solution)/shard_map/heads/pallas_call | solution.py:158
  75.0 4.7 %collective-permute-done.6.recv_ref = bf16[896,256]{1,0:T(8,128)(2,1)S(1)} collective-permute-done((bf16[896,256]{1,0:T(8,128)(2,1)S(1)}, bf16[896,256]{1,0:T(8,128)(2,1)S(1)}, u32[]{:S(2)}, u32[]{:S(2)}) %collective-permute-start.6) | collective-permute-done | bytes 458784 | tf_op jit(solution)/shard_map/ppermute | solution.py:23
  80.2 6.6 %heads.6 = (bf16[384,1024]{1,0:T(8,128)(2,1)}, bf16[384,1024]{1,0:T(8,128)(2,1)}, bf16[1536,256]{1,0:T(8,128)(2,1)}, bf16[1536,256]{1,0:T(8,128)(2,1)}, f32[896,...) custom-call(s32[1]{0:T(128)} %bitcast.refs_0_.choice_ref, ...), custom_call_target="tpu_custom_call", output_to_operand_aliasing={{0}: (13, {}), {1}: (14, {})} | custom-call | flops 5637144576 | bytes 5505024 | tf_op jit(solution)/shard_map/heads/pallas_call | solution.py:158
  88.8 2.9 %collective-permute-start.11 = (bf16[224,256]{1,0:T(8,128)(2,1)S(1)}, bf16[224,256]{1,0:T(8,128)(2,1)S(1)}, u32[]{:S(2)}, u32[]{:S(2)}) collective-permute-start(bf16[224,256]{1,0:T(8,128)(2,1)S(1)} %get-tuple-element.76.refs_0_), channel_id=1, source_target_pairs={{0,16},{4,20},{8,24},{12,28},{16,0},{20,4},{24,8},{28,12},{1,17},{... | collective-permute-start | bytes 344072 | tf_op jit(solution)/shard_map/ppermute | solution.py:23
  91.8 6.5 %heads.7 = (bf16[384,1024]{1,0:T(8,128)(2,1)}, bf16[384,1024]{1,0:T(8,128)(2,1)}, bf16[1536,256]{1,0:T(8,128)(2,1)}, bf16[1536,256]{1,0:T(8,128)(2,1)}, f32[896,...) custom-call(s32[1]{0:T(128)} %bitcast.refs_0_.choice_ref, ...), custom_call_target="tpu_custom_call", output_to_operand_aliasing={{0}: (13, {}), {1}: (14, {})} | custom-call | flops 5637144576 | bytes 5505024 | tf_op jit(solution)/shard_map/heads/pallas_call | solution.py:158
  99.1 2.2 %collective-permute-start.15 = (bf16[224,256]{1,0:T(8,128)(2,1)S(1)}, bf16[224,256]{1,0:T(8,128)(2,1)S(1)}, u32[]{:S(2)}, u32[]{:S(2)}) collective-permute-start(bf16[224,256]{1,0:T(8,128)(2,1)S(1)} %add.55.refs_0_.own_ref), channel_id=1, source_target_pairs={{0,16},{4,20},{8,24},{12,28},{16,0},{20,4},{24,8},{28,12},{1,17},{... | collective-permute-start | bytes 344072 | tf_op jit(solution)/shard_map/ppermute | solution.py:23
  103.8 10.1 %state_terms.1 = (bf16[768,896]{1,0:T(8,128)(2,1)S(1)}, bf16[768,896]{1,0:T(8,128)(2,1)S(1)}) custom-call(bf16[1536,256]{1,0:T(8,128)(2,1)} %get-tuple-element.80.refs_0_, bf16[1536,256]{1,0:T(8,128)(2,1)} %get-tuple-element.81.refs_1_, bf16[1536,256]{1,0:T(8,128)(2,1)} %get-tuple-element.82.refs_2_, bf16[1536,256]{1,0:T(8,128)(2,1)} %get-tuple-element.83.refs_3_, ...), custom_call_target="tpu_custom_call" | custom-call | flops 11274289152 | bytes 11010048 | tf_op jit(solution)/shard_map/state_terms/pallas_call | solution.py:245
  117.2 2.1 %collective-permute-start.18 = (bf16[224,256]{1,0:T(8,128)(2,1)S(1)}, bf16[224,256]{1,0:T(8,128)(2,1)S(1)}, u32[]{:S(2)}, u32[]{:S(2)}) collective-permute-start(bf16[224,256]{1,0:T(8,128)(2,1)S(1)} %get-tuple-element.100.refs_0_), channel_id=1, source_target_pairs={{0,16},{4,20},{8,24},{12,28},{16,0},{20,4},{24,8},{28,12},{1,17},{... | collective-permute-start | bytes 344072 | tf_op jit(solution)/shard_map/ppermute | solution.py:23
  119.3 8.4 %collective-permute-done.20.recv_ref = bf16[448,256]{1,0:T(8,128)(2,1)S(1)} collective-permute-done((bf16[448,256]{1,0:T(8,128)(2,1)S(1)}, bf16[448,256]{1,0:T(8,128)(2,1)S(1)}, u32[]{:S(2)}, u32[]{:S(2)}) %collective-permute-start.20) | collective-permute-done | bytes 229408 | tf_op jit(solution)/shard_map/ppermute | solution.py:23
  136.5 4.5 %collective-permute-done.24.recv_ref = bf16[448,256]{1,0:T(8,128)(2,1)S(1)} collective-permute-done((bf16[448,256]{1,0:T(8,128)(2,1)S(1)}, bf16[448,256]{1,0:T(8,128)(2,1)S(1)}, u32[]{:S(2)}, u32[]{:S(2)}) %collective-permute-start.24) | collective-permute-done | bytes 229408 | tf_op jit(solution)/shard_map/ppermute | solution.py:23
  141.0 2.0 collective-permute-start.28
  146.0 6.4 %collective-permute-done.23.recv_ref = bf16[224,256]{1,0:T(8,128)(2,1)S(1)} collective-permute-done((bf16[224,256]{1,0:T(8,128)(2,1)S(1)}, bf16[224,256]{1,0:T(8,128)(2,1)S(1)}, u32[]{:S(2)}, u32[]{:S(2)}) %collective-permute-start.23) | collective-permute-done | bytes 114720 | tf_op jit(solution)/shard_map/ppermute | solution.py:23
  152.5 2.0 collective-permute-done.22.recv_ref
  156.8 4.2 %collective-permute-done.26.recv_ref = bf16[448,256]{1,0:T(8,128)(2,1)S(1)} collective-permute-done((bf16[448,256]{1,0:T(8,128)(2,1)S(1)}, bf16[448,256]{1,0:T(8,128)(2,1)S(1)}, u32[]{:S(2)}, u32[]{:S(2)}) %collective-permute-start.26) | collective-permute-done | bytes 229408 | tf_op jit(solution)/shard_map/ppermute | solution.py:23
  165.3 3.6 %all-to-all-start.3 = ((bf16[8,2,32,896]{3,2,1,0:T(8,128)(2,1)}), bf16[8,2,32,896]{3,2,1,0:T(8,128)(2,1)S(1)}, u32[]{:S(2)}, u32[]{:S(2)}) async-start(bf16[8,2,32,896]{3,2,1,0:T(8,128)(2,1)} %bitcast.13.refs_2_), calls=%async_computation.3 | async-start | bytes 1835008 | tf_op jit(solution)/shard_map/all_to_all | solution.py:524
  172.3 16.3 %collective-permute-done.29.recv_ref = bf16[448,256]{1,0:T(8,128)(2,1)S(1)} collective-permute-done((bf16[448,256]{1,0:T(8,128)(2,1)S(1)}, bf16[448,256]{1,0:T(8,128)(2,1)S(1)}, u32[]{:S(2)}, u32[]{:S(2)}) %collective-permute-start.29) | collective-permute-done | bytes 229408 | tf_op jit(solution)/shard_map/ppermute | solution.py:23
  192.7 8.0 %collective-permute-done.30.recv_ref = bf16[896,256]{1,0:T(8,128)(2,1)S(1)} collective-permute-done((bf16[896,256]{1,0:T(8,128)(2,1)S(1)}, bf16[896,256]{1,0:T(8,128)(2,1)S(1)}, u32[]{:S(2)}, u32[]{:S(2)}) %collective-permute-start.30) | collective-permute-done | bytes 458784 | tf_op jit(solution)/shard_map/ppermute | solution.py:23
  (108 shorter events, 49.8 us)
Async XLA Ops:
  33.6 16.2 %all-to-all-start.1 = ((bf16[8,2,16,896]{3,2,1,0:T(8,128)(2,1)}), bf16[8,2,16,896]{3,2,1,0:T(8,128)(2,1)S(1)}, u32[]{:S(2)}, u32[]{:S(2)}) async-start(bf16[8,2,16,896]{3,2,1,0:T(8,128)(2,1)} %bitcast.2), calls=%async_computation.1 | async-start | bytes 917504 | tf_op jit(solution)/shard_map/all_to_all | solution.py:477
  37.9 14.5 %collective-permute-start.3 = (bf16[192,896]{1,0:T(8,128)(2,1)S(1)}, bf16[192,896]{1,0:T(8,128)(2,1)S(1)}, u32[]{:S(2)}, u32[]{:S(2)}) collective-permute-start(bf16[192,896]{1,0:T(8,128)(2,1)S(1)} %bitcast.21), channel_id=1, source_target_pairs={{0,2},{1,3},{2,0},{3,1},{4,6},{5,7},{6,4},{7,5},{8,10},{9,11},{10,... | collective-permute-start | bytes 1032200 | tf_op jit(solution)/shard_map/ppermute | solution.py:23
  65.8 14.0 %collective-permute-start.6 = (bf16[896,256]{1,0:T(8,128)(2,1)S(1)}, bf16[896,256]{1,0:T(8,128)(2,1)S(1)}, u32[]{:S(2)}, u32[]{:S(2)}) collective-permute-start(bf16[896,256]{1,0:T(8,128)(2,1)S(1)} %get-tuple-element.65.refs_15_), channel_id=1, source_target_pairs={{0,4},{4,0},{8,12},{12,8},{16,20},{20,16},{24,28},{28,24},{1,5},{5... | collective-permute-start | bytes 1376264 | tf_op jit(solution)/shard_map/ppermute | solution.py:23
  74.9 16.7 %collective-permute-start.7 = (bf16[896,256]{1,0:T(8,128)(2,1)S(1)}, bf16[896,256]{1,0:T(8,128)(2,1)S(1)}, u32[]{:S(2)}, u32[]{:S(2)}) collective-permute-start(bf16[896,256]{1,0:T(8,128)(2,1)S(1)} %get-tuple-element.69.refs_0_), channel_id=1, source_target_pairs={{0,4},{4,0},{8,12},{12,8},{16,20},{20,16},{24,28},{28,24},{1,5},{5... | collective-permute-start | bytes 1376264 | tf_op jit(solution)/shard_map/ppermute | solution.py:23
  86.8 15.4 %collective-permute-start.9 = (bf16[896,256]{1,0:T(8,128)(2,1)S(1)}, bf16[896,256]{1,0:T(8,128)(2,1)S(1)}, u32[]{:S(2)}, u32[]{:S(2)}) collective-permute-start(bf16[896,256]{1,0:T(8,128)(2,1)S(1)} %get-tuple-element.75.refs_0_), channel_id=1, source_target_pairs={{0,4},{4,0},{8,12},{12,8},{16,20},{20,16},{24,28},{28,24},{1,5},{5... | collective-permute-start | bytes 1376264 | tf_op jit(solution)/shard_map/ppermute | solution.py:23
  88.8 10.3 %collective-permute-start.11 = (bf16[224,256]{1,0:T(8,128)(2,1)S(1)}, bf16[224,256]{1,0:T(8,128)(2,1)S(1)}, u32[]{:S(2)}, u32[]{:S(2)}) collective-permute-start(bf16[224,256]{1,0:T(8,128)(2,1)S(1)} %get-tuple-element.76.refs_0_), channel_id=1, source_target_pairs={{0,16},{4,20},{8,24},{12,28},{16,0},{20,4},{24,8},{28,12},{1,17},{... | collective-permute-start | bytes 344072 | tf_op jit(solution)/shard_map/ppermute | solution.py:23
  91.8 9.5 %collective-permute-start.10 = (bf16[448,256]{1,0:T(8,128)(2,1)S(1)}, bf16[448,256]{1,0:T(8,128)(2,1)S(1)}, u32[]{:S(2)}, u32[]{:S(2)}) collective-permute-start(bf16[448,256]{1,0:T(8,128)(2,1)S(1)} %get-tuple-element.77.refs_15_), channel_id=1, source_target_pairs={{0,8},{4,12},{8,0},{12,4},{16,24},{20,28},{24,16},{28,20},{1,9},{5... | collective-permute-start | bytes 688136 | tf_op jit(solution)/shard_map/ppermute | solution.py:23
  98.3 15.6 %collective-permute-start.14 = (bf16[896,256]{1,0:T(8,128)(2,1)S(1)}, bf16[896,256]{1,0:T(8,128)(2,1)S(1)}, u32[]{:S(2)}, u32[]{:S(2)}) collective-permute-start(bf16[896,256]{1,0:T(8,128)(2,1)S(1)} %get-tuple-element.91.refs_0_), channel_id=1, source_target_pairs={{0,4},{4,0},{8,12},{12,8},{16,20},{20,16},{24,28},{28,24},{1,5},{5... | collective-permute-start | bytes 1376264 | tf_op jit(solution)/shard_map/ppermute | solution.py:23
  99.1 14.8 %collective-permute-start.15 = (bf16[224,256]{1,0:T(8,128)(2,1)S(1)}, bf16[224,256]{1,0:T(8,128)(2,1)S(1)}, u32[]{:S(2)}, u32[]{:S(2)}) collective-permute-start(bf16[224,256]{1,0:T(8,128)(2,1)S(1)} %add.55.refs_0_.own_ref), channel_id=1, source_target_pairs={{0,16},{4,20},{8,24},{12,28},{16,0},{20,4},{24,8},{28,12},{1,17},{... | collective-permute-start | bytes 344072 | tf_op jit(solution)/shard_map/ppermute | solution.py:23
  101.4 12.8 %collective-permute-start.12 = (bf16[224,256]{1,0:T(8,128)(2,1)S(1)}, bf16[224,256]{1,0:T(8,128)(2,1)S(1)}, u32[]{:S(2)}, u32[]{:S(2)}) collective-permute-start(bf16[224,256]{1,0:T(8,128)(2,1)S(1)} %get-tuple-element.92.refs_0_), channel_id=1, source_target_pairs={{0,16},{4,20},{8,24},{12,28},{16,0},{20,4},{24,8},{28,12},{1,17},{... | collective-permute-start | bytes 344072 | tf_op jit(solution)/shard_map/ppermute | solution.py:23
  102.4 11.7 %collective-permute-start.13 = (bf16[448,256]{1,0:T(8,128)(2,1)S(1)}, bf16[448,256]{1,0:T(8,128)(2,1)S(1)}, u32[]{:S(2)}, u32[]{:S(2)}) collective-permute-start(bf16[448,256]{1,0:T(8,128)(2,1)S(1)} %get-tuple-element.93.refs_10_), channel_id=1, source_target_pairs={{0,8},{4,12},{8,0},{12,4},{16,24},{20,28},{24,16},{28,20},{1,9},{5... | collective-permute-start | bytes 688136 | tf_op jit(solution)/shard_map/ppermute | solution.py:23
  114.2 18.0 %collective-permute-start.16 = (bf16[768,896]{1,0:T(8,128)(2,1)S(1)}, bf16[768,896]{1,0:T(8,128)(2,1)S(1)}, u32[]{:S(2)}, u32[]{:S(2)}) collective-permute-start(bf16[768,896]{1,0:T(8,128)(2,1)S(1)} %get-tuple-element.101.refs_0_), channel_id=1, source_target_pairs={{0,1},{1,0},{2,3},{3,2},{4,5},{5,4},{6,7},{7,6},{8,9},{9,8},{10,11... | collective-permute-start | bytes 4128776 | tf_op jit(solution)/shard_map/ppermute | solution.py:23
  114.3 13.4 %collective-permute-start.20 = (bf16[448,256]{1,0:T(8,128)(2,1)S(1)}, bf16[448,256]{1,0:T(8,128)(2,1)S(1)}, u32[]{:S(2)}, u32[]{:S(2)}) collective-permute-start(bf16[448,256]{1,0:T(8,128)(2,1)S(1)} %join.8.refs_0_.own_ref), channel_id=1, source_target_pairs={{0,8},{4,12},{8,0},{12,4},{16,24},{20,28},{24,16},{28,20},{1,9},{5... | collective-permute-start | bytes 688136 | tf_op jit(solution)/shard_map/ppermute | solution.py:23
  115.0 17.1 %collective-permute-start.17 = (bf16[448,256]{1,0:T(8,128)(2,1)S(1)}, bf16[448,256]{1,0:T(8,128)(2,1)S(1)}, u32[]{:S(2)}, u32[]{:S(2)}) collective-permute-start(bf16[448,256]{1,0:T(8,128)(2,1)S(1)} %get-tuple-element.99.refs_0_), channel_id=1, source_target_pairs={{0,8},{4,12},{8,0},{12,4},{16,24},{20,28},{24,16},{28,20},{1,9},{5... | collective-permute-start | bytes 688136 | tf_op jit(solution)/shard_map/ppermute | solution.py:23
  116.4 11.9 %collective-permute-start.19 = (bf16[224,256]{1,0:T(8,128)(2,1)S(1)}, bf16[224,256]{1,0:T(8,128)(2,1)S(1)}, u32[]{:S(2)}, u32[]{:S(2)}) collective-permute-start(bf16[224,256]{1,0:T(8,128)(2,1)S(1)} %add.56.refs_0_.own_ref), channel_id=1, source_target_pairs={{0,16},{4,20},{8,24},{12,28},{16,0},{20,4},{24,8},{28,12},{1,17},{... | collective-permute-start | bytes 344072 | tf_op jit(solution)/shard_map/ppermute | solution.py:23
  117.2 13.1 %collective-permute-start.18 = (bf16[224,256]{1,0:T(8,128)(2,1)S(1)}, bf16[224,256]{1,0:T(8,128)(2,1)S(1)}, u32[]{:S(2)}, u32[]{:S(2)}) collective-permute-start(bf16[224,256]{1,0:T(8,128)(2,1)S(1)} %get-tuple-element.100.refs_0_), channel_id=1, source_target_pairs={{0,16},{4,20},{8,24},{12,28},{16,0},{20,4},{24,8},{28,12},{1,17},{... | collective-permute-start | bytes 344072 | tf_op jit(solution)/shard_map/ppermute | solution.py:23
  132.5 29.7 %collective-permute-start.21 = (bf16[384,896]{1,0:T(8,128)(2,1)S(1)}, bf16[384,896]{1,0:T(8,128)(2,1)S(1)}, u32[]{:S(2)}, u32[]{:S(2)}) collective-permute-start(bf16[384,896]{1,0:T(8,128)(2,1)S(1)} %get-tuple-element.106.refs_0_), channel_id=1, source_target_pairs={{0,2},{1,3},{2,0},{3,1},{4,6},{5,7},{6,4},{7,5},{8,10},{9,11},{10,... | collective-permute-start | bytes 2064392 | tf_op jit(solution)/shard_map/ppermute | solution.py:23
  135.2 20.3 %collective-permute-start.27 = (bf16[896,256]{1,0:T(8,128)(2,1)S(1)}, bf16[896,256]{1,0:T(8,128)(2,1)S(1)}, u32[]{:S(2)}, u32[]{:S(2)}) collective-permute-start(bf16[896,256]{1,0:T(8,128)(2,1)S(1)} %join.9.refs_0_.own_ref), channel_id=1, source_target_pairs={{0,4},{4,0},{8,12},{12,8},{16,20},{20,16},{24,28},{28,24},{1,5},{5... | collective-permute-start | bytes 1376264 | tf_op jit(solution)/shard_map/ppermute | solution.py:23
  141.0 22.9 %collective-permute-start.28 = (bf16[896,256]{1,0:T(8,128)(2,1)S(1)}, bf16[896,256]{1,0:T(8,128)(2,1)S(1)}, u32[]{:S(2)}, u32[]{:S(2)}) collective-permute-start(bf16[896,256]{1,0:T(8,128)(2,1)S(1)} %join.11.refs_0_.own_ref), channel_id=1, source_target_pairs={{0,4},{4,0},{8,12},{12,8},{16,20},{20,16},{24,28},{28,24},{1,5},{5... | collective-permute-start | bytes 1376264 | tf_op jit(solution)/shard_map/ppermute | solution.py:23
  144.4 10.1 %collective-permute-start.22 = (bf16[224,256]{1,0:T(8,128)(2,1)S(1)}, bf16[224,256]{1,0:T(8,128)(2,1)S(1)}, u32[]{:S(2)}, u32[]{:S(2)}) collective-permute-start(bf16[224,256]{1,0:T(8,128)(2,1)S(1)} %get-tuple-element.104.refs_0_), channel_id=1, source_target_pairs={{0,16},{4,20},{8,24},{12,28},{16,0},{20,4},{24,8},{28,12},{1,17},{... | collective-permute-start | bytes 344072 | tf_op jit(solution)/shard_map/ppermute | solution.py:23
  165.3 36.7 %all-to-all-start.3 = ((bf16[8,2,32,896]{3,2,1,0:T(8,128)(2,1)}), bf16[8,2,32,896]{3,2,1,0:T(8,128)(2,1)S(1)}, u32[]{:S(2)}, u32[]{:S(2)}) async-start(bf16[8,2,32,896]{3,2,1,0:T(8,128)(2,1)} %bitcast.13.refs_2_), calls=%async_computation.3 | async-start | bytes 1835008 | tf_op jit(solution)/shard_map/all_to_all | solution.py:524
  168.9 19.7 %collective-permute-start.29 = (bf16[448,256]{1,0:T(8,128)(2,1)S(1)}, bf16[448,256]{1,0:T(8,128)(2,1)S(1)}, u32[]{:S(2)}, u32[]{:S(2)}) collective-permute-start(bf16[448,256]{1,0:T(8,128)(2,1)S(1)} %join.14.refs_0_.own_ref), channel_id=1, source_target_pairs={{0,8},{4,12},{8,0},{12,4},{16,24},{20,28},{24,16},{28,20},{1,9},{5... | collective-permute-start | bytes 688136 | tf_op jit(solution)/shard_map/ppermute | solution.py:23
  170.8 20.5 %collective-permute-start.31 = (bf16[896,256]{1,0:T(8,128)(2,1)S(1)}, bf16[896,256]{1,0:T(8,128)(2,1)S(1)}, u32[]{:S(2)}, u32[]{:S(2)}) collective-permute-start(bf16[896,256]{1,0:T(8,128)(2,1)S(1)} %join.13.refs_0_.own_ref), channel_id=1, source_target_pairs={{0,4},{4,0},{8,12},{12,8},{16,20},{20,16},{24,28},{28,24},{1,5},{5... | collective-permute-start | bytes 1376264 | tf_op jit(solution)/shard_map/ppermute | solution.py:23
  188.6 12.0 %collective-permute-start.30 = (bf16[896,256]{1,0:T(8,128)(2,1)S(1)}, bf16[896,256]{1,0:T(8,128)(2,1)S(1)}, u32[]{:S(2)}, u32[]{:S(2)}) collective-permute-start(bf16[896,256]{1,0:T(8,128)(2,1)S(1)} %join.15.refs_2_.own_ref), channel_id=1, source_target_pairs={{0,4},{4,0},{8,12},{12,8},{16,20},{20,16},{24,28},{28,24},{1,5},{5... | collective-permute-start | bytes 1376264 | tf_op jit(solution)/shard_map/ppermute | solution.py:23
  (12 other events, 120.5 us)

commit v6 on v5

--- a/solution.py
+++ b/solution.py
@@ -425,8 +425,8 @@
     period, left, launched = 0, rest, False
     while min(done) < steps or left:
         turn = list(done)
-        for j in range(chunks):
-            if turn[j] < steps - 1:
+        for j in [chunks - 1, *range(chunks - 1)]:
+            if turn[j] < steps - 1 - (j == chunks - 1):
                 step(j)
         if left > 1 and period != 1:
             order.append("rest")
@@ -434,7 +434,9 @@
         for j in range(chunks):
             if turn[j] == steps - 1:
                 step(j)
-        if left == 1 and not launched and min(done) >= steps - 2:
+        if turn[-1] == steps - 2:
+            step(chunks - 1)
+        if left == 1 and not launched and done[-1] >= steps - 1:
             order.append("launch")
             launched = True
         if left == 1 and launched and min(done) == steps:

time: 204 us -> 207 us (1.015)
  waiting for transfers between devices: 78 us -> 81.3 us
  transfers between devices with their start and end apart: 34 -> 34, of which waited for: 16 -> 14; matrix products, arithmetic and copies ran while one was open for 1% -> 1% of each run, Pallas kernels for 17% -> 18%
where the time goes in v6:
time: 207 us; the launch traced here: 206 us
  waiting for transfers between devices  81.3 us (39%)
  Pallas kernels  44.9 us (22%)
  starting transfers between devices  42.7 us (21%)
  blocking collectives  28 us (14%)
  local copies, waits for them, and re-layouts  6.28 us (3%)
    ppermute x32, waiting for transfers between devices, swap(): return lax.ppermute(value, axis, [(i, i ^ 1 << bit) for i in range(count)])  69.5 us
    ppermute x32, starting transfers between devices, swap(): return lax.ppermute(value, axis, [(i, i ^ 1 << bit) for i in range(count)])  34.9 us
    pallas_call x4, Pallas kernels, run_heads(): pl.pallas_call(functools.partial(head_kernel, groups, spans, head_dim, st...  26 us
    all_to_all x1, blocking collectives, body(): lax.all_to_all(out, 'dp', split_axis=0, concat_axis=0, tiled=True)  14.4 us
    all_to_all x1, blocking collectives, body(): lax.all_to_all(asked.reshape(shards, capacity), 'dp', split_axis=0, conca...  13.5 us
    all_to_all x1, waiting for transfers between devices, body(): lax.all_to_all(out, 'dp', split_axis=0, concat_axis=0, tiled=True)  11.8 us
    pallas_call x1, Pallas kernels, run_state(): pl.pallas_call(functools.partial(state_kernel, groups, widths, len(after)...  10.1 us
    pallas_call x27, Pallas kernels, small(): pl.pallas_call(kernel, out_shape=outs, in_specs=[pl.BlockSpec(memory_spac...  8.81 us
  transfers between devices with their start and end apart: 34, of which 14 were waited for; matrix products, arithmetic and copies ran while one was open for 1% of the time, Pallas kernels for 18%

profile of v6, /device:TPU:0, one launch (start us, length us, event | category | flops | bytes accessed | tf_op | source)
XLA Modules:
  0.0 206.1 jit_solution(17634425580875741837)
XLA Ops:
  2.8 13.5 %all_to_all.21 = s32[8,1,2]{2,1,0:T(1,128)S(1)} all-to-all(s32[8,1,2]{2,1,0:T(1,128)S(1)} %bitcast.36), channel_id=1, replica_groups=mesh['dp'=8,'mp'=4] {'dp'}, dimensions={0} | all-to-all | bytes 128 | tf_op jit(solution)/shard_map/all_to_all | solution.py:470
  19.2 14.4 %all_to_all.22 = bf16[8,2,16,896]{3,2,1,0:T(8,128)(2,1)S(1)} all-to-all(bf16[8,2,16,896]{3,2,1,0:T(8,128)(2,1)S(1)} %bitcast.33), channel_id=1, replica_groups=mesh['dp'=8,'mp'=4] {'dp'}, dimensions={0} | all-to-all | bytes 917504 | tf_op jit(solution)/shard_map/all_to_all | solution.py:479
  33.6 3.5 %all-to-all-start.2 = ((bf16[8,2,16,896]{3,2,1,0:T(8,128)(2,1)}), bf16[8,2,16,896]{3,2,1,0:T(8,128)(2,1)S(1)}, u32[]{:S(2)}, u32[]{:S(2)}) async-start(bf16[8,2,16,896]{3,2,1,0:T(8,128)(2,1)} %bitcast.7), calls=%async_computation.2 | async-start | bytes 917504 | tf_op jit(solution)/shard_map/all_to_all | solution.py:479
  37.9 11.8 %all-to-all-done.2 = bf16[8,2,16,896]{3,2,1,0:T(8,128)(2,1)S(1)} async-done(((bf16[8,2,16,896]{3,2,1,0:T(8,128)(2,1)}), bf16[8,2,16,896]{3,2,1,0:T(8,128)(2,1)S(1)}, u32[]{:S(2)}, u32[]{:S(2)}) %all-to-all-start.2) | async-done | bytes 458784 | tf_op jit(solution)/shard_map/all_to_all | solution.py:479
  53.0 7.4 %collective-permute-done.3.refs_6_ = bf16[192,896]{1,0:T(8,128)(2,1)S(1)} collective-permute-done((bf16[192,896]{1,0:T(8,128)(2,1)S(1)}, bf16[192,896]{1,0:T(8,128)(2,1)S(1)}, u32[]{:S(2)}, u32[]{:S(2)}) %collective-permute-start.3) | collective-permute-done | bytes 344096 | tf_op jit(solution)/shard_map/ppermute | solution.py:23
  60.4 3.7 %collective-permute-done.2.refs_5_ = bf16[192,896]{1,0:T(8,128)(2,1)S(1)} collective-permute-done((bf16[192,896]{1,0:T(8,128)(2,1)S(1)}, bf16[192,896]{1,0:T(8,128)(2,1)S(1)}, u32[]{:S(2)}, u32[]{:S(2)}) %collective-permute-start.2) | collective-permute-done | bytes 344096 | tf_op jit(solution)/shard_map/ppermute | solution.py:23
  65.7 6.5 %heads.4 = (bf16[384,1024]{1,0:T(8,128)(2,1)}, bf16[384,1024]{1,0:T(8,128)(2,1)}, bf16[1536,256]{1,0:T(8,128)(2,1)}, bf16[1536,256]{1,0:T(8,128)(2,1)}, f32[896,...) custom-call(s32[1]{0:T(128)} %bitcast.refs_0_.choice_ref, bf16[192,896]{1,0:T(8,128)(2,1)S(1)} %bitcast.23, ...), custom_call_target="tpu_custom_call" | custom-call | flops 5637144576 | bytes 5505024 | tf_op jit(solution)/shard_map/heads/pallas_call | solution.py:158
  72.2 3.7 %collective-permute-start.6 = (bf16[896,256]{1,0:T(8,128)(2,1)S(1)}, bf16[896,256]{1,0:T(8,128)(2,1)S(1)}, u32[]{:S(2)}, u32[]{:S(2)}) collective-permute-start(bf16[896,256]{1,0:T(8,128)(2,1)S(1)} %get-tuple-element.65.refs_15_), channel_id=1, source_target_pairs={{0,4},{4,0},{8,12},{12,8},{16,20},{20,16},{24,28},{28,24},{1,5},{5... | collective-permute-start | bytes 1376264 | tf_op jit(solution)/shard_map/ppermute | solution.py:23
  75.8 6.5 %heads.5 = (bf16[384,1024]{1,0:T(8,128)(2,1)}, bf16[384,1024]{1,0:T(8,128)(2,1)}, bf16[1536,256]{1,0:T(8,128)(2,1)}, bf16[1536,256]{1,0:T(8,128)(2,1)}, f32[896,...) custom-call(s32[1]{0:T(128)} %bitcast.refs_0_.choice_ref, ...), custom_call_target="tpu_custom_call", output_to_operand_aliasing={{0}: (13, {}), {1}: (14, {})} | custom-call | flops 5637144576 | bytes 5505024 | tf_op jit(solution)/shard_map/heads/pallas_call | solution.py:158
  82.4 4.7 %collective-permute-done.6.recv_ref = bf16[896,256]{1,0:T(8,128)(2,1)S(1)} collective-permute-done((bf16[896,256]{1,0:T(8,128)(2,1)S(1)}, bf16[896,256]{1,0:T(8,128)(2,1)S(1)}, u32[]{:S(2)}, u32[]{:S(2)}) %collective-permute-start.6) | collective-permute-done | bytes 458784 | tf_op jit(solution)/shard_map/ppermute | solution.py:23
  87.3 6.6 %heads.6 = (bf16[384,1024]{1,0:T(8,128)(2,1)}, bf16[384,1024]{1,0:T(8,128)(2,1)}, bf16[1536,256]{1,0:T(8,128)(2,1)}, bf16[1536,256]{1,0:T(8,128)(2,1)}, f32[896,...) custom-call(s32[1]{0:T(128)} %bitcast.refs_0_.choice_ref, ...), custom_call_target="tpu_custom_call", output_to_operand_aliasing={{0}: (13, {}), {1}: (14, {})} | custom-call | flops 5637144576 | bytes 5505024 | tf_op jit(solution)/shard_map/heads/pallas_call | solution.py:158
  96.2 2.8 %collective-permute-start.11 = (bf16[224,256]{1,0:T(8,128)(2,1)S(1)}, bf16[224,256]{1,0:T(8,128)(2,1)S(1)}, u32[]{:S(2)}, u32[]{:S(2)}) collective-permute-start(bf16[224,256]{1,0:T(8,128)(2,1)S(1)} %get-tuple-element.76.refs_0_), channel_id=1, source_target_pairs={{0,16},{4,20},{8,24},{12,28},{16,0},{20,4},{24,8},{28,12},{1,17},{... | collective-permute-start | bytes 344072 | tf_op jit(solution)/shard_map/ppermute | solution.py:23
  99.2 6.5 %heads.7 = (bf16[384,1024]{1,0:T(8,128)(2,1)}, bf16[384,1024]{1,0:T(8,128)(2,1)}, bf16[1536,256]{1,0:T(8,128)(2,1)}, bf16[1536,256]{1,0:T(8,128)(2,1)}, f32[896,...) custom-call(s32[1]{0:T(128)} %bitcast.refs_0_.choice_ref, ...), custom_call_target="tpu_custom_call", output_to_operand_aliasing={{0}: (13, {}), {1}: (14, {})} | custom-call | flops 5637144576 | bytes 5505024 | tf_op jit(solution)/shard_map/heads/pallas_call | solution.py:158
  106.5 2.2 %collective-permute-start.15 = (bf16[224,256]{1,0:T(8,128)(2,1)S(1)}, bf16[224,256]{1,0:T(8,128)(2,1)S(1)}, u32[]{:S(2)}, u32[]{:S(2)}) collective-permute-start(bf16[224,256]{1,0:T(8,128)(2,1)S(1)} %add.55.refs_0_.own_ref), channel_id=1, source_target_pairs={{0,16},{4,20},{8,24},{12,28},{16,0},{20,4},{24,8},{28,12},{1,17},{... | collective-permute-start | bytes 344072 | tf_op jit(solution)/shard_map/ppermute | solution.py:23
  111.1 10.1 %state_terms.1 = (bf16[768,896]{1,0:T(8,128)(2,1)S(1)}, bf16[768,896]{1,0:T(8,128)(2,1)S(1)}) custom-call(bf16[1536,256]{1,0:T(8,128)(2,1)} %get-tuple-element.80.refs_0_, bf16[1536,256]{1,0:T(8,128)(2,1)} %get-tuple-element.81.refs_1_, bf16[1536,256]{1,0:T(8,128)(2,1)} %get-tuple-element.82.refs_2_, bf16[1536,256]{1,0:T(8,128)(2,1)} %get-tuple-element.83.refs_3_, ...), custom_call_target="tpu_custom_call" | custom-call | flops 11274289152 | bytes 11010048 | tf_op jit(solution)/shard_map/state_terms/pallas_call | solution.py:245
  126.7 8.4 %collective-permute-done.20.recv_ref = bf16[448,256]{1,0:T(8,128)(2,1)S(1)} collective-permute-done((bf16[448,256]{1,0:T(8,128)(2,1)S(1)}, bf16[448,256]{1,0:T(8,128)(2,1)S(1)}, u32[]{:S(2)}, u32[]{:S(2)}) %collective-permute-start.20) | collective-permute-done | bytes 229408 | tf_op jit(solution)/shard_map/ppermute | solution.py:23
  135.1 4.4 %collective-permute-done.19.recv_ref = bf16[448,256]{1,0:T(8,128)(2,1)S(1)} collective-permute-done((bf16[448,256]{1,0:T(8,128)(2,1)S(1)}, bf16[448,256]{1,0:T(8,128)(2,1)S(1)}, u32[]{:S(2)}, u32[]{:S(2)}) %collective-permute-start.19) | collective-permute-done | bytes 229408 | tf_op jit(solution)/shard_map/ppermute | solution.py:23
  146.6 6.9 %collective-permute-done.24.recv_ref = bf16[224,256]{1,0:T(8,128)(2,1)S(1)} collective-permute-done((bf16[224,256]{1,0:T(8,128)(2,1)S(1)}, bf16[224,256]{1,0:T(8,128)(2,1)S(1)}, u32[]{:S(2)}, u32[]{:S(2)}) %collective-permute-start.24) | collective-permute-done | bytes 114720 | tf_op jit(solution)/shard_map/ppermute | solution.py:23
  154.9 2.2 %collective-permute-start.26 = (bf16[224,256]{1,0:T(8,128)(2,1)S(1)}, bf16[224,256]{1,0:T(8,128)(2,1)S(1)}, u32[]{:S(2)}, u32[]{:S(2)}) collective-permute-start(bf16[224,256]{1,0:T(8,128)(2,1)S(1)} %add.58.refs_0_.own_ref), channel_id=1, source_target_pairs={{0,16},{4,20},{8,24},{12,28},{16,0},{20,4},{24,8},{28,12},{1,17},{... | collective-permute-start | bytes 344072 | tf_op jit(solution)/shard_map/ppermute | solution.py:23
  159.2 2.4 %collective-permute-done.26.recv_ref = bf16[224,256]{1,0:T(8,128)(2,1)S(1)} collective-permute-done((bf16[224,256]{1,0:T(8,128)(2,1)S(1)}, bf16[224,256]{1,0:T(8,128)(2,1)S(1)}, u32[]{:S(2)}, u32[]{:S(2)}) %collective-permute-start.26) | collective-permute-done | bytes 114720 | tf_op jit(solution)/shard_map/ppermute | solution.py:23
  161.6 2.2 %collective-permute-done.25.recv_ref = bf16[448,256]{1,0:T(8,128)(2,1)S(1)} collective-permute-done((bf16[448,256]{1,0:T(8,128)(2,1)S(1)}, bf16[448,256]{1,0:T(8,128)(2,1)S(1)}, u32[]{:S(2)}, u32[]{:S(2)}) %collective-permute-start.25) | collective-permute-done | bytes 229408 | tf_op jit(solution)/shard_map/ppermute | solution.py:23
  170.1 6.7 %collective-permute-done.29.recv_ref = bf16[896,256]{1,0:T(8,128)(2,1)S(1)} collective-permute-done((bf16[896,256]{1,0:T(8,128)(2,1)S(1)}, bf16[896,256]{1,0:T(8,128)(2,1)S(1)}, u32[]{:S(2)}, u32[]{:S(2)}) %collective-permute-start.29) | collective-permute-done | bytes 458784 | tf_op jit(solution)/shard_map/ppermute | solution.py:23
  178.3 4.3 %all-to-all-start.3 = ((bf16[8,2,32,896]{3,2,1,0:T(8,128)(2,1)}), bf16[8,2,32,896]{3,2,1,0:T(8,128)(2,1)S(1)}, u32[]{:S(2)}, u32[]{:S(2)}) async-start(bf16[8,2,32,896]{3,2,1,0:T(8,128)(2,1)} %bitcast.13.refs_2_), calls=%async_computation.3 | async-start | bytes 1835008 | tf_op jit(solution)/shard_map/all_to_all | solution.py:526
  184.7 18.1 %collective-permute-done.31.recv_ref = bf16[896,256]{1,0:T(8,128)(2,1)S(1)} collective-permute-done((bf16[896,256]{1,0:T(8,128)(2,1)S(1)}, bf16[896,256]{1,0:T(8,128)(2,1)S(1)}, u32[]{:S(2)}, u32[]{:S(2)}) %collective-permute-start.31) | collective-permute-done | bytes 458784 | tf_op jit(solution)/shard_map/ppermute | solution.py:23
  (108 shorter events, 45.4 us)
Async XLA Ops:
  33.6 16.2 %all-to-all-start.2 = ((bf16[8,2,16,896]{3,2,1,0:T(8,128)(2,1)}), bf16[8,2,16,896]{3,2,1,0:T(8,128)(2,1)S(1)}, u32[]{:S(2)}, u32[]{:S(2)}) async-start(bf16[8,2,16,896]{3,2,1,0:T(8,128)(2,1)} %bitcast.7), calls=%async_computation.2 | async-start | bytes 917504 | tf_op jit(solution)/shard_map/all_to_all | solution.py:479
  51.9 12.1 %collective-permute-start.2 = (bf16[192,896]{1,0:T(8,128)(2,1)S(1)}, bf16[192,896]{1,0:T(8,128)(2,1)S(1)}, u32[]{:S(2)}, u32[]{:S(2)}) collective-permute-start(bf16[192,896]{1,0:T(8,128)(2,1)S(1)} %bitcast.21), channel_id=1, source_target_pairs={{0,2},{1,3},{2,0},{3,1},{4,6},{5,7},{6,4},{7,5},{8,10},{9,11},{10,... | collective-permute-start | bytes 1032200 | tf_op jit(solution)/shard_map/ppermute | solution.py:23
  52.4 11.6 %collective-permute-start.1 = (bf16[192,896]{1,0:T(8,128)(2,1)S(1)}, bf16[192,896]{1,0:T(8,128)(2,1)S(1)}, u32[]{:S(2)}, u32[]{:S(2)}) collective-permute-start(bf16[192,896]{1,0:T(8,128)(2,1)S(1)} %bitcast.28), channel_id=1, source_target_pairs={{0,1},{1,0},{2,3},{3,2},{4,5},{5,4},{6,7},{7,6},{8,9},{9,8},{10,11... | collective-permute-start | bytes 1032200 | tf_op jit(solution)/shard_map/ppermute | solution.py:23
  72.2 15.0 %collective-permute-start.6 = (bf16[896,256]{1,0:T(8,128)(2,1)S(1)}, bf16[896,256]{1,0:T(8,128)(2,1)S(1)}, u32[]{:S(2)}, u32[]{:S(2)}) collective-permute-start(bf16[896,256]{1,0:T(8,128)(2,1)S(1)} %get-tuple-element.65.refs_15_), channel_id=1, source_target_pairs={{0,4},{4,0},{8,12},{12,8},{16,20},{20,16},{24,28},{28,24},{1,5},{5... | collective-permute-start | bytes 1376264 | tf_op jit(solution)/shard_map/ppermute | solution.py:23
  82.3 16.6 %collective-permute-start.7 = (bf16[896,256]{1,0:T(8,128)(2,1)S(1)}, bf16[896,256]{1,0:T(8,128)(2,1)S(1)}, u32[]{:S(2)}, u32[]{:S(2)}) collective-permute-start(bf16[896,256]{1,0:T(8,128)(2,1)S(1)} %get-tuple-element.69.refs_0_), channel_id=1, source_target_pairs={{0,4},{4,0},{8,12},{12,8},{16,20},{20,16},{24,28},{28,24},{1,5},{5... | collective-permute-start | bytes 1376264 | tf_op jit(solution)/shard_map/ppermute | solution.py:23
  93.9 15.6 %collective-permute-start.9 = (bf16[896,256]{1,0:T(8,128)(2,1)S(1)}, bf16[896,256]{1,0:T(8,128)(2,1)S(1)}, u32[]{:S(2)}, u32[]{:S(2)}) collective-permute-start(bf16[896,256]{1,0:T(8,128)(2,1)S(1)} %get-tuple-element.75.refs_0_), channel_id=1, source_target_pairs={{0,4},{4,0},{8,12},{12,8},{16,20},{20,16},{24,28},{28,24},{1,5},{5... | collective-permute-start | bytes 1376264 | tf_op jit(solution)/shard_map/ppermute | solution.py:23
  105.6 15.7 %collective-permute-start.14 = (bf16[896,256]{1,0:T(8,128)(2,1)S(1)}, bf16[896,256]{1,0:T(8,128)(2,1)S(1)}, u32[]{:S(2)}, u32[]{:S(2)}) collective-permute-start(bf16[896,256]{1,0:T(8,128)(2,1)S(1)} %get-tuple-element.91.refs_0_), channel_id=1, source_target_pairs={{0,4},{4,0},{8,12},{12,8},{16,20},{20,16},{24,28},{28,24},{1,5},{5... | collective-permute-start | bytes 1376264 | tf_op jit(solution)/shard_map/ppermute | solution.py:23
  106.5 14.8 %collective-permute-start.15 = (bf16[224,256]{1,0:T(8,128)(2,1)S(1)}, bf16[224,256]{1,0:T(8,128)(2,1)S(1)}, u32[]{:S(2)}, u32[]{:S(2)}) collective-permute-start(bf16[224,256]{1,0:T(8,128)(2,1)S(1)} %add.55.refs_0_.own_ref), channel_id=1, source_target_pairs={{0,16},{4,20},{8,24},{12,28},{16,0},{20,4},{24,8},{28,12},{1,17},{... | collective-permute-start | bytes 344072 | tf_op jit(solution)/shard_map/ppermute | solution.py:23
  108.7 12.8 %collective-permute-start.12 = (bf16[224,256]{1,0:T(8,128)(2,1)S(1)}, bf16[224,256]{1,0:T(8,128)(2,1)S(1)}, u32[]{:S(2)}, u32[]{:S(2)}) collective-permute-start(bf16[224,256]{1,0:T(8,128)(2,1)S(1)} %get-tuple-element.92.refs_0_), channel_id=1, source_target_pairs={{0,16},{4,20},{8,24},{12,28},{16,0},{20,4},{24,8},{28,12},{1,17},{... | collective-permute-start | bytes 344072 | tf_op jit(solution)/shard_map/ppermute | solution.py:23
  109.7 11.8 %collective-permute-start.13 = (bf16[448,256]{1,0:T(8,128)(2,1)S(1)}, bf16[448,256]{1,0:T(8,128)(2,1)S(1)}, u32[]{:S(2)}, u32[]{:S(2)}) collective-permute-start(bf16[448,256]{1,0:T(8,128)(2,1)S(1)} %get-tuple-element.93.refs_10_), channel_id=1, source_target_pairs={{0,8},{4,12},{8,0},{12,4},{16,24},{20,28},{24,16},{28,20},{1,9},{5... | collective-permute-start | bytes 688136 | tf_op jit(solution)/shard_map/ppermute | solution.py:23
  121.6 23.1 %collective-permute-start.16 = (bf16[768,896]{1,0:T(8,128)(2,1)S(1)}, bf16[768,896]{1,0:T(8,128)(2,1)S(1)}, u32[]{:S(2)}, u32[]{:S(2)}) collective-permute-start(bf16[768,896]{1,0:T(8,128)(2,1)S(1)} %get-tuple-element.101.refs_0_), channel_id=1, source_target_pairs={{0,1},{1,0},{2,3},{3,2},{4,5},{5,4},{6,7},{7,6},{8,9},{9,8},{10,11... | collective-permute-start | bytes 4128776 | tf_op jit(solution)/shard_map/ppermute | solution.py:23
  121.7 13.4 %collective-permute-start.20 = (bf16[448,256]{1,0:T(8,128)(2,1)S(1)}, bf16[448,256]{1,0:T(8,128)(2,1)S(1)}, u32[]{:S(2)}, u32[]{:S(2)}) collective-permute-start(bf16[448,256]{1,0:T(8,128)(2,1)S(1)} %get-tuple-element.99.refs_0_), channel_id=1, source_target_pairs={{0,8},{4,12},{8,0},{12,4},{16,24},{20,28},{24,16},{28,20},{1,9},{5... | collective-permute-start | bytes 688136 | tf_op jit(solution)/shard_map/ppermute | solution.py:23
  122.4 17.1 %collective-permute-start.19 = (bf16[448,256]{1,0:T(8,128)(2,1)S(1)}, bf16[448,256]{1,0:T(8,128)(2,1)S(1)}, u32[]{:S(2)}, u32[]{:S(2)}) collective-permute-start(bf16[448,256]{1,0:T(8,128)(2,1)S(1)} %join.8.refs_0_.own_ref), channel_id=1, source_target_pairs={{0,8},{4,12},{8,0},{12,4},{16,24},{20,28},{24,16},{28,20},{1,9},{5... | collective-permute-start | bytes 688136 | tf_op jit(solution)/shard_map/ppermute | solution.py:23
  123.8 17.8 %collective-permute-start.18 = (bf16[224,256]{1,0:T(8,128)(2,1)S(1)}, bf16[224,256]{1,0:T(8,128)(2,1)S(1)}, u32[]{:S(2)}, u32[]{:S(2)}) collective-permute-start(bf16[224,256]{1,0:T(8,128)(2,1)S(1)} %add.56.refs_0_.own_ref), channel_id=1, source_target_pairs={{0,16},{4,20},{8,24},{12,28},{16,0},{20,4},{24,8},{28,12},{1,17},{... | collective-permute-start | bytes 344072 | tf_op jit(solution)/shard_map/ppermute | solution.py:23
  124.6 19.2 %collective-permute-start.17 = (bf16[224,256]{1,0:T(8,128)(2,1)S(1)}, bf16[224,256]{1,0:T(8,128)(2,1)S(1)}, u32[]{:S(2)}, u32[]{:S(2)}) collective-permute-start(bf16[224,256]{1,0:T(8,128)(2,1)S(1)} %get-tuple-element.100.refs_0_), channel_id=1, source_target_pairs={{0,16},{4,20},{8,24},{12,28},{16,0},{20,4},{24,8},{28,12},{1,17},{... | collective-permute-start | bytes 344072 | tf_op jit(solution)/shard_map/ppermute | solution.py:23
  139.5 18.2 %collective-permute-start.27 = (bf16[896,256]{1,0:T(8,128)(2,1)S(1)}, bf16[896,256]{1,0:T(8,128)(2,1)S(1)}, u32[]{:S(2)}, u32[]{:S(2)}) collective-permute-start(bf16[896,256]{1,0:T(8,128)(2,1)S(1)} %join.9.refs_0_.own_ref), channel_id=1, source_target_pairs={{0,4},{4,0},{8,12},{12,8},{16,20},{20,16},{24,28},{28,24},{1,5},{5... | collective-permute-start | bytes 1376264 | tf_op jit(solution)/shard_map/ppermute | solution.py:23
  141.6 12.0 %collective-permute-start.23 = (bf16[448,256]{1,0:T(8,128)(2,1)S(1)}, bf16[448,256]{1,0:T(8,128)(2,1)S(1)}, u32[]{:S(2)}, u32[]{:S(2)}) collective-permute-start(bf16[448,256]{1,0:T(8,128)(2,1)S(1)} %join.10.refs_0_.own_ref), channel_id=1, source_target_pairs={{0,8},{4,12},{8,0},{12,4},{16,24},{20,28},{24,16},{28,20},{1,9},{5... | collective-permute-start | bytes 688136 | tf_op jit(solution)/shard_map/ppermute | solution.py:23
  141.6 11.9 %collective-permute-start.24 = (bf16[224,256]{1,0:T(8,128)(2,1)S(1)}, bf16[224,256]{1,0:T(8,128)(2,1)S(1)}, u32[]{:S(2)}, u32[]{:S(2)}) collective-permute-start(bf16[224,256]{1,0:T(8,128)(2,1)S(1)} %get-tuple-element.104.refs_0_), channel_id=1, source_target_pairs={{0,16},{4,20},{8,24},{12,28},{16,0},{20,4},{24,8},{28,12},{1,17},{... | collective-permute-start | bytes 344072 | tf_op jit(solution)/shard_map/ppermute | solution.py:23
  145.0 20.2 %collective-permute-start.21 = (bf16[384,896]{1,0:T(8,128)(2,1)S(1)}, bf16[384,896]{1,0:T(8,128)(2,1)S(1)}, u32[]{:S(2)}, u32[]{:S(2)}) collective-permute-start(bf16[384,896]{1,0:T(8,128)(2,1)S(1)} %get-tuple-element.106.refs_0_), channel_id=1, source_target_pairs={{0,2},{1,3},{2,0},{3,1},{4,6},{5,7},{6,4},{7,5},{8,10},{9,11},{10,... | collective-permute-start | bytes 2064392 | tf_op jit(solution)/shard_map/ppermute | solution.py:23
  157.1 11.6 %collective-permute-start.30 = (bf16[896,256]{1,0:T(8,128)(2,1)S(1)}, bf16[896,256]{1,0:T(8,128)(2,1)S(1)}, u32[]{:S(2)}, u32[]{:S(2)}) collective-permute-start(bf16[896,256]{1,0:T(8,128)(2,1)S(1)} %join.11.refs_0_.own_ref), channel_id=1, source_target_pairs={{0,4},{4,0},{8,12},{12,8},{16,20},{20,16},{24,28},{28,24},{1,5},{5... | collective-permute-start | bytes 1376264 | tf_op jit(solution)/shard_map/ppermute | solution.py:23
  163.8 13.0 %collective-permute-start.29 = (bf16[896,256]{1,0:T(8,128)(2,1)S(1)}, bf16[896,256]{1,0:T(8,128)(2,1)S(1)}, u32[]{:S(2)}, u32[]{:S(2)}) collective-permute-start(bf16[896,256]{1,0:T(8,128)(2,1)S(1)} %join.14.refs_0_.own_ref), channel_id=1, source_target_pairs={{0,4},{4,0},{8,12},{12,8},{16,20},{20,16},{24,28},{28,24},{1,5},{5... | collective-permute-start | bytes 1376264 | tf_op jit(solution)/shard_map/ppermute | solution.py:23
  163.9 14.3 %collective-permute-start.28 = (bf16[448,256]{1,0:T(8,128)(2,1)S(1)}, bf16[448,256]{1,0:T(8,128)(2,1)S(1)}, u32[]{:S(2)}, u32[]{:S(2)}) collective-permute-start(bf16[448,256]{1,0:T(8,128)(2,1)S(1)} %join.13.refs_0_.own_ref), channel_id=1, source_target_pairs={{0,8},{4,12},{8,0},{12,4},{16,24},{20,28},{24,16},{28,20},{1,9},{5... | collective-permute-start | bytes 688136 | tf_op jit(solution)/shard_map/ppermute | solution.py:23
  178.3 25.9 %all-to-all-start.3 = ((bf16[8,2,32,896]{3,2,1,0:T(8,128)(2,1)}), bf16[8,2,32,896]{3,2,1,0:T(8,128)(2,1)S(1)}, u32[]{:S(2)}, u32[]{:S(2)}) async-start(bf16[8,2,32,896]{3,2,1,0:T(8,128)(2,1)} %bitcast.13.refs_2_), calls=%async_computation.3 | async-start | bytes 1835008 | tf_op jit(solution)/shard_map/all_to_all | solution.py:526
  182.6 20.2 %collective-permute-start.31 = (bf16[896,256]{1,0:T(8,128)(2,1)S(1)}, bf16[896,256]{1,0:T(8,128)(2,1)S(1)}, u32[]{:S(2)}, u32[]{:S(2)}) collective-permute-start(bf16[896,256]{1,0:T(8,128)(2,1)S(1)} %join.15.own_ref.refs_2_), channel_id=1, source_target_pairs={{0,4},{4,0},{8,12},{12,8},{16,20},{20,16},{24,28},{28,24},{1,5},{5... | collective-permute-start | bytes 1376264 | tf_op jit(solution)/shard_map/ppermute | solution.py:23
  (12 other events, 135.7 us)

commit v7 on v6

--- a/solution.py
+++ b/solution.py
@@ -425,7 +425,7 @@
     period, left, launched = 0, rest, False
     while min(done) < steps or left:
         turn = list(done)
-        for j in [chunks - 1, *range(chunks - 1)]:
+        for j in range(chunks):
             if turn[j] < steps - 1 - (j == chunks - 1):
                 step(j)
         if left > 1 and period != 1:
@@ -479,6 +479,9 @@
         came.append(lax.all_to_all(out, "dp", split_axis=0, concat_axis=0, tiled=True))
     blocks = {}
     for h in range(halves):
+        if h:
+            first = (1 << (mp_bits - 1), h - 1)
+            came[h], blocks[first] = lax.optimization_barrier((came[h], blocks[first]))
         back = came[h].reshape(slot_count, piece, enc_width)
         picked = jnp.take(back, slot_index, axis=0, mode="clip").reshape(pair_count * piece, enc_width)
         blocks[0, h] = picked

time: 207 us -> 194 us (0.937)
  waiting for transfers between devices: 81.3 us -> 63.5 us
  starting transfers between devices: 42.7 us -> 47.7 us
    ppermute x32, waiting for transfers between devices: 69.5 us -> 53.2 us  [swap(): return lax.ppermute(value, axis, [(i, i ^ 1 << bit) for i in range(count)])]
    ppermute x32, starting transfers between devices: 34.9 us -> 40.3 us  [swap(): return lax.ppermute(value, axis, [(i, i ^ 1 << bit) for i in range(count)])]
  transfers between devices with their start and end apart: 34 -> 34, of which waited for: 14 -> 12; matrix products, arithmetic and copies ran while one was open for 1% -> 1% of each run, Pallas kernels for 18% -> 19%
where the time goes in v7:
time: 194 us; the launch traced here: 193 us
  waiting for transfers between devices  63.5 us (33%)
  starting transfers between devices  47.7 us (25%)
  Pallas kernels  44.9 us (23%)
  blocking collectives  28 us (14%)
  local copies, waits for them, and re-layouts  6.28 us (3%)
    ppermute x32, waiting for transfers between devices, swap(): return lax.ppermute(value, axis, [(i, i ^ 1 << bit) for i in range(count)])  53.2 us
    ppermute x32, starting transfers between devices, swap(): return lax.ppermute(value, axis, [(i, i ^ 1 << bit) for i in range(count)])  40.3 us
    pallas_call x4, Pallas kernels, run_heads(): pl.pallas_call(functools.partial(head_kernel, groups, spans, head_dim, st...  26 us
    all_to_all x1, blocking collectives, body(): lax.all_to_all(out, 'dp', split_axis=0, concat_axis=0, tiled=True)  14.4 us
    all_to_all x1, blocking collectives, body(): lax.all_to_all(asked.reshape(shards, capacity), 'dp', split_axis=0, conca...  13.5 us
    all_to_all x1, waiting for transfers between devices, body(): lax.all_to_all(out, 'dp', split_axis=0, concat_axis=0, tiled=True)  10.3 us
    pallas_call x1, Pallas kernels, run_state(): pl.pallas_call(functools.partial(state_kernel, groups, widths, len(after)...  10.1 us
    pallas_call x27, Pallas kernels, small(): pl.pallas_call(kernel, out_shape=outs, in_specs=[pl.BlockSpec(memory_spac...  8.8 us
  transfers between devices with their start and end apart: 34, of which 12 were waited for; matrix products, arithmetic and copies ran while one was open for 1% of the time, Pallas kernels for 19%

profile of v7, /device:TPU:0, one launch (start us, length us, event | category | flops | bytes accessed | tf_op | source)
XLA Modules:
  0.0 193.2 jit_solution(9443140004528776485)
XLA Ops:
  2.8 13.5 %all_to_all.21 = s32[8,1,2]{2,1,0:T(1,128)S(1)} all-to-all(s32[8,1,2]{2,1,0:T(1,128)S(1)} %bitcast.36), channel_id=1, replica_groups=mesh['dp'=8,'mp'=4] {'dp'}, dimensions={0} | all-to-all | bytes 128 | tf_op jit(solution)/shard_map/all_to_all | solution.py:470
  19.2 14.4 %all_to_all.22 = bf16[8,2,16,896]{3,2,1,0:T(8,128)(2,1)S(1)} all-to-all(bf16[8,2,16,896]{3,2,1,0:T(8,128)(2,1)S(1)} %bitcast.33), channel_id=1, replica_groups=mesh['dp'=8,'mp'=4] {'dp'}, dimensions={0} | all-to-all | bytes 917504 | tf_op jit(solution)/shard_map/all_to_all | solution.py:479
  33.6 3.5 %all-to-all-start.2 = ((bf16[8,2,16,896]{3,2,1,0:T(8,128)(2,1)}), bf16[8,2,16,896]{3,2,1,0:T(8,128)(2,1)S(1)}, u32[]{:S(2)}, u32[]{:S(2)}) async-start(bf16[8,2,16,896]{3,2,1,0:T(8,128)(2,1)} %bitcast.7), calls=%async_computation.2 | async-start | bytes 917504 | tf_op jit(solution)/shard_map/all_to_all | solution.py:479
  39.5 10.3 %all-to-all-done.2 = bf16[8,2,16,896]{3,2,1,0:T(8,128)(2,1)S(1)} async-done(((bf16[8,2,16,896]{3,2,1,0:T(8,128)(2,1)}), bf16[8,2,16,896]{3,2,1,0:T(8,128)(2,1)S(1)}, u32[]{:S(2)}, u32[]{:S(2)}) %all-to-all-start.2) | async-done | bytes 458784 | tf_op jit(solution)/shard_map/all_to_all | solution.py:479
  52.4 5.2 %collective-permute-done.3.refs_6_ = bf16[192,896]{1,0:T(8,128)(2,1)S(1)} collective-permute-done((bf16[192,896]{1,0:T(8,128)(2,1)S(1)}, bf16[192,896]{1,0:T(8,128)(2,1)S(1)}, u32[]{:S(2)}, u32[]{:S(2)}) %collective-permute-start.3) | collective-permute-done | bytes 344096 | tf_op jit(solution)/shard_map/ppermute | solution.py:23
  59.3 6.5 %heads.4 = (bf16[384,1024]{1,0:T(8,128)(2,1)}, bf16[384,1024]{1,0:T(8,128)(2,1)}, bf16[1536,256]{1,0:T(8,128)(2,1)}, bf16[1536,256]{1,0:T(8,128)(2,1)}, f32[896,...) custom-call(s32[1]{0:T(128)} %bitcast.refs_0_.choice_ref, bf16[192,896]{1,0:T(8,128)(2,1)S(1)} %bitcast.23, ...), custom_call_target="tpu_custom_call" | custom-call | flops 5637144576 | bytes 5505024 | tf_op jit(solution)/shard_map/heads/pallas_call | solution.py:158
  65.8 2.7 %collective-permute-start.6 = (bf16[896,256]{1,0:T(8,128)(2,1)S(1)}, bf16[896,256]{1,0:T(8,128)(2,1)S(1)}, u32[]{:S(2)}, u32[]{:S(2)}) collective-permute-start(bf16[896,256]{1,0:T(8,128)(2,1)S(1)} %get-tuple-element.69.refs_15_), channel_id=1, source_target_pairs={{0,4},{4,0},{8,12},{12,8},{16,20},{20,16},{24,28},{28,24},{1,5},{5... | collective-permute-start | bytes 1376264 | tf_op jit(solution)/shard_map/ppermute | solution.py:23
  68.5 6.5 %heads.5 = (bf16[384,1024]{1,0:T(8,128)(2,1)}, bf16[384,1024]{1,0:T(8,128)(2,1)}, bf16[1536,256]{1,0:T(8,128)(2,1)}, bf16[1536,256]{1,0:T(8,128)(2,1)}, f32[896,...) custom-call(s32[1]{0:T(128)} %bitcast.refs_0_.choice_ref, ...), custom_call_target="tpu_custom_call", output_to_operand_aliasing={{0}: (13, {}), {1}: (14, {})} | custom-call | flops 5637144576 | bytes 5505024 | tf_op jit(solution)/shard_map/heads/pallas_call | solution.py:158
  75.0 4.7 %collective-permute-done.6.recv_ref = bf16[896,256]{1,0:T(8,128)(2,1)S(1)} collective-permute-done((bf16[896,256]{1,0:T(8,128)(2,1)S(1)}, bf16[896,256]{1,0:T(8,128)(2,1)S(1)}, u32[]{:S(2)}, u32[]{:S(2)}) %collective-permute-start.6) | collective-permute-done | bytes 458784 | tf_op jit(solution)/shard_map/ppermute | solution.py:23
  80.2 6.6 %heads.6 = (bf16[384,1024]{1,0:T(8,128)(2,1)}, bf16[384,1024]{1,0:T(8,128)(2,1)}, bf16[1536,256]{1,0:T(8,128)(2,1)}, bf16[1536,256]{1,0:T(8,128)(2,1)}, f32[896,...) custom-call(s32[1]{0:T(128)} %bitcast.refs_0_.choice_ref, ...), custom_call_target="tpu_custom_call", output_to_operand_aliasing={{0}: (13, {}), {1}: (14, {})} | custom-call | flops 5637144576 | bytes 5505024 | tf_op jit(solution)/shard_map/heads/pallas_call | solution.py:158
  88.8 2.8 %collective-permute-start.11 = (bf16[224,256]{1,0:T(8,128)(2,1)S(1)}, bf16[224,256]{1,0:T(8,128)(2,1)S(1)}, u32[]{:S(2)}, u32[]{:S(2)}) collective-permute-start(bf16[224,256]{1,0:T(8,128)(2,1)S(1)} %get-tuple-element.80.refs_0_), channel_id=1, source_target_pairs={{0,16},{4,20},{8,24},{12,28},{16,0},{20,4},{24,8},{28,12},{1,17},{... | collective-permute-start | bytes 344072 | tf_op jit(solution)/shard_map/ppermute | solution.py:23
  91.8 6.5 %heads.7 = (bf16[384,1024]{1,0:T(8,128)(2,1)}, bf16[384,1024]{1,0:T(8,128)(2,1)}, bf16[1536,256]{1,0:T(8,128)(2,1)}, bf16[1536,256]{1,0:T(8,128)(2,1)}, f32[896,...) custom-call(s32[1]{0:T(128)} %bitcast.refs_0_.choice_ref, ...), custom_call_target="tpu_custom_call", output_to_operand_aliasing={{0}: (13, {}), {1}: (14, {})} | custom-call | flops 5637144576 | bytes 5505024 | tf_op jit(solution)/shard_map/heads/pallas_call | solution.py:158
  99.1 2.2 %collective-permute-start.15 = (bf16[224,256]{1,0:T(8,128)(2,1)S(1)}, bf16[224,256]{1,0:T(8,128)(2,1)S(1)}, u32[]{:S(2)}, u32[]{:S(2)}) collective-permute-start(bf16[224,256]{1,0:T(8,128)(2,1)S(1)} %add.55.refs_0_.own_ref), channel_id=1, source_target_pairs={{0,16},{4,20},{8,24},{12,28},{16,0},{20,4},{24,8},{28,12},{1,17},{... | collective-permute-start | bytes 344072 | tf_op jit(solution)/shard_map/ppermute | solution.py:23
  103.8 10.1 %state_terms.1 = (bf16[768,896]{1,0:T(8,128)(2,1)S(1)}, bf16[768,896]{1,0:T(8,128)(2,1)S(1)}) custom-call(bf16[1536,256]{1,0:T(8,128)(2,1)} %get-tuple-element.84.refs_0_, bf16[1536,256]{1,0:T(8,128)(2,1)} %get-tuple-element.85.refs_1_, bf16[1536,256]{1,0:T(8,128)(2,1)} %get-tuple-element.86.refs_2_, bf16[1536,256]{1,0:T(8,128)(2,1)} %get-tuple-element.87.refs_3_, ...), custom_call_target="tpu_custom_call" | custom-call | flops 11274289152 | bytes 11010048 | tf_op jit(solution)/shard_map/state_terms/pallas_call | solution.py:245
  115.0 2.1 %collective-permute-start.19 = (bf16[224,256]{1,0:T(8,128)(2,1)S(1)}, bf16[224,256]{1,0:T(8,128)(2,1)S(1)}, u32[]{:S(2)}, u32[]{:S(2)}) collective-permute-start(bf16[224,256]{1,0:T(8,128)(2,1)S(1)} %add.56.refs_0_.own_ref), channel_id=1, source_target_pairs={{0,16},{4,20},{8,24},{12,28},{16,0},{20,4},{24,8},{28,12},{1,17},{... | collective-permute-start | bytes 344072 | tf_op jit(solution)/shard_map/ppermute | solution.py:23
  117.2 2.1 %collective-permute-start.18 = (bf16[224,256]{1,0:T(8,128)(2,1)S(1)}, bf16[224,256]{1,0:T(8,128)(2,1)S(1)}, u32[]{:S(2)}, u32[]{:S(2)}) collective-permute-start(bf16[224,256]{1,0:T(8,128)(2,1)S(1)} %get-tuple-element.104.refs_0_), channel_id=1, source_target_pairs={{0,16},{4,20},{8,24},{12,28},{16,0},{20,4},{24,8},{28,12},{1,17},{... | collective-permute-start | bytes 344072 | tf_op jit(solution)/shard_map/ppermute | solution.py:23
  119.3 8.4 %collective-permute-done.20.recv_ref = bf16[448,256]{1,0:T(8,128)(2,1)S(1)} collective-permute-done((bf16[448,256]{1,0:T(8,128)(2,1)S(1)}, bf16[448,256]{1,0:T(8,128)(2,1)S(1)}, u32[]{:S(2)}, u32[]{:S(2)}) %collective-permute-start.20) | collective-permute-done | bytes 229408 | tf_op jit(solution)/shard_map/ppermute | solution.py:23
  130.8 3.4 %collective-permute-start.23 = (bf16[224,256]{1,0:T(8,128)(2,1)S(1)}, bf16[224,256]{1,0:T(8,128)(2,1)S(1)}, u32[]{:S(2)}, u32[]{:S(2)}) collective-permute-start(bf16[224,256]{1,0:T(8,128)(2,1)S(1)} %add.57.refs_0_.own_ref), channel_id=1, source_target_pairs={{0,16},{4,20},{8,24},{12,28},{16,0},{20,4},{24,8},{28,12},{1,17},{... | collective-permute-start | bytes 344072 | tf_op jit(solution)/shard_map/ppermute | solution.py:23
  136.2 3.3 %collective-permute-done.24.recv_ref = bf16[448,256]{1,0:T(8,128)(2,1)S(1)} collective-permute-done((bf16[448,256]{1,0:T(8,128)(2,1)S(1)}, bf16[448,256]{1,0:T(8,128)(2,1)S(1)}, u32[]{:S(2)}, u32[]{:S(2)}) %collective-permute-start.24) | collective-permute-done | bytes 229408 | tf_op jit(solution)/shard_map/ppermute | solution.py:23
  143.8 4.2 %collective-permute-done.22.recv_ref = bf16[224,256]{1,0:T(8,128)(2,1)S(1)} collective-permute-done((bf16[224,256]{1,0:T(8,128)(2,1)S(1)}, bf16[224,256]{1,0:T(8,128)(2,1)S(1)}, u32[]{:S(2)}, u32[]{:S(2)}) %collective-permute-start.22) | collective-permute-done | bytes 114720 | tf_op jit(solution)/shard_map/ppermute | solution.py:23
  151.3 2.9 %collective-permute-start.25 = (bf16[224,256]{1,0:T(8,128)(2,1)S(1)}, bf16[224,256]{1,0:T(8,128)(2,1)S(1)}, u32[]{:S(2)}, u32[]{:S(2)}) collective-permute-start(bf16[224,256]{1,0:T(8,128)(2,1)S(1)} %add.58.refs_0_.own_ref), channel_id=1, source_target_pairs={{0,16},{4,20},{8,24},{12,28},{16,0},{20,4},{24,8},{28,12},{1,17},{... | collective-permute-start | bytes 344072 | tf_op jit(solution)/shard_map/ppermute | solution.py:23
  154.2 5.3 %collective-permute-done.25.recv_ref = bf16[224,256]{1,0:T(8,128)(2,1)S(1)} collective-permute-done((bf16[224,256]{1,0:T(8,128)(2,1)S(1)}, bf16[224,256]{1,0:T(8,128)(2,1)S(1)}, u32[]{:S(2)}, u32[]{:S(2)}) %collective-permute-start.25) | collective-permute-done | bytes 114720 | tf_op jit(solution)/shard_map/ppermute | solution.py:23
  165.6 3.9 %all-to-all-start.3 = ((bf16[8,2,32,896]{3,2,1,0:T(8,128)(2,1)}), bf16[8,2,32,896]{3,2,1,0:T(8,128)(2,1)S(1)}, u32[]{:S(2)}, u32[]{:S(2)}) async-start(bf16[8,2,32,896]{3,2,1,0:T(8,128)(2,1)} %bitcast.13.refs_2_), calls=%async_computation.3 | async-start | bytes 1835008 | tf_op jit(solution)/shard_map/all_to_all | solution.py:529
  171.6 18.3 %collective-permute-done.31.recv_ref = bf16[896,256]{1,0:T(8,128)(2,1)S(1)} collective-permute-done((bf16[896,256]{1,0:T(8,128)(2,1)S(1)}, bf16[896,256]{1,0:T(8,128)(2,1)S(1)}, u32[]{:S(2)}, u32[]{:S(2)}) %collective-permute-start.31) | collective-permute-done | bytes 458784 | tf_op jit(solution)/shard_map/ppermute | solution.py:23
  (108 shorter events, 42.7 us)
Async XLA Ops:
  33.6 16.2 %all-to-all-start.2 = ((bf16[8,2,16,896]{3,2,1,0:T(8,128)(2,1)}), bf16[8,2,16,896]{3,2,1,0:T(8,128)(2,1)S(1)}, u32[]{:S(2)}, u32[]{:S(2)}) async-start(bf16[8,2,16,896]{3,2,1,0:T(8,128)(2,1)} %bitcast.7), calls=%async_computation.2 | async-start | bytes 917504 | tf_op jit(solution)/shard_map/all_to_all | solution.py:479
  37.9 11.8 %collective-permute-start = (bf16[192,896]{1,0:T(8,128)(2,1)S(1)}, bf16[192,896]{1,0:T(8,128)(2,1)S(1)}, u32[]{:S(2)}, u32[]{:S(2)}) collective-permute-start(bf16[192,896]{1,0:T(8,128)(2,1)S(1)} %bitcast.21), channel_id=1, source_target_pairs={{0,2},{1,3},{2,0},{3,1},{4,6},{5,7},{6,4},{7,5},{8,10},{9,11},{10,... | collective-permute-start | bytes 1032200 | tf_op jit(solution)/shard_map/ppermute | solution.py:23
  65.8 14.0 %collective-permute-start.6 = (bf16[896,256]{1,0:T(8,128)(2,1)S(1)}, bf16[896,256]{1,0:T(8,128)(2,1)S(1)}, u32[]{:S(2)}, u32[]{:S(2)}) collective-permute-start(bf16[896,256]{1,0:T(8,128)(2,1)S(1)} %get-tuple-element.69.refs_15_), channel_id=1, source_target_pairs={{0,4},{4,0},{8,12},{12,8},{16,20},{20,16},{24,28},{28,24},{1,5},{5... | collective-permute-start | bytes 1376264 | tf_op jit(solution)/shard_map/ppermute | solution.py:23
  74.9 16.6 %collective-permute-start.7 = (bf16[896,256]{1,0:T(8,128)(2,1)S(1)}, bf16[896,256]{1,0:T(8,128)(2,1)S(1)}, u32[]{:S(2)}, u32[]{:S(2)}) collective-permute-start(bf16[896,256]{1,0:T(8,128)(2,1)S(1)} %get-tuple-element.73.refs_0_), channel_id=1, source_target_pairs={{0,4},{4,0},{8,12},{12,8},{16,20},{20,16},{24,28},{28,24},{1,5},{5... | collective-permute-start | bytes 1376264 | tf_op jit(solution)/shard_map/ppermute | solution.py:23
  86.8 15.4 %collective-permute-start.9 = (bf16[896,256]{1,0:T(8,128)(2,1)S(1)}, bf16[896,256]{1,0:T(8,128)(2,1)S(1)}, u32[]{:S(2)}, u32[]{:S(2)}) collective-permute-start(bf16[896,256]{1,0:T(8,128)(2,1)S(1)} %get-tuple-element.79.refs_0_), channel_id=1, source_target_pairs={{0,4},{4,0},{8,12},{12,8},{16,20},{20,16},{24,28},{28,24},{1,5},{5... | collective-permute-start | bytes 1376264 | tf_op jit(solution)/shard_map/ppermute | solution.py:23
  88.8 10.3 %collective-permute-start.11 = (bf16[224,256]{1,0:T(8,128)(2,1)S(1)}, bf16[224,256]{1,0:T(8,128)(2,1)S(1)}, u32[]{:S(2)}, u32[]{:S(2)}) collective-permute-start(bf16[224,256]{1,0:T(8,128)(2,1)S(1)} %get-tuple-element.80.refs_0_), channel_id=1, source_target_pairs={{0,16},{4,20},{8,24},{12,28},{16,0},{20,4},{24,8},{28,12},{1,17},{... | collective-permute-start | bytes 344072 | tf_op jit(solution)/shard_map/ppermute | solution.py:23
  91.7 9.6 %collective-permute-start.10 = (bf16[448,256]{1,0:T(8,128)(2,1)S(1)}, bf16[448,256]{1,0:T(8,128)(2,1)S(1)}, u32[]{:S(2)}, u32[]{:S(2)}) collective-permute-start(bf16[448,256]{1,0:T(8,128)(2,1)S(1)} %get-tuple-element.81.refs_15_), channel_id=1, source_target_pairs={{0,8},{4,12},{8,0},{12,4},{16,24},{20,28},{24,16},{28,20},{1,9},{5... | collective-permute-start | bytes 688136 | tf_op jit(solution)/shard_map/ppermute | solution.py:23
  98.3 15.7 %collective-permute-start.14 = (bf16[896,256]{1,0:T(8,128)(2,1)S(1)}, bf16[896,256]{1,0:T(8,128)(2,1)S(1)}, u32[]{:S(2)}, u32[]{:S(2)}) collective-permute-start(bf16[896,256]{1,0:T(8,128)(2,1)S(1)} %get-tuple-element.95.refs_0_), channel_id=1, source_target_pairs={{0,4},{4,0},{8,12},{12,8},{16,20},{20,16},{24,28},{28,24},{1,5},{5... | collective-permute-start | bytes 1376264 | tf_op jit(solution)/shard_map/ppermute | solution.py:23
  99.1 14.8 %collective-permute-start.15 = (bf16[224,256]{1,0:T(8,128)(2,1)S(1)}, bf16[224,256]{1,0:T(8,128)(2,1)S(1)}, u32[]{:S(2)}, u32[]{:S(2)}) collective-permute-start(bf16[224,256]{1,0:T(8,128)(2,1)S(1)} %add.55.refs_0_.own_ref), channel_id=1, source_target_pairs={{0,16},{4,20},{8,24},{12,28},{16,0},{20,4},{24,8},{28,12},{1,17},{... | collective-permute-start | bytes 344072 | tf_op jit(solution)/shard_map/ppermute | solution.py:23
  101.3 12.8 %collective-permute-start.12 = (bf16[224,256]{1,0:T(8,128)(2,1)S(1)}, bf16[224,256]{1,0:T(8,128)(2,1)S(1)}, u32[]{:S(2)}, u32[]{:S(2)}) collective-permute-start(bf16[224,256]{1,0:T(8,128)(2,1)S(1)} %get-tuple-element.96.refs_0_), channel_id=1, source_target_pairs={{0,16},{4,20},{8,24},{12,28},{16,0},{20,4},{24,8},{28,12},{1,17},{... | collective-permute-start | bytes 344072 | tf_op jit(solution)/shard_map/ppermute | solution.py:23
  102.3 11.8 %collective-permute-start.13 = (bf16[448,256]{1,0:T(8,128)(2,1)S(1)}, bf16[448,256]{1,0:T(8,128)(2,1)S(1)}, u32[]{:S(2)}, u32[]{:S(2)}) collective-permute-start(bf16[448,256]{1,0:T(8,128)(2,1)S(1)} %get-tuple-element.97.refs_10_), channel_id=1, source_target_pairs={{0,8},{4,12},{8,0},{12,4},{16,24},{20,28},{24,16},{28,20},{1,9},{5... | collective-permute-start | bytes 688136 | tf_op jit(solution)/shard_map/ppermute | solution.py:23
  114.2 20.2 %collective-permute-start.16 = (bf16[768,896]{1,0:T(8,128)(2,1)S(1)}, bf16[768,896]{1,0:T(8,128)(2,1)S(1)}, u32[]{:S(2)}, u32[]{:S(2)}) collective-permute-start(bf16[768,896]{1,0:T(8,128)(2,1)S(1)} %get-tuple-element.105.refs_0_), channel_id=1, source_target_pairs={{0,1},{1,0},{2,3},{3,2},{4,5},{5,4},{6,7},{7,6},{8,9},{9,8},{10,11... | collective-permute-start | bytes 4128776 | tf_op jit(solution)/shard_map/ppermute | solution.py:23
  114.3 13.4 %collective-permute-start.20 = (bf16[448,256]{1,0:T(8,128)(2,1)S(1)}, bf16[448,256]{1,0:T(8,128)(2,1)S(1)}, u32[]{:S(2)}, u32[]{:S(2)}) collective-permute-start(bf16[448,256]{1,0:T(8,128)(2,1)S(1)} %join.8.refs_0_.own_ref), channel_id=1, source_target_pairs={{0,8},{4,12},{8,0},{12,4},{16,24},{20,28},{24,16},{28,20},{1,9},{5... | collective-permute-start | bytes 688136 | tf_op jit(solution)/shard_map/ppermute | solution.py:23
  115.0 12.7 %collective-permute-start.19 = (bf16[224,256]{1,0:T(8,128)(2,1)S(1)}, bf16[224,256]{1,0:T(8,128)(2,1)S(1)}, u32[]{:S(2)}, u32[]{:S(2)}) collective-permute-start(bf16[224,256]{1,0:T(8,128)(2,1)S(1)} %add.56.refs_0_.own_ref), channel_id=1, source_target_pairs={{0,16},{4,20},{8,24},{12,28},{16,0},{20,4},{24,8},{28,12},{1,17},{... | collective-permute-start | bytes 344072 | tf_op jit(solution)/shard_map/ppermute | solution.py:23
  117.1 17.2 %collective-permute-start.17 = (bf16[448,256]{1,0:T(8,128)(2,1)S(1)}, bf16[448,256]{1,0:T(8,128)(2,1)S(1)}, u32[]{:S(2)}, u32[]{:S(2)}) collective-permute-start(bf16[448,256]{1,0:T(8,128)(2,1)S(1)} %get-tuple-element.103.refs_0_), channel_id=1, source_target_pairs={{0,8},{4,12},{8,0},{12,4},{16,24},{20,28},{24,16},{28,20},{1,9},{5... | collective-permute-start | bytes 688136 | tf_op jit(solution)/shard_map/ppermute | solution.py:23
  117.2 13.6 %collective-permute-start.18 = (bf16[224,256]{1,0:T(8,128)(2,1)S(1)}, bf16[224,256]{1,0:T(8,128)(2,1)S(1)}, u32[]{:S(2)}, u32[]{:S(2)}) collective-permute-start(bf16[224,256]{1,0:T(8,128)(2,1)S(1)} %get-tuple-element.104.refs_0_), channel_id=1, source_target_pairs={{0,16},{4,20},{8,24},{12,28},{16,0},{20,4},{24,8},{28,12},{1,17},{... | collective-permute-start | bytes 344072 | tf_op jit(solution)/shard_map/ppermute | solution.py:23
  127.8 11.8 %collective-permute-start.24 = (bf16[448,256]{1,0:T(8,128)(2,1)S(1)}, bf16[448,256]{1,0:T(8,128)(2,1)S(1)}, u32[]{:S(2)}, u32[]{:S(2)}) collective-permute-start(bf16[448,256]{1,0:T(8,128)(2,1)S(1)} %join.10.refs_0_.own_ref), channel_id=1, source_target_pairs={{0,8},{4,12},{8,0},{12,4},{16,24},{20,28},{24,16},{28,20},{1,9},{5... | collective-permute-start | bytes 688136 | tf_op jit(solution)/shard_map/ppermute | solution.py:23
  127.8 20.2 %collective-permute-start.27 = (bf16[896,256]{1,0:T(8,128)(2,1)S(1)}, bf16[896,256]{1,0:T(8,128)(2,1)S(1)}, u32[]{:S(2)}, u32[]{:S(2)}) collective-permute-start(bf16[896,256]{1,0:T(8,128)(2,1)S(1)} %join.9.refs_0_.own_ref), channel_id=1, source_target_pairs={{0,4},{4,0},{8,12},{12,8},{16,20},{20,16},{24,28},{28,24},{1,5},{5... | collective-permute-start | bytes 1376264 | tf_op jit(solution)/shard_map/ppermute | solution.py:23
  134.7 25.3 %collective-permute-start.21 = (bf16[384,896]{1,0:T(8,128)(2,1)S(1)}, bf16[384,896]{1,0:T(8,128)(2,1)S(1)}, u32[]{:S(2)}, u32[]{:S(2)}) collective-permute-start(bf16[384,896]{1,0:T(8,128)(2,1)S(1)} %get-tuple-element.110.refs_0_), channel_id=1, source_target_pairs={{0,2},{1,3},{2,0},{3,1},{4,6},{5,7},{6,4},{7,5},{8,10},{9,11},{10,... | collective-permute-start | bytes 2064392 | tf_op jit(solution)/shard_map/ppermute | solution.py:23
  139.6 9.8 %collective-permute-start.26 = (bf16[448,256]{1,0:T(8,128)(2,1)S(1)}, bf16[448,256]{1,0:T(8,128)(2,1)S(1)}, u32[]{:S(2)}, u32[]{:S(2)}) collective-permute-start(bf16[448,256]{1,0:T(8,128)(2,1)S(1)} %join.12.refs_0_.own_ref), channel_id=1, source_target_pairs={{0,8},{4,12},{8,0},{12,4},{16,24},{20,28},{24,16},{28,20},{1,9},{5... | collective-permute-start | bytes 688136 | tf_op jit(solution)/shard_map/ppermute | solution.py:23
  142.4 19.3 %collective-permute-start.30 = (bf16[896,256]{1,0:T(8,128)(2,1)S(1)}, bf16[896,256]{1,0:T(8,128)(2,1)S(1)}, u32[]{:S(2)}, u32[]{:S(2)}) collective-permute-start(bf16[896,256]{1,0:T(8,128)(2,1)S(1)} %join.11.refs_0_.own_ref), channel_id=1, source_target_pairs={{0,4},{4,0},{8,12},{12,8},{16,20},{20,16},{24,28},{28,24},{1,5},{5... | collective-permute-start | bytes 1376264 | tf_op jit(solution)/shard_map/ppermute | solution.py:23
  149.5 14.3 %collective-permute-start.29 = (bf16[896,256]{1,0:T(8,128)(2,1)S(1)}, bf16[896,256]{1,0:T(8,128)(2,1)S(1)}, u32[]{:S(2)}, u32[]{:S(2)}) collective-permute-start(bf16[896,256]{1,0:T(8,128)(2,1)S(1)} %join.13.refs_0_.own_ref), channel_id=1, source_target_pairs={{0,4},{4,0},{8,12},{12,8},{16,20},{20,16},{24,28},{28,24},{1,5},{5... | collective-permute-start | bytes 1376264 | tf_op jit(solution)/shard_map/ppermute | solution.py:23
  165.6 25.6 %all-to-all-start.3 = ((bf16[8,2,32,896]{3,2,1,0:T(8,128)(2,1)}), bf16[8,2,32,896]{3,2,1,0:T(8,128)(2,1)S(1)}, u32[]{:S(2)}, u32[]{:S(2)}) async-start(bf16[8,2,32,896]{3,2,1,0:T(8,128)(2,1)} %bitcast.13.refs_2_), calls=%async_computation.3 | async-start | bytes 1835008 | tf_op jit(solution)/shard_map/all_to_all | solution.py:529
  169.5 20.4 %collective-permute-start.31 = (bf16[896,256]{1,0:T(8,128)(2,1)S(1)}, bf16[896,256]{1,0:T(8,128)(2,1)S(1)}, u32[]{:S(2)}, u32[]{:S(2)}) collective-permute-start(bf16[896,256]{1,0:T(8,128)(2,1)S(1)} %join.15.own_ref.refs_2_), channel_id=1, source_target_pairs={{0,4},{4,0},{8,12},{12,8},{16,20},{20,16},{24,28},{28,24},{1,5},{5... | collective-permute-start | bytes 1376264 | tf_op jit(solution)/shard_map/ppermute | solution.py:23
  (12 other events, 118.3 us)

commit v8 on v7

--- a/solution.py
+++ b/solution.py
@@ -492,6 +492,8 @@
 
     heads = local_width // head_dim
     counts = [min(2, heads - first) for first in range(0, heads, 2)]
+    if len(counts) > 2 and counts[-1] == 2:
+        counts[-1:] = [1, 1]
     bits = list(range(dp_bits))
     choices = [((dp_index >> bit) & 1).astype(jnp.int32).reshape(1) for bit in bits]
     sums = []

time: 194 us -> 221 us (1.14)
  local copies, waits for them, and re-layouts: 6.28 us -> 21.5 us
  waiting for transfers between devices: 63.5 us -> 52.3 us
  starting transfers between devices: 47.7 us -> 58.3 us
  Pallas kernels: 44.9 us -> 55 us
    unnamed x5 -> x55, local copies, waits for them, and re-layouts: 0.78 us -> 16.1 us
    ppermute x32 -> x38, waiting for transfers between devices: 53.2 us -> 38.2 us  [swap(): return lax.ppermute(value, axis, [(i, i ^ 1 << bit) for i in range(count)])]
    all_to_all x1, starting transfers between devices: 3.86 us -> 9.58 us  [body(): lax.all_to_all(outgoing, 'dp', split_axis=0, concat_axis=0, tiled=True)]
    pallas_call x4 -> x5, Pallas kernels: 26 us -> 31.6 us  [run_heads(): pl.pallas_call(functools.partial(head_kernel, groups, spans, head_dim, st...]
    ppermute x32 -> x38, starting transfers between devices: 40.3 us -> 45.2 us  [swap(): return lax.ppermute(value, axis, [(i, i ^ 1 << bit) for i in range(count)])]
    pallas_call x27 -> x33, Pallas kernels: 8.8 us -> 13.1 us  [small(): pl.pallas_call(kernel, out_shape=outs, in_specs=[pl.BlockSpec(memory_spac...]
    all_to_all x1, waiting for transfers between devices: 0.01 us -> 3.89 us  [body(): lax.all_to_all(outgoing, 'dp', split_axis=0, concat_axis=0, tiled=True)]
  transfers between devices with their start and end apart: 34 -> 40, of which waited for: 12 -> 11; matrix products, arithmetic and copies ran while one was open for 1% -> 1% of each run, Pallas kernels for 19% -> 21%
where the time goes in v8:
time: 221 us; the launch traced here: 219 us
  starting transfers between devices  58.3 us (26%)
  Pallas kernels  55 us (25%)
  waiting for transfers between devices  52.3 us (24%)
  blocking collectives  28 us (13%)
  local copies, waits for them, and re-layouts  21.5 us (10%)
  other arithmetic  2.87 us (1%)
    ppermute x38, starting transfers between devices, swap(): return lax.ppermute(value, axis, [(i, i ^ 1 << bit) for i in range(count)])  45.2 us
    ppermute x38, waiting for transfers between devices, swap(): return lax.ppermute(value, axis, [(i, i ^ 1 << bit) for i in range(count)])  38.2 us
    pallas_call x5, Pallas kernels, run_heads(): pl.pallas_call(functools.partial(head_kernel, groups, spans, head_dim, st...  31.6 us
    unnamed x55, local copies, waits for them, and re-layouts  16.1 us
    all_to_all x1, blocking collectives, body(): lax.all_to_all(out, 'dp', split_axis=0, concat_axis=0, tiled=True)  14.4 us
    all_to_all x1, blocking collectives, body(): lax.all_to_all(asked.reshape(shards, capacity), 'dp', split_axis=0, conca...  13.5 us
    pallas_call x33, Pallas kernels, small(): pl.pallas_call(kernel, out_shape=outs, in_specs=[pl.BlockSpec(memory_spac...  13.1 us
    all_to_all x1, waiting for transfers between devices, body(): lax.all_to_all(out, 'dp', split_axis=0, concat_axis=0, tiled=True)  10.3 us
  transfers between devices with their start and end apart: 40, of which 11 were waited for; matrix products, arithmetic and copies ran while one was open for 1% of the time, Pallas kernels for 21%

profile of v8, /device:TPU:0, one launch (start us, length us, event | category | flops | bytes accessed | tf_op | source)
XLA Modules:
  0.0 219.4 jit_solution(857587974708850474)
XLA Ops:
  3.4 13.5 %all_to_all.21 = s32[8,1,2]{2,1,0:T(1,128)S(1)} all-to-all(s32[8,1,2]{2,1,0:T(1,128)S(1)} %bitcast.38), channel_id=1, replica_groups=mesh['dp'=8,'mp'=4] {'dp'}, dimensions={0} | all-to-all | bytes 128 | tf_op jit(solution)/shard_map/all_to_all | solution.py:470
  20.3 14.4 %all_to_all.22 = bf16[8,2,16,896]{3,2,1,0:T(8,128)(2,1)S(1)} all-to-all(bf16[8,2,16,896]{3,2,1,0:T(8,128)(2,1)S(1)} %bitcast.35), channel_id=1, replica_groups=mesh['dp'=8,'mp'=4] {'dp'}, dimensions={0} | all-to-all | bytes 917504 | tf_op jit(solution)/shard_map/all_to_all | solution.py:479
  34.7 3.5 %all-to-all-start.2 = ((bf16[8,2,16,896]{3,2,1,0:T(8,128)(2,1)}), bf16[8,2,16,896]{3,2,1,0:T(8,128)(2,1)S(1)}, u32[]{:S(2)}, u32[]{:S(2)}) async-start(bf16[8,2,16,896]{3,2,1,0:T(8,128)(2,1)} %bitcast.7), calls=%async_computation.2 | async-start | bytes 917504 | tf_op jit(solution)/shard_map/all_to_all | solution.py:479
  40.6 10.3 %all-to-all-done.2 = bf16[8,2,16,896]{3,2,1,0:T(8,128)(2,1)S(1)} async-done(((bf16[8,2,16,896]{3,2,1,0:T(8,128)(2,1)}), bf16[8,2,16,896]{3,2,1,0:T(8,128)(2,1)S(1)}, u32[]{:S(2)}, u32[]{:S(2)}) %all-to-all-start.2) | async-done | bytes 458784 | tf_op jit(solution)/shard_map/all_to_all | solution.py:479
  53.6 5.2 %collective-permute-done.3.refs_6_ = bf16[192,896]{1,0:T(8,128)(2,1)S(1)} collective-permute-done((bf16[192,896]{1,0:T(8,128)(2,1)S(1)}, bf16[192,896]{1,0:T(8,128)(2,1)S(1)}, u32[]{:S(2)}, u32[]{:S(2)}) %collective-permute-start.3) | collective-permute-done | bytes 344096 | tf_op jit(solution)/shard_map/ppermute | solution.py:23
  63.2 6.5 %heads.5 = (bf16[384,1024]{1,0:T(8,128)(2,1)}, bf16[384,1024]{1,0:T(8,128)(2,1)}, bf16[1536,256]{1,0:T(8,128)(2,1)}, bf16[1536,256]{1,0:T(8,128)(2,1)}, f32[896,...) custom-call(s32[1]{0:T(128)} %bitcast.refs_0_.choice_ref, bf16[192,896]{1,0:T(8,128)(2,1)S(1)} %bitcast.23, ...), custom_call_target="tpu_custom_call" | custom-call | flops 5637144576 | bytes 5505024 | tf_op jit(solution)/shard_map/heads/pallas_call | solution.py:158
  69.8 2.7 %collective-permute-start.6 = (bf16[896,256]{1,0:T(8,128)(2,1)S(1)}, bf16[896,256]{1,0:T(8,128)(2,1)S(1)}, u32[]{:S(2)}, u32[]{:S(2)}) collective-permute-start(bf16[896,256]{1,0:T(8,128)(2,1)S(1)} %get-tuple-element.82.refs_15_), channel_id=1, source_target_pairs={{0,4},{4,0},{8,12},{12,8},{16,20},{20,16},{24,28},{28,24},{1,5},{5... | collective-permute-start | bytes 1376264 | tf_op jit(solution)/shard_map/ppermute | solution.py:23
  76.4 7.3 %heads.6 = (bf16[384,1024]{1,0:T(8,128)(2,1)}, bf16[384,1024]{1,0:T(8,128)(2,1)}, bf16[1536,256]{1,0:T(8,128)(2,1)}, bf16[1536,256]{1,0:T(8,128)(2,1)}, f32[896,...) custom-call(s32[1]{0:T(128)} %bitcast.refs_0_.choice_ref, ...), custom_call_target="tpu_custom_call", output_to_operand_aliasing={{0}: (13, {}), {1}: (14, {})} | custom-call | flops 5637144576 | bytes 5505024 | tf_op jit(solution)/shard_map/heads/pallas_call | solution.py:158
  85.7 6.6 %heads.7 = (bf16[384,1024]{1,0:T(8,128)(2,1)}, bf16[384,1024]{1,0:T(8,128)(2,1)}, bf16[1536,256]{1,0:T(8,128)(2,1)}, bf16[1536,256]{1,0:T(8,128)(2,1)}, f32[896,...) custom-call(s32[1]{0:T(128)} %bitcast.refs_0_.choice_ref, ...), custom_call_target="tpu_custom_call", output_to_operand_aliasing={{0}: (13, {}), {1}: (14, {})} | custom-call | flops 5637144576 | bytes 5505024 | tf_op jit(solution)/shard_map/heads/pallas_call | solution.py:158
  95.2 2.8 %collective-permute-start.11 = (bf16[224,256]{1,0:T(8,128)(2,1)S(1)}, bf16[224,256]{1,0:T(8,128)(2,1)S(1)}, u32[]{:S(2)}, u32[]{:S(2)}) collective-permute-start(bf16[224,256]{1,0:T(8,128)(2,1)S(1)} %get-tuple-element.93.refs_0_), channel_id=1, source_target_pairs={{0,16},{4,20},{8,24},{12,28},{16,0},{20,4},{24,8},{28,12},{1,17},{... | collective-permute-start | bytes 344072 | tf_op jit(solution)/shard_map/ppermute | solution.py:23
  106.1 5.5 %heads.8 = (bf16[384,1024]{1,0:T(8,128)(2,1)}, bf16[384,1024]{1,0:T(8,128)(2,1)}, bf16[1536,128]{1,0:T(8,128)(2,1)}, bf16[1536,128]{1,0:T(8,128)(2,1)}, f32[896,...) custom-call(s32[1]{0:T(128)} %bitcast.refs_0_.choice_ref, ...), custom_call_target="tpu_custom_call", output_to_operand_aliasing={{0}: (13, {}), {1}: (14, {})} | custom-call | flops 2818572288 | bytes 5505024 | tf_op jit(solution)/shard_map/heads/pallas_call | solution.py:158
  118.1 5.7 %heads.9 = (bf16[384,1024]{1,0:T(8,128)(2,1)}, bf16[384,1024]{1,0:T(8,128)(2,1)}, bf16[1536,128]{1,0:T(8,128)(2,1)}, bf16[1536,128]{1,0:T(8,128)(2,1)}, f32[896,...) custom-call(s32[1]{0:T(128)} %bitcast.refs_0_.choice_ref, ...), custom_call_target="tpu_custom_call", output_to_operand_aliasing={{0}: (13, {}), {1}: (14, {})} | custom-call | flops 2818572288 | bytes 5505024 | tf_op jit(solution)/shard_map/heads/pallas_call | solution.py:158
  131.3 10.2 %state_terms.1 = (bf16[768,896]{1,0:T(8,128)(2,1)S(1)}, bf16[768,896]{1,0:T(8,128)(2,1)S(1)}) custom-call(bf16[1536,256]{1,0:T(8,128)(2,1)} %get-tuple-element.105.refs_0_, bf16[1536,256]{1,0:T(8,128)(2,1)} %get-tuple-element.106.refs_1_, bf16[1536,256]{1,0:T(8,128)(2,1)} %get-tuple-element.107.refs_2_, bf16[1536,128]{1,0:T(8,128)(2,1)} %get-tuple-element.108.refs_3_, ...), custom_call_target="tpu_custom_call" | custom-call | flops 11274289152 | bytes 11010048 | tf_op jit(solution)/shard_map/state_terms/pallas_call | solution.py:245
  143.4 2.9 %collective-permute-start.24 = (bf16[224,256]{1,0:T(8,128)(2,1)S(1)}, bf16[224,256]{1,0:T(8,128)(2,1)S(1)}, u32[]{:S(2)}, u32[]{:S(2)}) collective-permute-start(bf16[224,256]{1,0:T(8,128)(2,1)S(1)} %add.58.refs_0_.own_ref), channel_id=1, source_target_pairs={{0,16},{4,20},{8,24},{12,28},{16,0},{20,4},{24,8},{28,12},{1,17},{... | collective-permute-start | bytes 344072 | tf_op jit(solution)/shard_map/ppermute | solution.py:23
  146.4 6.4 %collective-permute-done.25.recv_ref = bf16[448,256]{1,0:T(8,128)(2,1)S(1)} collective-permute-done((bf16[448,256]{1,0:T(8,128)(2,1)S(1)}, bf16[448,256]{1,0:T(8,128)(2,1)S(1)}, u32[]{:S(2)}, u32[]{:S(2)}) %collective-permute-start.25) | collective-permute-done | bytes 229408 | tf_op jit(solution)/shard_map/ppermute | solution.py:23
  152.9 5.0 %collective-permute-done.23.recv_ref = bf16[224,128]{1,0:T(8,128)(2,1)S(1)} collective-permute-done((bf16[224,128]{1,0:T(8,128)(2,1)S(1)}, bf16[224,128]{1,0:T(8,128)(2,1)S(1)}, u32[]{:S(2)}, u32[]{:S(2)}) %collective-permute-start.23) | collective-permute-done | bytes 57376 | tf_op jit(solution)/shard_map/ppermute | solution.py:23
  162.7 3.1 %collective-permute-done.29.recv_ref = bf16[448,256]{1,0:T(8,128)(2,1)S(1)} collective-permute-done((bf16[448,256]{1,0:T(8,128)(2,1)S(1)}, bf16[448,256]{1,0:T(8,128)(2,1)S(1)}, u32[]{:S(2)}, u32[]{:S(2)}) %collective-permute-start.29) | collective-permute-done | bytes 229408 | tf_op jit(solution)/shard_map/ppermute | solution.py:23
  168.3 5.0 %collective-permute-done.28.recv_ref = bf16[224,128]{1,0:T(8,128)(2,1)S(1)} collective-permute-done((bf16[224,128]{1,0:T(8,128)(2,1)S(1)}, bf16[224,128]{1,0:T(8,128)(2,1)S(1)}, u32[]{:S(2)}, u32[]{:S(2)}) %collective-permute-start.28) | collective-permute-done | bytes 57376 | tf_op jit(solution)/shard_map/ppermute | solution.py:23
  173.4 3.6 %collective-permute-start.27 = (bf16[224,128]{1,0:T(8,128)(2,1)S(1)}, bf16[224,128]{1,0:T(8,128)(2,1)S(1)}, u32[]{:S(2)}, u32[]{:S(2)}) collective-permute-start(bf16[224,128]{1,0:T(8,128)(2,1)S(1)} %get-tuple-element.131.refs_0_), channel_id=1, source_target_pairs={{0,16},{4,20},{8,24},{12,28},{16,0},{20,4},{24,8},{28,12},{1,17},{... | collective-permute-start | bytes 172040 | tf_op jit(solution)/shard_map/ppermute | solution.py:23
  181.4 2.5 %collective-permute-start.31 = (bf16[224,128]{1,0:T(8,128)(2,1)S(1)}, bf16[224,128]{1,0:T(8,128)(2,1)S(1)}, u32[]{:S(2)}, u32[]{:S(2)}) collective-permute-start(bf16[224,128]{1,0:T(8,128)(2,1)S(1)} %add.60.refs_2_.own_ref), channel_id=1, source_target_pairs={{0,16},{4,20},{8,24},{12,28},{16,0},{20,4},{24,8},{28,12},{1,17},{... | collective-permute-start | bytes 172040 | tf_op jit(solution)/shard_map/ppermute | solution.py:23
  183.9 2.6 %collective-permute-done.31.recv_ref = bf16[224,128]{1,0:T(8,128)(2,1)S(1)} collective-permute-done((bf16[224,128]{1,0:T(8,128)(2,1)S(1)}, bf16[224,128]{1,0:T(8,128)(2,1)S(1)}, u32[]{:S(2)}, u32[]{:S(2)}) %collective-permute-start.31) | collective-permute-done | bytes 57376 | tf_op jit(solution)/shard_map/ppermute | solution.py:23
  193.1 9.6 %all-to-all-start.3 = ((bf16[8,2,32,896]{3,2,1,0:T(8,128)(2,1)}), bf16[8,2,32,896]{3,2,1,0:T(8,128)(2,1)S(1)}, u32[]{:S(2)}, u32[]{:S(2)}) async-start(bf16[8,2,32,896]{3,2,1,0:T(8,128)(2,1)} %bitcast.13.refs_2_), calls=%async_computation.3 | async-start | bytes 1835008 | tf_op jit(solution)/shard_map/all_to_all | solution.py:531
  204.8 7.8 %collective-permute-done.37.recv_ref = bf16[896,128]{1,0:T(8,128)(2,1)S(1)} collective-permute-done((bf16[896,128]{1,0:T(8,128)(2,1)S(1)}, bf16[896,128]{1,0:T(8,128)(2,1)S(1)}, u32[]{:S(2)}, u32[]{:S(2)}) %collective-permute-start.37) | collective-permute-done | bytes 229408 | tf_op jit(solution)/shard_map/ppermute | solution.py:23
  213.6 3.9 %all-to-all-done.3 = bf16[8,2,32,896]{3,2,1,0:T(8,128)(2,1)S(1)} async-done(((bf16[8,2,32,896]{3,2,1,0:T(8,128)(2,1)}), bf16[8,2,32,896]{3,2,1,0:T(8,128)(2,1)S(1)}, u32[]{:S(2)}, u32[]{:S(2)}) %all-to-all-start.3) | async-done | bytes 917536 | tf_op jit(solution)/shard_map/all_to_all | solution.py:531
  (177 shorter events, 71.4 us)
Async XLA Ops:
  34.7 16.2 %all-to-all-start.2 = ((bf16[8,2,16,896]{3,2,1,0:T(8,128)(2,1)}), bf16[8,2,16,896]{3,2,1,0:T(8,128)(2,1)S(1)}, u32[]{:S(2)}, u32[]{:S(2)}) async-start(bf16[8,2,16,896]{3,2,1,0:T(8,128)(2,1)} %bitcast.7), calls=%async_computation.2 | async-start | bytes 917504 | tf_op jit(solution)/shard_map/all_to_all | solution.py:479
  39.1 11.8 %collective-permute-start = (bf16[192,896]{1,0:T(8,128)(2,1)S(1)}, bf16[192,896]{1,0:T(8,128)(2,1)S(1)}, u32[]{:S(2)}, u32[]{:S(2)}) collective-permute-start(bf16[192,896]{1,0:T(8,128)(2,1)S(1)} %bitcast.21), channel_id=1, source_target_pairs={{0,2},{1,3},{2,0},{3,1},{4,6},{5,7},{6,4},{7,5},{8,10},{9,11},{10,... | collective-permute-start | bytes 1032200 | tf_op jit(solution)/shard_map/ppermute | solution.py:23
  69.8 14.0 %collective-permute-start.6 = (bf16[896,256]{1,0:T(8,128)(2,1)S(1)}, bf16[896,256]{1,0:T(8,128)(2,1)S(1)}, u32[]{:S(2)}, u32[]{:S(2)}) collective-permute-start(bf16[896,256]{1,0:T(8,128)(2,1)S(1)} %get-tuple-element.82.refs_15_), channel_id=1, source_target_pairs={{0,4},{4,0},{8,12},{12,8},{16,20},{20,16},{24,28},{28,24},{1,5},{5... | collective-permute-start | bytes 1376264 | tf_op jit(solution)/shard_map/ppermute | solution.py:23
  83.6 14.4 %collective-permute-start.7 = (bf16[896,256]{1,0:T(8,128)(2,1)}, bf16[896,256]{1,0:T(8,128)(2,1)}, u32[]{:S(2)}, u32[]{:S(2)}) collective-permute-start(bf16[896,256]{1,0:T(8,128)(2,1)} %get-tuple-element.86.refs_0_), channel_id=1, source_target_pairs={{0,4},{4,0},{8,12},{12,8},{16,20},{20,16},{24,28},{28,24},{1,5},{5... | collective-permute-start | bytes 1376264 | tf_op jit(solution)/shard_map/ppermute | solution.py:23
  92.3 23.3 %collective-permute-start.9 = (bf16[896,256]{1,0:T(8,128)(2,1)S(1)}, bf16[896,256]{1,0:T(8,128)(2,1)}, u32[]{:S(2)}, u32[]{:S(2)}) collective-permute-start(bf16[896,256]{1,0:T(8,128)(2,1)S(1)} %get-tuple-element.92.refs_0_), channel_id=1, source_target_pairs={{0,4},{4,0},{8,12},{12,8},{16,20},{20,16},{24,28},{28,24},{1,5},{5... | collective-permute-start | bytes 1376264 | tf_op jit(solution)/shard_map/ppermute | solution.py:23
  95.2 17.2 %collective-permute-start.11 = (bf16[224,256]{1,0:T(8,128)(2,1)S(1)}, bf16[224,256]{1,0:T(8,128)(2,1)S(1)}, u32[]{:S(2)}, u32[]{:S(2)}) collective-permute-start(bf16[224,256]{1,0:T(8,128)(2,1)S(1)} %get-tuple-element.93.refs_0_), channel_id=1, source_target_pairs={{0,16},{4,20},{8,24},{12,28},{16,0},{20,4},{24,8},{28,12},{1,17},{... | collective-permute-start | bytes 344072 | tf_op jit(solution)/shard_map/ppermute | solution.py:23
  99.1 14.8 %collective-permute-start.10 = (bf16[448,256]{1,0:T(8,128)(2,1)S(1)}, bf16[448,256]{1,0:T(8,128)(2,1)S(1)}, u32[]{:S(2)}, u32[]{:S(2)}) collective-permute-start(bf16[448,256]{1,0:T(8,128)(2,1)S(1)} %get-tuple-element.94.refs_15_), channel_id=1, source_target_pairs={{0,8},{4,12},{8,0},{12,4},{16,24},{20,28},{24,16},{28,20},{1,9},{5... | collective-permute-start | bytes 688136 | tf_op jit(solution)/shard_map/ppermute | solution.py:23
  111.6 17.6 %collective-permute-start.12 = (bf16[896,128]{1,0:T(8,128)(2,1)S(1)}, bf16[896,128]{1,0:T(8,128)(2,1)S(1)}, u32[]{:S(2)}, u32[]{:S(2)}) collective-permute-start(bf16[896,128]{1,0:T(8,128)(2,1)S(1)} %get-tuple-element.100.refs_0_), channel_id=1, source_target_pairs={{0,4},{4,0},{8,12},{12,8},{16,20},{20,16},{24,28},{28,24},{1,5},{5... | collective-permute-start | bytes 688136 | tf_op jit(solution)/shard_map/ppermute | solution.py:23
  112.4 13.4 %collective-permute-start.15 = (bf16[224,256]{1,0:T(8,128)(2,1)S(1)}, bf16[224,256]{1,0:T(8,128)(2,1)S(1)}, u32[]{:S(2)}, u32[]{:S(2)}) collective-permute-start(bf16[224,256]{1,0:T(8,128)(2,1)S(1)} %add.56.refs_0_.own_ref), channel_id=1, source_target_pairs={{0,16},{4,20},{8,24},{12,28},{16,0},{20,4},{24,8},{28,12},{1,17},{... | collective-permute-start | bytes 344072 | tf_op jit(solution)/shard_map/ppermute | solution.py:23
  114.0 12.0 %collective-permute-start.14 = (bf16[224,256]{1,0:T(8,128)(2,1)S(1)}, bf16[224,256]{1,0:T(8,128)(2,1)S(1)}, u32[]{:S(2)}, u32[]{:S(2)}) collective-permute-start(bf16[224,256]{1,0:T(8,128)(2,1)S(1)} %get-tuple-element.101.refs_0_), channel_id=1, source_target_pairs={{0,16},{4,20},{8,24},{12,28},{16,0},{20,4},{24,8},{28,12},{1,17},{... | collective-permute-start | bytes 344072 | tf_op jit(solution)/shard_map/ppermute | solution.py:23
  116.7 11.6 %collective-permute-start.13 = (bf16[448,256]{1,0:T(8,128)(2,1)S(1)}, bf16[448,256]{1,0:T(8,128)(2,1)S(1)}, u32[]{:S(2)}, u32[]{:S(2)}) collective-permute-start(bf16[448,256]{1,0:T(8,128)(2,1)S(1)} %get-tuple-element.102.refs_15_), channel_id=1, source_target_pairs={{0,8},{4,12},{8,0},{12,4},{16,24},{20,28},{24,16},{28,20},{1,9},{5... | collective-permute-start | bytes 688136 | tf_op jit(solution)/shard_map/ppermute | solution.py:23
  123.9 17.7 %collective-permute-start.19 = (bf16[896,128]{1,0:T(8,128)(2,1)S(1)}, bf16[896,128]{1,0:T(8,128)(2,1)S(1)}, u32[]{:S(2)}, u32[]{:S(2)}) collective-permute-start(bf16[896,128]{1,0:T(8,128)(2,1)S(1)} %get-tuple-element.118.refs_0_), channel_id=1, source_target_pairs={{0,4},{4,0},{8,12},{12,8},{16,20},{20,16},{24,28},{28,24},{1,5},{5... | collective-permute-start | bytes 688136 | tf_op jit(solution)/shard_map/ppermute | solution.py:23
  125.9 15.6 %collective-permute-start.20 = (bf16[448,256]{1,0:T(8,128)(2,1)S(1)}, bf16[448,256]{1,0:T(8,128)(2,1)S(1)}, u32[]{:S(2)}, u32[]{:S(2)}) collective-permute-start(bf16[448,256]{1,0:T(8,128)(2,1)S(1)} %join.10.refs_0_.own_ref), channel_id=1, source_target_pairs={{0,8},{4,12},{8,0},{12,4},{16,24},{20,28},{24,16},{28,20},{1,9},{5... | collective-permute-start | bytes 688136 | tf_op jit(solution)/shard_map/ppermute | solution.py:23
  126.1 15.7 %collective-permute-start.16 = (bf16[224,256]{1,0:T(8,128)(2,1)S(1)}, bf16[224,256]{1,0:T(8,128)(2,1)S(1)}, u32[]{:S(2)}, u32[]{:S(2)}) collective-permute-start(bf16[224,256]{1,0:T(8,128)(2,1)S(1)} %add.57.refs_0_.own_ref), channel_id=1, source_target_pairs={{0,16},{4,20},{8,24},{12,28},{16,0},{20,4},{24,8},{28,12},{1,17},{... | collective-permute-start | bytes 344072 | tf_op jit(solution)/shard_map/ppermute | solution.py:23
  128.3 13.4 %collective-permute-start.17 = (bf16[224,256]{1,0:T(8,128)(2,1)S(1)}, bf16[224,256]{1,0:T(8,128)(2,1)S(1)}, u32[]{:S(2)}, u32[]{:S(2)}) collective-permute-start(bf16[224,256]{1,0:T(8,128)(2,1)S(1)} %get-tuple-element.119.refs_0_), channel_id=1, source_target_pairs={{0,16},{4,20},{8,24},{12,28},{16,0},{20,4},{24,8},{28,12},{1,17},{... | collective-permute-start | bytes 344072 | tf_op jit(solution)/shard_map/ppermute | solution.py:23
  129.2 12.4 %collective-permute-start.18 = (bf16[448,128]{1,0:T(8,128)(2,1)S(1)}, bf16[448,128]{1,0:T(8,128)(2,1)S(1)}, u32[]{:S(2)}, u32[]{:S(2)}) collective-permute-start(bf16[448,128]{1,0:T(8,128)(2,1)S(1)} %get-tuple-element.120.refs_12_), channel_id=1, source_target_pairs={{0,8},{4,12},{8,0},{12,4},{16,24},{20,28},{24,16},{28,20},{1,9},{5... | collective-permute-start | bytes 344072 | tf_op jit(solution)/shard_map/ppermute | solution.py:23
  141.8 16.2 %collective-permute-start.21 = (bf16[768,896]{1,0:T(8,128)(2,1)S(1)}, bf16[768,896]{1,0:T(8,128)(2,1)S(1)}, u32[]{:S(2)}, u32[]{:S(2)}) collective-permute-start(bf16[768,896]{1,0:T(8,128)(2,1)S(1)} %get-tuple-element.128.refs_0_), channel_id=1, source_target_pairs={{0,1},{1,0},{2,3},{3,2},{4,5},{5,4},{6,7},{7,6},{8,9},{9,8},{10,11... | collective-permute-start | bytes 4128776 | tf_op jit(solution)/shard_map/ppermute | solution.py:23
  142.0 19.4 %collective-permute-start.30 = (bf16[896,256]{1,0:T(8,128)(2,1)S(1)}, bf16[896,256]{1,0:T(8,128)(2,1)S(1)}, u32[]{:S(2)}, u32[]{:S(2)}) collective-permute-start(bf16[896,256]{1,0:T(8,128)(2,1)S(1)} %join.11.refs_0_.own_ref), channel_id=1, source_target_pairs={{0,4},{4,0},{8,12},{12,8},{16,20},{20,16},{24,28},{28,24},{1,5},{5... | collective-permute-start | bytes 1376264 | tf_op jit(solution)/shard_map/ppermute | solution.py:23
  146.3 11.5 %collective-permute-start.22 = (bf16[448,128]{1,0:T(8,128)(2,1)S(1)}, bf16[448,128]{1,0:T(8,128)(2,1)S(1)}, u32[]{:S(2)}, u32[]{:S(2)}) collective-permute-start(bf16[448,128]{1,0:T(8,128)(2,1)S(1)} %get-tuple-element.126.refs_0_), channel_id=1, source_target_pairs={{0,8},{4,12},{8,0},{12,4},{16,24},{20,28},{24,16},{28,20},{1,9},{5... | collective-permute-start | bytes 344072 | tf_op jit(solution)/shard_map/ppermute | solution.py:23
  158.3 30.7 %collective-permute-start.26 = (bf16[384,896]{1,0:T(8,128)(2,1)S(1)}, bf16[384,896]{1,0:T(8,128)(2,1)S(1)}, u32[]{:S(2)}, u32[]{:S(2)}) collective-permute-start(bf16[384,896]{1,0:T(8,128)(2,1)S(1)} %get-tuple-element.133.refs_0_), channel_id=1, source_target_pairs={{0,2},{1,3},{2,0},{3,1},{4,6},{5,7},{6,4},{7,5},{8,10},{9,11},{10,... | collective-permute-start | bytes 2064392 | tf_op jit(solution)/shard_map/ppermute | solution.py:23
  159.8 19.4 %collective-permute-start.33 = (bf16[896,256]{1,0:T(8,128)(2,1)S(1)}, bf16[896,256]{1,0:T(8,128)(2,1)S(1)}, u32[]{:S(2)}, u32[]{:S(2)}) collective-permute-start(bf16[896,256]{1,0:T(8,128)(2,1)S(1)} %join.13.refs_0_.own_ref), channel_id=1, source_target_pairs={{0,4},{4,0},{8,12},{12,8},{16,20},{20,16},{24,28},{28,24},{1,5},{5... | collective-permute-start | bytes 1376264 | tf_op jit(solution)/shard_map/ppermute | solution.py:23
  165.9 24.8 %collective-permute-start.36 = (bf16[896,256]{1,0:T(8,128)(2,1)S(1)}, bf16[896,256]{1,0:T(8,128)(2,1)S(1)}, u32[]{:S(2)}, u32[]{:S(2)}) collective-permute-start(bf16[896,256]{1,0:T(8,128)(2,1)S(1)} %join.15.refs_0_.own_ref), channel_id=1, source_target_pairs={{0,4},{4,0},{8,12},{12,8},{16,20},{20,16},{24,28},{28,24},{1,5},{5... | collective-permute-start | bytes 1376264 | tf_op jit(solution)/shard_map/ppermute | solution.py:23
  180.8 11.3 %collective-permute-start.35 = (bf16[896,128]{1,0:T(8,128)(2,1)S(1)}, bf16[896,128]{1,0:T(8,128)(2,1)S(1)}, u32[]{:S(2)}, u32[]{:S(2)}) collective-permute-start(bf16[896,128]{1,0:T(8,128)(2,1)S(1)} %join.17.refs_0_.own_ref), channel_id=1, source_target_pairs={{0,4},{4,0},{8,12},{12,8},{16,20},{20,16},{24,28},{28,24},{1,5},{5... | collective-permute-start | bytes 688136 | tf_op jit(solution)/shard_map/ppermute | solution.py:23
  193.1 24.4 %all-to-all-start.3 = ((bf16[8,2,32,896]{3,2,1,0:T(8,128)(2,1)}), bf16[8,2,32,896]{3,2,1,0:T(8,128)(2,1)S(1)}, u32[]{:S(2)}, u32[]{:S(2)}) async-start(bf16[8,2,32,896]{3,2,1,0:T(8,128)(2,1)} %bitcast.13.refs_2_), calls=%async_computation.3 | async-start | bytes 1835008 | tf_op jit(solution)/shard_map/all_to_all | solution.py:531
  (43 other events, 291.8 us)

commit v9 on v7

--- a/solution.py
+++ b/solution.py
@@ -425,7 +425,7 @@
     period, left, launched = 0, rest, False
     while min(done) < steps or left:
         turn = list(done)
-        for j in range(chunks):
+        for j in [chunks - 1, *range(chunks - 1)] if period == 1 else range(chunks):
             if turn[j] < steps - 1 - (j == chunks - 1):
                 step(j)
         if left > 1 and period != 1:

time: 194 us -> 196 us (1.010)
  waiting for transfers between devices: 63.5 us -> 68.7 us
  starting transfers between devices: 47.7 us -> 44.9 us
    ppermute x32, waiting for transfers between devices: 53.2 us -> 58.4 us  [swap(): return lax.ppermute(value, axis, [(i, i ^ 1 << bit) for i in range(count)])]
    ppermute x32, starting transfers between devices: 40.3 us -> 37.1 us  [swap(): return lax.ppermute(value, axis, [(i, i ^ 1 << bit) for i in range(count)])]
  transfers between devices with their start and end apart: 34 -> 34, of which waited for: 12 -> 13; matrix products, arithmetic and copies ran while one was open for 1% -> 1% of each run, Pallas kernels for 19% -> 19%
where the time goes in v9:
time: 196 us
  waiting for transfers between devices  68.7 us (35%)
  starting transfers between devices  44.9 us (23%)
  Pallas kernels  44.8 us (23%)
  blocking collectives  28 us (14%)
  local copies, waits for them, and re-layouts  6.27 us (3%)
    ppermute x32, waiting for transfers between devices, swap(): return lax.ppermute(value, axis, [(i, i ^ 1 << bit) for i in range(count)])  58.4 us
    ppermute x32, starting transfers between devices, swap(): return lax.ppermute(value, axis, [(i, i ^ 1 << bit) for i in range(count)])  37.1 us
    pallas_call x4, Pallas kernels, run_heads(): pl.pallas_call(functools.partial(head_kernel, groups, spans, head_dim, st...  26 us
    all_to_all x1, blocking collectives, body(): lax.all_to_all(out, 'dp', split_axis=0, concat_axis=0, tiled=True)  14.4 us
    all_to_all x1, blocking collectives, body(): lax.all_to_all(asked.reshape(shards, capacity), 'dp', split_axis=0, conca...  13.5 us
    all_to_all x1, waiting for transfers between devices, body(): lax.all_to_all(out, 'dp', split_axis=0, concat_axis=0, tiled=True)  10.3 us
    pallas_call x1, Pallas kernels, run_state(): pl.pallas_call(functools.partial(state_kernel, groups, widths, len(after)...  10.1 us
    pallas_call x27, Pallas kernels, small(): pl.pallas_call(kernel, out_shape=outs, in_specs=[pl.BlockSpec(memory_spac...  8.72 us
  transfers between devices with their start and end apart: 34, of which 13 were waited for; matrix products, arithmetic and copies ran while one was open for 1% of the time, Pallas kernels for 19%

profile of v9, /device:TPU:0, one launch (start us, length us, event | category | flops | bytes accessed | tf_op | source)
XLA Modules:
  0.0 195.5 jit_solution(17417912687996238837)
XLA Ops:
  2.8 13.5 %all_to_all.21 = s32[8,1,2]{2,1,0:T(1,128)S(1)} all-to-all(s32[8,1,2]{2,1,0:T(1,128)S(1)} %bitcast.36), channel_id=1, replica_groups=mesh['dp'=8,'mp'=4] {'dp'}, dimensions={0} | all-to-all | bytes 128 | tf_op jit(solution)/shard_map/all_to_all | solution.py:470
  19.2 14.4 %all_to_all.22 = bf16[8,2,16,896]{3,2,1,0:T(8,128)(2,1)S(1)} all-to-all(bf16[8,2,16,896]{3,2,1,0:T(8,128)(2,1)S(1)} %bitcast.33), channel_id=1, replica_groups=mesh['dp'=8,'mp'=4] {'dp'}, dimensions={0} | all-to-all | bytes 917504 | tf_op jit(solution)/shard_map/all_to_all | solution.py:479
  33.6 3.5 %all-to-all-start.2 = ((bf16[8,2,16,896]{3,2,1,0:T(8,128)(2,1)}), bf16[8,2,16,896]{3,2,1,0:T(8,128)(2,1)S(1)}, u32[]{:S(2)}, u32[]{:S(2)}) async-start(bf16[8,2,16,896]{3,2,1,0:T(8,128)(2,1)} %bitcast.7), calls=%async_computation.2 | async-start | bytes 917504 | tf_op jit(solution)/shard_map/all_to_all | solution.py:479
  39.5 10.3 %all-to-all-done.2 = bf16[8,2,16,896]{3,2,1,0:T(8,128)(2,1)S(1)} async-done(((bf16[8,2,16,896]{3,2,1,0:T(8,128)(2,1)}), bf16[8,2,16,896]{3,2,1,0:T(8,128)(2,1)S(1)}, u32[]{:S(2)}, u32[]{:S(2)}) %all-to-all-start.2) | async-done | bytes 458784 | tf_op jit(solution)/shard_map/all_to_all | solution.py:479
  52.4 5.2 %collective-permute-done.3.refs_6_ = bf16[192,896]{1,0:T(8,128)(2,1)S(1)} collective-permute-done((bf16[192,896]{1,0:T(8,128)(2,1)S(1)}, bf16[192,896]{1,0:T(8,128)(2,1)S(1)}, u32[]{:S(2)}, u32[]{:S(2)}) %collective-permute-start.3) | collective-permute-done | bytes 344096 | tf_op jit(solution)/shard_map/ppermute | solution.py:23
  59.3 6.5 %heads.4 = (bf16[384,1024]{1,0:T(8,128)(2,1)}, bf16[384,1024]{1,0:T(8,128)(2,1)}, bf16[1536,256]{1,0:T(8,128)(2,1)}, bf16[1536,256]{1,0:T(8,128)(2,1)}, f32[896,...) custom-call(s32[1]{0:T(128)} %bitcast.refs_0_.choice_ref, bf16[192,896]{1,0:T(8,128)(2,1)S(1)} %bitcast.23, ...), custom_call_target="tpu_custom_call" | custom-call | flops 5637144576 | bytes 5505024 | tf_op jit(solution)/shard_map/heads/pallas_call | solution.py:158
  65.8 2.7 %collective-permute-start.6 = (bf16[896,256]{1,0:T(8,128)(2,1)S(1)}, bf16[896,256]{1,0:T(8,128)(2,1)S(1)}, u32[]{:S(2)}, u32[]{:S(2)}) collective-permute-start(bf16[896,256]{1,0:T(8,128)(2,1)S(1)} %get-tuple-element.69.refs_15_), channel_id=1, source_target_pairs={{0,4},{4,0},{8,12},{12,8},{16,20},{20,16},{24,28},{28,24},{1,5},{5... | collective-permute-start | bytes 1376264 | tf_op jit(solution)/shard_map/ppermute | solution.py:23
  68.5 6.5 %heads.5 = (bf16[384,1024]{1,0:T(8,128)(2,1)}, bf16[384,1024]{1,0:T(8,128)(2,1)}, bf16[1536,256]{1,0:T(8,128)(2,1)}, bf16[1536,256]{1,0:T(8,128)(2,1)}, f32[896,...) custom-call(s32[1]{0:T(128)} %bitcast.refs_0_.choice_ref, ...), custom_call_target="tpu_custom_call", output_to_operand_aliasing={{0}: (13, {}), {1}: (14, {})} | custom-call | flops 5637144576 | bytes 5505024 | tf_op jit(solution)/shard_map/heads/pallas_call | solution.py:158
  75.0 4.7 %collective-permute-done.6.recv_ref = bf16[896,256]{1,0:T(8,128)(2,1)S(1)} collective-permute-done((bf16[896,256]{1,0:T(8,128)(2,1)S(1)}, bf16[896,256]{1,0:T(8,128)(2,1)S(1)}, u32[]{:S(2)}, u32[]{:S(2)}) %collective-permute-start.6) | collective-permute-done | bytes 458784 | tf_op jit(solution)/shard_map/ppermute | solution.py:23
  80.2 6.6 %heads.6 = (bf16[384,1024]{1,0:T(8,128)(2,1)}, bf16[384,1024]{1,0:T(8,128)(2,1)}, bf16[1536,256]{1,0:T(8,128)(2,1)}, bf16[1536,256]{1,0:T(8,128)(2,1)}, f32[896,...) custom-call(s32[1]{0:T(128)} %bitcast.refs_0_.choice_ref, ...), custom_call_target="tpu_custom_call", output_to_operand_aliasing={{0}: (13, {}), {1}: (14, {})} | custom-call | flops 5637144576 | bytes 5505024 | tf_op jit(solution)/shard_map/heads/pallas_call | solution.py:158
  88.8 2.8 %collective-permute-start.11 = (bf16[224,256]{1,0:T(8,128)(2,1)S(1)}, bf16[224,256]{1,0:T(8,128)(2,1)S(1)}, u32[]{:S(2)}, u32[]{:S(2)}) collective-permute-start(bf16[224,256]{1,0:T(8,128)(2,1)S(1)} %get-tuple-element.80.refs_0_), channel_id=1, source_target_pairs={{0,16},{4,20},{8,24},{12,28},{16,0},{20,4},{24,8},{28,12},{1,17},{... | collective-permute-start | bytes 344072 | tf_op jit(solution)/shard_map/ppermute | solution.py:23
  91.8 6.5 %heads.7 = (bf16[384,1024]{1,0:T(8,128)(2,1)}, bf16[384,1024]{1,0:T(8,128)(2,1)}, bf16[1536,256]{1,0:T(8,128)(2,1)}, bf16[1536,256]{1,0:T(8,128)(2,1)}, f32[896,...) custom-call(s32[1]{0:T(128)} %bitcast.refs_0_.choice_ref, ...), custom_call_target="tpu_custom_call", output_to_operand_aliasing={{0}: (13, {}), {1}: (14, {})} | custom-call | flops 5637144576 | bytes 5505024 | tf_op jit(solution)/shard_map/heads/pallas_call | solution.py:158
  99.1 2.2 %collective-permute-start.15 = (bf16[224,256]{1,0:T(8,128)(2,1)S(1)}, bf16[224,256]{1,0:T(8,128)(2,1)S(1)}, u32[]{:S(2)}, u32[]{:S(2)}) collective-permute-start(bf16[224,256]{1,0:T(8,128)(2,1)S(1)} %add.55.refs_0_.own_ref), channel_id=1, source_target_pairs={{0,16},{4,20},{8,24},{12,28},{16,0},{20,4},{24,8},{28,12},{1,17},{... | collective-permute-start | bytes 344072 | tf_op jit(solution)/shard_map/ppermute | solution.py:23
  103.8 10.1 %state_terms.1 = (bf16[768,896]{1,0:T(8,128)(2,1)S(1)}, bf16[768,896]{1,0:T(8,128)(2,1)S(1)}) custom-call(bf16[1536,256]{1,0:T(8,128)(2,1)} %get-tuple-element.84.refs_0_, bf16[1536,256]{1,0:T(8,128)(2,1)} %get-tuple-element.85.refs_1_, bf16[1536,256]{1,0:T(8,128)(2,1)} %get-tuple-element.86.refs_2_, bf16[1536,256]{1,0:T(8,128)(2,1)} %get-tuple-element.87.refs_3_, ...), custom_call_target="tpu_custom_call" | custom-call | flops 11274289152 | bytes 11010048 | tf_op jit(solution)/shard_map/state_terms/pallas_call | solution.py:245
  117.2 2.1 %collective-permute-start.18 = (bf16[224,256]{1,0:T(8,128)(2,1)S(1)}, bf16[224,256]{1,0:T(8,128)(2,1)S(1)}, u32[]{:S(2)}, u32[]{:S(2)}) collective-permute-start(bf16[224,256]{1,0:T(8,128)(2,1)S(1)} %get-tuple-element.104.refs_0_), channel_id=1, source_target_pairs={{0,16},{4,20},{8,24},{12,28},{16,0},{20,4},{24,8},{28,12},{1,17},{... | collective-permute-start | bytes 344072 | tf_op jit(solution)/shard_map/ppermute | solution.py:23
  119.3 8.4 %collective-permute-done.20.recv_ref = bf16[448,256]{1,0:T(8,128)(2,1)S(1)} collective-permute-done((bf16[448,256]{1,0:T(8,128)(2,1)S(1)}, bf16[448,256]{1,0:T(8,128)(2,1)S(1)}, u32[]{:S(2)}, u32[]{:S(2)}) %collective-permute-start.20) | collective-permute-done | bytes 229408 | tf_op jit(solution)/shard_map/ppermute | solution.py:23
  128.3 2.7 %collective-permute-start.25 = (bf16[448,256]{1,0:T(8,128)(2,1)S(1)}, bf16[448,256]{1,0:T(8,128)(2,1)S(1)}, u32[]{:S(2)}, u32[]{:S(2)}) collective-permute-start(bf16[448,256]{1,0:T(8,128)(2,1)S(1)} %join.10.refs_0_.own_ref), channel_id=1, source_target_pairs={{0,8},{4,12},{8,0},{12,4},{16,24},{20,28},{24,16},{28,20},{1,9},{5... | collective-permute-start | bytes 688136 | tf_op jit(solution)/shard_map/ppermute | solution.py:23
  137.5 6.5 %collective-permute-done.22.recv_ref = bf16[224,256]{1,0:T(8,128)(2,1)S(1)} collective-permute-done((bf16[224,256]{1,0:T(8,128)(2,1)S(1)}, bf16[224,256]{1,0:T(8,128)(2,1)S(1)}, u32[]{:S(2)}, u32[]{:S(2)}) %collective-permute-start.22) | collective-permute-done | bytes 114720 | tf_op jit(solution)/shard_map/ppermute | solution.py:23
  148.7 3.0 %collective-permute-done.26.recv_ref = bf16[448,256]{1,0:T(8,128)(2,1)S(1)} collective-permute-done((bf16[448,256]{1,0:T(8,128)(2,1)S(1)}, bf16[448,256]{1,0:T(8,128)(2,1)S(1)}, u32[]{:S(2)}, u32[]{:S(2)}) %collective-permute-start.26) | collective-permute-done | bytes 229408 | tf_op jit(solution)/shard_map/ppermute | solution.py:23
  154.1 6.2 %collective-permute-done.23.recv_ref = bf16[224,256]{1,0:T(8,128)(2,1)S(1)} collective-permute-done((bf16[224,256]{1,0:T(8,128)(2,1)S(1)}, bf16[224,256]{1,0:T(8,128)(2,1)S(1)}, u32[]{:S(2)}, u32[]{:S(2)}) %collective-permute-start.23) | collective-permute-done | bytes 114720 | tf_op jit(solution)/shard_map/ppermute | solution.py:23
  163.6 3.1 %collective-permute-done.29.recv_ref = bf16[896,256]{1,0:T(8,128)(2,1)S(1)} collective-permute-done((bf16[896,256]{1,0:T(8,128)(2,1)S(1)}, bf16[896,256]{1,0:T(8,128)(2,1)S(1)}, u32[]{:S(2)}, u32[]{:S(2)}) %collective-permute-start.29) | collective-permute-done | bytes 458784 | tf_op jit(solution)/shard_map/ppermute | solution.py:23
  168.1 4.3 %all-to-all-start.3 = ((bf16[8,2,32,896]{3,2,1,0:T(8,128)(2,1)}), bf16[8,2,32,896]{3,2,1,0:T(8,128)(2,1)S(1)}, u32[]{:S(2)}, u32[]{:S(2)}) async-start(bf16[8,2,32,896]{3,2,1,0:T(8,128)(2,1)} %bitcast.13.refs_2_), calls=%async_computation.3 | async-start | bytes 1835008 | tf_op jit(solution)/shard_map/all_to_all | solution.py:529
  172.4 2.0 %collective-permute-start.31 = (bf16[896,256]{1,0:T(8,128)(2,1)S(1)}, bf16[896,256]{1,0:T(8,128)(2,1)S(1)}, u32[]{:S(2)}, u32[]{:S(2)}) collective-permute-start(bf16[896,256]{1,0:T(8,128)(2,1)S(1)} %join.15.own_ref.refs_2_), channel_id=1, source_target_pairs={{0,4},{4,0},{8,12},{12,8},{16,20},{20,16},{24,28},{28,24},{1,5},{5... | collective-permute-start | bytes 1376264 | tf_op jit(solution)/shard_map/ppermute | solution.py:23
  174.5 17.8 %collective-permute-done.31.recv_ref = bf16[896,256]{1,0:T(8,128)(2,1)S(1)} collective-permute-done((bf16[896,256]{1,0:T(8,128)(2,1)S(1)}, bf16[896,256]{1,0:T(8,128)(2,1)S(1)}, u32[]{:S(2)}, u32[]{:S(2)}) %collective-permute-start.31) | collective-permute-done | bytes 458784 | tf_op jit(solution)/shard_map/ppermute | solution.py:23
  (108 shorter events, 42.9 us)
Async XLA Ops:
  33.6 16.2 %all-to-all-start.2 = ((bf16[8,2,16,896]{3,2,1,0:T(8,128)(2,1)}), bf16[8,2,16,896]{3,2,1,0:T(8,128)(2,1)S(1)}, u32[]{:S(2)}, u32[]{:S(2)}) async-start(bf16[8,2,16,896]{3,2,1,0:T(8,128)(2,1)} %bitcast.7), calls=%async_computation.2 | async-start | bytes 917504 | tf_op jit(solution)/shard_map/all_to_all | solution.py:479
  37.9 11.8 %collective-permute-start = (bf16[192,896]{1,0:T(8,128)(2,1)S(1)}, bf16[192,896]{1,0:T(8,128)(2,1)S(1)}, u32[]{:S(2)}, u32[]{:S(2)}) collective-permute-start(bf16[192,896]{1,0:T(8,128)(2,1)S(1)} %bitcast.21), channel_id=1, source_target_pairs={{0,2},{1,3},{2,0},{3,1},{4,6},{5,7},{6,4},{7,5},{8,10},{9,11},{10,... | collective-permute-start | bytes 1032200 | tf_op jit(solution)/shard_map/ppermute | solution.py:23
  65.8 14.0 %collective-permute-start.6 = (bf16[896,256]{1,0:T(8,128)(2,1)S(1)}, bf16[896,256]{1,0:T(8,128)(2,1)S(1)}, u32[]{:S(2)}, u32[]{:S(2)}) collective-permute-start(bf16[896,256]{1,0:T(8,128)(2,1)S(1)} %get-tuple-element.69.refs_15_), channel_id=1, source_target_pairs={{0,4},{4,0},{8,12},{12,8},{16,20},{20,16},{24,28},{28,24},{1,5},{5... | collective-permute-start | bytes 1376264 | tf_op jit(solution)/shard_map/ppermute | solution.py:23
  74.9 16.6 %collective-permute-start.7 = (bf16[896,256]{1,0:T(8,128)(2,1)S(1)}, bf16[896,256]{1,0:T(8,128)(2,1)S(1)}, u32[]{:S(2)}, u32[]{:S(2)}) collective-permute-start(bf16[896,256]{1,0:T(8,128)(2,1)S(1)} %get-tuple-element.73.refs_0_), channel_id=1, source_target_pairs={{0,4},{4,0},{8,12},{12,8},{16,20},{20,16},{24,28},{28,24},{1,5},{5... | collective-permute-start | bytes 1376264 | tf_op jit(solution)/shard_map/ppermute | solution.py:23
  86.8 15.4 %collective-permute-start.9 = (bf16[896,256]{1,0:T(8,128)(2,1)S(1)}, bf16[896,256]{1,0:T(8,128)(2,1)S(1)}, u32[]{:S(2)}, u32[]{:S(2)}) collective-permute-start(bf16[896,256]{1,0:T(8,128)(2,1)S(1)} %get-tuple-element.79.refs_0_), channel_id=1, source_target_pairs={{0,4},{4,0},{8,12},{12,8},{16,20},{20,16},{24,28},{28,24},{1,5},{5... | collective-permute-start | bytes 1376264 | tf_op jit(solution)/shard_map/ppermute | solution.py:23
  88.8 10.3 %collective-permute-start.11 = (bf16[224,256]{1,0:T(8,128)(2,1)S(1)}, bf16[224,256]{1,0:T(8,128)(2,1)S(1)}, u32[]{:S(2)}, u32[]{:S(2)}) collective-permute-start(bf16[224,256]{1,0:T(8,128)(2,1)S(1)} %get-tuple-element.80.refs_0_), channel_id=1, source_target_pairs={{0,16},{4,20},{8,24},{12,28},{16,0},{20,4},{24,8},{28,12},{1,17},{... | collective-permute-start | bytes 344072 | tf_op jit(solution)/shard_map/ppermute | solution.py:23
  98.3 15.7 %collective-permute-start.14 = (bf16[896,256]{1,0:T(8,128)(2,1)S(1)}, bf16[896,256]{1,0:T(8,128)(2,1)S(1)}, u32[]{:S(2)}, u32[]{:S(2)}) collective-permute-start(bf16[896,256]{1,0:T(8,128)(2,1)S(1)} %get-tuple-element.95.refs_0_), channel_id=1, source_target_pairs={{0,4},{4,0},{8,12},{12,8},{16,20},{20,16},{24,28},{28,24},{1,5},{5... | collective-permute-start | bytes 1376264 | tf_op jit(solution)/shard_map/ppermute | solution.py:23
  99.1 14.8 %collective-permute-start.15 = (bf16[224,256]{1,0:T(8,128)(2,1)S(1)}, bf16[224,256]{1,0:T(8,128)(2,1)S(1)}, u32[]{:S(2)}, u32[]{:S(2)}) collective-permute-start(bf16[224,256]{1,0:T(8,128)(2,1)S(1)} %add.55.refs_0_.own_ref), channel_id=1, source_target_pairs={{0,16},{4,20},{8,24},{12,28},{16,0},{20,4},{24,8},{28,12},{1,17},{... | collective-permute-start | bytes 344072 | tf_op jit(solution)/shard_map/ppermute | solution.py:23
  101.3 12.8 %collective-permute-start.12 = (bf16[224,256]{1,0:T(8,128)(2,1)S(1)}, bf16[224,256]{1,0:T(8,128)(2,1)S(1)}, u32[]{:S(2)}, u32[]{:S(2)}) collective-permute-start(bf16[224,256]{1,0:T(8,128)(2,1)S(1)} %get-tuple-element.96.refs_0_), channel_id=1, source_target_pairs={{0,16},{4,20},{8,24},{12,28},{16,0},{20,4},{24,8},{28,12},{1,17},{... | collective-permute-start | bytes 344072 | tf_op jit(solution)/shard_map/ppermute | solution.py:23
  102.3 11.8 %collective-permute-start.13 = (bf16[448,256]{1,0:T(8,128)(2,1)S(1)}, bf16[448,256]{1,0:T(8,128)(2,1)S(1)}, u32[]{:S(2)}, u32[]{:S(2)}) collective-permute-start(bf16[448,256]{1,0:T(8,128)(2,1)S(1)} %get-tuple-element.97.refs_10_), channel_id=1, source_target_pairs={{0,8},{4,12},{8,0},{12,4},{16,24},{20,28},{24,16},{28,20},{1,9},{5... | collective-permute-start | bytes 688136 | tf_op jit(solution)/shard_map/ppermute | solution.py:23
  114.2 21.4 %collective-permute-start.16 = (bf16[768,896]{1,0:T(8,128)(2,1)S(1)}, bf16[768,896]{1,0:T(8,128)(2,1)S(1)}, u32[]{:S(2)}, u32[]{:S(2)}) collective-permute-start(bf16[768,896]{1,0:T(8,128)(2,1)S(1)} %get-tuple-element.105.refs_0_), channel_id=1, source_target_pairs={{0,1},{1,0},{2,3},{3,2},{4,5},{5,4},{6,7},{7,6},{8,9},{9,8},{10,11... | collective-permute-start | bytes 4128776 | tf_op jit(solution)/shard_map/ppermute | solution.py:23
  114.3 13.4 %collective-permute-start.20 = (bf16[448,256]{1,0:T(8,128)(2,1)S(1)}, bf16[448,256]{1,0:T(8,128)(2,1)S(1)}, u32[]{:S(2)}, u32[]{:S(2)}) collective-permute-start(bf16[448,256]{1,0:T(8,128)(2,1)S(1)} %join.8.refs_0_.own_ref), channel_id=1, source_target_pairs={{0,8},{4,12},{8,0},{12,4},{16,24},{20,28},{24,16},{28,20},{1,9},{5... | collective-permute-start | bytes 688136 | tf_op jit(solution)/shard_map/ppermute | solution.py:23
  115.0 17.6 %collective-permute-start.17 = (bf16[448,256]{1,0:T(8,128)(2,1)S(1)}, bf16[448,256]{1,0:T(8,128)(2,1)S(1)}, u32[]{:S(2)}, u32[]{:S(2)}) collective-permute-start(bf16[448,256]{1,0:T(8,128)(2,1)S(1)} %get-tuple-element.103.refs_0_), channel_id=1, source_target_pairs={{0,8},{4,12},{8,0},{12,4},{16,24},{20,28},{24,16},{28,20},{1,9},{5... | collective-permute-start | bytes 688136 | tf_op jit(solution)/shard_map/ppermute | solution.py:23
  116.4 11.9 %collective-permute-start.19 = (bf16[224,256]{1,0:T(8,128)(2,1)S(1)}, bf16[224,256]{1,0:T(8,128)(2,1)S(1)}, u32[]{:S(2)}, u32[]{:S(2)}) collective-permute-start(bf16[224,256]{1,0:T(8,128)(2,1)S(1)} %add.56.refs_0_.own_ref), channel_id=1, source_target_pairs={{0,16},{4,20},{8,24},{12,28},{16,0},{20,4},{24,8},{28,12},{1,17},{... | collective-permute-start | bytes 344072 | tf_op jit(solution)/shard_map/ppermute | solution.py:23
  117.2 15.2 %collective-permute-start.18 = (bf16[224,256]{1,0:T(8,128)(2,1)S(1)}, bf16[224,256]{1,0:T(8,128)(2,1)S(1)}, u32[]{:S(2)}, u32[]{:S(2)}) collective-permute-start(bf16[224,256]{1,0:T(8,128)(2,1)S(1)} %get-tuple-element.104.refs_0_), channel_id=1, source_target_pairs={{0,16},{4,20},{8,24},{12,28},{16,0},{20,4},{24,8},{28,12},{1,17},{... | collective-permute-start | bytes 344072 | tf_op jit(solution)/shard_map/ppermute | solution.py:23
  128.3 15.7 %collective-permute-start.25 = (bf16[448,256]{1,0:T(8,128)(2,1)S(1)}, bf16[448,256]{1,0:T(8,128)(2,1)S(1)}, u32[]{:S(2)}, u32[]{:S(2)}) collective-permute-start(bf16[448,256]{1,0:T(8,128)(2,1)S(1)} %join.10.refs_0_.own_ref), channel_id=1, source_target_pairs={{0,8},{4,12},{8,0},{12,4},{16,24},{20,28},{24,16},{28,20},{1,9},{5... | collective-permute-start | bytes 688136 | tf_op jit(solution)/shard_map/ppermute | solution.py:23
  131.0 16.3 %collective-permute-start.27 = (bf16[896,256]{1,0:T(8,128)(2,1)S(1)}, bf16[896,256]{1,0:T(8,128)(2,1)S(1)}, u32[]{:S(2)}, u32[]{:S(2)}) collective-permute-start(bf16[896,256]{1,0:T(8,128)(2,1)S(1)} %join.9.refs_0_.own_ref), channel_id=1, source_target_pairs={{0,4},{4,0},{8,12},{12,8},{16,20},{20,16},{24,28},{28,24},{1,5},{5... | collective-permute-start | bytes 1376264 | tf_op jit(solution)/shard_map/ppermute | solution.py:23
  132.7 11.4 %collective-permute-start.22 = (bf16[224,256]{1,0:T(8,128)(2,1)S(1)}, bf16[224,256]{1,0:T(8,128)(2,1)S(1)}, u32[]{:S(2)}, u32[]{:S(2)}) collective-permute-start(bf16[224,256]{1,0:T(8,128)(2,1)S(1)} %get-tuple-element.108.refs_0_), channel_id=1, source_target_pairs={{0,16},{4,20},{8,24},{12,28},{16,0},{20,4},{24,8},{28,12},{1,17},{... | collective-permute-start | bytes 344072 | tf_op jit(solution)/shard_map/ppermute | solution.py:23
  133.9 11.4 %collective-permute-start.24 = (bf16[224,256]{1,0:T(8,128)(2,1)S(1)}, bf16[224,256]{1,0:T(8,128)(2,1)S(1)}, u32[]{:S(2)}, u32[]{:S(2)}) collective-permute-start(bf16[224,256]{1,0:T(8,128)(2,1)S(1)} %add.57.refs_0_.own_ref), channel_id=1, source_target_pairs={{0,16},{4,20},{8,24},{12,28},{16,0},{20,4},{24,8},{28,12},{1,17},{... | collective-permute-start | bytes 344072 | tf_op jit(solution)/shard_map/ppermute | solution.py:23
  136.0 24.5 %collective-permute-start.21 = (bf16[384,896]{1,0:T(8,128)(2,1)S(1)}, bf16[384,896]{1,0:T(8,128)(2,1)S(1)}, u32[]{:S(2)}, u32[]{:S(2)}) collective-permute-start(bf16[384,896]{1,0:T(8,128)(2,1)S(1)} %get-tuple-element.110.refs_0_), channel_id=1, source_target_pairs={{0,2},{1,3},{2,0},{3,1},{4,6},{5,7},{6,4},{7,5},{8,10},{9,11},{10,... | collective-permute-start | bytes 2064392 | tf_op jit(solution)/shard_map/ppermute | solution.py:23
  145.4 16.8 %collective-permute-start.30 = (bf16[896,256]{1,0:T(8,128)(2,1)S(1)}, bf16[896,256]{1,0:T(8,128)(2,1)S(1)}, u32[]{:S(2)}, u32[]{:S(2)}) collective-permute-start(bf16[896,256]{1,0:T(8,128)(2,1)S(1)} %join.11.refs_0_.own_ref), channel_id=1, source_target_pairs={{0,4},{4,0},{8,12},{12,8},{16,20},{20,16},{24,28},{28,24},{1,5},{5... | collective-permute-start | bytes 1376264 | tf_op jit(solution)/shard_map/ppermute | solution.py:23
  151.7 14.9 %collective-permute-start.29 = (bf16[896,256]{1,0:T(8,128)(2,1)S(1)}, bf16[896,256]{1,0:T(8,128)(2,1)S(1)}, u32[]{:S(2)}, u32[]{:S(2)}) collective-permute-start(bf16[896,256]{1,0:T(8,128)(2,1)S(1)} %join.13.refs_0_.own_ref), channel_id=1, source_target_pairs={{0,4},{4,0},{8,12},{12,8},{16,20},{20,16},{24,28},{28,24},{1,5},{5... | collective-permute-start | bytes 1376264 | tf_op jit(solution)/shard_map/ppermute | solution.py:23
  168.1 25.6 %all-to-all-start.3 = ((bf16[8,2,32,896]{3,2,1,0:T(8,128)(2,1)}), bf16[8,2,32,896]{3,2,1,0:T(8,128)(2,1)S(1)}, u32[]{:S(2)}, u32[]{:S(2)}) async-start(bf16[8,2,32,896]{3,2,1,0:T(8,128)(2,1)} %bitcast.13.refs_2_), calls=%async_computation.3 | async-start | bytes 1835008 | tf_op jit(solution)/shard_map/all_to_all | solution.py:529
  172.4 19.9 %collective-permute-start.31 = (bf16[896,256]{1,0:T(8,128)(2,1)S(1)}, bf16[896,256]{1,0:T(8,128)(2,1)S(1)}, u32[]{:S(2)}, u32[]{:S(2)}) collective-permute-start(bf16[896,256]{1,0:T(8,128)(2,1)S(1)} %join.15.own_ref.refs_2_), channel_id=1, source_target_pairs={{0,4},{4,0},{8,12},{12,8},{16,20},{20,16},{24,28},{28,24},{1,5},{5... | collective-permute-start | bytes 1376264 | tf_op jit(solution)/shard_map/ppermute | solution.py:23
  (12 other events, 118.3 us)

commit v10 on v7

--- a/solution.py
+++ b/solution.py
@@ -470,12 +470,13 @@
     incoming = lax.all_to_all(
         asked.reshape(shards, capacity), "dp", split_axis=0, concat_axis=0, tiled=True
     ).reshape(slot_count)
-    slab_rows = jnp.take(states, jnp.minimum(incoming, stored - 1), axis=0, mode="clip")
+    wanted = jnp.minimum(incoming, stored - 1)
     halves = 2
     piece = slab_len // halves
     came = []
     for h in range(halves):
-        out = slab_rows[:, h * piece : (h + 1) * piece].reshape(shards, capacity, piece, enc_width)
+        out = jnp.take(states[:, h * piece : (h + 1) * piece], wanted, axis=0, mode="clip")
+        out = out.reshape(shards, capacity, piece, enc_width)
         came.append(lax.all_to_all(out, "dp", split_axis=0, concat_axis=0, tiled=True))
     blocks = {}
     for h in range(halves):

time: 194 us -> 195 us (level)
  blocking collectives: 28 us -> 0 us
  waiting for transfers between devices: 63.5 us -> 80.3 us
  starting transfers between devices: 47.7 us -> 57.4 us
  local copies, waits for them, and re-layouts: 6.28 us -> 9.15 us
    all_to_all x2 -> x0, blocking collectives: 28 us -> none  [the longest x1 14.4 us: body(): lax.all_to_all(out, 'dp', split_axis=0, concat_axis=0, tiled=True)]
    all_to_all x1 -> x2, waiting for transfers between devices: 10.3 us -> 20.6 us  [body(): lax.all_to_all(out, 'dp', split_axis=0, concat_axis=0, tiled=True)]
    all_to_all x0 -> x1, starting transfers between devices: none -> 7.28 us  [body(): lax.all_to_all(asked.reshape(shards, capacity), 'dp', split_axis=0, conca...]
    all_to_all x0 -> x1, waiting for transfers between devices: none -> 5.3 us  [body(): lax.all_to_all(asked.reshape(shards, capacity), 'dp', split_axis=0, conca...]
    all_to_all x1 -> x2, starting transfers between devices: 3.52 us -> 7.14 us  [body(): lax.all_to_all(out, 'dp', split_axis=0, concat_axis=0, tiled=True)]
    gather x1 -> x2, local copies, waits for them, and re-layouts: 0.7 us -> 2.73 us  [body(): jnp.take(states[:, h * piece:(h + 1) * piece], wanted, axis=0, mode='clip')]
  transfers between devices with their start and end apart: 34 -> 36, of which waited for: 12 -> 14; matrix products, arithmetic and copies ran while one was open for 1% -> 3% of each run, Pallas kernels for 19% -> 19%
where the time goes in v10:
time: 195 us
  waiting for transfers between devices  80.3 us (41%)
  starting transfers between devices  57.4 us (29%)
  Pallas kernels  44.8 us (23%)
  local copies, waits for them, and re-layouts  9.15 us (5%)
    ppermute x32, waiting for transfers between devices, swap(): return lax.ppermute(value, axis, [(i, i ^ 1 << bit) for i in range(count)])  54.4 us
    ppermute x32, starting transfers between devices, swap(): return lax.ppermute(value, axis, [(i, i ^ 1 << bit) for i in range(count)])  39.2 us
    pallas_call x4, Pallas kernels, run_heads(): pl.pallas_call(functools.partial(head_kernel, groups, spans, head_dim, st...  26 us
    all_to_all x2, waiting for transfers between devices, body(): lax.all_to_all(out, 'dp', split_axis=0, concat_axis=0, tiled=True)  20.6 us
    pallas_call x1, Pallas kernels, run_state(): pl.pallas_call(functools.partial(state_kernel, groups, widths, len(after)...  10.1 us
    pallas_call x27, Pallas kernels, small(): pl.pallas_call(kernel, out_shape=outs, in_specs=[pl.BlockSpec(memory_spac...  8.73 us
    all_to_all x1, starting transfers between devices, body(): lax.all_to_all(asked.reshape(shards, capacity), 'dp', split_axis=0, conca...  7.28 us
    all_to_all x2, starting transfers between devices, body(): lax.all_to_all(out, 'dp', split_axis=0, concat_axis=0, tiled=True)  7.14 us
  transfers between devices with their start and end apart: 36, of which 14 were waited for; matrix products, arithmetic and copies ran while one was open for 3% of the time, Pallas kernels for 19%

profile of v10, /device:TPU:0, one launch (start us, length us, event | category | flops | bytes accessed | tf_op | source)
XLA Modules:
  0.0 194.5 jit_solution(3570166788019411266)
XLA Ops:
  3.3 7.3 %all-to-all-start = ((s32[8,1,2]{2,1,0:T(1,128)}), s32[8,1,2]{2,1,0:T(1,128)S(1)}, u32[]{:S(2)}, u32[]{:S(2)}) async-start(s32[8,1,2]{2,1,0:T(1,128)} %bitcast.1), calls=%async_computation | async-start | bytes 8192 | tf_op jit(solution)/shard_map/all_to_all | solution.py:470
  11.7 5.3 %all-to-all-done = s32[8,1,2]{2,1,0:T(1,128)S(1)} async-done(((s32[8,1,2]{2,1,0:T(1,128)}), s32[8,1,2]{2,1,0:T(1,128)S(1)}, u32[]{:S(2)}, u32[]{:S(2)}) %all-to-all-start) | async-done | bytes 96 | tf_op jit(solution)/shard_map/all_to_all | solution.py:470
  19.6 3.5 %all-to-all-start.1 = ((bf16[8,2,16,896]{3,2,1,0:T(8,128)(2,1)}), bf16[8,2,16,896]{3,2,1,0:T(8,128)(2,1)S(1)}, u32[]{:S(2)}, u32[]{:S(2)}) async-start(bf16[8,2,16,896]{3,2,1,0:T(8,128)(2,1)} %bitcast.2), calls=%async_computation.1 | async-start | bytes 917504 | tf_op jit(solution)/shard_map/all_to_all | solution.py:480
  24.5 10.5 %all-to-all-done.1 = bf16[8,2,16,896]{3,2,1,0:T(8,128)(2,1)S(1)} async-done(((bf16[8,2,16,896]{3,2,1,0:T(8,128)(2,1)}), bf16[8,2,16,896]{3,2,1,0:T(8,128)(2,1)S(1)}, u32[]{:S(2)}, u32[]{:S(2)}) %all-to-all-start.1) | async-done | bytes 458784 | tf_op jit(solution)/shard_map/all_to_all | solution.py:480
  35.0 3.7 %all-to-all-start.2 = ((bf16[8,2,16,896]{3,2,1,0:T(8,128)(2,1)}), bf16[8,2,16,896]{3,2,1,0:T(8,128)(2,1)S(1)}, u32[]{:S(2)}, u32[]{:S(2)}) async-start(bf16[8,2,16,896]{3,2,1,0:T(8,128)(2,1)} %bitcast.7), calls=%async_computation.2 | async-start | bytes 917504 | tf_op jit(solution)/shard_map/all_to_all | solution.py:480
  41.0 10.1 %all-to-all-done.2 = bf16[8,2,16,896]{3,2,1,0:T(8,128)(2,1)S(1)} async-done(((bf16[8,2,16,896]{3,2,1,0:T(8,128)(2,1)}), bf16[8,2,16,896]{3,2,1,0:T(8,128)(2,1)S(1)}, u32[]{:S(2)}, u32[]{:S(2)}) %all-to-all-start.2) | async-done | bytes 458784 | tf_op jit(solution)/shard_map/all_to_all | solution.py:480
  53.8 5.2 %collective-permute-done.3.refs_6_ = bf16[192,896]{1,0:T(8,128)(2,1)S(1)} collective-permute-done((bf16[192,896]{1,0:T(8,128)(2,1)S(1)}, bf16[192,896]{1,0:T(8,128)(2,1)S(1)}, u32[]{:S(2)}, u32[]{:S(2)}) %collective-permute-start.3) | collective-permute-done | bytes 344096 | tf_op jit(solution)/shard_map/ppermute | solution.py:23
  60.7 6.5 %heads.4 = (bf16[384,1024]{1,0:T(8,128)(2,1)}, bf16[384,1024]{1,0:T(8,128)(2,1)}, bf16[1536,256]{1,0:T(8,128)(2,1)}, bf16[1536,256]{1,0:T(8,128)(2,1)}, f32[896,...) custom-call(s32[1]{0:T(128)} %bitcast.refs_0_.choice_ref, bf16[192,896]{1,0:T(8,128)(2,1)S(1)} %bitcast.23, ...), custom_call_target="tpu_custom_call" | custom-call | flops 5637144576 | bytes 5505024 | tf_op jit(solution)/shard_map/heads/pallas_call | solution.py:158
  68.7 6.5 %heads.5 = (bf16[384,1024]{1,0:T(8,128)(2,1)}, bf16[384,1024]{1,0:T(8,128)(2,1)}, bf16[1536,256]{1,0:T(8,128)(2,1)}, bf16[1536,256]{1,0:T(8,128)(2,1)}, f32[896,...) custom-call(s32[1]{0:T(128)} %bitcast.refs_0_.choice_ref, ...), custom_call_target="tpu_custom_call", output_to_operand_aliasing={{0}: (13, {}), {1}: (14, {})} | custom-call | flops 5637144576 | bytes 5505024 | tf_op jit(solution)/shard_map/heads/pallas_call | solution.py:158
  75.9 4.8 %collective-permute-done.6.recv_ref = bf16[896,256]{1,0:T(8,128)(2,1)S(1)} collective-permute-done((bf16[896,256]{1,0:T(8,128)(2,1)S(1)}, bf16[896,256]{1,0:T(8,128)(2,1)S(1)}, u32[]{:S(2)}, u32[]{:S(2)}) %collective-permute-start.6) | collective-permute-done | bytes 458784 | tf_op jit(solution)/shard_map/ppermute | solution.py:23
  81.6 6.6 %heads.6 = (bf16[384,1024]{1,0:T(8,128)(2,1)}, bf16[384,1024]{1,0:T(8,128)(2,1)}, bf16[1536,256]{1,0:T(8,128)(2,1)}, bf16[1536,256]{1,0:T(8,128)(2,1)}, f32[896,...) custom-call(s32[1]{0:T(128)} %bitcast.refs_0_.choice_ref, ...), custom_call_target="tpu_custom_call", output_to_operand_aliasing={{0}: (13, {}), {1}: (14, {})} | custom-call | flops 5637144576 | bytes 5505024 | tf_op jit(solution)/shard_map/heads/pallas_call | solution.py:158
  89.9 3.1 %collective-permute-start.11 = (bf16[224,256]{1,0:T(8,128)(2,1)S(1)}, bf16[224,256]{1,0:T(8,128)(2,1)S(1)}, u32[]{:S(2)}, u32[]{:S(2)}) collective-permute-start(bf16[224,256]{1,0:T(8,128)(2,1)S(1)} %get-tuple-element.80.refs_0_), channel_id=1, source_target_pairs={{0,16},{4,20},{8,24},{12,28},{16,0},{20,4},{24,8},{28,12},{1,17},{... | collective-permute-start | bytes 344072 | tf_op jit(solution)/shard_map/ppermute | solution.py:23
  93.2 6.5 %heads.7 = (bf16[384,1024]{1,0:T(8,128)(2,1)}, bf16[384,1024]{1,0:T(8,128)(2,1)}, bf16[1536,256]{1,0:T(8,128)(2,1)}, bf16[1536,256]{1,0:T(8,128)(2,1)}, f32[896,...) custom-call(s32[1]{0:T(128)} %bitcast.refs_0_.choice_ref, ...), custom_call_target="tpu_custom_call", output_to_operand_aliasing={{0}: (13, {}), {1}: (14, {})} | custom-call | flops 5637144576 | bytes 5505024 | tf_op jit(solution)/shard_map/heads/pallas_call | solution.py:158
  100.5 2.2 %collective-permute-start.15 = (bf16[224,256]{1,0:T(8,128)(2,1)S(1)}, bf16[224,256]{1,0:T(8,128)(2,1)S(1)}, u32[]{:S(2)}, u32[]{:S(2)}) collective-permute-start(bf16[224,256]{1,0:T(8,128)(2,1)S(1)} %add.55.refs_0_.own_ref), channel_id=1, source_target_pairs={{0,16},{4,20},{8,24},{12,28},{16,0},{20,4},{24,8},{28,12},{1,17},{... | collective-permute-start | bytes 344072 | tf_op jit(solution)/shard_map/ppermute | solution.py:23
  105.1 10.1 %state_terms.1 = (bf16[768,896]{1,0:T(8,128)(2,1)S(1)}, bf16[768,896]{1,0:T(8,128)(2,1)S(1)}) custom-call(bf16[1536,256]{1,0:T(8,128)(2,1)} %get-tuple-element.84.refs_0_, bf16[1536,256]{1,0:T(8,128)(2,1)} %get-tuple-element.85.refs_1_, bf16[1536,256]{1,0:T(8,128)(2,1)} %get-tuple-element.86.refs_2_, bf16[1536,256]{1,0:T(8,128)(2,1)} %get-tuple-element.87.refs_3_, ...), custom_call_target="tpu_custom_call" | custom-call | flops 11274289152 | bytes 11010048 | tf_op jit(solution)/shard_map/state_terms/pallas_call | solution.py:245
  116.4 2.2 %collective-permute-start.19 = (bf16[224,256]{1,0:T(8,128)(2,1)S(1)}, bf16[224,256]{1,0:T(8,128)(2,1)S(1)}, u32[]{:S(2)}, u32[]{:S(2)}) collective-permute-start(bf16[224,256]{1,0:T(8,128)(2,1)S(1)} %add.56.refs_0_.own_ref), channel_id=1, source_target_pairs={{0,16},{4,20},{8,24},{12,28},{16,0},{20,4},{24,8},{28,12},{1,17},{... | collective-permute-start | bytes 344072 | tf_op jit(solution)/shard_map/ppermute | solution.py:23
  120.6 8.4 %collective-permute-done.20.recv_ref = bf16[448,256]{1,0:T(8,128)(2,1)S(1)} collective-permute-done((bf16[448,256]{1,0:T(8,128)(2,1)S(1)}, bf16[448,256]{1,0:T(8,128)(2,1)S(1)}, u32[]{:S(2)}, u32[]{:S(2)}) %collective-permute-start.20) | collective-permute-done | bytes 229408 | tf_op jit(solution)/shard_map/ppermute | solution.py:23
  132.2 3.4 %collective-permute-start.23 = (bf16[224,256]{1,0:T(8,128)(2,1)S(1)}, bf16[224,256]{1,0:T(8,128)(2,1)S(1)}, u32[]{:S(2)}, u32[]{:S(2)}) collective-permute-start(bf16[224,256]{1,0:T(8,128)(2,1)S(1)} %add.57.refs_0_.own_ref), channel_id=1, source_target_pairs={{0,16},{4,20},{8,24},{12,28},{16,0},{20,4},{24,8},{28,12},{1,17},{... | collective-permute-start | bytes 344072 | tf_op jit(solution)/shard_map/ppermute | solution.py:23
  137.6 3.3 %collective-permute-done.24.recv_ref = bf16[448,256]{1,0:T(8,128)(2,1)S(1)} collective-permute-done((bf16[448,256]{1,0:T(8,128)(2,1)S(1)}, bf16[448,256]{1,0:T(8,128)(2,1)S(1)}, u32[]{:S(2)}, u32[]{:S(2)}) %collective-permute-start.24) | collective-permute-done | bytes 229408 | tf_op jit(solution)/shard_map/ppermute | solution.py:23
  144.2 5.2 %collective-permute-done.22.recv_ref = bf16[224,256]{1,0:T(8,128)(2,1)S(1)} collective-permute-done((bf16[224,256]{1,0:T(8,128)(2,1)S(1)}, bf16[224,256]{1,0:T(8,128)(2,1)S(1)}, u32[]{:S(2)}, u32[]{:S(2)}) %collective-permute-start.22) | collective-permute-done | bytes 114720 | tf_op jit(solution)/shard_map/ppermute | solution.py:23
  152.7 2.6 %collective-permute-start.25 = (bf16[224,256]{1,0:T(8,128)(2,1)S(1)}, bf16[224,256]{1,0:T(8,128)(2,1)S(1)}, u32[]{:S(2)}, u32[]{:S(2)}) collective-permute-start(bf16[224,256]{1,0:T(8,128)(2,1)S(1)} %add.58.refs_0_.own_ref), channel_id=1, source_target_pairs={{0,16},{4,20},{8,24},{12,28},{16,0},{20,4},{24,8},{28,12},{1,17},{... | collective-permute-start | bytes 344072 | tf_op jit(solution)/shard_map/ppermute | solution.py:23
  155.4 5.5 %collective-permute-done.25.recv_ref = bf16[224,256]{1,0:T(8,128)(2,1)S(1)} collective-permute-done((bf16[224,256]{1,0:T(8,128)(2,1)S(1)}, bf16[224,256]{1,0:T(8,128)(2,1)S(1)}, u32[]{:S(2)}, u32[]{:S(2)}) %collective-permute-start.25) | collective-permute-done | bytes 114720 | tf_op jit(solution)/shard_map/ppermute | solution.py:23
  167.0 3.9 %all-to-all-start.3 = ((bf16[8,2,32,896]{3,2,1,0:T(8,128)(2,1)}), bf16[8,2,32,896]{3,2,1,0:T(8,128)(2,1)S(1)}, u32[]{:S(2)}, u32[]{:S(2)}) async-start(bf16[8,2,32,896]{3,2,1,0:T(8,128)(2,1)} %bitcast.13.refs_2_), calls=%async_computation.3 | async-start | bytes 1835008 | tf_op jit(solution)/shard_map/all_to_all | solution.py:530
  173.0 18.3 %collective-permute-done.31.recv_ref = bf16[896,256]{1,0:T(8,128)(2,1)S(1)} collective-permute-done((bf16[896,256]{1,0:T(8,128)(2,1)S(1)}, bf16[896,256]{1,0:T(8,128)(2,1)S(1)}, u32[]{:S(2)}, u32[]{:S(2)}) %collective-permute-start.31) | collective-permute-done | bytes 458784 | tf_op jit(solution)/shard_map/ppermute | solution.py:23
  (109 shorter events, 49.0 us)
Async XLA Ops:
  3.3 13.7 %all-to-all-start = ((s32[8,1,2]{2,1,0:T(1,128)}), s32[8,1,2]{2,1,0:T(1,128)S(1)}, u32[]{:S(2)}, u32[]{:S(2)}) async-start(s32[8,1,2]{2,1,0:T(1,128)} %bitcast.1), calls=%async_computation | async-start | bytes 8192 | tf_op jit(solution)/shard_map/all_to_all | solution.py:470
  19.6 15.3 %all-to-all-start.1 = ((bf16[8,2,16,896]{3,2,1,0:T(8,128)(2,1)}), bf16[8,2,16,896]{3,2,1,0:T(8,128)(2,1)S(1)}, u32[]{:S(2)}, u32[]{:S(2)}) async-start(bf16[8,2,16,896]{3,2,1,0:T(8,128)(2,1)} %bitcast.2), calls=%async_computation.1 | async-start | bytes 917504 | tf_op jit(solution)/shard_map/all_to_all | solution.py:480
  35.0 16.2 %all-to-all-start.2 = ((bf16[8,2,16,896]{3,2,1,0:T(8,128)(2,1)}), bf16[8,2,16,896]{3,2,1,0:T(8,128)(2,1)S(1)}, u32[]{:S(2)}, u32[]{:S(2)}) async-start(bf16[8,2,16,896]{3,2,1,0:T(8,128)(2,1)} %bitcast.7), calls=%async_computation.2 | async-start | bytes 917504 | tf_op jit(solution)/shard_map/all_to_all | solution.py:480
  39.5 11.7 %collective-permute-start = (bf16[192,896]{1,0:T(8,128)(2,1)S(1)}, bf16[192,896]{1,0:T(8,128)(2,1)S(1)}, u32[]{:S(2)}, u32[]{:S(2)}) collective-permute-start(bf16[192,896]{1,0:T(8,128)(2,1)S(1)} %bitcast.21), channel_id=1, source_target_pairs={{0,2},{1,3},{2,0},{3,1},{4,6},{5,7},{6,4},{7,5},{8,10},{9,11},{10,... | collective-permute-start | bytes 1032200 | tf_op jit(solution)/shard_map/ppermute | solution.py:23
  67.2 13.4 %collective-permute-start.6 = (bf16[896,256]{1,0:T(8,128)(2,1)S(1)}, bf16[896,256]{1,0:T(8,128)(2,1)S(1)}, u32[]{:S(2)}, u32[]{:S(2)}) collective-permute-start(bf16[896,256]{1,0:T(8,128)(2,1)S(1)} %get-tuple-element.69.refs_15_), channel_id=1, source_target_pairs={{0,4},{4,0},{8,12},{12,8},{16,20},{20,16},{24,28},{28,24},{1,5},{5... | collective-permute-start | bytes 1376264 | tf_op jit(solution)/shard_map/ppermute | solution.py:23
  75.2 17.8 %collective-permute-start.7 = (bf16[896,256]{1,0:T(8,128)(2,1)S(1)}, bf16[896,256]{1,0:T(8,128)(2,1)S(1)}, u32[]{:S(2)}, u32[]{:S(2)}) collective-permute-start(bf16[896,256]{1,0:T(8,128)(2,1)S(1)} %get-tuple-element.73.refs_0_), channel_id=1, source_target_pairs={{0,4},{4,0},{8,12},{12,8},{16,20},{20,16},{24,28},{28,24},{1,5},{5... | collective-permute-start | bytes 1376264 | tf_op jit(solution)/shard_map/ppermute | solution.py:23
  88.2 15.4 %collective-permute-start.9 = (bf16[896,256]{1,0:T(8,128)(2,1)S(1)}, bf16[896,256]{1,0:T(8,128)(2,1)S(1)}, u32[]{:S(2)}, u32[]{:S(2)}) collective-permute-start(bf16[896,256]{1,0:T(8,128)(2,1)S(1)} %get-tuple-element.79.refs_0_), channel_id=1, source_target_pairs={{0,4},{4,0},{8,12},{12,8},{16,20},{20,16},{24,28},{28,24},{1,5},{5... | collective-permute-start | bytes 1376264 | tf_op jit(solution)/shard_map/ppermute | solution.py:23
  89.9 10.5 %collective-permute-start.11 = (bf16[224,256]{1,0:T(8,128)(2,1)S(1)}, bf16[224,256]{1,0:T(8,128)(2,1)S(1)}, u32[]{:S(2)}, u32[]{:S(2)}) collective-permute-start(bf16[224,256]{1,0:T(8,128)(2,1)S(1)} %get-tuple-element.80.refs_0_), channel_id=1, source_target_pairs={{0,16},{4,20},{8,24},{12,28},{16,0},{20,4},{24,8},{28,12},{1,17},{... | collective-permute-start | bytes 344072 | tf_op jit(solution)/shard_map/ppermute | solution.py:23
  99.7 15.6 %collective-permute-start.14 = (bf16[896,256]{1,0:T(8,128)(2,1)S(1)}, bf16[896,256]{1,0:T(8,128)(2,1)S(1)}, u32[]{:S(2)}, u32[]{:S(2)}) collective-permute-start(bf16[896,256]{1,0:T(8,128)(2,1)S(1)} %get-tuple-element.95.refs_0_), channel_id=1, source_target_pairs={{0,4},{4,0},{8,12},{12,8},{16,20},{20,16},{24,28},{28,24},{1,5},{5... | collective-permute-start | bytes 1376264 | tf_op jit(solution)/shard_map/ppermute | solution.py:23
  100.5 14.8 %collective-permute-start.15 = (bf16[224,256]{1,0:T(8,128)(2,1)S(1)}, bf16[224,256]{1,0:T(8,128)(2,1)S(1)}, u32[]{:S(2)}, u32[]{:S(2)}) collective-permute-start(bf16[224,256]{1,0:T(8,128)(2,1)S(1)} %add.55.refs_0_.own_ref), channel_id=1, source_target_pairs={{0,16},{4,20},{8,24},{12,28},{16,0},{20,4},{24,8},{28,12},{1,17},{... | collective-permute-start | bytes 344072 | tf_op jit(solution)/shard_map/ppermute | solution.py:23
  102.7 12.8 %collective-permute-start.12 = (bf16[224,256]{1,0:T(8,128)(2,1)S(1)}, bf16[224,256]{1,0:T(8,128)(2,1)S(1)}, u32[]{:S(2)}, u32[]{:S(2)}) collective-permute-start(bf16[224,256]{1,0:T(8,128)(2,1)S(1)} %get-tuple-element.96.refs_0_), channel_id=1, source_target_pairs={{0,16},{4,20},{8,24},{12,28},{16,0},{20,4},{24,8},{28,12},{1,17},{... | collective-permute-start | bytes 344072 | tf_op jit(solution)/shard_map/ppermute | solution.py:23
  103.7 11.7 %collective-permute-start.13 = (bf16[448,256]{1,0:T(8,128)(2,1)S(1)}, bf16[448,256]{1,0:T(8,128)(2,1)S(1)}, u32[]{:S(2)}, u32[]{:S(2)}) collective-permute-start(bf16[448,256]{1,0:T(8,128)(2,1)S(1)} %get-tuple-element.97.refs_10_), channel_id=1, source_target_pairs={{0,8},{4,12},{8,0},{12,4},{16,24},{20,28},{24,16},{28,20},{1,9},{5... | collective-permute-start | bytes 688136 | tf_op jit(solution)/shard_map/ppermute | solution.py:23
  115.5 20.2 %collective-permute-start.16 = (bf16[768,896]{1,0:T(8,128)(2,1)S(1)}, bf16[768,896]{1,0:T(8,128)(2,1)S(1)}, u32[]{:S(2)}, u32[]{:S(2)}) collective-permute-start(bf16[768,896]{1,0:T(8,128)(2,1)S(1)} %get-tuple-element.105.refs_0_), channel_id=1, source_target_pairs={{0,1},{1,0},{2,3},{3,2},{4,5},{5,4},{6,7},{7,6},{8,9},{9,8},{10,11... | collective-permute-start | bytes 4128776 | tf_op jit(solution)/shard_map/ppermute | solution.py:23
  115.6 13.4 %collective-permute-start.20 = (bf16[448,256]{1,0:T(8,128)(2,1)S(1)}, bf16[448,256]{1,0:T(8,128)(2,1)S(1)}, u32[]{:S(2)}, u32[]{:S(2)}) collective-permute-start(bf16[448,256]{1,0:T(8,128)(2,1)S(1)} %join.8.refs_0_.own_ref), channel_id=1, source_target_pairs={{0,8},{4,12},{8,0},{12,4},{16,24},{20,28},{24,16},{28,20},{1,9},{5... | collective-permute-start | bytes 688136 | tf_op jit(solution)/shard_map/ppermute | solution.py:23
  116.4 12.7 %collective-permute-start.19 = (bf16[224,256]{1,0:T(8,128)(2,1)S(1)}, bf16[224,256]{1,0:T(8,128)(2,1)S(1)}, u32[]{:S(2)}, u32[]{:S(2)}) collective-permute-start(bf16[224,256]{1,0:T(8,128)(2,1)S(1)} %add.56.refs_0_.own_ref), channel_id=1, source_target_pairs={{0,16},{4,20},{8,24},{12,28},{16,0},{20,4},{24,8},{28,12},{1,17},{... | collective-permute-start | bytes 344072 | tf_op jit(solution)/shard_map/ppermute | solution.py:23
  118.5 17.1 %collective-permute-start.17 = (bf16[448,256]{1,0:T(8,128)(2,1)S(1)}, bf16[448,256]{1,0:T(8,128)(2,1)S(1)}, u32[]{:S(2)}, u32[]{:S(2)}) collective-permute-start(bf16[448,256]{1,0:T(8,128)(2,1)S(1)} %get-tuple-element.103.refs_0_), channel_id=1, source_target_pairs={{0,8},{4,12},{8,0},{12,4},{16,24},{20,28},{24,16},{28,20},{1,9},{5... | collective-permute-start | bytes 688136 | tf_op jit(solution)/shard_map/ppermute | solution.py:23
  118.6 13.6 %collective-permute-start.18 = (bf16[224,256]{1,0:T(8,128)(2,1)S(1)}, bf16[224,256]{1,0:T(8,128)(2,1)S(1)}, u32[]{:S(2)}, u32[]{:S(2)}) collective-permute-start(bf16[224,256]{1,0:T(8,128)(2,1)S(1)} %get-tuple-element.104.refs_0_), channel_id=1, source_target_pairs={{0,16},{4,20},{8,24},{12,28},{16,0},{20,4},{24,8},{28,12},{1,17},{... | collective-permute-start | bytes 344072 | tf_op jit(solution)/shard_map/ppermute | solution.py:23
  129.1 11.8 %collective-permute-start.24 = (bf16[448,256]{1,0:T(8,128)(2,1)S(1)}, bf16[448,256]{1,0:T(8,128)(2,1)S(1)}, u32[]{:S(2)}, u32[]{:S(2)}) collective-permute-start(bf16[448,256]{1,0:T(8,128)(2,1)S(1)} %join.10.refs_0_.own_ref), channel_id=1, source_target_pairs={{0,8},{4,12},{8,0},{12,4},{16,24},{20,28},{24,16},{28,20},{1,9},{5... | collective-permute-start | bytes 688136 | tf_op jit(solution)/shard_map/ppermute | solution.py:23
  129.2 20.3 %collective-permute-start.27 = (bf16[896,256]{1,0:T(8,128)(2,1)S(1)}, bf16[896,256]{1,0:T(8,128)(2,1)S(1)}, u32[]{:S(2)}, u32[]{:S(2)}) collective-permute-start(bf16[896,256]{1,0:T(8,128)(2,1)S(1)} %join.9.refs_0_.own_ref), channel_id=1, source_target_pairs={{0,4},{4,0},{8,12},{12,8},{16,20},{20,16},{24,28},{28,24},{1,5},{5... | collective-permute-start | bytes 1376264 | tf_op jit(solution)/shard_map/ppermute | solution.py:23
  136.0 25.4 %collective-permute-start.21 = (bf16[384,896]{1,0:T(8,128)(2,1)S(1)}, bf16[384,896]{1,0:T(8,128)(2,1)S(1)}, u32[]{:S(2)}, u32[]{:S(2)}) collective-permute-start(bf16[384,896]{1,0:T(8,128)(2,1)S(1)} %get-tuple-element.110.refs_0_), channel_id=1, source_target_pairs={{0,2},{1,3},{2,0},{3,1},{4,6},{5,7},{6,4},{7,5},{8,10},{9,11},{10,... | collective-permute-start | bytes 2064392 | tf_op jit(solution)/shard_map/ppermute | solution.py:23
  143.8 19.3 %collective-permute-start.30 = (bf16[896,256]{1,0:T(8,128)(2,1)S(1)}, bf16[896,256]{1,0:T(8,128)(2,1)S(1)}, u32[]{:S(2)}, u32[]{:S(2)}) collective-permute-start(bf16[896,256]{1,0:T(8,128)(2,1)S(1)} %join.11.refs_0_.own_ref), channel_id=1, source_target_pairs={{0,4},{4,0},{8,12},{12,8},{16,20},{20,16},{24,28},{28,24},{1,5},{5... | collective-permute-start | bytes 1376264 | tf_op jit(solution)/shard_map/ppermute | solution.py:23
  150.9 14.3 %collective-permute-start.29 = (bf16[896,256]{1,0:T(8,128)(2,1)S(1)}, bf16[896,256]{1,0:T(8,128)(2,1)S(1)}, u32[]{:S(2)}, u32[]{:S(2)}) collective-permute-start(bf16[896,256]{1,0:T(8,128)(2,1)S(1)} %join.13.refs_0_.own_ref), channel_id=1, source_target_pairs={{0,4},{4,0},{8,12},{12,8},{16,20},{20,16},{24,28},{28,24},{1,5},{5... | collective-permute-start | bytes 1376264 | tf_op jit(solution)/shard_map/ppermute | solution.py:23
  167.0 25.6 %all-to-all-start.3 = ((bf16[8,2,32,896]{3,2,1,0:T(8,128)(2,1)}), bf16[8,2,32,896]{3,2,1,0:T(8,128)(2,1)S(1)}, u32[]{:S(2)}, u32[]{:S(2)}) async-start(bf16[8,2,32,896]{3,2,1,0:T(8,128)(2,1)} %bitcast.13.refs_2_), calls=%async_computation.3 | async-start | bytes 1835008 | tf_op jit(solution)/shard_map/all_to_all | solution.py:530
  170.9 20.4 %collective-permute-start.31 = (bf16[896,256]{1,0:T(8,128)(2,1)S(1)}, bf16[896,256]{1,0:T(8,128)(2,1)S(1)}, u32[]{:S(2)}, u32[]{:S(2)}) collective-permute-start(bf16[896,256]{1,0:T(8,128)(2,1)S(1)} %join.15.own_ref.refs_2_), channel_id=1, source_target_pairs={{0,4},{4,0},{8,12},{12,8},{16,20},{20,16},{24,28},{28,24},{1,5},{5... | collective-permute-start | bytes 1376264 | tf_op jit(solution)/shard_map/ppermute | solution.py:23
  (13 other events, 122.5 us)
